TPU v7x, 256 devices: a whole 4x4x8 slice. The times are simulated.
256 devices in a mesh: table: 8 (over y, core), seq: 8 (over z), tensor: 4 (over x).
Axes of the slice: x: 4, y: 4, z: 8, core: 2. Of those that a mesh axis runs over, the one named last changes fastest.
Arguments:
- table: bfloat16 [131072, 512], P(('table', 'seq'), 'tensor'), may hold values from -6 to 6
- owner: int32 [65536, 1], P(('table', 'seq')), may hold values from 0 to 63; in each aligned block of 1024 rows (0 to 1023, 1024 to 2047, ...) at most 24 rows name the same one
- local_row: int32 [65536], P(('table', 'seq')), may hold values from 0 to 2047
- segment_ids: int32 [64, 1024], P(('table', 'seq')), may hold values from 0 to 3, never falling along the last dimension, each value on 1 to 512 neighbouring positions
- proj_in: bfloat16 [4, 512, 512], P(None, None, 'tensor'), may hold values from -0.25 to 0.25
- proj_out: bfloat16 [512, 512], P('tensor'), may hold values from -0.25 to 0.25
- grad_out: bfloat16 [65536, 512], P(('table', 'seq'), 'tensor'), may hold values from -6 to 6
Outputs:
- layer_out: bfloat16 [65536, 512], P(('table', 'seq'), 'tensor')
- table_grad: float32 [131072, 512], P(('table', 'seq'), 'tensor')
- proj_in_grad: float32 [4, 512, 512], P(None, None, 'tensor')
- proj_out_grad: float32 [512, 512], P('tensor')
Inputs may be any that keep to these rules, and one draw needn't show every extreme that they name: Among the events of one owner block, each owner is named at most 24 times, a bound that some block reaches. `segment_ids`: within a row, ids never fall; each history has 1 to 512 events, one exactly 512.
All inputs are finite; a program needn't handle non-finite values.
Results may differ from a plain program's by a relative error of at most 0.02.
Values may be sent and summed in bfloat16 or wider, within the bound.
No kernel may reach another device: no remote copies, remote signals or barrier semaphores. Data moves between devices by JAX's collectives and lax.ppermute only.
A program may use at most 64 MiB of HBM per device.

v0:
```python
import jax
import jax.numpy as jnp
from jax import lax
from jax.sharding import PartitionSpec as P

HD = 128
SEQ_MOST = 512


def norm_parts(xf):
    mean = jnp.mean(xf, axis=1, keepdims=True)
    var = jnp.mean((xf - mean) ** 2, axis=1, keepdims=True)
    return (mean, lax.rsqrt(var + 1e-05))


def branch_mixed(normed, w_in, seg):
    tok = normed.shape[0]
    parts = [
        jax.nn.silu(jnp.dot(normed, w_in[c], preferred_element_type=jnp.float32)).astype(
            jnp.bfloat16
        )
        for c in range(4)
    ]
    gate_part, values, queries, keys = parts
    block = min(512, tok)
    position = jnp.arange(tok)
    pieces = []
    for start in range(0, tok, block):
        query_block = queries[start : start + block, 0:HD]
        scores = jnp.dot(query_block, keys.T, preferred_element_type=jnp.float32) * HD ** (-0.5)
        qpos = position[start : start + block]
        allowed = (seg[start : start + block][:, None] == seg[None, :]) & (
            position[None, :] <= qpos[:, None]
        )
        weights = (jnp.where(allowed, jax.nn.silu(scores), 0.0) / SEQ_MOST).astype(jnp.bfloat16)
        pieces.append(jnp.dot(weights, values, preferred_element_type=jnp.float32))
    attended = jnp.concatenate(pieces, axis=0)
    head_mean = jnp.mean(attended, axis=1, keepdims=True)
    head_var = jnp.mean((attended - head_mean) ** 2, axis=1, keepdims=True)
    head_outs = [(attended - head_mean) * lax.rsqrt(head_var + 1e-05)]
    return (jnp.concatenate(head_outs, axis=1) * gate_part.astype(jnp.float32)).astype(jnp.bfloat16)


def branch(xf, w_in, w_out, seg):
    mean, scale = norm_parts(xf)
    normed = ((xf - mean) * scale).astype(jnp.bfloat16)
    mixed = branch_mixed(normed, w_in, seg)
    return jnp.dot(mixed, w_out, preferred_element_type=jnp.float32)


def send_requests(requests):
    return lax.all_to_all(requests, ("table", "seq"), split_axis=0, concat_axis=0, tiled=True)


def send_rows(fetched):
    return lax.all_to_all(fetched, ("table", "seq"), split_axis=0, concat_axis=0, tiled=True)


def send_grads(slot_grads):
    return lax.all_to_all(
        slot_grads.astype(jnp.bfloat16), ("table", "seq"), split_axis=0, concat_axis=0, tiled=True
    ).astype(slot_grads.dtype)


def body(table, owner, local_row, segment_ids, proj_in, proj_out, grad_out):
    owners = lax.axis_size(("table", "seq"))
    tok = local_row.shape[0]
    width = table.shape[1]
    capacity = max(2, 3 * tok // (2 * owners))
    target = owner[:, 0]
    onehot = (target[:, None] == jnp.arange(owners, dtype=jnp.int32)[None, :]).astype(jnp.int32)
    earlier = jnp.cumsum(onehot, axis=0) - onehot
    rank_in = jnp.sum(earlier * onehot, axis=1)
    slot = target * capacity + rank_in
    requests = (
        jnp.zeros((owners * capacity,), jnp.int32).at[slot].set(local_row).reshape(owners, capacity)
    )
    received = send_requests(requests)
    fetched = table[received.reshape(-1)].reshape(owners, capacity, width)
    returned = send_rows(fetched)
    x_local = returned.reshape(owners * capacity, width)[slot]
    x_full, g_full = (
        lax.all_gather(x_local, "tensor", axis=1, tiled=True),
        lax.all_gather(grad_out, "tensor", axis=1, tiled=True),
    )
    xf = x_full.astype(jnp.float32)
    seg = segment_ids[0]
    result, pull = jax.vjp(lambda a, b, c: branch(a, b, c, seg), xf, proj_in, proj_out)
    out_part = lax.psum_scatter(
        result.astype(jnp.bfloat16), "tensor", scatter_dimension=1, tiled=True
    ).astype(jnp.float32)
    d_x, d_in, d_out = pull(g_full.astype(jnp.float32))
    dx_part = lax.psum_scatter(
        d_x.astype(jnp.bfloat16), "tensor", scatter_dimension=1, tiled=True
    ).astype(jnp.float32)
    layer_out = (x_local.astype(jnp.float32) + out_part).astype(jnp.bfloat16)
    dx_local = grad_out.astype(jnp.float32) + dx_part
    slot_grads = (
        jnp.zeros((owners * capacity, width), jnp.float32)
        .at[slot]
        .set(dx_local)
        .reshape(owners, capacity, width)
    )
    arrived = send_grads(slot_grads)
    table_grad = (
        jnp.zeros(table.shape, jnp.float32)
        .at[received.reshape(-1)]
        .add(arrived.reshape(owners * capacity, width))
    )
    grad_in, grad_outw = lax.psum(
        (d_in.astype(jnp.float32), d_out.astype(jnp.float32)), ("table", "seq")
    )
    return (layer_out, table_grad, grad_in, grad_outw)


def solution(mesh):
    in_specs = (
        P(("table", "seq"), "tensor"),
        P(("table", "seq"), None),
        P(("table", "seq")),
        P(("table", "seq"), None),
        P(None, None, "tensor"),
        P("tensor", None),
        P(("table", "seq"), "tensor"),
    )
    out_specs = (
        P(("table", "seq"), "tensor"),
        P(("table", "seq"), "tensor"),
        P(None, None, "tensor"),
        P("tensor", None),
    )
    return jax.shard_map(body, mesh=mesh, in_specs=in_specs, out_specs=out_specs, check_vma=False)
```

profile of v0, /device:TPU:1, one launch (start us, length us, event | category | flops | bytes accessed | tf_op | source)
XLA Modules:
  0.0 409.5 jit_solution(13354178367828148336)
XLA Ops:
  8.0 18.0 %reduce-window.6 = s32[64,8,128]{2,1,0:T(8,128)S(1)} reduce-window(s32[64,8,128]{2,1,0:T(8,128)S(1)} %fusion.51, s32[]{:T(128)} %constant.47.clone.1), window={size=1x1x128 pad=0_0x0_0x127_0}, to_apply=%region_0.0 | reduce-window | flops 8323072 | bytes 524292 | tf_op jit(solution)/shard_map/reduce-window
  26.6 4.5 %scatter_custom_fusion = s32[1536]{0:T(1024)S(1)} fusion(s32[1024]{0:T(1024)S(1)} %bitcast.107, s32[1024]{0:T(1024)} %param.9, s32[]{:T(128)} %constant.47.clone.1), kind=kCustom, calls=%fused_computation.160 | custom fusion | bytes 6656 | tf_op jit(solution)/shard_map/scatter | solution.py:76
  31.2 22.2 %all_to_all.19 = s32[64,1,24]{2,1,0:T(1,128)S(1)} all-to-all(s32[64,1,24]{2,1,0:T(1,128)S(1)} %bitcast.102), channel_id=1, replica_groups=mesh['table'=8,'seq'=8,'tensor'=4] {'table','seq'}, dimensions={0} | all-to-all | bytes 12288 | tf_op jit(solution)/shard_map/all_to_all | solution.py:52
  55.4 4.1 gather_fusion
  59.4 5.1 %all-to-all-start.1 = ((bf16[64,24,128]{2,1,0:T(8,128)(2,1)}), bf16[64,24,128]{2,1,0:T(8,128)(2,1)S(1)}, u32[]{:S(2)}, u32[]{:S(2)}) async-start(bf16[64,24,128]{2,1,0:T(8,128)(2,1)} %bitcast.7), calls=%async_computation.1 | async-start | bytes 786432 | tf_op jit(solution)/shard_map/all_to_all | solution.py:56
  64.6 14.8 %all-to-all-done.1 = bf16[64,24,128]{2,1,0:T(8,128)(2,1)S(1)} async-done(((bf16[64,24,128]{2,1,0:T(8,128)(2,1)}), bf16[64,24,128]{2,1,0:T(8,128)(2,1)S(1)}, u32[]{:S(2)}, u32[]{:S(2)}) %all-to-all-start.1) | async-done | bytes 393248 | tf_op jit(solution)/shard_map/all_to_all | solution.py:56
  79.4 3.2 gather_fusion.1
  84.6 21.4 %all-gather.6.cloned.1.call-done = bf16[1024,512]{0,1:T(8,128)(2,1)} async-done(((bf16[1024,128]{0,1:T(8,128)(2,1)}), bf16[1024,512]{0,1:T(8,128)(2,1)}) %all-gather.6.cloned.1.call-update) | async-done | bytes 1048592 | tf_op jit(solution)/shard_map/all_gather | solution.py:83
  105.9 1.5 convert_reduce_fusion
  107.4 1.5 fusion.8
  109.0 1.3 multiply_convert_fusion.6
  110.3 1.3 multiply_convert_fusion.5
  112.1 3.1 multiply_convert_fusion.1
  115.3 1.3 multiply_convert_fusion.4
  118.7 2.2 fusion.57
  120.9 15.6 %all-gather.4.cloned.1.call-done = bf16[1024,512]{1,0:T(8,128)(2,1)} async-done(((bf16[1024,128]{1,0:T(8,128)(2,1)}), bf16[1024,512]{1,0:T(8,128)(2,1)}) %all-gather.4.cloned.1.call-update) | async-done | bytes 1048592 | tf_op jit(solution)/shard_map/all_gather | solution.py:84
  136.6 2.1 multiply_reduce_fusion.3
  138.7 1.2 multiply_reduce_fusion.2
  141.1 1.7 fusion.13
  142.9 2.0 fusion.16
  152.1 1.5 fusion.7
  154.1 1.3 copy.38
  155.6 1.4 fusion.28
  160.0 20.3 %reduce-scatter.5.cloned.1.call-done = bf16[1024,128]{0,1:T(8,128)(2,1)} async-done(((bf16[1024,512]{0,1:T(8,128)(2,1)}), bf16[1024,128]{0,1:T(8,128)(2,1)}) %reduce-scatter.5.cloned.1.call-update) | async-done | bytes 262160 | tf_op jit(solution)/shard_map/reduce_scatter | solution.py:93
  181.6 3.4 scatter_custom_fusion.1
  185.8 12.1 %all-to-all-start.2 = ((bf16[64,24,128]{2,1,0:T(8,128)(2,1)}), bf16[64,24,128]{2,1,0:T(8,128)(2,1)S(1)}, u32[]{:S(2)}, u32[]{:S(2)}) async-start(bf16[64,24,128]{2,1,0:T(8,128)(2,1)} %bitcast.16), calls=%async_computation.3 | async-start | bytes 786432 | tf_op jit(solution)/shard_map/all_to_all | solution.py:60
  198.9 10.4 %reduce-scatter.7.cloned.1.call-done = bf16[128,1024]{1,0:T(8,128)(2,1)} async-done(((bf16[512,1024]{1,0:T(8,128)(2,1)}), bf16[128,1024]{1,0:T(8,128)(2,1)}) %reduce-scatter.7.cloned.1.call-update) | async-done | bytes 262160
  209.4 1.1 copy.39
  211.3 1.3 all-to-all-done.2
  212.6 9.9 %scatter_custom_fusion.2 = f32[2048,128]{1,0:T(8,128)} fusion(s32[1536]{0:T(1024)} %copy-done.31, bf16[1536,128]{1,0:T(8,128)(2,1)S(1)} %bitcast.99, f32[]{:T(128)} %constant.51.clone.1), kind=kCustom, calls=%fused_computation.68 | custom fusion | flops 393216 | bytes 1442304 | tf_op jit(solution)/shard_map/scatter-add | solution.py:108
  222.5 177.4 %all-reduce.9.cloned.1.call-done = (f32[4,512,128]{2,1,0:T(8,128)}, f32[128,512]{1,0:T(8,128)}) async-done(((f32[4,512,128]{2,1,0:T(8,128)}, f32[128,512]{1,0:T(8,128)}), (f32[4,512,128]{2,1,0:T(8,128)}, f32[128,512]{1,0:T(8,128)})) %all-reduce.9.cloned.1.call-update) | async-done | bytes 1310736 | tf_op jit(solution)/shard_map/psum | solution.py:110
  399.9 2.3 copy.44
  (171 shorter events, 24.1 us)
Async XLA Ops:
  7.2 48.2 %copy-start = (bf16[2048,128]{1,0:T(8,128)(2,1)S(1)}, bf16[2048,128]{1,0:T(8,128)(2,1)}, u32[]{:S(2)}) copy-start(bf16[2048,128]{1,0:T(8,128)(2,1)} %param.7) | copy-start | bytes 1572868
  7.2 19.3 %copy-start.28 = (s32[1024,1]{0,1:T(1,128)S(1)}, s32[1024,1]{0,1:T(1,128)}, u32[]{:S(2)}) copy-start(s32[1024,1]{0,1:T(1,128)} %param.8) | copy-start | bytes 12292
  26.6 37.9 %copy-start.34 = (s32[1024,1]{0,1:T(1,128)}, s32[1024,1]{0,1:T(1,128)S(1)}, u32[]{:S(2)}) copy-start(s32[1024,1]{0,1:T(1,128)S(1)} %compare_select_fusion.1) | copy-start | bytes 12292
  59.4 25.0 %copy-start.35 = (s32[1,1024]{1,0:T(1,128)S(1)}, s32[1,1024]{1,0:T(1,128)}, u32[]{:S(2)}) copy-start(s32[1,1024]{1,0:T(1,128)} %param.10) | copy-start | bytes 12292
  59.4 20.0 %all-to-all-start.1 = ((bf16[64,24,128]{2,1,0:T(8,128)(2,1)}), bf16[64,24,128]{2,1,0:T(8,128)(2,1)S(1)}, u32[]{:S(2)}, u32[]{:S(2)}) async-start(bf16[64,24,128]{2,1,0:T(8,128)(2,1)} %bitcast.7), calls=%async_computation.1 | async-start | bytes 786432 | tf_op jit(solution)/shard_map/all_to_all | solution.py:56
  64.5 41.4 %all-gather.6.cloned.1.call-start = ((), (), s32[]{:S(2)}) async-start(), calls=%async_computation.7 | async-start | bytes 1310720 | tf_op jit(solution)/shard_map/all_gather | solution.py:83
  82.6 26.4 %copy-start.21 = (bf16[4,512,128]{2,1,0:T(8,128)(2,1)S(1)}, bf16[4,512,128]{2,1,0:T(8,128)(2,1)}, u32[]{:S(2)}) copy-start(bf16[4,512,128]{2,1,0:T(8,128)(2,1)} %param.11) | copy-start | bytes 1572868
  83.5 53.1 %all-gather.4.cloned.1.call-start = ((), (), s32[]{:S(2)}) async-start(), calls=%async_computation.5 | async-start | bytes 1310720 | tf_op jit(solution)/shard_map/all_gather | solution.py:84
  84.2 96.1 %reduce-scatter.5.cloned.1.call-start = ((), (), s32[]{:S(2)}) async-start(), calls=%async_computation.6 | async-start | bytes 1310720 | tf_op jit(solution)/shard_map/reduce_scatter | solution.py:93
  84.5 27.6 %copy-start.41 = (s32[1,512]{1,0:T(1,128)}, s32[1,512]{1,0:T(1,128)S(1)}, u32[]{:S(2)}) copy-start(s32[1,512]{1,0:T(1,128)S(1)} %get-tuple-element.17) | copy-start | bytes 6148
  84.5 27.6 %copy-start.43 = (s32[1,512]{1,0:T(1,128)}, s32[1,512]{1,0:T(1,128)S(1)}, u32[]{:S(2)}) copy-start(s32[1,512]{1,0:T(1,128)S(1)} %get-tuple-element.18) | copy-start | bytes 6148
  84.5 27.6 %copy-start.37 = (s32[512]{0:T(512)}, s32[512]{0:T(512)S(1)}, u32[]{:S(2)}) copy-start(s32[512]{0:T(512)S(1)} %slice.41) | copy-start | bytes 6148
  84.6 27.5 %copy-start.39 = (s32[512]{0:T(512)}, s32[512]{0:T(512)S(1)}, u32[]{:S(2)}) copy-start(s32[512]{0:T(512)S(1)} %slice.47) | copy-start | bytes 6148
  105.9 3.1 copy-start.1
  109.0 9.1 %copy-start.32 = (f32[1024]{0:T(1024)}, f32[1024]{0:T(1024)S(1)}, u32[]{:S(2)}) copy-start(f32[1024]{0:T(1024)S(1)} %fusion.85) | copy-start | bytes 12292
  111.6 3.6 copy-start.2
  112.1 3.2 copy-start.5
  117.0 19.5 %copy-start.23 = (bf16[128,512]{1,0:T(8,128)(2,1)S(1)}, bf16[128,512]{1,0:T(8,128)(2,1)}, u32[]{:S(2)}) copy-start(bf16[128,512]{1,0:T(8,128)(2,1)} %param.12) | copy-start | bytes 393220
  136.6 3.4 copy-start.15
  138.7 2.4 copy-start.6
  138.7 2.4 copy-start.14
  138.7 2.4 copy-start.36
  138.7 2.4 copy-start.40
  138.7 2.4 copy-start.44
  141.0 7.4 %copy-start.11 = (bf16[1024,128]{1,0:T(8,128)(2,1)}, bf16[1024,128]{1,0:T(8,128)(2,1)S(1)}, u32[]{:S(2)}) copy-start(bf16[1024,128]{1,0:T(8,128)(2,1)S(1)} %get-tuple-element.12) | copy-start | bytes 786436
  142.9 2.5 copy-start.3
  145.9 3.7 copy-start.24
  146.8 2.8 copy-start.26
  153.6 55.8 %reduce-scatter.7.cloned.1.call-start = ((), (), s32[]{:S(2)}) async-start(), calls=%async_computation.8 | async-start | bytes 1310720
  185.8 26.9 %all-to-all-start.2 = ((bf16[64,24,128]{2,1,0:T(8,128)(2,1)}), bf16[64,24,128]{2,1,0:T(8,128)(2,1)S(1)}, u32[]{:S(2)}, u32[]{:S(2)}) async-start(bf16[64,24,128]{2,1,0:T(8,128)(2,1)} %bitcast.16), calls=%async_computation.3 | async-start | bytes 786432 | tf_op jit(solution)/shard_map/all_to_all | solution.py:60
  197.8 202.1 %all-reduce.9.cloned.1.call-start = ((), (), s32[]{:S(2)}) async-start(), calls=%async_computation.9 | async-start | bytes 2621440 | tf_op jit(solution)/shard_map/psum | solution.py:110
  399.9 2.3 copy-start.16
  (26 other events, 40.3 us)
Sparse Core Ops, SparseCore 0:
  83.6 22.2 all-gather.5
  107.7 28.7 all-gather.3
  153.7 26.5 reduce-scatter.4
  183.5 25.8 reduce-scatter.6
  213.3 186.5 all-reduce.8
where the time goes:
time: 411 us; the launch traced here: 409 us
  waiting for transfers between devices  262 us (64%)
  other arithmetic  41.1 us (10%)
  matrix products  26.1 us (6%)
  local copies, waits for them, and re-layouts  25.8 us (6%)
  blocking collectives  22.2 us (5%)
  starting transfers between devices  17.5 us (4%)
  between operations  14.7 us (4%)
    psum x1, waiting for transfers between devices, body(): lax.psum((d_in.astype(jnp.float32), d_out.astype(jnp.float32)), ('table',...  177 us
    all_to_all x1, blocking collectives, send_requests(): lax.all_to_all(requests, ('table', 'seq'), split_axis=0, concat_axis=0, t...  22.2 us
    all_gather x1, waiting for transfers between devices, body(): lax.all_gather(x_local, 'tensor', axis=1, tiled=True)  21.4 us
    reduce_scatter x1, waiting for transfers between devices, body(): lax.psum_scatter(d_x.astype(jnp.bfloat16), 'tensor', scatter_dimension=1,...  20.3 us
    another operation x3, other arithmetic  18.2 us
    all_gather x1, waiting for transfers between devices, body(): lax.all_gather(grad_out, 'tensor', axis=1, tiled=True)  15.6 us
    all_to_all x1, waiting for transfers between devices, send_rows(): lax.all_to_all(fetched, ('table', 'seq'), split_axis=0, concat_axis=0, ti...  14.8 us
    all_to_all x1, starting transfers between devices, send_grads(): lax.all_to_all(slot_grads.astype(jnp.bfloat16), ('table', 'seq'), split_a...  12.1 us
  transfers between devices with their start and end apart: 7, of which 7 were waited for; matrix products, arithmetic and copies ran while one was open for 9% of the time, Pallas kernels for 0%

commit v1 on v0

v1 whole, which is shorter than its diff:
```python
import functools

import jax
import jax.numpy as jnp
from jax import lax
from jax.experimental import pallas as pl
from jax.experimental.pallas import tpu as pltpu
from jax.sharding import PartitionSpec as P

HD = 128
SEQ_MOST = 512
TOK = 1024
D = 512
NT = 4
NOWN = 64
CAP = 24
SLOTS = NOWN * CAP
ROWS = 2048
QB = 256
BOTH = ("table", "seq")
BF = jnp.bfloat16
F32 = jnp.float32
I32 = jnp.int32
VM = pl.BlockSpec(memory_space=pltpu.VMEM)
SM = pl.BlockSpec(memory_space=pltpu.SMEM)
PARAMS = pltpu.CompilerParams(vmem_limit_bytes=56 * 1024 * 1024)


def iota(shape, dim):
    return lax.broadcasted_iota(I32, shape, dim)


def dot(a, b, ca, cb):
    return lax.dot_general(a, b, (((ca,), (cb,)), ((), ())), preferred_element_type=F32)


def route_kernel(owner_ref, row_ref, req_ref, slot_ref):
    upper = (iota((128, 128), 0) < iota((128, 128), 1)).astype(BF)
    ones = jnp.ones((128, 128), BF)
    scan = jnp.concatenate([upper, ones], axis=1)
    carry = jnp.zeros((NOWN, 128), F32)
    high = jnp.zeros((NOWN, 128), F32)
    low = jnp.zeros((NOWN, 128), F32)
    for b in range(TOK // 128):
        own = owner_ref[b : b + 1, :]
        row = row_ref[b : b + 1, :]
        hot = iota((NOWN, 128), 0) == own
        hot_f = hot.astype(F32)
        hot_b = hot_f.astype(BF)
        sums = dot(hot_b, scan, 1, 0)
        rank = jnp.sum(hot_f * (sums[:, :128] + carry), axis=0, keepdims=True)
        carry = carry + sums[:, 128:]
        rank_i = rank.astype(I32)
        slot_ref[b : b + 1, :] = own * CAP + rank_i
        place = iota((128, 128), 0) == rank_i
        row_hi = jnp.where(place, (row >> 6).astype(F32), 0.0).astype(BF)
        row_lo = jnp.where(place, (row & 63).astype(F32), 0.0).astype(BF)
        high = high + dot(hot_b, row_hi, 1, 1)
        low = low + dot(hot_b, row_lo, 1, 1)
    req_ref[...] = high.astype(I32) * 64 + low.astype(I32)


def route(owner, row):
    return pl.pallas_call(
        route_kernel,
        out_shape=(
            jax.ShapeDtypeStruct((NOWN, 128), I32),
            jax.ShapeDtypeStruct((TOK // 128, 128), I32),
        ),
        in_specs=[VM, VM],
        out_specs=(VM, VM),
        compiler_params=PARAMS,
        name="route",
    )(owner, row)


def fetch_kernel(req_ref, table_ref, out_ref, wide, got):
    wide[...] = table_ref[...].astype(F32)

    def step(r, carry):
        for c in range(CAP):
            got[pl.ds(r * CAP + c, 1), :] = wide[pl.ds(req_ref[r, c], 1), :]
        return carry

    lax.fori_loop(0, NOWN, step, 0)
    out_ref[...] = got[...].astype(BF)


def fetch(req, table):
    return pl.pallas_call(
        fetch_kernel,
        out_shape=jax.ShapeDtypeStruct((SLOTS, 128), BF),
        in_specs=[SM, VM],
        out_specs=VM,
        scratch_shapes=[pltpu.VMEM((ROWS, 128), F32), pltpu.VMEM((SLOTS, 128), F32)],
        compiler_params=PARAMS,
        name="fetch",
    )(req, table)


def column(row_vector):
    wide = jnp.broadcast_to(row_vector.astype(F32), (128, 128))
    return jnp.transpose(wide)


def place_kernel(slot_ref, back_ref, x_ref):
    back = back_ref[...]
    for b in range(TOK // 128):
        col = column(slot_ref[b : b + 1, :]).astype(I32)
        hot = jnp.concatenate(
            [(col == iota((128, 128), 1) + 128 * k).astype(F32).astype(BF) for k in range(SLOTS // 128)],
            axis=1,
        )
        x_ref[b * 128 : (b + 1) * 128, :] = dot(hot, back, 1, 0).astype(BF)


def place(slot, back):
    return pl.pallas_call(
        place_kernel,
        out_shape=jax.ShapeDtypeStruct((TOK, 128), BF),
        in_specs=[VM, VM],
        out_specs=VM,
        compiler_params=PARAMS,
        name="place",
    )(slot, back)


def layer_kernel(
    pos_ref, seg_ref, x0, x1, x2, x3, g0, g1, g2, g3, win_ref, wout_ref,
    dx0, dx1, dx2, dx3, u_ref, y_ref, dp_ref,
    w, wo, pre, act, segc, aw, dsil, dout, dkv, du,
):
    xs, gs, dxs = (x0, x1, x2, x3), (g0, g1, g2, g3), (dx0, dx1, dx2, dx3)
    me = pos_ref[0]
    for k in range(NT):
        at = pl.multiple_of(lax.rem(me + k, NT) * 128, 128)
        for c in range(4):
            w[k * 128 : (k + 1) * 128, c * 128 : (c + 1) * 128] = win_ref[c, pl.ds(at, 128), :]
        wo[:, k * 128 : (k + 1) * 128] = wout_ref[:, pl.ds(at, 128)]
    for b in range(TOK // 128):
        segc[b * 128 : (b + 1) * 128, :] = column(
            seg_ref[0:1, b * 128 : (b + 1) * 128]
        )

    def stats(r0, n):
        x = [r[r0 : r0 + n, :].astype(F32) for r in xs]
        mean = jnp.sum(x[0] + x[1] + x[2] + x[3], axis=1, keepdims=True) * (1.0 / D)
        x = [v - mean for v in x]
        var = jnp.sum(x[0] * x[0] + x[1] * x[1] + x[2] * x[2] + x[3] * x[3], axis=1, keepdims=True)
        scale = lax.rsqrt(var * (1.0 / D) + 1e-05)
        return [v * scale for v in x], scale

    step = 64
    for q in range(TOK // QB):
        lo = q * QB
        for r0 in range(lo, lo + QB, step):
            n, _ = stats(r0, step)
            for k in range(NT):
                u_ref[r0 : r0 + step, k * 128 : (k + 1) * 128] = n[k].astype(BF)
        pre[lo : lo + QB, :] = dot(u_ref[lo : lo + QB, :], w[...], 1, 0)
        for r0 in range(lo, lo + QB, step):
            p = pre[r0 : r0 + step, :]
            s = 0.5 + 0.5 * jnp.tanh(0.5 * p)
            ps = p * s
            act[r0 : r0 + step, :] = ps.astype(BF)
            pre[r0 : r0 + step, :] = s + ps * (1.0 - s)

    dkv[...] = jnp.zeros((TOK, 256), F32)
    for q in range(TOK // QB):
        lo = q * QB
        k0 = max(0, lo - SEQ_MOST)
        width = lo + QB - k0
        queries = act[lo : lo + QB, 256:384]
        o = jnp.zeros((QB, HD), F32)
        for kb in range(k0, lo + QB, QB):
            sc = dot(queries, act[kb : kb + QB, 384:512], 1, 1) * (HD ** (-0.5))
            for j in range(0, QB, 128):
                same = segc[lo : lo + QB, :] == seg_ref[0:1, kb + j : kb + j + 128].astype(F32)
                if kb == lo:
                    same = same & (iota((QB, 128), 1) + j <= iota((QB, 128), 0))
                v = sc[:, j : j + 128]
                s = 0.5 + 0.5 * jnp.tanh(0.5 * v)
                vs = v * s
                at = kb - k0 + j
                aw[:, at : at + 128] = jnp.where(same, vs * (1.0 / SEQ_MOST), 0.0).astype(BF)
                dsil[:, at : at + 128] = jnp.where(
                    same, (s + vs * (1.0 - s)) * (HD ** (-0.5) / SEQ_MOST), 0.0
                )
        o = dot(aw[:, 0:width], act[k0 : lo + QB, 128:256], 1, 0)
        gate = act[lo : lo + QB, 0:128].astype(F32)
        mean = jnp.sum(o, axis=1, keepdims=True) * (1.0 / HD)
        o = o - mean
        scale = lax.rsqrt(jnp.sum(o * o, axis=1, keepdims=True) * (1.0 / HD) + 1e-05)
        n = o * scale
        y_ref[lo : lo + QB, :] = (n * gate).astype(BF)
        dy = dot(gs[0][lo : lo + QB, :], wo[:, 0:128], 1, 1)
        for k in range(1, NT):
            dy = dy + dot(gs[k][lo : lo + QB, :], wo[:, k * 128 : (k + 1) * 128], 1, 1)
        dy = dy.astype(BF).astype(F32)
        dgate = (dy * n).astype(BF).astype(F32)
        dn = dy * gate
        m1 = jnp.sum(dn, axis=1, keepdims=True) * (1.0 / HD)
        m2 = jnp.sum(dn * n, axis=1, keepdims=True) * (1.0 / HD)
        do = ((dn - m1 - n * m2) * scale).astype(BF)
        dp_ref[lo : lo + QB, 0:128] = (dgate * pre[lo : lo + QB, 0:128]).astype(BF)
        dq = jnp.zeros((QB, HD), F32)
        for kb in range(k0, lo + QB, QB):
            at = kb - k0
            da = dot(do, act[kb : kb + QB, 128:256], 1, 1).astype(BF).astype(F32)
            ds = (da * dsil[:, at : at + QB]).astype(BF)
            dq = dq + dot(ds, act[kb : kb + QB, 384:512], 1, 0)
            dkv[kb : kb + QB, 0:128] += dot(aw[:, at : at + QB], do, 0, 0)
            dkv[kb : kb + QB, 128:256] += dot(ds, queries, 0, 0)
        dq = dq.astype(BF).astype(F32)
        dp_ref[lo : lo + QB, 256:384] = (dq * pre[lo : lo + QB, 256:384]).astype(BF)

    for q in range(TOK // QB):
        lo = q * QB
        dvb = dkv[lo : lo + QB, 0:128].astype(BF).astype(F32)
        dkb = dkv[lo : lo + QB, 128:256].astype(BF).astype(F32)
        dp_ref[lo : lo + QB, 128:256] = (dvb * pre[lo : lo + QB, 128:256]).astype(BF)
        dp_ref[lo : lo + QB, 384:512] = (dkb * pre[lo : lo + QB, 384:512]).astype(BF)
        du[...] = dot(dp_ref[lo : lo + QB, :], w[...], 1, 1).astype(BF).astype(F32)
        for r in range(0, QB, step):
            n, scale = stats(lo + r, step)
            d = [du[r : r + step, k * 128 : (k + 1) * 128] for k in range(NT)]
            m1 = jnp.sum(d[0] + d[1] + d[2] + d[3], axis=1, keepdims=True) * (1.0 / D)
            m2 = jnp.sum(
                d[0] * n[0] + d[1] * n[1] + d[2] * n[2] + d[3] * n[3], axis=1, keepdims=True
            ) * (1.0 / D)
            for k in range(NT):
                dxs[k][lo + r : lo + r + step, :] = ((d[k] - m1 - n[k] * m2) * scale).astype(BF)


def layer(pos, seg, xs, gs, w_in, w_out):
    piece = jax.ShapeDtypeStruct((TOK, 128), BF)
    wide = jax.ShapeDtypeStruct((TOK, D), BF)
    return pl.pallas_call(
        layer_kernel,
        out_shape=(piece,) * 4 + (wide, piece, wide),
        in_specs=[SM] + [VM] * 11,
        out_specs=(VM,) * 7,
        scratch_shapes=[
            pltpu.VMEM((D, 512), BF),
            pltpu.VMEM((HD, D), BF),
            pltpu.VMEM((TOK, 512), F32),
            pltpu.VMEM((TOK, 512), BF),
            pltpu.VMEM((TOK, 128), F32),
            pltpu.VMEM((QB, 768), BF),
            pltpu.VMEM((QB, 768), F32),
            pltpu.VMEM((QB, 128), BF),
            pltpu.VMEM((TOK, 256), F32),
            pltpu.VMEM((QB, 512), F32),
        ],
        compiler_params=PARAMS,
        name="layer",
    )(pos, seg, *xs, *gs, w_in, w_out)


def proj_kernel(pos_ref, y_ref, u_ref, dp_ref, g0, g1, g2, g3, wout_ref, z0, z1, z2, z3, dw_ref):
    me = pos_ref[0]
    gs, zs = (g0, g1, g2, g3), (z0, z1, z2, z3)
    for k in range(NT):
        feat = lax.rem(me + k, NT)
        at = pl.multiple_of(feat * 128, 128)
        zs[k][...] = dot(y_ref[...], wout_ref[:, pl.ds(at, 128)], 1, 0).astype(BF)
        dw = dot(u_ref[:, k * 128 : (k + 1) * 128], dp_ref[...], 0, 0)
        for c in range(4):
            dw_ref[pl.ds(pl.multiple_of(c * 512 + at, 128), 128), :] = dw[:, c * 128 : (c + 1) * 128]
        dw_ref[pl.ds(pl.multiple_of(2048 + at, 128), 128), :] = dot(y_ref[...], gs[k][...], 0, 0)


def project(pos, y, u, dp, gs, w_out):
    piece = jax.ShapeDtypeStruct((TOK, 128), BF)
    return pl.pallas_call(
        proj_kernel,
        out_shape=(piece,) * 4 + (jax.ShapeDtypeStruct((2560, 128), F32),),
        in_specs=[SM] + [VM] * 8,
        out_specs=(VM,) * 5,
        compiler_params=PARAMS,
        name="project",
    )(pos, y, u, dp, *gs, w_out)


def slots_kernel(slot_ref, grad_ref, d0, d1, d2, d3, out_ref):
    dx = grad_ref[...].astype(F32) + (
        d0[...].astype(F32) + d1[...].astype(F32) + d2[...].astype(F32) + d3[...].astype(F32)
    )
    dx = dx.astype(BF)
    for s in range(SLOTS // 128):
        hot = jnp.concatenate(
            [
                (slot_ref[b : b + 1, :] == iota((128, 128), 0) + 128 * s).astype(F32).astype(BF)
                for b in range(TOK // 128)
            ],
            axis=1,
        )
        out_ref[s * 128 : (s + 1) * 128, :] = dot(hot, dx, 1, 0).astype(BF)


def to_slots(slot, grad, parts):
    return pl.pallas_call(
        slots_kernel,
        out_shape=jax.ShapeDtypeStruct((SLOTS, 128), BF),
        in_specs=[VM] * 6,
        out_specs=VM,
        compiler_params=PARAMS,
        name="to_slots",
    )(slot, grad, *parts)


def add_rows_kernel(req_ref, arrived_ref, out_ref):
    arrived = arrived_ref[...]
    for s in range(ROWS // 128):
        hot = jnp.concatenate(
            [
                (req_ref[b : b + 1, :] == iota((128, 128), 0) + 128 * s).astype(F32).astype(BF)
                for b in range(SLOTS // 128)
            ],
            axis=1,
        )
        out_ref[s * 128 : (s + 1) * 128, :] = dot(hot, arrived, 1, 0)


def add_rows(req, arrived):
    return pl.pallas_call(
        add_rows_kernel,
        out_shape=jax.ShapeDtypeStruct((ROWS, 128), F32),
        in_specs=[VM, VM],
        out_specs=VM,
        compiler_params=PARAMS,
        name="add_rows",
    )(req, arrived)


def shift(x, axis, fn, n):
    return lax.ppermute(x, axis, [(i, fn(i)) for i in range(n)])


def gather_pieces(x):
    return [x] + [shift(x, "tensor", lambda i, k=k: (i - k) % NT, NT) for k in (1, 3, 2)]


def order(pieces):
    own, one, three, two = pieces
    return [own, one, two, three]


def scatter_pieces(parts):
    return [parts[0]] + [shift(parts[k], "tensor", lambda i, k=k: (i + k) % NT, NT) for k in (1, 3, 2)]


def pick(x, i):
    return lax.dynamic_index_in_dim(x, i, 0, keepdims=False)


def reduce_weights(part):
    at = lax.axis_index("table")
    core, y = at % 2, at // 2
    halves = part.reshape(2, 1280, 128)
    other = shift(pick(halves, 1 - core).astype(BF), "table", lambda i: i ^ 1, 8)
    mine = (pick(halves, core) + other.astype(F32)).reshape(4, 320, 128)
    total = pick(mine, y)
    got = [
        shift(pick(mine, (y + k) % 4).astype(BF), "table", lambda i, k=k: (i + 2 * k) % 8, 8)
        for k in range(1, 4)
    ]
    for v in got:
        total = total + v.astype(F32)
    for bit in (1, 2, 4):
        total = total.astype(BF)
        total = total.astype(F32) + shift(total, "seq", lambda i, b=bit: i ^ b, 8).astype(F32)
    total = total.astype(BF)
    parts = [total] + [
        shift(total, "table", lambda i, k=k: (i - 2 * k) % 8, 8) for k in range(1, 4)
    ]
    stacked = jnp.roll(jnp.stack(parts), y, axis=0).reshape(1280, 128)
    other = shift(stacked, "table", lambda i: i ^ 1, 8)
    whole = jnp.where(
        core == 0, jnp.concatenate([stacked, other]), jnp.concatenate([other, stacked])
    )
    return whole.astype(F32)


def body(table, owner, local_row, segment_ids, proj_in, proj_out, grad_out):
    pos = lax.axis_index("tensor").astype(I32).reshape(1)
    requests, slot = route(owner.reshape(8, 128), local_row.reshape(8, 128))
    gs = order(gather_pieces(grad_out))
    received = lax.all_to_all(requests, BOTH, split_axis=0, concat_axis=0, tiled=True)
    rows = fetch(received, table)
    back = lax.all_to_all(rows.reshape(NOWN, CAP, 128), BOTH, split_axis=0, concat_axis=0, tiled=True)
    x = place(slot, back.reshape(SLOTS, 128))
    xs = order(gather_pieces(x))
    d0, d1, d2, d3, u, y, dp = layer(pos, segment_ids, xs, gs, proj_in, proj_out)
    dparts = scatter_pieces([d0, d1, d2, d3])
    z0, z1, z2, z3, dw = project(pos, y, u, dp, gs, proj_out)
    grads = to_slots(slot, grad_out, dparts)
    arrived = lax.all_to_all(grads.reshape(NOWN, CAP, 128), BOTH, split_axis=0, concat_axis=0, tiled=True)
    zparts = scatter_pieces([z0, z1, z2, z3])
    layer_out = (
        x.astype(F32)
        + (zparts[0].astype(F32) + zparts[1].astype(F32) + zparts[2].astype(F32) + zparts[3].astype(F32))
    ).astype(BF)
    flat = received[:, :CAP].reshape(SLOTS // 128, 128)
    table_grad = add_rows(flat, arrived.reshape(SLOTS, 128))
    whole = reduce_weights(dw)
    grad_in = whole[:2048].reshape(4, 512, 128)
    grad_outw = whole[2048:].reshape(4, 128, 128).transpose(1, 0, 2).reshape(128, 512)
    return layer_out, table_grad, grad_in, grad_outw


def solution(mesh):
    in_specs = (
        P(BOTH, "tensor"),
        P(BOTH, None),
        P(BOTH),
        P(BOTH, None),
        P(None, None, "tensor"),
        P("tensor", None),
        P(BOTH, "tensor"),
    )
    out_specs = (
        P(BOTH, "tensor"),
        P(BOTH, "tensor"),
        P(None, None, "tensor"),
        P("tensor", None),
    )
    return jax.shard_map(body, mesh=mesh, in_specs=in_specs, out_specs=out_specs, check_vma=False)
```

time: 411 us -> 164 us (0.40)
  waiting for transfers between devices: 262 us -> 39.1 us
  starting transfers between devices: 17.5 us -> 57.4 us
  other arithmetic: 41.1 us -> 2.27 us
  Pallas kernels: 0 us -> 32.2 us
  matrix products: 26.1 us -> 0 us
  local copies, waits for them, and re-layouts: 25.8 us -> 6.93 us
  between operations: 14.7 us -> 0.85 us
    psum x1 -> x0, waiting for transfers between devices: 177 us -> none  [body(): lax.psum((d_in.astype(jnp.float32), d_out.astype(jnp.float32)), ('table',...]
    all_gather x2 -> x0, waiting for transfers between devices: 37 us -> none  [the longest x1 21.4 us: body(): lax.all_gather(x_local, 'tensor', axis=1, tiled=True)]
    ppermute x0 -> x23, starting transfers between devices: none -> 35 us  [shift(): return lax.ppermute(x, axis, [(i, fn(i)) for i in range(n)])]
    pallas_call x0 -> x7, Pallas kernels: none -> 32.2 us  [the longest x1 11.4 us: layer(): pl.pallas_call(layer_kernel, out_shape=(piece,) * 4 + (wide, piece, wide)...]
    ppermute x0 -> x23, waiting for transfers between devices: none -> 27.7 us  [shift(): return lax.ppermute(x, axis, [(i, fn(i)) for i in range(n)])]
    dot_general x27 -> x0, matrix products: 26.1 us -> none  [the longest x12 11.5 us: branch_mixed(): jnp.dot(normed, w_in[c], preferred_element_type=jnp.float32)]
    reduce_scatter x1 -> x0, waiting for transfers between devices: 20.3 us -> none  [body(): lax.psum_scatter(d_x.astype(jnp.bfloat16), 'tensor', scatter_dimension=1,...]
    another operation x3 -> x0, other arithmetic: 18.2 us -> none
  transfers between devices with their start and end apart: 7 -> 25, of which waited for: 7 -> 13; matrix products, arithmetic and copies ran while one was open for 9% -> 1% of each run, Pallas kernels for 0% -> 6%
where the time goes in v1:
time: 164 us; the launch traced here: 161 us
  starting transfers between devices  57.4 us (35%)
  waiting for transfers between devices  39.1 us (24%)
  Pallas kernels  32.2 us (20%)
  blocking collectives  22.3 us (14%)
  local copies, waits for them, and re-layouts  6.93 us (4%)
  other arithmetic  2.27 us (1%)
    ppermute x23, starting transfers between devices, shift(): return lax.ppermute(x, axis, [(i, fn(i)) for i in range(n)])  35 us
    ppermute x23, waiting for transfers between devices, shift(): return lax.ppermute(x, axis, [(i, fn(i)) for i in range(n)])  27.7 us
    all_to_all x1, blocking collectives, body(): lax.all_to_all(requests, BOTH, split_axis=0, concat_axis=0, tiled=True)  22.3 us
    all_to_all x1, starting transfers between devices, body(): lax.all_to_all(grads.reshape(NOWN, CAP, 128), BOTH, split_axis=0, concat_...  17.2 us
    pallas_call x1, Pallas kernels, layer(): pl.pallas_call(layer_kernel, out_shape=(piece,) * 4 + (wide, piece, wide)...  11.4 us
    all_to_all x1, waiting for transfers between devices, body(): lax.all_to_all(rows.reshape(NOWN, CAP, 128), BOTH, split_axis=0, concat_a...  9.97 us
    all_to_all x1, starting transfers between devices, body(): lax.all_to_all(rows.reshape(NOWN, CAP, 128), BOTH, split_axis=0, concat_a...  5.16 us
    pallas_call x1, Pallas kernels, project(): pl.pallas_call(proj_kernel, out_shape=(piece,) * 4 + (jax.ShapeDtypeStruc...  4.3 us
  transfers between devices with their start and end apart: 25, of which 13 were waited for; matrix products, arithmetic and copies ran while one was open for 1% of the time, Pallas kernels for 6%

profile of v1, /device:TPU:1, one launch (start us, length us, event | category | flops | bytes accessed | tf_op | source)
XLA Modules:
  0.0 161.0 jit_solution(2608734769955062574)
XLA Ops:
  0.6 2.9 %route.1 = (s32[64,128]{1,0:T(8,128)}, s32[8,128]{1,0:T(8,128)}) custom-call(s32[8,128]{1,0:T(8,128)} %bitcast.66, s32[8,128]{1,0:T(8,128)} %bitcast.67), custom_call_target="tpu_custom_call" | custom-call | tf_op jit(solution)/shard_map/route/pallas_call | solution.py:64
  3.6 22.3 %all_to_all.21 = s32[64,1,128]{2,1,0:T(1,128)} all-to-all(s32[64,1,128]{2,1,0:T(1,128)} %bitcast.65), channel_id=1, replica_groups=mesh['table'=8,'seq'=8,'tensor'=4] {'table','seq'}, dimensions={0} | all-to-all | bytes 65536 | tf_op jit(solution)/shard_map/all_to_all | solution.py:389
  25.8 3.6 %fetch.1 = bf16[1536,128]{1,0:T(8,128)(2,1)} custom-call(s32[64,128]{1,0:T(8,128)} %bitcast.63, bf16[2048,128]{1,0:T(8,128)(2,1)} %table_ref.1), custom_call_target="tpu_custom_call" | custom-call | tf_op jit(solution)/shard_map/fetch/pallas_call | solution.py:90
  29.4 5.2 %all-to-all-start.1 = ((bf16[64,24,128]{2,1,0:T(8,128)(2,1)}), bf16[64,24,128]{2,1,0:T(8,128)(2,1)S(1)}, u32[]{:S(2)}, u32[]{:S(2)}) async-start(bf16[64,24,128]{2,1,0:T(8,128)(2,1)} %bitcast.54), calls=%async_computation.1 | async-start | bytes 786432 | tf_op jit(solution)/shard_map/all_to_all | solution.py:391
  34.6 1.3 collective-permute-start.5
  35.9 2.4 %collective-permute-start.4 = (bf16[1024,128]{1,0:T(8,128)(2,1)S(1)}, bf16[1024,128]{1,0:T(8,128)(2,1)S(1)}, u32[]{:S(2)}, u32[]{:S(2)}) collective-permute-start(bf16[1024,128]{1,0:T(8,128)(2,1)S(1)} %copy-done.1), channel_id=1, source_target_pairs={{0,2},{1,3},{2,0},{3,1},{4,6},{5,7},{6,4},{7,5},{8,10},{9,11},{10,... | collective-permute-start | bytes 786440 | tf_op jit(solution)/shard_map/ppermute | solution.py:337
  39.5 10.0 %all-to-all-done.1 = bf16[64,24,128]{2,1,0:T(8,128)(2,1)S(1)} async-done(((bf16[64,24,128]{2,1,0:T(8,128)(2,1)}), bf16[64,24,128]{2,1,0:T(8,128)(2,1)S(1)}, u32[]{:S(2)}, u32[]{:S(2)}) %all-to-all-start.1) | async-done | bytes 393248 | tf_op jit(solution)/shard_map/all_to_all | solution.py:391
  50.2 3.1 %place.1.x0 = bf16[1024,128]{1,0:T(8,128)(2,1)} custom-call(s32[8,128]{1,0:T(8,128)} %get-tuple-element.18.slot_ref, bf16[1536,128]{1,0:T(8,128)(2,1)} %bitcast.52), custom_call_target="tpu_custom_call" | custom-call | tf_op jit(solution)/shard_map/place/pallas_call | solution.py:118
  54.6 2.4 %collective-permute-start.1 = (bf16[1024,128]{1,0:T(8,128)(2,1)}, bf16[1024,128]{1,0:T(8,128)(2,1)S(1)}, u32[]{:S(2)}, u32[]{:S(2)}) collective-permute-start(bf16[1024,128]{1,0:T(8,128)(2,1)} %place.1.x0), channel_id=1, source_target_pairs={{0,2},{1,3},{2,0},{3,1},{4,6},{5,7},{6,4},{7,5},{8,10},{9,11},{10,... | collective-permute-start | bytes 786440 | tf_op jit(solution)/shard_map/ppermute | solution.py:337
  58.2 3.4 %collective-permute-done.2.x3 = bf16[1024,128]{1,0:T(8,128)(2,1)S(1)} collective-permute-done((bf16[1024,128]{1,0:T(8,128)(2,1)}, bf16[1024,128]{1,0:T(8,128)(2,1)S(1)}, u32[]{:S(2)}, u32[]{:S(2)}) %collective-permute-start.2) | collective-permute-done | bytes 262176 | tf_op jit(solution)/shard_map/ppermute | solution.py:337
  61.6 6.6 %collective-permute-done.1.x2 = bf16[1024,128]{1,0:T(8,128)(2,1)S(1)} collective-permute-done((bf16[1024,128]{1,0:T(8,128)(2,1)}, bf16[1024,128]{1,0:T(8,128)(2,1)S(1)}, u32[]{:S(2)}, u32[]{:S(2)}) %collective-permute-start.1) | collective-permute-done | bytes 262176 | tf_op jit(solution)/shard_map/ppermute | solution.py:337
  69.0 11.4 %layer.1 = (bf16[1024,128]{1,0:T(8,128)(2,1)}, bf16[1024,128]{1,0:T(8,128)(2,1)}, bf16[1024,128]{1,0:T(8,128)(2,1)}, bf16[1024,128]{1,0:T(8,128)(2,1)}, bf16[102...) custom-call(s32[1]{0:T(128)} %bitcast.7.pos_ref, s32[1,1024]{1,0:T(1,128)} %seg_ref.1, ...), custom_call_target="tpu_custom_call" | custom-call | tf_op jit(solution)/shard_map/layer/pallas_call | solution.py:238
  80.3 4.3 %project.1 = (bf16[1024,128]{1,0:T(8,128)(2,1)}, bf16[1024,128]{1,0:T(8,128)(2,1)}, bf16[1024,128]{1,0:T(8,128)(2,1)}, bf16[1024,128]{1,0:T(8,128)(2,1)}, f32[2560,128]{1,0:T(8,128)}) custom-call(s32[1]{0:T(128)} %bitcast.7.pos_ref, bf16[1024,128]{1,0:T(8,128)(2,1)} %get-tuple-element.20.y_ref, bf16[1024,512]{1,0:T(8,128)(2,1)} %get-tuple-element.21.u_ref, ...), custom_call_target="tpu_custom_call" | custom-call | tf_op jit(solution)/shard_map/project/pallas_call | solution.py:275
  85.8 2.0 %collective-permute-start.12 = (bf16[1280,128]{1,0:T(8,128)(2,1)S(1)}, bf16[1280,128]{1,0:T(8,128)(2,1)S(1)}, u32[]{:S(2)}, u32[]{:S(2)}) collective-permute-start(bf16[1280,128]{1,0:T(8,128)(2,1)S(1)} %fusion.1), channel_id=1, source_target_pairs={{0,32},{32,0},{64,96},{96,64},{128,160},{160,128},{192,224},{224,1... | collective-permute-start | bytes 983048 | tf_op jit(solution)/shard_map/ppermute | solution.py:337
  91.0 1.9 %collective-permute-start.15 = (bf16[320,128]{1,0:T(8,128)(2,1)S(1)}, bf16[320,128]{1,0:T(8,128)(2,1)S(1)}, u32[]{:S(2)}, u32[]{:S(2)}) collective-permute-start(bf16[320,128]{1,0:T(8,128)(2,1)S(1)} %get-tuple-element.43), channel_id=1, source_target_pairs={{0,192},{32,224},{64,0},{96,32},{128,64},{160,96},{192,128},{224,1... | collective-permute-start | bytes 245768 | tf_op jit(solution)/shard_map/ppermute | solution.py:337
  93.8 1.3 collective-permute-done.13
  95.2 2.6 %collective-permute-done.14 = bf16[320,128]{1,0:T(8,128)(2,1)S(1)} collective-permute-done((bf16[320,128]{1,0:T(8,128)(2,1)S(1)}, bf16[320,128]{1,0:T(8,128)(2,1)S(1)}, u32[]{:S(2)}, u32[]{:S(2)}) %collective-permute-start.14) | collective-permute-done | bytes 81952 | tf_op jit(solution)/shard_map/ppermute | solution.py:337
  97.8 1.4 collective-permute-start.16
  99.2 2.2 %collective-permute-done.16 = bf16[320,128]{1,0:T(8,128)(2,1)S(1)} collective-permute-done((bf16[320,128]{1,0:T(8,128)(2,1)S(1)}, bf16[320,128]{1,0:T(8,128)(2,1)S(1)}, u32[]{:S(2)}, u32[]{:S(2)}) %collective-permute-start.16) | collective-permute-done | bytes 81952 | tf_op jit(solution)/shard_map/ppermute | solution.py:337
  102.3 3.5 %collective-permute-done.17 = bf16[320,128]{1,0:T(8,128)(2,1)S(1)} collective-permute-done((bf16[320,128]{1,0:T(8,128)(2,1)S(1)}, bf16[320,128]{1,0:T(8,128)(2,1)S(1)}, u32[]{:S(2)}, u32[]{:S(2)}) %collective-permute-start.17) | collective-permute-done | bytes 81952 | tf_op jit(solution)/shard_map/ppermute | solution.py:337
  105.8 2.3 %collective-permute-start.18 = (bf16[320,128]{1,0:T(8,128)(2,1)S(1)}, bf16[320,128]{1,0:T(8,128)(2,1)S(1)}, u32[]{:S(2)}, u32[]{:S(2)}) collective-permute-start(bf16[320,128]{1,0:T(8,128)(2,1)S(1)} %add_convert_fusion.2), channel_id=1, source_target_pairs={{0,16},{4,20},{8,24},{12,28},{16,0},{20,4},{24,8},{28,12},{1,17},{... | collective-permute-start | bytes 245768 | tf_op jit(solution)/shard_map/ppermute | solution.py:337
  109.0 1.7 %collective-permute-start.10 = (bf16[1024,128]{1,0:T(8,128)(2,1)S(1)}, bf16[1024,128]{1,0:T(8,128)(2,1)S(1)}, u32[]{:S(2)}, u32[]{:S(2)}) collective-permute-start(bf16[1024,128]{1,0:T(8,128)(2,1)S(1)} %copy-done.17), channel_id=1, source_target_pairs={{0,3},{1,0},{2,1},{3,2},{4,7},{5,4},{6,5},{7,6},{8,11},{9,8},{10,9... | collective-permute-start | bytes 786440 | tf_op jit(solution)/shard_map/ppermute | solution.py:337
  113.1 1.5 collective-permute-start.19
  115.2 2.1 %collective-permute-start.7 = (bf16[1024,128]{1,0:T(8,128)(2,1)}, bf16[1024,128]{1,0:T(8,128)(2,1)S(1)}, u32[]{:S(2)}, u32[]{:S(2)}) collective-permute-start(bf16[1024,128]{1,0:T(8,128)(2,1)} %get-tuple-element.25), channel_id=1, source_target_pairs={{0,3},{1,0},{2,1},{3,2},{4,7},{5,4},{6,5},{7,6},{8,11},{9,8},{10,9... | collective-permute-start | bytes 786440 | tf_op jit(solution)/shard_map/ppermute | solution.py:337
  119.1 3.1 %to_slots.1 = bf16[1536,128]{1,0:T(8,128)(2,1)} custom-call(s32[8,128]{1,0:T(8,128)} %get-tuple-element.18.slot_ref, bf16[1024,128]{1,0:T(8,128)(2,1)} %grad_ref.1, bf16[1024,128]{1,0:T(8,128)(2,1)} %get-tuple-element.27.d0, bf16[1024,128]{1,0:T(8,128)(2,1)} %copy-done.12, bf16[1024,128]{1,0:T(8,128)(2,1)} %copy-done.13, bf16[1024,128]{1,0:T(8,128)(2,1)} %copy-done.14), custom_call_target="tpu_custom_call" | custom-call | tf_op jit(solution)/shard_map/to_slots/pallas_call | solution.py:302
  122.2 17.2 %all-to-all-start.2 = ((bf16[64,24,128]{2,1,0:T(8,128)(2,1)}), bf16[64,24,128]{2,1,0:T(8,128)(2,1)S(1)}, u32[]{:S(2)}, u32[]{:S(2)}) async-start(bf16[64,24,128]{2,1,0:T(8,128)(2,1)} %bitcast.55), calls=%async_computation.2 | async-start | bytes 786432 | tf_op jit(solution)/shard_map/all_to_all | solution.py:398
  139.5 1.5 collective-permute-start.21
  141.0 2.6 %collective-permute-start.20 = (bf16[320,128]{1,0:T(8,128)(2,1)S(1)}, bf16[320,128]{1,0:T(8,128)(2,1)S(1)}, u32[]{:S(2)}, u32[]{:S(2)}) collective-permute-start(bf16[320,128]{1,0:T(8,128)(2,1)S(1)} %get-tuple-element.41), channel_id=1, source_target_pairs={{0,128},{32,160},{64,192},{96,224},{128,0},{160,32},{192,64},{224,... | collective-permute-start | bytes 245768 | tf_op jit(solution)/shard_map/ppermute | solution.py:337
  143.6 5.2 %collective-permute-done.20 = bf16[320,128]{1,0:T(8,128)(2,1)S(1)} collective-permute-done((bf16[320,128]{1,0:T(8,128)(2,1)S(1)}, bf16[320,128]{1,0:T(8,128)(2,1)S(1)}, u32[]{:S(2)}, u32[]{:S(2)}) %collective-permute-start.20) | collective-permute-done | bytes 81952 | tf_op jit(solution)/shard_map/ppermute | solution.py:337
  149.0 2.3 %collective-permute-start.22 = (bf16[1280,128]{1,0:T(8,128)(2,1)S(1)}, bf16[1280,128]{1,0:T(8,128)(2,1)S(1)}, u32[]{:S(2)}, u32[]{:S(2)}) collective-permute-start(bf16[1280,128]{1,0:T(8,128)(2,1)S(1)} %bitcast.56), channel_id=1, source_target_pairs={{0,32},{32,0},{64,96},{96,64},{128,160},{160,128},{192,224},{224,1... | collective-permute-start | bytes 983048 | tf_op jit(solution)/shard_map/ppermute | solution.py:337
  152.9 1.4 all-to-all-done.2
  155.0 3.8 %add_rows.1 = f32[2048,128]{1,0:T(8,128)} custom-call(s32[12,128]{1,0:T(8,128)} %reshape.61.req_ref, bf16[1536,128]{1,0:T(8,128)(2,1)} %bitcast.53), custom_call_target="tpu_custom_call" | custom-call | tf_op jit(solution)/shard_map/add_rows/pallas_call | solution.py:326
  (86 shorter events, 21.6 us)
Async XLA Ops:
  0.6 34.0 %copy-start.1 = (bf16[1024,128]{1,0:T(8,128)(2,1)S(1)}, bf16[1024,128]{1,0:T(8,128)(2,1)}, u32[]{:S(2)}) copy-start(bf16[1024,128]{1,0:T(8,128)(2,1)} %grad_ref.1) | copy-start | bytes 786436
  29.4 20.0 %all-to-all-start.1 = ((bf16[64,24,128]{2,1,0:T(8,128)(2,1)}), bf16[64,24,128]{2,1,0:T(8,128)(2,1)S(1)}, u32[]{:S(2)}, u32[]{:S(2)}) async-start(bf16[64,24,128]{2,1,0:T(8,128)(2,1)} %bitcast.54), calls=%async_computation.1 | async-start | bytes 786432 | tf_op jit(solution)/shard_map/all_to_all | solution.py:391
  34.6 22.4 %collective-permute-start.5 = (bf16[1024,128]{1,0:T(8,128)(2,1)S(1)}, bf16[1024,128]{1,0:T(8,128)(2,1)S(1)}, u32[]{:S(2)}, u32[]{:S(2)}) collective-permute-start(bf16[1024,128]{1,0:T(8,128)(2,1)S(1)} %copy-done.1), channel_id=1, source_target_pairs={{0,1},{1,2},{2,3},{3,0},{4,5},{5,6},{6,7},{7,4},{8,9},{9,10},{10,1... | collective-permute-start | bytes 786440 | tf_op jit(solution)/shard_map/ppermute | solution.py:337
  35.9 22.3 %collective-permute-start.4 = (bf16[1024,128]{1,0:T(8,128)(2,1)S(1)}, bf16[1024,128]{1,0:T(8,128)(2,1)S(1)}, u32[]{:S(2)}, u32[]{:S(2)}) collective-permute-start(bf16[1024,128]{1,0:T(8,128)(2,1)S(1)} %copy-done.1), channel_id=1, source_target_pairs={{0,2},{1,3},{2,0},{3,1},{4,6},{5,7},{6,4},{7,5},{8,10},{9,11},{10,... | collective-permute-start | bytes 786440 | tf_op jit(solution)/shard_map/ppermute | solution.py:337
  38.3 19.8 %collective-permute-start.3 = (bf16[1024,128]{1,0:T(8,128)(2,1)S(1)}, bf16[1024,128]{1,0:T(8,128)(2,1)S(1)}, u32[]{:S(2)}, u32[]{:S(2)}) collective-permute-start(bf16[1024,128]{1,0:T(8,128)(2,1)S(1)} %copy-done.1), channel_id=1, source_target_pairs={{0,3},{1,0},{2,1},{3,2},{4,7},{5,4},{6,5},{7,6},{8,11},{9,8},{10,9... | collective-permute-start | bytes 786440 | tf_op jit(solution)/shard_map/ppermute | solution.py:337
  53.3 8.2 %collective-permute-start.2 = (bf16[1024,128]{1,0:T(8,128)(2,1)}, bf16[1024,128]{1,0:T(8,128)(2,1)S(1)}, u32[]{:S(2)}, u32[]{:S(2)}) collective-permute-start(bf16[1024,128]{1,0:T(8,128)(2,1)} %place.1.x0), channel_id=1, source_target_pairs={{0,1},{1,2},{2,3},{3,0},{4,5},{5,6},{6,7},{7,4},{8,9},{9,10},{10,1... | collective-permute-start | bytes 786440 | tf_op jit(solution)/shard_map/ppermute | solution.py:337
  54.6 13.6 %collective-permute-start.1 = (bf16[1024,128]{1,0:T(8,128)(2,1)}, bf16[1024,128]{1,0:T(8,128)(2,1)S(1)}, u32[]{:S(2)}, u32[]{:S(2)}) collective-permute-start(bf16[1024,128]{1,0:T(8,128)(2,1)} %place.1.x0), channel_id=1, source_target_pairs={{0,2},{1,3},{2,0},{3,1},{4,6},{5,7},{6,4},{7,5},{8,10},{9,11},{10,... | collective-permute-start | bytes 786440 | tf_op jit(solution)/shard_map/ppermute | solution.py:337
  57.0 11.3 %collective-permute-start = (bf16[1024,128]{1,0:T(8,128)(2,1)}, bf16[1024,128]{1,0:T(8,128)(2,1)S(1)}, u32[]{:S(2)}, u32[]{:S(2)}) collective-permute-start(bf16[1024,128]{1,0:T(8,128)(2,1)} %place.1.x0), channel_id=1, source_target_pairs={{0,3},{1,0},{2,1},{3,2},{4,7},{5,4},{6,5},{7,6},{8,11},{9,8},{10,9... | collective-permute-start | bytes 786440 | tf_op jit(solution)/shard_map/ppermute | solution.py:337
  85.8 3.2 %collective-permute-start.12 = (bf16[1280,128]{1,0:T(8,128)(2,1)S(1)}, bf16[1280,128]{1,0:T(8,128)(2,1)S(1)}, u32[]{:S(2)}, u32[]{:S(2)}) collective-permute-start(bf16[1280,128]{1,0:T(8,128)(2,1)S(1)} %fusion.1), channel_id=1, source_target_pairs={{0,32},{32,0},{64,96},{96,64},{128,160},{160,128},{192,224},{224,1... | collective-permute-start | bytes 983048 | tf_op jit(solution)/shard_map/ppermute | solution.py:337
  87.8 21.3 %copy-start.17 = (bf16[1024,128]{1,0:T(8,128)(2,1)S(1)}, bf16[1024,128]{1,0:T(8,128)(2,1)}, u32[]{:S(2)}) copy-start(bf16[1024,128]{1,0:T(8,128)(2,1)} %get-tuple-element.29) | copy-start | bytes 786436
  87.8 23.0 %copy-start.16 = (bf16[1024,128]{1,0:T(8,128)(2,1)S(1)}, bf16[1024,128]{1,0:T(8,128)(2,1)}, u32[]{:S(2)}) copy-start(bf16[1024,128]{1,0:T(8,128)(2,1)} %get-tuple-element.30) | copy-start | bytes 786436
  90.2 27.1 %copy-start.15 = (bf16[1024,128]{1,0:T(8,128)(2,1)S(1)}, bf16[1024,128]{1,0:T(8,128)(2,1)}, u32[]{:S(2)}) copy-start(bf16[1024,128]{1,0:T(8,128)(2,1)} %get-tuple-element.26) | copy-start | bytes 786436
  90.2 4.9 %collective-permute-start.13 = (bf16[320,128]{1,0:T(8,128)(2,1)S(1)}, bf16[320,128]{1,0:T(8,128)(2,1)S(1)}, u32[]{:S(2)}, u32[]{:S(2)}) collective-permute-start(bf16[320,128]{1,0:T(8,128)(2,1)S(1)} %get-tuple-element.42), channel_id=1, source_target_pairs={{0,64},{32,96},{64,128},{96,160},{128,192},{160,224},{192,0},{224,... | collective-permute-start | bytes 245768 | tf_op jit(solution)/shard_map/ppermute | solution.py:337
  91.0 4.1 %collective-permute-start.15 = (bf16[320,128]{1,0:T(8,128)(2,1)S(1)}, bf16[320,128]{1,0:T(8,128)(2,1)S(1)}, u32[]{:S(2)}, u32[]{:S(2)}) collective-permute-start(bf16[320,128]{1,0:T(8,128)(2,1)S(1)} %get-tuple-element.43), channel_id=1, source_target_pairs={{0,192},{32,224},{64,0},{96,32},{128,64},{160,96},{192,128},{224,1... | collective-permute-start | bytes 245768 | tf_op jit(solution)/shard_map/ppermute | solution.py:337
  93.0 4.8 %collective-permute-start.14 = (bf16[320,128]{1,0:T(8,128)(2,1)S(1)}, bf16[320,128]{1,0:T(8,128)(2,1)S(1)}, u32[]{:S(2)}, u32[]{:S(2)}) collective-permute-start(bf16[320,128]{1,0:T(8,128)(2,1)S(1)} %get-tuple-element.44), channel_id=1, source_target_pairs={{0,128},{32,160},{64,192},{96,224},{128,0},{160,32},{192,64},{224,... | collective-permute-start | bytes 245768 | tf_op jit(solution)/shard_map/ppermute | solution.py:337
  97.8 3.6 %collective-permute-start.16 = (bf16[320,128]{1,0:T(8,128)(2,1)S(1)}, bf16[320,128]{1,0:T(8,128)(2,1)S(1)}, u32[]{:S(2)}, u32[]{:S(2)}) collective-permute-start(bf16[320,128]{1,0:T(8,128)(2,1)S(1)} %fusion.4), channel_id=1, source_target_pairs={{0,4},{4,0},{8,12},{12,8},{16,20},{20,16},{24,28},{28,24},{1,5},{5... | collective-permute-start | bytes 245768 | tf_op jit(solution)/shard_map/ppermute | solution.py:337
  101.4 4.3 %collective-permute-start.17 = (bf16[320,128]{1,0:T(8,128)(2,1)S(1)}, bf16[320,128]{1,0:T(8,128)(2,1)S(1)}, u32[]{:S(2)}, u32[]{:S(2)}) collective-permute-start(bf16[320,128]{1,0:T(8,128)(2,1)S(1)} %add_convert_fusion.3), channel_id=1, source_target_pairs={{0,8},{4,12},{8,0},{12,4},{16,24},{20,28},{24,16},{28,20},{1,9},{5... | collective-permute-start | bytes 245768 | tf_op jit(solution)/shard_map/ppermute | solution.py:337
  105.8 7.3 %collective-permute-start.18 = (bf16[320,128]{1,0:T(8,128)(2,1)S(1)}, bf16[320,128]{1,0:T(8,128)(2,1)S(1)}, u32[]{:S(2)}, u32[]{:S(2)}) collective-permute-start(bf16[320,128]{1,0:T(8,128)(2,1)S(1)} %add_convert_fusion.2), channel_id=1, source_target_pairs={{0,16},{4,20},{8,24},{12,28},{16,0},{20,4},{24,8},{28,12},{1,17},{... | collective-permute-start | bytes 245768 | tf_op jit(solution)/shard_map/ppermute | solution.py:337
  108.1 7.2 %collective-permute-start.9 = (bf16[1024,128]{1,0:T(8,128)(2,1)S(1)}, bf16[1024,128]{1,0:T(8,128)(2,1)S(1)}, u32[]{:S(2)}, u32[]{:S(2)}) collective-permute-start(bf16[1024,128]{1,0:T(8,128)(2,1)S(1)} %copy-done.18), channel_id=1, source_target_pairs={{0,1},{1,2},{2,3},{3,0},{4,5},{5,6},{6,7},{7,4},{8,9},{9,10},{10,1... | collective-permute-start | bytes 786440 | tf_op jit(solution)/shard_map/ppermute | solution.py:337
  109.0 8.2 %collective-permute-start.10 = (bf16[1024,128]{1,0:T(8,128)(2,1)S(1)}, bf16[1024,128]{1,0:T(8,128)(2,1)S(1)}, u32[]{:S(2)}, u32[]{:S(2)}) collective-permute-start(bf16[1024,128]{1,0:T(8,128)(2,1)S(1)} %copy-done.17), channel_id=1, source_target_pairs={{0,3},{1,0},{2,1},{3,2},{4,7},{5,4},{6,5},{7,6},{8,11},{9,8},{10,9... | collective-permute-start | bytes 786440 | tf_op jit(solution)/shard_map/ppermute | solution.py:337
  110.7 7.7 %collective-permute-start.11 = (bf16[1024,128]{1,0:T(8,128)(2,1)S(1)}, bf16[1024,128]{1,0:T(8,128)(2,1)S(1)}, u32[]{:S(2)}, u32[]{:S(2)}) collective-permute-start(bf16[1024,128]{1,0:T(8,128)(2,1)S(1)} %copy-done.16), channel_id=1, source_target_pairs={{0,2},{1,3},{2,0},{3,1},{4,6},{5,7},{6,4},{7,5},{8,10},{9,11},{10,... | collective-permute-start | bytes 786440 | tf_op jit(solution)/shard_map/ppermute | solution.py:337
  113.1 27.9 %collective-permute-start.19 = (bf16[320,128]{1,0:T(8,128)(2,1)S(1)}, bf16[320,128]{1,0:T(8,128)(2,1)S(1)}, u32[]{:S(2)}, u32[]{:S(2)}) collective-permute-start(bf16[320,128]{1,0:T(8,128)(2,1)S(1)} %get-tuple-element.41), channel_id=1, source_target_pairs={{0,192},{32,224},{64,0},{96,32},{128,64},{160,96},{192,128},{224,1... | collective-permute-start | bytes 245768 | tf_op jit(solution)/shard_map/ppermute | solution.py:337
  114.6 37.4 %collective-permute-start.6 = (bf16[1024,128]{1,0:T(8,128)(2,1)}, bf16[1024,128]{1,0:T(8,128)(2,1)S(1)}, u32[]{:S(2)}, u32[]{:S(2)}) collective-permute-start(bf16[1024,128]{1,0:T(8,128)(2,1)} %get-tuple-element.24), channel_id=1, source_target_pairs={{0,1},{1,2},{2,3},{3,0},{4,5},{5,6},{6,7},{7,4},{8,9},{9,10},{10,1... | collective-permute-start | bytes 786440 | tf_op jit(solution)/shard_map/ppermute | solution.py:337
  115.2 36.7 %collective-permute-start.7 = (bf16[1024,128]{1,0:T(8,128)(2,1)}, bf16[1024,128]{1,0:T(8,128)(2,1)S(1)}, u32[]{:S(2)}, u32[]{:S(2)}) collective-permute-start(bf16[1024,128]{1,0:T(8,128)(2,1)} %get-tuple-element.25), channel_id=1, source_target_pairs={{0,3},{1,0},{2,1},{3,2},{4,7},{5,4},{6,5},{7,6},{8,11},{9,8},{10,9... | collective-permute-start | bytes 786440 | tf_op jit(solution)/shard_map/ppermute | solution.py:337
  117.3 34.7 %collective-permute-start.8 = (bf16[1024,128]{1,0:T(8,128)(2,1)S(1)}, bf16[1024,128]{1,0:T(8,128)(2,1)S(1)}, u32[]{:S(2)}, u32[]{:S(2)}) collective-permute-start(bf16[1024,128]{1,0:T(8,128)(2,1)S(1)} %copy-done.15), channel_id=1, source_target_pairs={{0,2},{1,3},{2,0},{3,1},{4,6},{5,7},{6,4},{7,5},{8,10},{9,11},{10,... | collective-permute-start | bytes 786440 | tf_op jit(solution)/shard_map/ppermute | solution.py:337
  122.2 29.1 %copy-start.7 = (s32[64,1,128]{2,1,0:T(1,128)S(1)}, s32[64,1,128]{2,1,0:T(1,128)}, u32[]{:S(2)}) copy-start(s32[64,1,128]{2,1,0:T(1,128)} %all_to_all.21) | copy-start | bytes 98308
  122.2 29.7 %copy-start = (bf16[1024,128]{1,0:T(8,128)(2,1)S(1)}, bf16[1024,128]{1,0:T(8,128)(2,1)}, u32[]{:S(2)}) copy-start(bf16[1024,128]{1,0:T(8,128)(2,1)} %place.1.x0) | copy-start | bytes 786436
  122.2 29.7 %copy-start.11 = (bf16[1024,128]{1,0:T(8,128)(2,1)S(1)}, bf16[1024,128]{1,0:T(8,128)(2,1)}, u32[]{:S(2)}) copy-start(bf16[1024,128]{1,0:T(8,128)(2,1)} %get-tuple-element.23) | copy-start | bytes 786436
  122.2 32.0 %all-to-all-start.2 = ((bf16[64,24,128]{2,1,0:T(8,128)(2,1)}), bf16[64,24,128]{2,1,0:T(8,128)(2,1)S(1)}, u32[]{:S(2)}, u32[]{:S(2)}) async-start(bf16[64,24,128]{2,1,0:T(8,128)(2,1)} %bitcast.55), calls=%async_computation.2 | async-start | bytes 786432 | tf_op jit(solution)/shard_map/all_to_all | solution.py:398
  139.5 9.3 %collective-permute-start.21 = (bf16[320,128]{1,0:T(8,128)(2,1)S(1)}, bf16[320,128]{1,0:T(8,128)(2,1)S(1)}, u32[]{:S(2)}, u32[]{:S(2)}) collective-permute-start(bf16[320,128]{1,0:T(8,128)(2,1)S(1)} %get-tuple-element.41), channel_id=1, source_target_pairs={{0,64},{32,96},{64,128},{96,160},{128,192},{160,224},{192,0},{224,... | collective-permute-start | bytes 245768 | tf_op jit(solution)/shard_map/ppermute | solution.py:337
  141.0 7.8 %collective-permute-start.20 = (bf16[320,128]{1,0:T(8,128)(2,1)S(1)}, bf16[320,128]{1,0:T(8,128)(2,1)S(1)}, u32[]{:S(2)}, u32[]{:S(2)}) collective-permute-start(bf16[320,128]{1,0:T(8,128)(2,1)S(1)} %get-tuple-element.41), channel_id=1, source_target_pairs={{0,128},{32,160},{64,192},{96,224},{128,0},{160,32},{192,64},{224,... | collective-permute-start | bytes 245768 | tf_op jit(solution)/shard_map/ppermute | solution.py:337
  149.0 9.8 %collective-permute-start.22 = (bf16[1280,128]{1,0:T(8,128)(2,1)S(1)}, bf16[1280,128]{1,0:T(8,128)(2,1)S(1)}, u32[]{:S(2)}, u32[]{:S(2)}) collective-permute-start(bf16[1280,128]{1,0:T(8,128)(2,1)S(1)} %bitcast.56), channel_id=1, source_target_pairs={{0,32},{32,0},{64,96},{96,64},{128,160},{160,128},{192,224},{224,1... | collective-permute-start | bytes 983048 | tf_op jit(solution)/shard_map/ppermute | solution.py:337
  (12 other events, 66.4 us)

commit v2 on v1

--- a/solution.py
+++ b/solution.py
@@ -125,12 +125,21 @@
     )(slot, back)
 
 
+def normed(xs, r0, n):
+    x = [r[r0 : r0 + n, :].astype(F32) for r in xs]
+    mean = jnp.sum(x[0] + x[1] + x[2] + x[3], axis=1, keepdims=True) * (1.0 / D)
+    x = [v - mean for v in x]
+    var = jnp.sum(x[0] * x[0] + x[1] * x[1] + x[2] * x[2] + x[3] * x[3], axis=1, keepdims=True)
+    scale = lax.rsqrt(var * (1.0 / D) + 1e-05)
+    return [v * scale for v in x], scale
+
+
 def layer_kernel(
     pos_ref, seg_ref, x0, x1, x2, x3, g0, g1, g2, g3, win_ref, wout_ref,
-    dx0, dx1, dx2, dx3, u_ref, y_ref, dp_ref,
-    w, wo, pre, act, segc, aw, dsil, dout, dkv, du,
+    u_ref, y_ref, dp_ref, w,
+    wo, pre, act, segc, aw, dsil, dkv,
 ):
-    xs, gs, dxs = (x0, x1, x2, x3), (g0, g1, g2, g3), (dx0, dx1, dx2, dx3)
+    xs, gs = (x0, x1, x2, x3), (g0, g1, g2, g3)
     me = pos_ref[0]
     for k in range(NT):
         at = pl.multiple_of(lax.rem(me + k, NT) * 128, 128)
@@ -142,19 +151,11 @@
             seg_ref[0:1, b * 128 : (b + 1) * 128]
         )
 
-    def stats(r0, n):
-        x = [r[r0 : r0 + n, :].astype(F32) for r in xs]
-        mean = jnp.sum(x[0] + x[1] + x[2] + x[3], axis=1, keepdims=True) * (1.0 / D)
-        x = [v - mean for v in x]
-        var = jnp.sum(x[0] * x[0] + x[1] * x[1] + x[2] * x[2] + x[3] * x[3], axis=1, keepdims=True)
-        scale = lax.rsqrt(var * (1.0 / D) + 1e-05)
-        return [v * scale for v in x], scale
-
     step = 64
     for q in range(TOK // QB):
         lo = q * QB
         for r0 in range(lo, lo + QB, step):
-            n, _ = stats(r0, step)
+            n, _ = normed(xs, r0, step)
             for k in range(NT):
                 u_ref[r0 : r0 + step, k * 128 : (k + 1) * 128] = n[k].astype(BF)
         pre[lo : lo + QB, :] = dot(u_ref[lo : lo + QB, :], w[...], 1, 0)
@@ -220,9 +221,71 @@
         dkb = dkv[lo : lo + QB, 128:256].astype(BF).astype(F32)
         dp_ref[lo : lo + QB, 128:256] = (dvb * pre[lo : lo + QB, 128:256]).astype(BF)
         dp_ref[lo : lo + QB, 384:512] = (dkb * pre[lo : lo + QB, 384:512]).astype(BF)
+
+
+def layer(pos, seg, xs, gs, w_in, w_out):
+    wide = jax.ShapeDtypeStruct((TOK, D), BF)
+    return pl.pallas_call(
+        layer_kernel,
+        out_shape=(
+            wide,
+            jax.ShapeDtypeStruct((TOK, 128), BF),
+            wide,
+            jax.ShapeDtypeStruct((D, 512), BF),
+        ),
+        in_specs=[SM] + [VM] * 11,
+        out_specs=(VM,) * 4,
+        scratch_shapes=[
+            pltpu.VMEM((HD, D), BF),
+            pltpu.VMEM((TOK, 512), F32),
+            pltpu.VMEM((TOK, 512), BF),
+            pltpu.VMEM((TOK, 128), F32),
+            pltpu.VMEM((QB, 768), BF),
+            pltpu.VMEM((QB, 768), F32),
+            pltpu.VMEM((TOK, 256), F32),
+        ],
+        compiler_params=PARAMS,
+        name="layer",
+    )(pos, seg, *xs, *gs, w_in, w_out)
+
+
+def weights_kernel(pos_ref, y_ref, u_ref, dp_ref, g0, g1, g2, g3, mine_ref, other_ref, dw_ref):
+    me, core = pos_ref[0], pos_ref[1]
+    gs = (g0, g1, g2, g3)
+    for k in range(NT):
+        at = pl.multiple_of(lax.rem(me + k, NT) * 128, 128)
+        dw = dot(u_ref[:, k * 128 : (k + 1) * 128], dp_ref[...], 0, 0)
+        for c in range(4):
+            dw_ref[pl.ds(pl.multiple_of(c * 512 + at, 128), 128), :] = dw[:, c * 128 : (c + 1) * 128]
+        dw_ref[pl.ds(pl.multiple_of(2048 + at, 128), 128), :] = dot(y_ref[...], gs[k][...], 0, 0)
+    mine_ref[...] = dw_ref[pl.ds(pl.multiple_of(core * 1280, 1280), 1280), :]
+    other_ref[...] = dw_ref[pl.ds(pl.multiple_of(1280 - core * 1280, 1280), 1280), :].astype(BF)
+
+
+def weights(pos, y, u, dp, gs):
+    return pl.pallas_call(
+        weights_kernel,
+        out_shape=(jax.ShapeDtypeStruct((1280, 128), F32), jax.ShapeDtypeStruct((1280, 128), BF)),
+        in_specs=[SM] + [VM] * 7,
+        out_specs=(VM,) * 2,
+        scratch_shapes=[pltpu.VMEM((2560, 128), F32)],
+        compiler_params=PARAMS,
+        name="weights",
+    )(pos, y, u, dp, *gs)
+
+
+def input_kernel(dp_ref, w, x0, x1, x2, x3, y_ref, wout_ref, dx0, dx1, dx2, dx3, z_ref, du):
+    xs, dxs = (x0, x1, x2, x3), (dx0, dx1, dx2, dx3)
+    step = 64
+    for k in range(NT):
+        z_ref[k * TOK : (k + 1) * TOK, :] = dot(
+            y_ref[...], wout_ref[:, k * 128 : (k + 1) * 128], 1, 0
+        ).astype(BF)
+    for q in range(TOK // QB):
+        lo = q * QB
         du[...] = dot(dp_ref[lo : lo + QB, :], w[...], 1, 1).astype(BF).astype(F32)
         for r in range(0, QB, step):
-            n, scale = stats(lo + r, step)
+            n, scale = normed(xs, lo + r, step)
             d = [du[r : r + step, k * 128 : (k + 1) * 128] for k in range(NT)]
             m1 = jnp.sum(d[0] + d[1] + d[2] + d[3], axis=1, keepdims=True) * (1.0 / D)
             m2 = jnp.sum(
@@ -232,54 +295,17 @@
                 dxs[k][lo + r : lo + r + step, :] = ((d[k] - m1 - n[k] * m2) * scale).astype(BF)
 
 
-def layer(pos, seg, xs, gs, w_in, w_out):
+def input_grad(dp, w, xs, y, w_out):
     piece = jax.ShapeDtypeStruct((TOK, 128), BF)
-    wide = jax.ShapeDtypeStruct((TOK, D), BF)
-    return pl.pallas_call(
-        layer_kernel,
-        out_shape=(piece,) * 4 + (wide, piece, wide),
-        in_specs=[SM] + [VM] * 11,
-        out_specs=(VM,) * 7,
-        scratch_shapes=[
-            pltpu.VMEM((D, 512), BF),
-            pltpu.VMEM((HD, D), BF),
-            pltpu.VMEM((TOK, 512), F32),
-            pltpu.VMEM((TOK, 512), BF),
-            pltpu.VMEM((TOK, 128), F32),
-            pltpu.VMEM((QB, 768), BF),
-            pltpu.VMEM((QB, 768), F32),
-            pltpu.VMEM((QB, 128), BF),
-            pltpu.VMEM((TOK, 256), F32),
-            pltpu.VMEM((QB, 512), F32),
-        ],
-        compiler_params=PARAMS,
-        name="layer",
-    )(pos, seg, *xs, *gs, w_in, w_out)
-
-
-def proj_kernel(pos_ref, y_ref, u_ref, dp_ref, g0, g1, g2, g3, wout_ref, z0, z1, z2, z3, dw_ref):
-    me = pos_ref[0]
-    gs, zs = (g0, g1, g2, g3), (z0, z1, z2, z3)
-    for k in range(NT):
-        feat = lax.rem(me + k, NT)
-        at = pl.multiple_of(feat * 128, 128)
-        zs[k][...] = dot(y_ref[...], wout_ref[:, pl.ds(at, 128)], 1, 0).astype(BF)
-        dw = dot(u_ref[:, k * 128 : (k + 1) * 128], dp_ref[...], 0, 0)
-        for c in range(4):
-            dw_ref[pl.ds(pl.multiple_of(c * 512 + at, 128), 128), :] = dw[:, c * 128 : (c + 1) * 128]
-        dw_ref[pl.ds(pl.multiple_of(2048 + at, 128), 128), :] = dot(y_ref[...], gs[k][...], 0, 0)
-
-
-def project(pos, y, u, dp, gs, w_out):
-    piece = jax.ShapeDtypeStruct((TOK, 128), BF)
-    return pl.pallas_call(
-        proj_kernel,
-        out_shape=(piece,) * 4 + (jax.ShapeDtypeStruct((2560, 128), F32),),
-        in_specs=[SM] + [VM] * 8,
+    return pl.pallas_call(
+        input_kernel,
+        out_shape=(piece,) * 4 + (jax.ShapeDtypeStruct((NT * TOK, 128), BF),),
+        in_specs=[VM] * 8,
         out_specs=(VM,) * 5,
-        compiler_params=PARAMS,
-        name="project",
-    )(pos, y, u, dp, *gs, w_out)
+        scratch_shapes=[pltpu.VMEM((QB, 512), F32)],
+        compiler_params=PARAMS,
+        name="input_grad",
+    )(dp, w, *xs, y, w_out)
 
 
 def slots_kernel(slot_ref, grad_ref, d0, d1, d2, d3, out_ref):
@@ -333,6 +359,41 @@
     )(req, arrived)
 
 
+def join_kernel(y_ref, p0, p1, p2, p3, out_ref):
+    for k, p in enumerate((p0, p1, p2, p3)):
+        at = pl.multiple_of(lax.rem(y_ref[0] + k, 4) * 320, 320)
+        out_ref[pl.ds(at, 320), :] = p[...]
+
+
+def join(y, parts):
+    return pl.pallas_call(
+        join_kernel,
+        out_shape=jax.ShapeDtypeStruct((1280, 128), BF),
+        in_specs=[SM] + [VM] * 4,
+        out_specs=VM,
+        compiler_params=PARAMS,
+        name="join",
+    )(y, *parts)
+
+
+def unpack_kernel(whole_ref, in_ref, out_ref):
+    for c in range(4):
+        in_ref[c, :, :] = whole_ref[c * 512 : (c + 1) * 512, :].astype(F32)
+    for k in range(NT):
+        out_ref[:, k * 128 : (k + 1) * 128] = whole_ref[2048 + k * 128 : 2176 + k * 128, :].astype(F32)
+
+
+def unpack(whole):
+    return pl.pallas_call(
+        unpack_kernel,
+        out_shape=(jax.ShapeDtypeStruct((4, D, 128), F32), jax.ShapeDtypeStruct((HD, D), F32)),
+        in_specs=[VM],
+        out_specs=(VM, VM),
+        compiler_params=PARAMS,
+        name="unpack",
+    )(whole)
+
+
 def shift(x, axis, fn, n):
     return lax.ppermute(x, axis, [(i, fn(i)) for i in range(n)])
 
@@ -354,12 +415,11 @@
     return lax.dynamic_index_in_dim(x, i, 0, keepdims=False)
 
 
-def reduce_weights(part):
+def reduce_weights(mine, other, arrived):
     at = lax.axis_index("table")
     core, y = at % 2, at // 2
-    halves = part.reshape(2, 1280, 128)
-    other = shift(pick(halves, 1 - core).astype(BF), "table", lambda i: i ^ 1, 8)
-    mine = (pick(halves, core) + other.astype(F32)).reshape(4, 320, 128)
+    other = shift(other, "table", lambda i: i ^ 1, 8)
+    mine = (mine + other.astype(F32)).reshape(4, 320, 128)
     total = pick(mine, y)
     got = [
         shift(pick(mine, (y + k) % 4).astype(BF), "table", lambda i, k=k: (i + 2 * k) % 8, 8)
@@ -370,20 +430,22 @@
     for bit in (1, 2, 4):
         total = total.astype(BF)
         total = total.astype(F32) + shift(total, "seq", lambda i, b=bit: i ^ b, 8).astype(F32)
-    total = total.astype(BF)
+    total, arrived = lax.optimization_barrier((total.astype(BF), arrived))
     parts = [total] + [
         shift(total, "table", lambda i, k=k: (i - 2 * k) % 8, 8) for k in range(1, 4)
     ]
-    stacked = jnp.roll(jnp.stack(parts), y, axis=0).reshape(1280, 128)
-    other = shift(stacked, "table", lambda i: i ^ 1, 8)
-    whole = jnp.where(
-        core == 0, jnp.concatenate([stacked, other]), jnp.concatenate([other, stacked])
+    whole = lax.all_gather(
+        join(y.astype(I32).reshape(1), parts),
+        "table",
+        axis=0,
+        tiled=True,
+        axis_index_groups=[[2 * i, 2 * i + 1] for i in range(4)],
     )
-    return whole.astype(F32)
+    return unpack(whole), arrived
 
 
 def body(table, owner, local_row, segment_ids, proj_in, proj_out, grad_out):
-    pos = lax.axis_index("tensor").astype(I32).reshape(1)
+    pos = jnp.stack([lax.axis_index("tensor"), lax.axis_index("table") % 2]).astype(I32)
     requests, slot = route(owner.reshape(8, 128), local_row.reshape(8, 128))
     gs = order(gather_pieces(grad_out))
     received = lax.all_to_all(requests, BOTH, split_axis=0, concat_axis=0, tiled=True)
@@ -391,21 +453,19 @@
     back = lax.all_to_all(rows.reshape(NOWN, CAP, 128), BOTH, split_axis=0, concat_axis=0, tiled=True)
     x = place(slot, back.reshape(SLOTS, 128))
     xs = order(gather_pieces(x))
-    d0, d1, d2, d3, u, y, dp = layer(pos, segment_ids, xs, gs, proj_in, proj_out)
+    u, y, dp, w = layer(pos, segment_ids, xs, gs, proj_in, proj_out)
+    mine, other = weights(pos, y, u, dp, gs)
+    dp, mine, other = lax.optimization_barrier((dp, mine, other))
+    d0, d1, d2, d3, z = input_grad(dp, w, xs, y, proj_out)
     dparts = scatter_pieces([d0, d1, d2, d3])
-    z0, z1, z2, z3, dw = project(pos, y, u, dp, gs, proj_out)
     grads = to_slots(slot, grad_out, dparts)
+    grads, z = lax.optimization_barrier((grads, z))
     arrived = lax.all_to_all(grads.reshape(NOWN, CAP, 128), BOTH, split_axis=0, concat_axis=0, tiled=True)
-    zparts = scatter_pieces([z0, z1, z2, z3])
-    layer_out = (
-        x.astype(F32)
-        + (zparts[0].astype(F32) + zparts[1].astype(F32) + zparts[2].astype(F32) + zparts[3].astype(F32))
-    ).astype(BF)
+    zsum = lax.psum_scatter(z, "tensor", scatter_dimension=0, tiled=True)
+    layer_out = (x.astype(F32) + zsum.astype(F32)).astype(BF)
     flat = received[:, :CAP].reshape(SLOTS // 128, 128)
+    (grad_in, grad_outw), arrived = reduce_weights(mine, other, arrived)
     table_grad = add_rows(flat, arrived.reshape(SLOTS, 128))
-    whole = reduce_weights(dw)
-    grad_in = whole[:2048].reshape(4, 512, 128)
-    grad_outw = whole[2048:].reshape(4, 128, 128).transpose(1, 0, 2).reshape(128, 512)
     return layer_out, table_grad, grad_in, grad_outw
 
 

time: 164 us -> 188 us (1.15); the launches traced: 161 us -> 187 us
  starting transfers between devices: 57.4 us -> 39.4 us
  waiting for transfers between devices: 39.1 us -> 56.1 us
  between operations: 0.85 us -> 14.2 us
  blocking collectives: 22.3 us -> 31.4 us
  Pallas kernels: 32.2 us -> 38.7 us
  local copies, waits for them, and re-layouts: 6.93 us -> 4.75 us
    ppermute x23 -> x19, waiting for transfers between devices: 27.7 us -> 44.9 us  [shift(): return lax.ppermute(x, axis, [(i, fn(i)) for i in range(n)])]
    ppermute x23 -> x19, starting transfers between devices: 35 us -> 25.4 us  [shift(): return lax.ppermute(x, axis, [(i, fn(i)) for i in range(n)])]
    all_gather x0 -> x1, blocking collectives: none -> 8.96 us  [reduce_weights(): lax.all_gather(join(y.astype(I32).reshape(1), parts), 'table', axis=0, ti...]
    all_to_all x1, starting transfers between devices: 17.2 us -> 8.94 us  [body(): lax.all_to_all(grads.reshape(NOWN, CAP, 128), BOTH, split_axis=0, concat_...]
    pallas_call x2 -> x5, Pallas kernels: 15.7 us -> 22.2 us  [the longest x1 9.43 us: layer(): pl.pallas_call(layer_kernel, out_shape=(wide, jax.ShapeDtypeStruct((TOK,...]
    unnamed x45 -> x38, local copies, waits for them, and re-layouts: 3.85 us -> 4.03 us
  transfers between devices with their start and end apart: 25 -> 22, of which waited for: 13 -> 10; matrix products, arithmetic and copies ran while one was open for 1% -> 1% of each run, Pallas kernels for 6% -> 10%
where the time goes in v2:
time: 188 us; the launch traced here: 187 us
  waiting for transfers between devices  56.1 us (30%)
  starting transfers between devices  39.4 us (21%)
  Pallas kernels  38.7 us (21%)
  blocking collectives  31.4 us (17%)
  between operations  14.2 us (8%)
  local copies, waits for them, and re-layouts  4.75 us (3%)
  other arithmetic  2.55 us (1%)
    ppermute x19, waiting for transfers between devices, shift(): return lax.ppermute(x, axis, [(i, fn(i)) for i in range(n)])  44.9 us
    ppermute x19, starting transfers between devices, shift(): return lax.ppermute(x, axis, [(i, fn(i)) for i in range(n)])  25.4 us
    all_to_all x1, blocking collectives, body(): lax.all_to_all(requests, BOTH, split_axis=0, concat_axis=0, tiled=True)  22.4 us
    all_to_all x1, waiting for transfers between devices, body(): lax.all_to_all(rows.reshape(NOWN, CAP, 128), BOTH, split_axis=0, concat_a...  11.1 us
    pallas_call x1, Pallas kernels, layer(): pl.pallas_call(layer_kernel, out_shape=(wide, jax.ShapeDtypeStruct((TOK,...  9.43 us
    all_gather x1, blocking collectives, reduce_weights(): lax.all_gather(join(y.astype(I32).reshape(1), parts), 'table', axis=0, ti...  8.96 us
    all_to_all x1, starting transfers between devices, body(): lax.all_to_all(grads.reshape(NOWN, CAP, 128), BOTH, split_axis=0, concat_...  8.94 us
    all_to_all x1, starting transfers between devices, body(): lax.all_to_all(rows.reshape(NOWN, CAP, 128), BOTH, split_axis=0, concat_a...  4.98 us
  transfers between devices with their start and end apart: 22, of which 10 were waited for; matrix products, arithmetic and copies ran while one was open for 1% of the time, Pallas kernels for 10%

profile of v2, /device:TPU:1, one launch (start us, length us, event | category | flops | bytes accessed | tf_op | source)
XLA Modules:
  0.0 187.0 jit_solution(6724568721883235520)
XLA Ops:
  7.2 2.9 %route.1 = (s32[64,128]{1,0:T(8,128)}, s32[8,128]{1,0:T(8,128)}) custom-call(s32[8,128]{1,0:T(8,128)} %bitcast.37, s32[8,128]{1,0:T(8,128)} %bitcast.38), custom_call_target="tpu_custom_call" | custom-call | tf_op jit(solution)/shard_map/route/pallas_call | solution.py:64
  10.1 22.4 %all_to_all.21 = s32[64,1,128]{2,1,0:T(1,128)} all-to-all(s32[64,1,128]{2,1,0:T(1,128)} %bitcast.36), channel_id=1, replica_groups=mesh['table'=8,'seq'=8,'tensor'=4] {'table','seq'}, dimensions={0} | all-to-all | bytes 65536 | tf_op jit(solution)/shard_map/all_to_all | solution.py:451
  32.5 3.6 %fetch.1 = bf16[1536,128]{1,0:T(8,128)(2,1)} custom-call(s32[64,128]{1,0:T(8,128)} %bitcast.34, bf16[2048,128]{1,0:T(8,128)(2,1)} %table_ref.1), custom_call_target="tpu_custom_call" | custom-call | tf_op jit(solution)/shard_map/fetch/pallas_call | solution.py:90
  36.1 5.0 %all-to-all-start.1 = ((bf16[64,24,128]{2,1,0:T(8,128)(2,1)}), bf16[64,24,128]{2,1,0:T(8,128)(2,1)S(1)}, u32[]{:S(2)}, u32[]{:S(2)}) async-start(bf16[64,24,128]{2,1,0:T(8,128)(2,1)} %bitcast.33), calls=%async_computation.1 | async-start | bytes 786432 | tf_op jit(solution)/shard_map/all_to_all | solution.py:453
  41.1 2.6 %collective-permute-start.3 = (bf16[1024,128]{1,0:T(8,128)(2,1)S(1)}, bf16[1024,128]{1,0:T(8,128)(2,1)S(1)}, u32[]{:S(2)}, u32[]{:S(2)}) collective-permute-start(bf16[1024,128]{1,0:T(8,128)(2,1)S(1)} %copy-done.1), channel_id=1, source_target_pairs={{0,3},{1,0},{2,1},{3,2},{4,7},{5,4},{6,5},{7,6},{8,11},{9,8},{10,9... | collective-permute-start | bytes 786440 | tf_op jit(solution)/shard_map/ppermute | solution.py:398
  44.8 11.1 %all-to-all-done.1 = bf16[64,24,128]{2,1,0:T(8,128)(2,1)S(1)} async-done(((bf16[64,24,128]{2,1,0:T(8,128)(2,1)}), bf16[64,24,128]{2,1,0:T(8,128)(2,1)S(1)}, u32[]{:S(2)}, u32[]{:S(2)}) %all-to-all-start.1) | async-done | bytes 393248 | tf_op jit(solution)/shard_map/all_to_all | solution.py:453
  56.7 3.1 %place.1.x0 = bf16[1024,128]{1,0:T(8,128)(2,1)} custom-call(s32[8,128]{1,0:T(8,128)} %get-tuple-element.26.slot_ref, bf16[1536,128]{1,0:T(8,128)(2,1)} %bitcast.31), custom_call_target="tpu_custom_call" | custom-call | tf_op jit(solution)/shard_map/place/pallas_call | solution.py:118
  59.8 2.5 %collective-permute-start = (bf16[1024,128]{1,0:T(8,128)(2,1)}, bf16[1024,128]{1,0:T(8,128)(2,1)S(1)}, u32[]{:S(2)}, u32[]{:S(2)}) collective-permute-start(bf16[1024,128]{1,0:T(8,128)(2,1)} %place.1.x0), channel_id=1, source_target_pairs={{0,3},{1,0},{2,1},{3,2},{4,7},{5,4},{6,5},{7,6},{8,11},{9,8},{10,9... | collective-permute-start | bytes 786440 | tf_op jit(solution)/shard_map/ppermute | solution.py:398
  64.1 3.9 %collective-permute-done.x1 = bf16[1024,128]{1,0:T(8,128)(2,1)S(1)} collective-permute-done((bf16[1024,128]{1,0:T(8,128)(2,1)}, bf16[1024,128]{1,0:T(8,128)(2,1)S(1)}, u32[]{:S(2)}, u32[]{:S(2)}) %collective-permute-start) | collective-permute-done | bytes 262176 | tf_op jit(solution)/shard_map/ppermute | solution.py:398
  68.0 2.6 %collective-permute-done.1.x2 = bf16[1024,128]{1,0:T(8,128)(2,1)S(1)} collective-permute-done((bf16[1024,128]{1,0:T(8,128)(2,1)}, bf16[1024,128]{1,0:T(8,128)(2,1)S(1)}, u32[]{:S(2)}, u32[]{:S(2)}) %collective-permute-start.1) | collective-permute-done | bytes 262176 | tf_op jit(solution)/shard_map/ppermute | solution.py:398
  70.6 7.3 %collective-permute-done.2.x3 = bf16[1024,128]{1,0:T(8,128)(2,1)S(1)} collective-permute-done((bf16[1024,128]{1,0:T(8,128)(2,1)}, bf16[1024,128]{1,0:T(8,128)(2,1)S(1)}, u32[]{:S(2)}, u32[]{:S(2)}) %collective-permute-start.2) | collective-permute-done | bytes 262176 | tf_op jit(solution)/shard_map/ppermute | solution.py:398
  78.6 9.4 %layer.1 = (bf16[1024,512]{1,0:T(8,128)(2,1)}, bf16[1024,128]{1,0:T(8,128)(2,1)}, bf16[1024,512]{1,0:T(8,128)(2,1)}, bf16[512,512]{1,0:T(8,128)(2,1)}) custom-call(s32[2]{0:T(128)} %pad_add_fusion.pos_ref, s32[1,1024]{1,0:T(1,128)} %seg_ref.1, bf16[1024,128]{1,0:T(8,128)(2,1)} %place.1.x0, bf16[1024,128]{1,0:T(8,128)(2,1)} %copy-done.6, ...), custom_call_target="tpu_custom_call" | custom-call | tf_op jit(solution)/shard_map/layer/pallas_call | solution.py:228
  88.0 3.9 %weights.1 = (f32[1280,128]{1,0:T(8,128)}, bf16[1280,128]{1,0:T(8,128)(2,1)}) custom-call(s32[2]{0:T(128)} %pad_add_fusion.pos_ref, bf16[1024,128]{1,0:T(8,128)(2,1)} %get-tuple-element.29.y_ref, bf16[1024,512]{1,0:T(8,128)(2,1)} %get-tuple-element.30.u_ref, bf16[1024,512]{1,0:T(8,128)(2,1)} %get-tuple-element.33.dp_ref, bf16[1024,128]{1,0:T(8,128)(2,1)} %grad_ref.1, ...), custom_call_target="tpu_custom_call" | custom-call | tf_op jit(solution)/shard_map/weights/pallas_call | solution.py:266
  92.4 4.8 %input_grad.1 = (bf16[1024,128]{1,0:T(8,128)(2,1)}, bf16[1024,128]{1,0:T(8,128)(2,1)}, bf16[1024,128]{1,0:T(8,128)(2,1)}, bf16[1024,128]{1,0:T(8,128)(2,1)}, bf16[4096,128]{1,0:T(8,128)(2,1)}) custom-call(bf16[1024,512]{1,0:T(8,128)(2,1)} %get-tuple-element.33.dp_ref, bf16[512,512]{1,0:T(8,128)(2,1)} %get-tuple-element.34.w, bf16[1024,128]{1,0:T(8,128)(2,1)} %place.1.x0, ...), custom_call_target="tpu_custom_call" | custom-call | tf_op jit(solution)/shard_map/input_grad/pallas_call | solution.py:300
  97.3 2.7 %collective-permute-start.7 = (bf16[1024,128]{1,0:T(8,128)(2,1)}, bf16[1024,128]{1,0:T(8,128)(2,1)S(1)}, u32[]{:S(2)}, u32[]{:S(2)}) collective-permute-start(bf16[1024,128]{1,0:T(8,128)(2,1)} %get-tuple-element.37), channel_id=1, source_target_pairs={{0,3},{1,0},{2,1},{3,2},{4,7},{5,4},{6,5},{7,6},{8,11},{9,8},{10,9... | collective-permute-start | bytes 786440 | tf_op jit(solution)/shard_map/ppermute | solution.py:398
  100.0 12.3 %collective-permute-done.6.d1 = bf16[1024,128]{1,0:T(8,128)(2,1)S(1)} collective-permute-done((bf16[1024,128]{1,0:T(8,128)(2,1)}, bf16[1024,128]{1,0:T(8,128)(2,1)S(1)}, u32[]{:S(2)}, u32[]{:S(2)}) %collective-permute-start.6) | collective-permute-done | bytes 262176 | tf_op jit(solution)/shard_map/ppermute | solution.py:398
  113.1 3.1 %to_slots.1 = bf16[1536,128]{1,0:T(8,128)(2,1)} custom-call(s32[8,128]{1,0:T(8,128)} %get-tuple-element.26.slot_ref, bf16[1024,128]{1,0:T(8,128)(2,1)} %grad_ref.1, bf16[1024,128]{1,0:T(8,128)(2,1)} %get-tuple-element.35.d0, bf16[1024,128]{1,0:T(8,128)(2,1)} %copy-done.13, bf16[1024,128]{1,0:T(8,128)(2,1)} %copy-done.14, bf16[1024,128]{1,0:T(8,128)(2,1)} %copy-done.15), custom_call_target="tpu_custom_call" | custom-call | tf_op jit(solution)/shard_map/to_slots/pallas_call | solution.py:328
  116.3 1.1 copy-done.10
  118.3 1.6 collective-permute-start.11
  119.9 1.7 collective-permute-start.12
  122.0 2.2 %collective-permute-done.11 = bf16[320,128]{1,0:T(8,128)(2,1)S(1)} collective-permute-done((bf16[320,128]{1,0:T(8,128)(2,1)S(1)}, bf16[320,128]{1,0:T(8,128)(2,1)S(1)}, u32[]{:S(2)}, u32[]{:S(2)}) %collective-permute-start.11) | collective-permute-done | bytes 81952 | tf_op jit(solution)/shard_map/ppermute | solution.py:398
  125.3 8.9 %all-to-all-start.2 = ((bf16[64,24,128]{2,1,0:T(8,128)(2,1)}), bf16[64,24,128]{2,1,0:T(8,128)(2,1)S(1)}, u32[]{:S(2)}, u32[]{:S(2)}) async-start(bf16[64,24,128]{2,1,0:T(8,128)(2,1)} %bitcast.14), calls=%async_computation.3 | async-start | bytes 786432 | tf_op jit(solution)/shard_map/all_to_all | solution.py:463
  134.3 2.4 %collective-permute-start.14 = (bf16[320,128]{1,0:T(8,128)(2,1)S(1)}, bf16[320,128]{1,0:T(8,128)(2,1)S(1)}, u32[]{:S(2)}, u32[]{:S(2)}) collective-permute-start(bf16[320,128]{1,0:T(8,128)(2,1)S(1)} %add_convert_fusion.3), channel_id=1, source_target_pairs={{0,8},{4,12},{8,0},{12,4},{16,24},{20,28},{24,16},{28,20},{1,9},{5... | collective-permute-start | bytes 245768 | tf_op jit(solution)/shard_map/ppermute | solution.py:398
  136.6 12.4 %collective-permute-done.14 = bf16[320,128]{1,0:T(8,128)(2,1)S(1)} collective-permute-done((bf16[320,128]{1,0:T(8,128)(2,1)S(1)}, bf16[320,128]{1,0:T(8,128)(2,1)S(1)}, u32[]{:S(2)}, u32[]{:S(2)}) %collective-permute-start.14) | collective-permute-done | bytes 81952 | tf_op jit(solution)/shard_map/ppermute | solution.py:398
  149.1 3.6 %collective-permute-start.15 = (bf16[320,128]{1,0:T(8,128)(2,1)S(1)}, bf16[320,128]{1,0:T(8,128)(2,1)S(1)}, u32[]{:S(2)}, u32[]{:S(2)}) collective-permute-start(bf16[320,128]{1,0:T(8,128)(2,1)S(1)} %add_convert_fusion.2), channel_id=1, source_target_pairs={{0,16},{4,20},{8,24},{12,28},{16,0},{20,4},{24,8},{28,12},{1,17},{... | collective-permute-start | bytes 245768 | tf_op jit(solution)/shard_map/ppermute | solution.py:398
  152.7 3.7 %collective-permute-done.15 = bf16[320,128]{1,0:T(8,128)(2,1)S(1)} collective-permute-done((bf16[320,128]{1,0:T(8,128)(2,1)S(1)}, bf16[320,128]{1,0:T(8,128)(2,1)S(1)}, u32[]{:S(2)}, u32[]{:S(2)}) %collective-permute-start.15) | collective-permute-done | bytes 81952 | tf_op jit(solution)/shard_map/ppermute | solution.py:398
  156.5 2.7 %collective-permute-start.16 = (bf16[320,128]{1,0:T(8,128)(2,1)S(1)}, bf16[320,128]{1,0:T(8,128)(2,1)S(1)}, u32[]{:S(2)}, u32[]{:S(2)}) collective-permute-start(bf16[320,128]{1,0:T(8,128)(2,1)S(1)} %add_convert_fusion.1.p0), channel_id=1, source_target_pairs={{0,192},{32,224},{64,0},{96,32},{128,64},{160,96},{192,128},{224,1... | collective-permute-start | bytes 245768 | tf_op jit(solution)/shard_map/ppermute | solution.py:398
  160.9 3.8 %add_rows.1 = f32[2048,128]{1,0:T(8,128)} custom-call(s32[12,128]{1,0:T(8,128)} %reshape.44.req_ref, bf16[1536,128]{1,0:T(8,128)(2,1)} %bitcast.32), custom_call_target="tpu_custom_call" | custom-call | tf_op jit(solution)/shard_map/add_rows/pallas_call | solution.py:352
  165.5 1.8 join.1
  167.3 9.0 %all_gather.3.whole_ref = bf16[2560,128]{1,0:T(8,128)(2,1)} all-gather(bf16[1280,128]{1,0:T(8,128)(2,1)} %join.1), channel_id=1, replica_groups={{0,32},{64,96},{128,160},{192,224},{1,33},{65,97},{129,161},{193,225},{..., dimensions={0}, use_global_device_ids=true | all-gather | bytes 983040 | tf_op jit(solution)/shard_map/all_gather | solution.py:437
  176.2 2.2 %unpack.1 = (f32[4,512,128]{2,1,0:T(8,128)}, f32[128,512]{1,0:T(8,128)}) custom-call(bf16[2560,128]{1,0:T(8,128)(2,1)} %all_gather.3.whole_ref), custom_call_target="tpu_custom_call" | custom-call | tf_op jit(solution)/shard_map/unpack/pallas_call | solution.py:387
  178.5 1.7 add_convert_fusion
  (72 shorter events, 10.8 us)
Async XLA Ops:
  36.1 5.0 %copy-start.1 = (bf16[1024,128]{1,0:T(8,128)(2,1)S(1)}, bf16[1024,128]{1,0:T(8,128)(2,1)}, u32[]{:S(2)}) copy-start(bf16[1024,128]{1,0:T(8,128)(2,1)} %grad_ref.1) | copy-start | bytes 786436
  36.1 19.9 %all-to-all-start.1 = ((bf16[64,24,128]{2,1,0:T(8,128)(2,1)}), bf16[64,24,128]{2,1,0:T(8,128)(2,1)S(1)}, u32[]{:S(2)}, u32[]{:S(2)}) async-start(bf16[64,24,128]{2,1,0:T(8,128)(2,1)} %bitcast.33), calls=%async_computation.1 | async-start | bytes 786432 | tf_op jit(solution)/shard_map/all_to_all | solution.py:453
  41.1 137.4 %reduce-scatter.2.cloned.1.call-start = ((), (), s32[]{:S(2)}) async-start(), calls=%async_computation.4 | async-start | bytes 1310720 | tf_op jit(solution)/shard_map/reduce_scatter | solution.py:464
  41.1 21.7 %collective-permute-start.3 = (bf16[1024,128]{1,0:T(8,128)(2,1)S(1)}, bf16[1024,128]{1,0:T(8,128)(2,1)S(1)}, u32[]{:S(2)}, u32[]{:S(2)}) collective-permute-start(bf16[1024,128]{1,0:T(8,128)(2,1)S(1)} %copy-done.1), channel_id=1, source_target_pairs={{0,3},{1,0},{2,1},{3,2},{4,7},{5,4},{6,5},{7,6},{8,11},{9,8},{10,9... | collective-permute-start | bytes 786440 | tf_op jit(solution)/shard_map/ppermute | solution.py:398
  43.7 20.4 %collective-permute-start.4 = (bf16[1024,128]{1,0:T(8,128)(2,1)S(1)}, bf16[1024,128]{1,0:T(8,128)(2,1)S(1)}, u32[]{:S(2)}, u32[]{:S(2)}) collective-permute-start(bf16[1024,128]{1,0:T(8,128)(2,1)S(1)} %copy-done.1), channel_id=1, source_target_pairs={{0,2},{1,3},{2,0},{3,1},{4,6},{5,7},{6,4},{7,5},{8,10},{9,11},{10,... | collective-permute-start | bytes 786440 | tf_op jit(solution)/shard_map/ppermute | solution.py:398
  44.2 19.9 %collective-permute-start.5 = (bf16[1024,128]{1,0:T(8,128)(2,1)S(1)}, bf16[1024,128]{1,0:T(8,128)(2,1)S(1)}, u32[]{:S(2)}, u32[]{:S(2)}) collective-permute-start(bf16[1024,128]{1,0:T(8,128)(2,1)S(1)} %copy-done.1), channel_id=1, source_target_pairs={{0,1},{1,2},{2,3},{3,0},{4,5},{5,6},{6,7},{7,4},{8,9},{9,10},{10,1... | collective-permute-start | bytes 786440 | tf_op jit(solution)/shard_map/ppermute | solution.py:398
  59.8 8.2 %collective-permute-start = (bf16[1024,128]{1,0:T(8,128)(2,1)}, bf16[1024,128]{1,0:T(8,128)(2,1)S(1)}, u32[]{:S(2)}, u32[]{:S(2)}) collective-permute-start(bf16[1024,128]{1,0:T(8,128)(2,1)} %place.1.x0), channel_id=1, source_target_pairs={{0,3},{1,0},{2,1},{3,2},{4,7},{5,4},{6,5},{7,6},{8,11},{9,8},{10,9... | collective-permute-start | bytes 786440 | tf_op jit(solution)/shard_map/ppermute | solution.py:398
  62.3 8.3 %collective-permute-start.1 = (bf16[1024,128]{1,0:T(8,128)(2,1)}, bf16[1024,128]{1,0:T(8,128)(2,1)S(1)}, u32[]{:S(2)}, u32[]{:S(2)}) collective-permute-start(bf16[1024,128]{1,0:T(8,128)(2,1)} %place.1.x0), channel_id=1, source_target_pairs={{0,2},{1,3},{2,0},{3,1},{4,6},{5,7},{6,4},{7,5},{8,10},{9,11},{10,... | collective-permute-start | bytes 786440 | tf_op jit(solution)/shard_map/ppermute | solution.py:398
  62.8 15.0 %copy-start.4 = (bf16[1024,128]{1,0:T(8,128)(2,1)}, bf16[1024,128]{1,0:T(8,128)(2,1)S(1)}, u32[]{:S(2)}) copy-start(bf16[1024,128]{1,0:T(8,128)(2,1)S(1)} %collective-permute-done.3.g1) | copy-start | bytes 786436
  62.8 15.0 %collective-permute-start.2 = (bf16[1024,128]{1,0:T(8,128)(2,1)}, bf16[1024,128]{1,0:T(8,128)(2,1)S(1)}, u32[]{:S(2)}, u32[]{:S(2)}) collective-permute-start(bf16[1024,128]{1,0:T(8,128)(2,1)} %place.1.x0), channel_id=1, source_target_pairs={{0,1},{1,2},{2,3},{3,0},{4,5},{5,6},{6,7},{7,4},{8,9},{9,10},{10,1... | collective-permute-start | bytes 786440 | tf_op jit(solution)/shard_map/ppermute | solution.py:398
  64.1 13.8 %copy-start.5 = (bf16[1024,128]{1,0:T(8,128)(2,1)}, bf16[1024,128]{1,0:T(8,128)(2,1)S(1)}, u32[]{:S(2)}) copy-start(bf16[1024,128]{1,0:T(8,128)(2,1)S(1)} %collective-permute-done.4.g2) | copy-start | bytes 786436
  64.1 13.8 %copy-start.7 = (bf16[1024,128]{1,0:T(8,128)(2,1)}, bf16[1024,128]{1,0:T(8,128)(2,1)S(1)}, u32[]{:S(2)}) copy-start(bf16[1024,128]{1,0:T(8,128)(2,1)S(1)} %collective-permute-done.5.g3) | copy-start | bytes 786436
  68.0 9.9 %copy-start.6 = (bf16[1024,128]{1,0:T(8,128)(2,1)}, bf16[1024,128]{1,0:T(8,128)(2,1)S(1)}, u32[]{:S(2)}) copy-start(bf16[1024,128]{1,0:T(8,128)(2,1)S(1)} %collective-permute-done.x1) | copy-start | bytes 786436
  70.6 7.3 %copy-start.8 = (bf16[1024,128]{1,0:T(8,128)(2,1)}, bf16[1024,128]{1,0:T(8,128)(2,1)S(1)}, u32[]{:S(2)}) copy-start(bf16[1024,128]{1,0:T(8,128)(2,1)S(1)} %collective-permute-done.1.x2) | copy-start | bytes 786436
  92.0 24.3 %collective-permute-start.9 = (bf16[1280,128]{1,0:T(8,128)(2,1)}, bf16[1280,128]{1,0:T(8,128)(2,1)S(1)}, u32[]{:S(2)}, u32[]{:S(2)}) collective-permute-start(bf16[1280,128]{1,0:T(8,128)(2,1)} %get-tuple-element.42), channel_id=1, source_target_pairs={{0,32},{32,0},{64,96},{96,64},{128,160},{160,128},{192,224},{224,1... | collective-permute-start | bytes 983048 | tf_op jit(solution)/shard_map/ppermute | solution.py:398
  97.3 15.0 %collective-permute-start.6 = (bf16[1024,128]{1,0:T(8,128)(2,1)}, bf16[1024,128]{1,0:T(8,128)(2,1)S(1)}, u32[]{:S(2)}, u32[]{:S(2)}) collective-permute-start(bf16[1024,128]{1,0:T(8,128)(2,1)} %get-tuple-element.36), channel_id=1, source_target_pairs={{0,1},{1,2},{2,3},{3,0},{4,5},{5,6},{6,7},{7,4},{8,9},{9,10},{10,1... | collective-permute-start | bytes 786440 | tf_op jit(solution)/shard_map/ppermute | solution.py:398
  97.3 15.0 %collective-permute-start.7 = (bf16[1024,128]{1,0:T(8,128)(2,1)}, bf16[1024,128]{1,0:T(8,128)(2,1)S(1)}, u32[]{:S(2)}, u32[]{:S(2)}) collective-permute-start(bf16[1024,128]{1,0:T(8,128)(2,1)} %get-tuple-element.37), channel_id=1, source_target_pairs={{0,3},{1,0},{2,1},{3,2},{4,7},{5,4},{6,5},{7,6},{8,11},{9,8},{10,9... | collective-permute-start | bytes 786440 | tf_op jit(solution)/shard_map/ppermute | solution.py:398
  100.0 12.3 %collective-permute-start.8 = (bf16[1024,128]{1,0:T(8,128)(2,1)}, bf16[1024,128]{1,0:T(8,128)(2,1)S(1)}, u32[]{:S(2)}, u32[]{:S(2)}) collective-permute-start(bf16[1024,128]{1,0:T(8,128)(2,1)} %get-tuple-element.38), channel_id=1, source_target_pairs={{0,2},{1,3},{2,0},{3,1},{4,6},{5,7},{6,4},{7,5},{8,10},{9,11},{10,... | collective-permute-start | bytes 786440 | tf_op jit(solution)/shard_map/ppermute | solution.py:398
  117.4 4.6 %collective-permute-start.10 = (bf16[320,128]{1,0:T(8,128)(2,1)S(1)}, bf16[320,128]{1,0:T(8,128)(2,1)S(1)}, u32[]{:S(2)}, u32[]{:S(2)}) collective-permute-start(bf16[320,128]{1,0:T(8,128)(2,1)S(1)} %get-tuple-element.48), channel_id=1, source_target_pairs={{0,64},{32,96},{64,128},{96,160},{128,192},{160,224},{192,0},{224,... | collective-permute-start | bytes 245768 | tf_op jit(solution)/shard_map/ppermute | solution.py:398
  118.3 6.0 %collective-permute-start.11 = (bf16[320,128]{1,0:T(8,128)(2,1)S(1)}, bf16[320,128]{1,0:T(8,128)(2,1)S(1)}, u32[]{:S(2)}, u32[]{:S(2)}) collective-permute-start(bf16[320,128]{1,0:T(8,128)(2,1)S(1)} %get-tuple-element.50), channel_id=1, source_target_pairs={{0,128},{32,160},{64,192},{96,224},{128,0},{160,32},{192,64},{224,... | collective-permute-start | bytes 245768 | tf_op jit(solution)/shard_map/ppermute | solution.py:398
  119.9 4.3 %collective-permute-start.12 = (bf16[320,128]{1,0:T(8,128)(2,1)S(1)}, bf16[320,128]{1,0:T(8,128)(2,1)S(1)}, u32[]{:S(2)}, u32[]{:S(2)}) collective-permute-start(bf16[320,128]{1,0:T(8,128)(2,1)S(1)} %get-tuple-element.49), channel_id=1, source_target_pairs={{0,192},{32,224},{64,0},{96,32},{128,64},{160,96},{192,128},{224,1... | collective-permute-start | bytes 245768 | tf_op jit(solution)/shard_map/ppermute | solution.py:398
  124.3 10.0 %collective-permute-start.13 = (bf16[320,128]{1,0:T(8,128)(2,1)S(1)}, bf16[320,128]{1,0:T(8,128)(2,1)S(1)}, u32[]{:S(2)}, u32[]{:S(2)}) collective-permute-start(bf16[320,128]{1,0:T(8,128)(2,1)S(1)} %fusion.2), channel_id=1, source_target_pairs={{0,4},{4,0},{8,12},{12,8},{16,20},{20,16},{24,28},{28,24},{1,5},{5... | collective-permute-start | bytes 245768 | tf_op jit(solution)/shard_map/ppermute | solution.py:398
  125.3 31.1 %all-to-all-start.2 = ((bf16[64,24,128]{2,1,0:T(8,128)(2,1)}), bf16[64,24,128]{2,1,0:T(8,128)(2,1)S(1)}, u32[]{:S(2)}, u32[]{:S(2)}) async-start(bf16[64,24,128]{2,1,0:T(8,128)(2,1)} %bitcast.14), calls=%async_computation.3 | async-start | bytes 786432 | tf_op jit(solution)/shard_map/all_to_all | solution.py:463
  134.3 14.8 %collective-permute-start.14 = (bf16[320,128]{1,0:T(8,128)(2,1)S(1)}, bf16[320,128]{1,0:T(8,128)(2,1)S(1)}, u32[]{:S(2)}, u32[]{:S(2)}) collective-permute-start(bf16[320,128]{1,0:T(8,128)(2,1)S(1)} %add_convert_fusion.3), channel_id=1, source_target_pairs={{0,8},{4,12},{8,0},{12,4},{16,24},{20,28},{24,16},{28,20},{1,9},{5... | collective-permute-start | bytes 245768 | tf_op jit(solution)/shard_map/ppermute | solution.py:398
  149.1 11.2 %copy-start.12 = (s32[64,1,128]{2,1,0:T(1,128)S(1)}, s32[64,1,128]{2,1,0:T(1,128)}, u32[]{:S(2)}) copy-start(s32[64,1,128]{2,1,0:T(1,128)} %all_to_all.21) | copy-start | bytes 98308
  149.1 7.3 %collective-permute-start.15 = (bf16[320,128]{1,0:T(8,128)(2,1)S(1)}, bf16[320,128]{1,0:T(8,128)(2,1)S(1)}, u32[]{:S(2)}, u32[]{:S(2)}) collective-permute-start(bf16[320,128]{1,0:T(8,128)(2,1)S(1)} %add_convert_fusion.2), channel_id=1, source_target_pairs={{0,16},{4,20},{8,24},{12,28},{16,0},{20,4},{24,8},{28,12},{1,17},{... | collective-permute-start | bytes 245768 | tf_op jit(solution)/shard_map/ppermute | solution.py:398
  156.4 8.3 %copy-start.11 = (bf16[320,128]{1,0:T(8,128)(2,1)}, bf16[320,128]{1,0:T(8,128)(2,1)S(1)}, u32[]{:S(2)}) copy-start(bf16[320,128]{1,0:T(8,128)(2,1)S(1)} %add_convert_fusion.1.p0) | copy-start | bytes 245764
  156.4 4.5 %copy-start.3 = (bf16[64,24,128]{2,1,0:T(8,128)(2,1)}, bf16[64,24,128]{2,1,0:T(8,128)(2,1)S(1)}, u32[]{:S(2)}) copy-start(bf16[64,24,128]{2,1,0:T(8,128)(2,1)S(1)} %all-to-all-done.2) | copy-start | bytes 1179652
  156.5 8.3 %collective-permute-start.16 = (bf16[320,128]{1,0:T(8,128)(2,1)S(1)}, bf16[320,128]{1,0:T(8,128)(2,1)S(1)}, u32[]{:S(2)}, u32[]{:S(2)}) collective-permute-start(bf16[320,128]{1,0:T(8,128)(2,1)S(1)} %add_convert_fusion.1.p0), channel_id=1, source_target_pairs={{0,192},{32,224},{64,0},{96,32},{128,64},{160,96},{192,128},{224,1... | collective-permute-start | bytes 245768 | tf_op jit(solution)/shard_map/ppermute | solution.py:398
  159.2 5.5 %collective-permute-start.17 = (bf16[320,128]{1,0:T(8,128)(2,1)S(1)}, bf16[320,128]{1,0:T(8,128)(2,1)S(1)}, u32[]{:S(2)}, u32[]{:S(2)}) collective-permute-start(bf16[320,128]{1,0:T(8,128)(2,1)S(1)} %add_convert_fusion.1.p0), channel_id=1, source_target_pairs={{0,128},{32,160},{64,192},{96,224},{128,0},{160,32},{192,64},{224,... | collective-permute-start | bytes 245768 | tf_op jit(solution)/shard_map/ppermute | solution.py:398
  159.5 5.3 %collective-permute-start.18 = (bf16[320,128]{1,0:T(8,128)(2,1)S(1)}, bf16[320,128]{1,0:T(8,128)(2,1)S(1)}, u32[]{:S(2)}, u32[]{:S(2)}) collective-permute-start(bf16[320,128]{1,0:T(8,128)(2,1)S(1)} %add_convert_fusion.1.p0), channel_id=1, source_target_pairs={{0,64},{32,96},{64,128},{96,160},{128,192},{160,224},{192,0},{224,... | collective-permute-start | bytes 245768 | tf_op jit(solution)/shard_map/ppermute | solution.py:398
  176.2 2.3 %copy-start = (bf16[1024,128]{1,0:T(8,128)(2,1)S(1)}, bf16[1024,128]{1,0:T(8,128)(2,1)}, u32[]{:S(2)}) copy-start(bf16[1024,128]{1,0:T(8,128)(2,1)} %place.1.x0) | copy-start | bytes 786436
  (9 other events, 6.8 us)
Sparse Core Ops, SparseCore 0:
  116.4 21.6 reduce-scatter.1

commit v3 on v1

--- a/solution.py
+++ b/solution.py
@@ -74,15 +74,25 @@
     )(owner, row)
 
 
-def fetch_kernel(req_ref, table_ref, out_ref, wide, got):
-    wide[...] = table_ref[...].astype(F32)
-
-    def step(r, carry):
-        for c in range(CAP):
-            got[pl.ds(r * CAP + c, 1), :] = wide[pl.ds(req_ref[r, c], 1), :]
-        return carry
-
-    lax.fori_loop(0, NOWN, step, 0)
+def hot_where(high, value, low_hot):
+    return jnp.where(high == value, low_hot, jnp.zeros_like(low_hot))
+
+
+def fetch_kernel(req_ref, table_ref, out_ref, got):
+    half = ROWS // 2
+    both = jnp.concatenate([table_ref[:half, :], table_ref[half:, :]], axis=1)
+    for c0 in range(0, CAP, 4):
+        hots, uppers = [], []
+        for c in range(c0, c0 + 4):
+            row = jnp.broadcast_to(req_ref[:, c : c + 1], (NOWN, 128))
+            low = ((row & 127) == iota((NOWN, 128), 1)).astype(F32).astype(BF)
+            high = ((row >> 7) & 7).astype(F32).astype(BF)
+            hots.append(jnp.concatenate([hot_where(high, j, low) for j in range(8)], axis=1))
+            uppers.append(row >= half)
+        pair = dot(jnp.concatenate(hots, axis=0), both, 1, 0)
+        rows = jnp.where(jnp.concatenate(uppers, axis=0), pair[:, 128:], pair[:, :128])
+        for i in range(4):
+            got[pl.ds(c0 + i, NOWN, stride=CAP), :] = rows[i * NOWN : (i + 1) * NOWN, :]
     out_ref[...] = got[...].astype(BF)
 
 
@@ -90,9 +100,9 @@
     return pl.pallas_call(
         fetch_kernel,
         out_shape=jax.ShapeDtypeStruct((SLOTS, 128), BF),
-        in_specs=[SM, VM],
+        in_specs=[VM, VM],
         out_specs=VM,
-        scratch_shapes=[pltpu.VMEM((ROWS, 128), F32), pltpu.VMEM((SLOTS, 128), F32)],
+        scratch_shapes=[pltpu.VMEM((SLOTS, 128), F32)],
         compiler_params=PARAMS,
         name="fetch",
     )(req, table)
@@ -104,14 +114,21 @@
 
 
 def place_kernel(slot_ref, back_ref, x_ref):
-    back = back_ref[...]
-    for b in range(TOK // 128):
-        col = column(slot_ref[b : b + 1, :]).astype(I32)
-        hot = jnp.concatenate(
-            [(col == iota((128, 128), 1) + 128 * k).astype(F32).astype(BF) for k in range(SLOTS // 128)],
-            axis=1,
-        )
-        x_ref[b * 128 : (b + 1) * 128, :] = dot(hot, back, 1, 0).astype(BF)
+    half = SLOTS // 2
+    both = jnp.concatenate([back_ref[:half, :], back_ref[half:, :]], axis=1)
+    for b0 in range(0, TOK // 128, 2):
+        hots, uppers = [], []
+        for b in (b0, b0 + 1):
+            slot = column(slot_ref[b : b + 1, :]).astype(I32)
+            upper = slot >= half
+            slot = jnp.where(upper, slot - half, slot)
+            low = ((slot & 127) == iota((128, 128), 1)).astype(F32).astype(BF)
+            high = (slot >> 7).astype(F32).astype(BF)
+            hots.append(jnp.concatenate([hot_where(high, j, low) for j in range(half // 128)], axis=1))
+            uppers.append(upper)
+        pair = dot(jnp.concatenate(hots, axis=0), both, 1, 0)
+        rows = jnp.where(jnp.concatenate(uppers, axis=0), pair[:, 128:], pair[:, :128])
+        x_ref[b0 * 128 : b0 * 128 + 256, :] = rows.astype(BF)
 
 
 def place(slot, back):
@@ -257,45 +274,62 @@
     )(pos, seg, *xs, *gs, w_in, w_out)
 
 
-def proj_kernel(pos_ref, y_ref, u_ref, dp_ref, g0, g1, g2, g3, wout_ref, z0, z1, z2, z3, dw_ref):
-    me = pos_ref[0]
+def proj_kernel(
+    pos_ref, y_ref, u_ref, dp_ref, g0, g1, g2, g3, wout_ref, mine_ref, other_ref, z0, z1, z2, z3, dw_ref
+):
+    me, core = pos_ref[0], pos_ref[1]
     gs, zs = (g0, g1, g2, g3), (z0, z1, z2, z3)
     for k in range(NT):
-        feat = lax.rem(me + k, NT)
-        at = pl.multiple_of(feat * 128, 128)
-        zs[k][...] = dot(y_ref[...], wout_ref[:, pl.ds(at, 128)], 1, 0).astype(BF)
+        at = pl.multiple_of(lax.rem(me + k, NT) * 128, 128)
         dw = dot(u_ref[:, k * 128 : (k + 1) * 128], dp_ref[...], 0, 0)
         for c in range(4):
             dw_ref[pl.ds(pl.multiple_of(c * 512 + at, 128), 128), :] = dw[:, c * 128 : (c + 1) * 128]
         dw_ref[pl.ds(pl.multiple_of(2048 + at, 128), 128), :] = dot(y_ref[...], gs[k][...], 0, 0)
+        zs[k][...] = dot(y_ref[...], wout_ref[:, pl.ds(at, 128)], 1, 0).astype(BF)
+    mine_ref[...] = dw_ref[pl.ds(pl.multiple_of(core * 1280, 1280), 1280), :]
+    other_ref[...] = dw_ref[pl.ds(pl.multiple_of(1280 - core * 1280, 1280), 1280), :].astype(BF)
 
 
 def project(pos, y, u, dp, gs, w_out):
     piece = jax.ShapeDtypeStruct((TOK, 128), BF)
     return pl.pallas_call(
         proj_kernel,
-        out_shape=(piece,) * 4 + (jax.ShapeDtypeStruct((2560, 128), F32),),
+        out_shape=(jax.ShapeDtypeStruct((1280, 128), F32), jax.ShapeDtypeStruct((1280, 128), BF))
+        + (piece,) * 4,
         in_specs=[SM] + [VM] * 8,
-        out_specs=(VM,) * 5,
+        out_specs=(VM,) * 6,
+        scratch_shapes=[pltpu.VMEM((2560, 128), F32)],
         compiler_params=PARAMS,
         name="project",
     )(pos, y, u, dp, *gs, w_out)
+
+
+def spread(at_ref, blocks, size, values):
+    lows, highs, pairs = [], [], []
+    for b in range(blocks):
+        at = at_ref[b : b + 1, :]
+        upper = column((at >= size).astype(F32)) > 0.5
+        value = values[b * 128 : (b + 1) * 128, :]
+        pairs.append(
+            jnp.concatenate([jnp.where(upper, 0.0, value), jnp.where(upper, value, 0.0)], axis=1).astype(BF)
+        )
+        at = jnp.broadcast_to(jnp.where(at >= size, at - size, at), (128, 128))
+        lows.append(((at & 127) == iota((128, 128), 0)).astype(F32).astype(BF))
+        highs.append((at >> 7).astype(F32).astype(BF))
+    low = jnp.concatenate(lows, axis=1)
+    high = jnp.concatenate(highs, axis=1)
+    pair = jnp.concatenate(pairs, axis=0)
+    return [dot(hot_where(high, s, low), pair, 1, 0) for s in range(size // 128)]
 
 
 def slots_kernel(slot_ref, grad_ref, d0, d1, d2, d3, out_ref):
     dx = grad_ref[...].astype(F32) + (
         d0[...].astype(F32) + d1[...].astype(F32) + d2[...].astype(F32) + d3[...].astype(F32)
     )
-    dx = dx.astype(BF)
-    for s in range(SLOTS // 128):
-        hot = jnp.concatenate(
-            [
-                (slot_ref[b : b + 1, :] == iota((128, 128), 0) + 128 * s).astype(F32).astype(BF)
-                for b in range(TOK // 128)
-            ],
-            axis=1,
-        )
-        out_ref[s * 128 : (s + 1) * 128, :] = dot(hot, dx, 1, 0).astype(BF)
+    half = SLOTS // 2
+    for s, both in enumerate(spread(slot_ref, TOK // 128, half, dx)):
+        out_ref[s * 128 : (s + 1) * 128, :] = both[:, :128].astype(BF)
+        out_ref[half + s * 128 : half + (s + 1) * 128, :] = both[:, 128:].astype(BF)
 
 
 def to_slots(slot, grad, parts):
@@ -310,16 +344,10 @@
 
 
 def add_rows_kernel(req_ref, arrived_ref, out_ref):
-    arrived = arrived_ref[...]
-    for s in range(ROWS // 128):
-        hot = jnp.concatenate(
-            [
-                (req_ref[b : b + 1, :] == iota((128, 128), 0) + 128 * s).astype(F32).astype(BF)
-                for b in range(SLOTS // 128)
-            ],
-            axis=1,
-        )
-        out_ref[s * 128 : (s + 1) * 128, :] = dot(hot, arrived, 1, 0)
+    half = ROWS // 2
+    for s, both in enumerate(spread(req_ref, SLOTS // 128, half, arrived_ref[...].astype(F32))):
+        out_ref[s * 128 : (s + 1) * 128, :] = both[:, :128]
+        out_ref[half + s * 128 : half + (s + 1) * 128, :] = both[:, 128:]
 
 
 def add_rows(req, arrived):
@@ -333,6 +361,41 @@
     )(req, arrived)
 
 
+def join_kernel(y_ref, p0, p1, p2, p3, out_ref):
+    for k, p in enumerate((p0, p1, p2, p3)):
+        at = pl.multiple_of(lax.rem(y_ref[0] + k, 4) * 320, 320)
+        out_ref[pl.ds(at, 320), :] = p[...]
+
+
+def join(y, parts):
+    return pl.pallas_call(
+        join_kernel,
+        out_shape=jax.ShapeDtypeStruct((1280, 128), BF),
+        in_specs=[SM] + [VM] * 4,
+        out_specs=VM,
+        compiler_params=PARAMS,
+        name="join",
+    )(y, *parts)
+
+
+def unpack_kernel(whole_ref, in_ref, out_ref):
+    for c in range(4):
+        in_ref[c, :, :] = whole_ref[c * 512 : (c + 1) * 512, :].astype(F32)
+    for k in range(NT):
+        out_ref[:, k * 128 : (k + 1) * 128] = whole_ref[2048 + k * 128 : 2176 + k * 128, :].astype(F32)
+
+
+def unpack(whole):
+    return pl.pallas_call(
+        unpack_kernel,
+        out_shape=(jax.ShapeDtypeStruct((4, D, 128), F32), jax.ShapeDtypeStruct((HD, D), F32)),
+        in_specs=[VM],
+        out_specs=(VM, VM),
+        compiler_params=PARAMS,
+        name="unpack",
+    )(whole)
+
+
 def shift(x, axis, fn, n):
     return lax.ppermute(x, axis, [(i, fn(i)) for i in range(n)])
 
@@ -354,12 +417,11 @@
     return lax.dynamic_index_in_dim(x, i, 0, keepdims=False)
 
 
-def reduce_weights(part):
+def reduce_weights(mine, other, grads):
     at = lax.axis_index("table")
     core, y = at % 2, at // 2
-    halves = part.reshape(2, 1280, 128)
-    other = shift(pick(halves, 1 - core).astype(BF), "table", lambda i: i ^ 1, 8)
-    mine = (pick(halves, core) + other.astype(F32)).reshape(4, 320, 128)
+    other = shift(other, "table", lambda i: i ^ 1, 8)
+    mine = (mine + other.astype(F32)).reshape(4, 320, 128)
     total = pick(mine, y)
     got = [
         shift(pick(mine, (y + k) % 4).astype(BF), "table", lambda i, k=k: (i + 2 * k) % 8, 8)
@@ -367,24 +429,32 @@
     ]
     for v in got:
         total = total + v.astype(F32)
+    total, grads = lax.optimization_barrier((total.astype(BF), grads))
     for bit in (1, 2, 4):
+        total = total.astype(F32) + shift(total, "seq", lambda i, b=bit: i ^ b, 8).astype(F32)
         total = total.astype(BF)
-        total = total.astype(F32) + shift(total, "seq", lambda i, b=bit: i ^ b, 8).astype(F32)
-    total = total.astype(BF)
+    return total, grads
+
+
+def gather_weights(total):
+    y = lax.axis_index("table") // 2
     parts = [total] + [
         shift(total, "table", lambda i, k=k: (i - 2 * k) % 8, 8) for k in range(1, 4)
     ]
-    stacked = jnp.roll(jnp.stack(parts), y, axis=0).reshape(1280, 128)
-    other = shift(stacked, "table", lambda i: i ^ 1, 8)
-    whole = jnp.where(
-        core == 0, jnp.concatenate([stacked, other]), jnp.concatenate([other, stacked])
+    whole = lax.all_gather(
+        join(y.astype(I32).reshape(1), parts),
+        "table",
+        axis=0,
+        tiled=True,
+        axis_index_groups=[[2 * i, 2 * i + 1] for i in range(4)],
     )
-    return whole.astype(F32)
+    return unpack(whole)
 
 
 def body(table, owner, local_row, segment_ids, proj_in, proj_out, grad_out):
-    pos = lax.axis_index("tensor").astype(I32).reshape(1)
+    pos = jnp.stack([lax.axis_index("tensor"), lax.axis_index("table") % 2]).astype(I32)
     requests, slot = route(owner.reshape(8, 128), local_row.reshape(8, 128))
+    requests, pos = lax.optimization_barrier((requests, pos))
     gs = order(gather_pieces(grad_out))
     received = lax.all_to_all(requests, BOTH, split_axis=0, concat_axis=0, tiled=True)
     rows = fetch(received, table)
@@ -393,8 +463,9 @@
     xs = order(gather_pieces(x))
     d0, d1, d2, d3, u, y, dp = layer(pos, segment_ids, xs, gs, proj_in, proj_out)
     dparts = scatter_pieces([d0, d1, d2, d3])
-    z0, z1, z2, z3, dw = project(pos, y, u, dp, gs, proj_out)
+    mine, other, z0, z1, z2, z3 = project(pos, y, u, dp, gs, proj_out)
     grads = to_slots(slot, grad_out, dparts)
+    total, grads = reduce_weights(mine, other, grads)
     arrived = lax.all_to_all(grads.reshape(NOWN, CAP, 128), BOTH, split_axis=0, concat_axis=0, tiled=True)
     zparts = scatter_pieces([z0, z1, z2, z3])
     layer_out = (
@@ -402,10 +473,9 @@
         + (zparts[0].astype(F32) + zparts[1].astype(F32) + zparts[2].astype(F32) + zparts[3].astype(F32))
     ).astype(BF)
     flat = received[:, :CAP].reshape(SLOTS // 128, 128)
+    total, arrived, layer_out = lax.optimization_barrier((total, arrived, layer_out))
     table_grad = add_rows(flat, arrived.reshape(SLOTS, 128))
-    whole = reduce_weights(dw)
-    grad_in = whole[:2048].reshape(4, 512, 128)
-    grad_outw = whole[2048:].reshape(4, 128, 128).transpose(1, 0, 2).reshape(128, 512)
+    grad_in, grad_outw = gather_weights(total)
     return layer_out, table_grad, grad_in, grad_outw
 
 

time: 164 us -> 159 us (0.970); the launches traced: 161 us -> 158 us
  blocking collectives: 22.3 us -> 28.8 us
  starting transfers between devices: 57.4 us -> 52.3 us
  waiting for transfers between devices: 39.1 us -> 35.2 us
  local copies, waits for them, and re-layouts: 6.93 us -> 4.18 us
    all_gather x0 -> x1, blocking collectives: none -> 6.41 us  [gather_weights(): lax.all_gather(join(y.astype(I32).reshape(1), parts), 'table', axis=0, ti...]
    all_to_all x1, starting transfers between devices: 17.2 us -> 12.4 us  [body(): lax.all_to_all(grads.reshape(NOWN, CAP, 128), BOTH, split_axis=0, concat_...]
    pallas_call x1 -> x3, Pallas kernels: 4.3 us -> 8.42 us  [the longest x1 4.46 us: project(): pl.pallas_call(proj_kernel, out_shape=(jax.ShapeDtypeStruct((1280, 128),...]
    ppermute x23 -> x22, waiting for transfers between devices: 27.7 us -> 25.2 us  [shift(): return lax.ppermute(x, axis, [(i, fn(i)) for i in range(n)])]
    unnamed x45 -> x50, local copies, waits for them, and re-layouts: 3.85 us -> 3.46 us
    ppermute x23 -> x22, starting transfers between devices: 35 us -> 34.9 us  [shift(): return lax.ppermute(x, axis, [(i, fn(i)) for i in range(n)])]
  transfers between devices with their start and end apart: 25 -> 24, of which waited for: 13 -> 9; matrix products, arithmetic and copies ran while one was open for 1% -> 2% of each run, Pallas kernels for 6% -> 5%
where the time goes in v3:
time: 159 us; the launch traced here: 158 us
  starting transfers between devices  52.3 us (33%)
  waiting for transfers between devices  35.2 us (22%)
  Pallas kernels  33.8 us (21%)
  blocking collectives  28.8 us (18%)
  local copies, waits for them, and re-layouts  4.18 us (3%)
  other arithmetic  2.79 us (2%)
    ppermute x22, starting transfers between devices, shift(): return lax.ppermute(x, axis, [(i, fn(i)) for i in range(n)])  34.9 us
    ppermute x22, waiting for transfers between devices, shift(): return lax.ppermute(x, axis, [(i, fn(i)) for i in range(n)])  25.2 us
    all_to_all x1, blocking collectives, body(): lax.all_to_all(requests, BOTH, split_axis=0, concat_axis=0, tiled=True)  22.4 us
    all_to_all x1, starting transfers between devices, body(): lax.all_to_all(grads.reshape(NOWN, CAP, 128), BOTH, split_axis=0, concat_...  12.4 us
    pallas_call x1, Pallas kernels, layer(): pl.pallas_call(layer_kernel, out_shape=(piece,) * 4 + (wide, piece, wide)...  11.4 us
    all_to_all x1, waiting for transfers between devices, body(): lax.all_to_all(rows.reshape(NOWN, CAP, 128), BOTH, split_axis=0, concat_a...  9.98 us
    all_gather x1, blocking collectives, gather_weights(): lax.all_gather(join(y.astype(I32).reshape(1), parts), 'table', axis=0, ti...  6.41 us
    all_to_all x1, starting transfers between devices, body(): lax.all_to_all(rows.reshape(NOWN, CAP, 128), BOTH, split_axis=0, concat_a...  4.98 us
  transfers between devices with their start and end apart: 24, of which 9 were waited for; matrix products, arithmetic and copies ran while one was open for 2% of the time, Pallas kernels for 5%

profile of v3, /device:TPU:1, one launch (start us, length us, event | category | flops | bytes accessed | tf_op | source)
XLA Modules:
  0.0 158.0 jit_solution(7440611836219876283)
XLA Ops:
  1.3 2.9 %route.1 = (s32[64,128]{1,0:T(8,128)}, s32[8,128]{1,0:T(8,128)}) custom-call(s32[8,128]{1,0:T(8,128)} %bitcast.37, s32[8,128]{1,0:T(8,128)} %bitcast.38), custom_call_target="tpu_custom_call" | custom-call | tf_op jit(solution)/shard_map/route/pallas_call | solution.py:64
  4.2 22.4 %all_to_all.21 = s32[64,1,128]{2,1,0:T(1,128)} all-to-all(s32[64,1,128]{2,1,0:T(1,128)} %bitcast.36), channel_id=1, replica_groups=mesh['table'=8,'seq'=8,'tensor'=4] {'table','seq'}, dimensions={0} | all-to-all | bytes 65536 | tf_op jit(solution)/shard_map/all_to_all | solution.py:459
  26.6 2.9 %fetch.1 = bf16[1536,128]{1,0:T(8,128)(2,1)} custom-call(s32[64,128]{1,0:T(8,128)} %bitcast.34, bf16[2048,128]{1,0:T(8,128)(2,1)} %table_ref.1), custom_call_target="tpu_custom_call" | custom-call | tf_op jit(solution)/shard_map/fetch/pallas_call | solution.py:100
  29.5 5.0 %all-to-all-start.1 = ((bf16[64,24,128]{2,1,0:T(8,128)(2,1)}), bf16[64,24,128]{2,1,0:T(8,128)(2,1)S(1)}, u32[]{:S(2)}, u32[]{:S(2)}) async-start(bf16[64,24,128]{2,1,0:T(8,128)(2,1)} %bitcast.33), calls=%async_computation.1 | async-start | bytes 786432 | tf_op jit(solution)/shard_map/all_to_all | solution.py:461
  34.5 1.3 collective-permute-start.5
  35.8 2.5 %collective-permute-start.4 = (bf16[1024,128]{1,0:T(8,128)(2,1)S(1)}, bf16[1024,128]{1,0:T(8,128)(2,1)S(1)}, u32[]{:S(2)}, u32[]{:S(2)}) collective-permute-start(bf16[1024,128]{1,0:T(8,128)(2,1)S(1)} %copy-done.1), channel_id=1, source_target_pairs={{0,2},{1,3},{2,0},{3,1},{4,6},{5,7},{6,4},{7,5},{8,10},{9,11},{10,... | collective-permute-start | bytes 786440 | tf_op jit(solution)/shard_map/ppermute | solution.py:400
  39.4 10.0 %all-to-all-done.1 = bf16[64,24,128]{2,1,0:T(8,128)(2,1)S(1)} async-done(((bf16[64,24,128]{2,1,0:T(8,128)(2,1)}), bf16[64,24,128]{2,1,0:T(8,128)(2,1)S(1)}, u32[]{:S(2)}, u32[]{:S(2)}) %all-to-all-start.1) | async-done | bytes 393248 | tf_op jit(solution)/shard_map/all_to_all | solution.py:461
  50.1 2.4 %place.1.x0 = bf16[1024,128]{1,0:T(8,128)(2,1)} custom-call(s32[8,128]{1,0:T(8,128)} %get-tuple-element.30.slot_ref, bf16[1536,128]{1,0:T(8,128)(2,1)} %bitcast.31), custom_call_target="tpu_custom_call" | custom-call | tf_op jit(solution)/shard_map/place/pallas_call | solution.py:135
  52.5 1.2 collective-permute-start.2
  53.7 2.5 %collective-permute-start.1 = (bf16[1024,128]{1,0:T(8,128)(2,1)}, bf16[1024,128]{1,0:T(8,128)(2,1)S(1)}, u32[]{:S(2)}, u32[]{:S(2)}) collective-permute-start(bf16[1024,128]{1,0:T(8,128)(2,1)} %place.1.x0), channel_id=1, source_target_pairs={{0,2},{1,3},{2,0},{3,1},{4,6},{5,7},{6,4},{7,5},{8,10},{9,11},{10,... | collective-permute-start | bytes 786440 | tf_op jit(solution)/shard_map/ppermute | solution.py:400
  57.3 3.4 %collective-permute-done.2.x3 = bf16[1024,128]{1,0:T(8,128)(2,1)S(1)} collective-permute-done((bf16[1024,128]{1,0:T(8,128)(2,1)}, bf16[1024,128]{1,0:T(8,128)(2,1)S(1)}, u32[]{:S(2)}, u32[]{:S(2)}) %collective-permute-start.2) | collective-permute-done | bytes 262176 | tf_op jit(solution)/shard_map/ppermute | solution.py:400
  60.7 6.6 %collective-permute-done.1.x2 = bf16[1024,128]{1,0:T(8,128)(2,1)S(1)} collective-permute-done((bf16[1024,128]{1,0:T(8,128)(2,1)}, bf16[1024,128]{1,0:T(8,128)(2,1)S(1)}, u32[]{:S(2)}, u32[]{:S(2)}) %collective-permute-start.1) | collective-permute-done | bytes 262176 | tf_op jit(solution)/shard_map/ppermute | solution.py:400
  68.7 11.4 %layer.1 = (bf16[1024,128]{1,0:T(8,128)(2,1)}, bf16[1024,128]{1,0:T(8,128)(2,1)}, bf16[1024,128]{1,0:T(8,128)(2,1)}, bf16[1024,128]{1,0:T(8,128)(2,1)}, bf16[102...) custom-call(s32[2]{0:T(128)} %pad_add_fusion.pos_ref, s32[1,1024]{1,0:T(1,128)} %seg_ref.1, ...), custom_call_target="tpu_custom_call" | custom-call | tf_op jit(solution)/shard_map/layer/pallas_call | solution.py:255
  80.1 4.5 %project.1 = (f32[1280,128]{1,0:T(8,128)}, bf16[1280,128]{1,0:T(8,128)(2,1)}, bf16[1024,128]{1,0:T(8,128)(2,1)}, bf16[1024,128]{1,0:T(8,128)(2,1)}, bf16[1024,12...) custom-call(s32[2]{0:T(128)} %pad_add_fusion.pos_ref, bf16[1024,128]{1,0:T(8,128)(2,1)} %get-tuple-element.32.y_ref, ...), custom_call_target="tpu_custom_call" | custom-call | tf_op jit(solution)/shard_map/project/pallas_call | solution.py:295
  84.6 2.0 %collective-permute-start.6 = (bf16[1280,128]{1,0:T(8,128)(2,1)}, bf16[1280,128]{1,0:T(8,128)(2,1)S(1)}, u32[]{:S(2)}, u32[]{:S(2)}) collective-permute-start(bf16[1280,128]{1,0:T(8,128)(2,1)} %get-tuple-element.36), channel_id=1, source_target_pairs={{0,32},{32,0},{64,96},{96,64},{128,160},{160,128},{192,224},{224,1... | collective-permute-start | bytes 983048 | tf_op jit(solution)/shard_map/ppermute | solution.py:400
  87.0 2.3 %collective-permute-start.11 = (bf16[1024,128]{1,0:T(8,128)(2,1)S(1)}, bf16[1024,128]{1,0:T(8,128)(2,1)S(1)}, u32[]{:S(2)}, u32[]{:S(2)}) collective-permute-start(bf16[1024,128]{1,0:T(8,128)(2,1)S(1)} %copy-done.23), channel_id=1, source_target_pairs={{0,3},{1,0},{2,1},{3,2},{4,7},{5,4},{6,5},{7,6},{8,11},{9,8},{10,9... | collective-permute-start | bytes 786440 | tf_op jit(solution)/shard_map/ppermute | solution.py:400
  92.0 1.9 %collective-permute-start.9 = (bf16[320,128]{1,0:T(8,128)(2,1)S(1)}, bf16[320,128]{1,0:T(8,128)(2,1)S(1)}, u32[]{:S(2)}, u32[]{:S(2)}) collective-permute-start(bf16[320,128]{1,0:T(8,128)(2,1)S(1)} %get-tuple-element.53), channel_id=1, source_target_pairs={{0,192},{32,224},{64,0},{96,32},{128,64},{160,96},{192,128},{224,1... | collective-permute-start | bytes 245768 | tf_op jit(solution)/shard_map/ppermute | solution.py:400
  93.9 1.8 %collective-permute-done.10.d1 = bf16[1024,128]{1,0:T(8,128)(2,1)S(1)} collective-permute-done((bf16[1024,128]{1,0:T(8,128)(2,1)S(1)}, bf16[1024,128]{1,0:T(8,128)(2,1)S(1)}, u32[]{:S(2)}, u32[]{:S(2)}) %collective-permute-start.10) | collective-permute-done | bytes 262176 | tf_op jit(solution)/shard_map/ppermute | solution.py:400
  95.7 2.1 %collective-permute-start.8 = (bf16[320,128]{1,0:T(8,128)(2,1)S(1)}, bf16[320,128]{1,0:T(8,128)(2,1)S(1)}, u32[]{:S(2)}, u32[]{:S(2)}) collective-permute-start(bf16[320,128]{1,0:T(8,128)(2,1)S(1)} %get-tuple-element.54), channel_id=1, source_target_pairs={{0,128},{32,160},{64,192},{96,224},{128,0},{160,32},{192,64},{224,... | collective-permute-start | bytes 245768 | tf_op jit(solution)/shard_map/ppermute | solution.py:400
  97.8 3.2 %collective-permute-done.12.d3 = bf16[1024,128]{1,0:T(8,128)(2,1)S(1)} collective-permute-done((bf16[1024,128]{1,0:T(8,128)(2,1)S(1)}, bf16[1024,128]{1,0:T(8,128)(2,1)S(1)}, u32[]{:S(2)}, u32[]{:S(2)}) %collective-permute-start.12) | collective-permute-done | bytes 262176 | tf_op jit(solution)/shard_map/ppermute | solution.py:400
  101.7 2.8 %to_slots.1 = bf16[1536,128]{1,0:T(8,128)(2,1)} custom-call(s32[8,128]{1,0:T(8,128)} %get-tuple-element.30.slot_ref, bf16[1024,128]{1,0:T(8,128)(2,1)} %grad_ref.1, bf16[1024,128]{1,0:T(8,128)(2,1)} %get-tuple-element.37.d0, bf16[1024,128]{1,0:T(8,128)(2,1)} %copy-done.13, bf16[1024,128]{1,0:T(8,128)(2,1)} %copy-done.14, bf16[1024,128]{1,0:T(8,128)(2,1)} %copy-done.15), custom_call_target="tpu_custom_call" | custom-call | tf_op jit(solution)/shard_map/to_slots/pallas_call | solution.py:336
  105.7 2.2 %collective-permute-done.13 = bf16[320,128]{1,0:T(8,128)(2,1)S(1)} collective-permute-done((bf16[320,128]{1,0:T(8,128)(2,1)S(1)}, bf16[320,128]{1,0:T(8,128)(2,1)S(1)}, u32[]{:S(2)}, u32[]{:S(2)}) %collective-permute-start.13) | collective-permute-done | bytes 81952 | tf_op jit(solution)/shard_map/ppermute | solution.py:400
  108.8 12.4 %all-to-all-start.2 = ((bf16[64,24,128]{2,1,0:T(8,128)(2,1)}), bf16[64,24,128]{2,1,0:T(8,128)(2,1)S(1)}, u32[]{:S(2)}, u32[]{:S(2)}) async-start(bf16[64,24,128]{2,1,0:T(8,128)(2,1)} %bitcast.14), calls=%async_computation.2 | async-start | bytes 786432 | tf_op jit(solution)/shard_map/all_to_all | solution.py:469
  121.3 2.7 %collective-permute-start.17 = (bf16[1024,128]{1,0:T(8,128)(2,1)S(1)}, bf16[1024,128]{1,0:T(8,128)(2,1)S(1)}, u32[]{:S(2)}, u32[]{:S(2)}) collective-permute-start(bf16[1024,128]{1,0:T(8,128)(2,1)S(1)} %copy-done.20), channel_id=1, source_target_pairs={{0,3},{1,0},{2,1},{3,2},{4,7},{5,4},{6,5},{7,6},{8,11},{9,8},{10,9... | collective-permute-start | bytes 786440 | tf_op jit(solution)/shard_map/ppermute | solution.py:400
  124.0 5.4 %collective-permute-start.15 = (bf16[320,128]{1,0:T(8,128)(2,1)S(1)}, bf16[320,128]{1,0:T(8,128)(2,1)S(1)}, u32[]{:S(2)}, u32[]{:S(2)}) collective-permute-start(bf16[320,128]{1,0:T(8,128)(2,1)S(1)} %add_convert_fusion.2), channel_id=1, source_target_pairs={{0,16},{4,20},{8,24},{12,28},{16,0},{20,4},{24,8},{28,12},{1,17},{... | collective-permute-start | bytes 245768 | tf_op jit(solution)/shard_map/ppermute | solution.py:400
  129.4 6.2 %collective-permute-done.16 = bf16[1024,128]{1,0:T(8,128)(2,1)S(1)} collective-permute-done((bf16[1024,128]{1,0:T(8,128)(2,1)S(1)}, bf16[1024,128]{1,0:T(8,128)(2,1)S(1)}, u32[]{:S(2)}, u32[]{:S(2)}) %collective-permute-start.16) | collective-permute-done | bytes 262176 | tf_op jit(solution)/shard_map/ppermute | solution.py:400
  136.5 1.7 %collective-permute-done.15 = bf16[320,128]{1,0:T(8,128)(2,1)S(1)} collective-permute-done((bf16[320,128]{1,0:T(8,128)(2,1)S(1)}, bf16[320,128]{1,0:T(8,128)(2,1)S(1)}, u32[]{:S(2)}, u32[]{:S(2)}) %collective-permute-start.15) | collective-permute-done | bytes 81952 | tf_op jit(solution)/shard_map/ppermute | solution.py:400
  139.5 2.6 %collective-permute-start.20 = (bf16[320,128]{1,0:T(8,128)(2,1)S(1)}, bf16[320,128]{1,0:T(8,128)(2,1)S(1)}, u32[]{:S(2)}, u32[]{:S(2)}) collective-permute-start(bf16[320,128]{1,0:T(8,128)(2,1)S(1)} %add_convert_fusion.1.p0), channel_id=1, source_target_pairs={{0,128},{32,160},{64,192},{96,224},{128,0},{160,32},{192,64},{224,... | collective-permute-start | bytes 245768 | tf_op jit(solution)/shard_map/ppermute | solution.py:400
  143.9 3.1 %add_rows.1 = f32[2048,128]{1,0:T(8,128)} custom-call(s32[12,128]{1,0:T(8,128)} %reshape.46.req_ref, bf16[1536,128]{1,0:T(8,128)(2,1)} %bitcast.32), custom_call_target="tpu_custom_call" | custom-call | tf_op jit(solution)/shard_map/add_rows/pallas_call | solution.py:354
  147.7 1.8 %join.1 = bf16[1280,128]{1,0:T(8,128)(2,1)} custom-call(s32[1]{0:T(128)} %bitcast.16.y_ref, bf16[320,128]{1,0:T(8,128)(2,1)} %copy-done.7, bf16[320,128]{1,0:T(8,128)(2,1)} %copy-done.18, bf16[320,128]{1,0:T(8,128)(2,1)} %copy-done.17, bf16[320,128]{1,0:T(8,128)(2,1)} %copy-done.16), custom_call_target="tpu_custom_call" | custom-call | tf_op jit(solution)/shard_map/join/pallas_call | solution.py:371
  149.4 6.4 %all_gather.3.whole_ref = bf16[2560,128]{1,0:T(8,128)(2,1)} all-gather(bf16[1280,128]{1,0:T(8,128)(2,1)} %join.1), channel_id=1, replica_groups={{0,32},{64,96},{128,160},{192,224},{1,33},{65,97},{129,161},{193,225},{..., dimensions={0}, use_global_device_ids=true | all-gather | bytes 983040 | tf_op jit(solution)/shard_map/all_gather | solution.py:444
  155.8 2.2 %unpack.1 = (f32[4,512,128]{2,1,0:T(8,128)}, f32[128,512]{1,0:T(8,128)}) custom-call(bf16[2560,128]{1,0:T(8,128)(2,1)} %all_gather.3.whole_ref), custom_call_target="tpu_custom_call" | custom-call | tf_op jit(solution)/shard_map/unpack/pallas_call | solution.py:389
  (86 shorter events, 15.7 us)
Async XLA Ops:
  29.5 19.9 %all-to-all-start.1 = ((bf16[64,24,128]{2,1,0:T(8,128)(2,1)}), bf16[64,24,128]{2,1,0:T(8,128)(2,1)S(1)}, u32[]{:S(2)}, u32[]{:S(2)}) async-start(bf16[64,24,128]{2,1,0:T(8,128)(2,1)} %bitcast.33), calls=%async_computation.1 | async-start | bytes 786432 | tf_op jit(solution)/shard_map/all_to_all | solution.py:461
  34.5 21.6 %collective-permute-start.5 = (bf16[1024,128]{1,0:T(8,128)(2,1)S(1)}, bf16[1024,128]{1,0:T(8,128)(2,1)S(1)}, u32[]{:S(2)}, u32[]{:S(2)}) collective-permute-start(bf16[1024,128]{1,0:T(8,128)(2,1)S(1)} %copy-done.1), channel_id=1, source_target_pairs={{0,1},{1,2},{2,3},{3,0},{4,5},{5,6},{6,7},{7,4},{8,9},{9,10},{10,1... | collective-permute-start | bytes 786440 | tf_op jit(solution)/shard_map/ppermute | solution.py:400
  35.8 21.5 %collective-permute-start.4 = (bf16[1024,128]{1,0:T(8,128)(2,1)S(1)}, bf16[1024,128]{1,0:T(8,128)(2,1)S(1)}, u32[]{:S(2)}, u32[]{:S(2)}) collective-permute-start(bf16[1024,128]{1,0:T(8,128)(2,1)S(1)} %copy-done.1), channel_id=1, source_target_pairs={{0,2},{1,3},{2,0},{3,1},{4,6},{5,7},{6,4},{7,5},{8,10},{9,11},{10,... | collective-permute-start | bytes 786440 | tf_op jit(solution)/shard_map/ppermute | solution.py:400
  38.2 19.1 %collective-permute-start.3 = (bf16[1024,128]{1,0:T(8,128)(2,1)S(1)}, bf16[1024,128]{1,0:T(8,128)(2,1)S(1)}, u32[]{:S(2)}, u32[]{:S(2)}) collective-permute-start(bf16[1024,128]{1,0:T(8,128)(2,1)S(1)} %copy-done.1), channel_id=1, source_target_pairs={{0,3},{1,0},{2,1},{3,2},{4,7},{5,4},{6,5},{7,6},{8,11},{9,8},{10,9... | collective-permute-start | bytes 786440 | tf_op jit(solution)/shard_map/ppermute | solution.py:400
  52.5 8.2 %collective-permute-start.2 = (bf16[1024,128]{1,0:T(8,128)(2,1)}, bf16[1024,128]{1,0:T(8,128)(2,1)S(1)}, u32[]{:S(2)}, u32[]{:S(2)}) collective-permute-start(bf16[1024,128]{1,0:T(8,128)(2,1)} %place.1.x0), channel_id=1, source_target_pairs={{0,1},{1,2},{2,3},{3,0},{4,5},{5,6},{6,7},{7,4},{8,9},{9,10},{10,1... | collective-permute-start | bytes 786440 | tf_op jit(solution)/shard_map/ppermute | solution.py:400
  53.7 13.6 %collective-permute-start.1 = (bf16[1024,128]{1,0:T(8,128)(2,1)}, bf16[1024,128]{1,0:T(8,128)(2,1)S(1)}, u32[]{:S(2)}, u32[]{:S(2)}) collective-permute-start(bf16[1024,128]{1,0:T(8,128)(2,1)} %place.1.x0), channel_id=1, source_target_pairs={{0,2},{1,3},{2,0},{3,1},{4,6},{5,7},{6,4},{7,5},{8,10},{9,11},{10,... | collective-permute-start | bytes 786440 | tf_op jit(solution)/shard_map/ppermute | solution.py:400
  56.1 11.3 %copy-start.4 = (bf16[1024,128]{1,0:T(8,128)(2,1)}, bf16[1024,128]{1,0:T(8,128)(2,1)S(1)}, u32[]{:S(2)}) copy-start(bf16[1024,128]{1,0:T(8,128)(2,1)S(1)} %collective-permute-done.5.g3) | copy-start | bytes 786436
  56.1 11.3 %collective-permute-start = (bf16[1024,128]{1,0:T(8,128)(2,1)}, bf16[1024,128]{1,0:T(8,128)(2,1)S(1)}, u32[]{:S(2)}, u32[]{:S(2)}) collective-permute-start(bf16[1024,128]{1,0:T(8,128)(2,1)} %place.1.x0), channel_id=1, source_target_pairs={{0,3},{1,0},{2,1},{3,2},{4,7},{5,4},{6,5},{7,6},{8,11},{9,8},{10,9... | collective-permute-start | bytes 786440 | tf_op jit(solution)/shard_map/ppermute | solution.py:400
  57.3 10.1 %copy-start.5 = (bf16[1024,128]{1,0:T(8,128)(2,1)}, bf16[1024,128]{1,0:T(8,128)(2,1)S(1)}, u32[]{:S(2)}) copy-start(bf16[1024,128]{1,0:T(8,128)(2,1)S(1)} %collective-permute-done.4.g2) | copy-start | bytes 786436
  57.3 10.1 %copy-start.6 = (bf16[1024,128]{1,0:T(8,128)(2,1)}, bf16[1024,128]{1,0:T(8,128)(2,1)S(1)}, u32[]{:S(2)}) copy-start(bf16[1024,128]{1,0:T(8,128)(2,1)S(1)} %collective-permute-done.3.g1) | copy-start | bytes 786436
  84.6 5.2 %collective-permute-start.6 = (bf16[1280,128]{1,0:T(8,128)(2,1)}, bf16[1280,128]{1,0:T(8,128)(2,1)S(1)}, u32[]{:S(2)}, u32[]{:S(2)}) collective-permute-start(bf16[1280,128]{1,0:T(8,128)(2,1)} %get-tuple-element.36), channel_id=1, source_target_pairs={{0,32},{32,0},{64,96},{96,64},{128,160},{160,128},{192,224},{224,1... | collective-permute-start | bytes 983048 | tf_op jit(solution)/shard_map/ppermute | solution.py:400
  86.6 9.1 %collective-permute-start.10 = (bf16[1024,128]{1,0:T(8,128)(2,1)S(1)}, bf16[1024,128]{1,0:T(8,128)(2,1)S(1)}, u32[]{:S(2)}, u32[]{:S(2)}) collective-permute-start(bf16[1024,128]{1,0:T(8,128)(2,1)S(1)} %copy-done.24), channel_id=1, source_target_pairs={{0,1},{1,2},{2,3},{3,0},{4,5},{5,6},{6,7},{7,4},{8,9},{9,10},{10,1... | collective-permute-start | bytes 786440 | tf_op jit(solution)/shard_map/ppermute | solution.py:400
  87.0 10.8 %collective-permute-start.11 = (bf16[1024,128]{1,0:T(8,128)(2,1)S(1)}, bf16[1024,128]{1,0:T(8,128)(2,1)S(1)}, u32[]{:S(2)}, u32[]{:S(2)}) collective-permute-start(bf16[1024,128]{1,0:T(8,128)(2,1)S(1)} %copy-done.23), channel_id=1, source_target_pairs={{0,3},{1,0},{2,1},{3,2},{4,7},{5,4},{6,5},{7,6},{8,11},{9,8},{10,9... | collective-permute-start | bytes 786440 | tf_op jit(solution)/shard_map/ppermute | solution.py:400
  89.3 11.7 %collective-permute-start.12 = (bf16[1024,128]{1,0:T(8,128)(2,1)S(1)}, bf16[1024,128]{1,0:T(8,128)(2,1)S(1)}, u32[]{:S(2)}, u32[]{:S(2)}) collective-permute-start(bf16[1024,128]{1,0:T(8,128)(2,1)S(1)} %copy-done.22), channel_id=1, source_target_pairs={{0,2},{1,3},{2,0},{3,1},{4,6},{5,7},{6,4},{7,5},{8,10},{9,11},{10,... | collective-permute-start | bytes 786440 | tf_op jit(solution)/shard_map/ppermute | solution.py:400
  90.9 13.5 %collective-permute-start.7 = (bf16[320,128]{1,0:T(8,128)(2,1)S(1)}, bf16[320,128]{1,0:T(8,128)(2,1)S(1)}, u32[]{:S(2)}, u32[]{:S(2)}) collective-permute-start(bf16[320,128]{1,0:T(8,128)(2,1)S(1)} %get-tuple-element.52), channel_id=1, source_target_pairs={{0,64},{32,96},{64,128},{96,160},{128,192},{160,224},{192,0},{224,... | collective-permute-start | bytes 245768 | tf_op jit(solution)/shard_map/ppermute | solution.py:400
  92.0 12.5 %collective-permute-start.9 = (bf16[320,128]{1,0:T(8,128)(2,1)S(1)}, bf16[320,128]{1,0:T(8,128)(2,1)S(1)}, u32[]{:S(2)}, u32[]{:S(2)}) collective-permute-start(bf16[320,128]{1,0:T(8,128)(2,1)S(1)} %get-tuple-element.53), channel_id=1, source_target_pairs={{0,192},{32,224},{64,0},{96,32},{128,64},{160,96},{192,128},{224,1... | collective-permute-start | bytes 245768 | tf_op jit(solution)/shard_map/ppermute | solution.py:400
  95.7 8.8 %collective-permute-start.8 = (bf16[320,128]{1,0:T(8,128)(2,1)S(1)}, bf16[320,128]{1,0:T(8,128)(2,1)S(1)}, u32[]{:S(2)}, u32[]{:S(2)}) collective-permute-start(bf16[320,128]{1,0:T(8,128)(2,1)S(1)} %get-tuple-element.54), channel_id=1, source_target_pairs={{0,128},{32,160},{64,192},{96,224},{128,0},{160,32},{192,64},{224,... | collective-permute-start | bytes 245768 | tf_op jit(solution)/shard_map/ppermute | solution.py:400
  104.5 16.7 %copy-start.21 = (bf16[1024,128]{1,0:T(8,128)(2,1)S(1)}, bf16[1024,128]{1,0:T(8,128)(2,1)}, u32[]{:S(2)}) copy-start(bf16[1024,128]{1,0:T(8,128)(2,1)} %get-tuple-element.44) | copy-start | bytes 786436
  104.5 16.8 %copy-start.20 = (bf16[1024,128]{1,0:T(8,128)(2,1)S(1)}, bf16[1024,128]{1,0:T(8,128)(2,1)}, u32[]{:S(2)}) copy-start(bf16[1024,128]{1,0:T(8,128)(2,1)} %get-tuple-element.45) | copy-start | bytes 786436
  104.6 3.4 %collective-permute-start.13 = (bf16[320,128]{1,0:T(8,128)(2,1)S(1)}, bf16[320,128]{1,0:T(8,128)(2,1)S(1)}, u32[]{:S(2)}, u32[]{:S(2)}) collective-permute-start(bf16[320,128]{1,0:T(8,128)(2,1)S(1)} %fusion.2), channel_id=1, source_target_pairs={{0,4},{4,0},{8,12},{12,8},{16,20},{20,16},{24,28},{28,24},{1,5},{5... | collective-permute-start | bytes 245768 | tf_op jit(solution)/shard_map/ppermute | solution.py:400
  108.0 16.0 %collective-permute-start.14 = (bf16[320,128]{1,0:T(8,128)(2,1)S(1)}, bf16[320,128]{1,0:T(8,128)(2,1)S(1)}, u32[]{:S(2)}, u32[]{:S(2)}) collective-permute-start(bf16[320,128]{1,0:T(8,128)(2,1)S(1)} %add_convert_fusion.3), channel_id=1, source_target_pairs={{0,8},{4,12},{8,0},{12,4},{16,24},{20,28},{24,16},{28,20},{1,9},{5... | collective-permute-start | bytes 245768 | tf_op jit(solution)/shard_map/ppermute | solution.py:400
  108.8 15.2 %copy-start.19 = (bf16[1024,128]{1,0:T(8,128)(2,1)S(1)}, bf16[1024,128]{1,0:T(8,128)(2,1)}, u32[]{:S(2)}) copy-start(bf16[1024,128]{1,0:T(8,128)(2,1)} %get-tuple-element.46) | copy-start | bytes 786436
  108.8 26.7 %copy-start = (bf16[1024,128]{1,0:T(8,128)(2,1)S(1)}, bf16[1024,128]{1,0:T(8,128)(2,1)}, u32[]{:S(2)}) copy-start(bf16[1024,128]{1,0:T(8,128)(2,1)} %place.1.x0) | copy-start | bytes 786436
  108.8 26.7 %copy-start.12 = (bf16[1024,128]{1,0:T(8,128)(2,1)S(1)}, bf16[1024,128]{1,0:T(8,128)(2,1)}, u32[]{:S(2)}) copy-start(bf16[1024,128]{1,0:T(8,128)(2,1)} %get-tuple-element.43) | copy-start | bytes 786436
  108.8 29.4 %all-to-all-start.2 = ((bf16[64,24,128]{2,1,0:T(8,128)(2,1)}), bf16[64,24,128]{2,1,0:T(8,128)(2,1)S(1)}, u32[]{:S(2)}, u32[]{:S(2)}) async-start(bf16[64,24,128]{2,1,0:T(8,128)(2,1)} %bitcast.14), calls=%async_computation.2 | async-start | bytes 786432 | tf_op jit(solution)/shard_map/all_to_all | solution.py:469
  121.2 14.3 %collective-permute-start.16 = (bf16[1024,128]{1,0:T(8,128)(2,1)S(1)}, bf16[1024,128]{1,0:T(8,128)(2,1)S(1)}, u32[]{:S(2)}, u32[]{:S(2)}) collective-permute-start(bf16[1024,128]{1,0:T(8,128)(2,1)S(1)} %copy-done.21), channel_id=1, source_target_pairs={{0,1},{1,2},{2,3},{3,0},{4,5},{5,6},{6,7},{7,4},{8,9},{9,10},{10,1... | collective-permute-start | bytes 786440 | tf_op jit(solution)/shard_map/ppermute | solution.py:400
  121.3 14.2 %collective-permute-start.17 = (bf16[1024,128]{1,0:T(8,128)(2,1)S(1)}, bf16[1024,128]{1,0:T(8,128)(2,1)S(1)}, u32[]{:S(2)}, u32[]{:S(2)}) collective-permute-start(bf16[1024,128]{1,0:T(8,128)(2,1)S(1)} %copy-done.20), channel_id=1, source_target_pairs={{0,3},{1,0},{2,1},{3,2},{4,7},{5,4},{6,5},{7,6},{8,11},{9,8},{10,9... | collective-permute-start | bytes 786440 | tf_op jit(solution)/shard_map/ppermute | solution.py:400
  124.0 11.6 %collective-permute-start.18 = (bf16[1024,128]{1,0:T(8,128)(2,1)S(1)}, bf16[1024,128]{1,0:T(8,128)(2,1)S(1)}, u32[]{:S(2)}, u32[]{:S(2)}) collective-permute-start(bf16[1024,128]{1,0:T(8,128)(2,1)S(1)} %copy-done.19), channel_id=1, source_target_pairs={{0,2},{1,3},{2,0},{3,1},{4,6},{5,7},{6,4},{7,5},{8,10},{9,11},{10,... | collective-permute-start | bytes 786440 | tf_op jit(solution)/shard_map/ppermute | solution.py:400
  124.0 14.2 %collective-permute-start.15 = (bf16[320,128]{1,0:T(8,128)(2,1)S(1)}, bf16[320,128]{1,0:T(8,128)(2,1)S(1)}, u32[]{:S(2)}, u32[]{:S(2)}) collective-permute-start(bf16[320,128]{1,0:T(8,128)(2,1)S(1)} %add_convert_fusion.2), channel_id=1, source_target_pairs={{0,16},{4,20},{8,24},{12,28},{16,0},{20,4},{24,8},{28,12},{1,17},{... | collective-permute-start | bytes 245768 | tf_op jit(solution)/shard_map/ppermute | solution.py:400
  138.3 8.7 %collective-permute-start.21 = (bf16[320,128]{1,0:T(8,128)(2,1)S(1)}, bf16[320,128]{1,0:T(8,128)(2,1)S(1)}, u32[]{:S(2)}, u32[]{:S(2)}) collective-permute-start(bf16[320,128]{1,0:T(8,128)(2,1)S(1)} %add_convert_fusion.1.p0), channel_id=1, source_target_pairs={{0,64},{32,96},{64,128},{96,160},{128,192},{160,224},{192,0},{224,... | collective-permute-start | bytes 245768 | tf_op jit(solution)/shard_map/ppermute | solution.py:400
  139.5 7.5 %collective-permute-start.20 = (bf16[320,128]{1,0:T(8,128)(2,1)S(1)}, bf16[320,128]{1,0:T(8,128)(2,1)S(1)}, u32[]{:S(2)}, u32[]{:S(2)}) collective-permute-start(bf16[320,128]{1,0:T(8,128)(2,1)S(1)} %add_convert_fusion.1.p0), channel_id=1, source_target_pairs={{0,128},{32,160},{64,192},{96,224},{128,0},{160,32},{192,64},{224,... | collective-permute-start | bytes 245768 | tf_op jit(solution)/shard_map/ppermute | solution.py:400
  142.1 4.9 %collective-permute-start.19 = (bf16[320,128]{1,0:T(8,128)(2,1)S(1)}, bf16[320,128]{1,0:T(8,128)(2,1)S(1)}, u32[]{:S(2)}, u32[]{:S(2)}) collective-permute-start(bf16[320,128]{1,0:T(8,128)(2,1)S(1)} %add_convert_fusion.1.p0), channel_id=1, source_target_pairs={{0,192},{32,224},{64,0},{96,32},{128,64},{160,96},{192,128},{224,1... | collective-permute-start | bytes 245768 | tf_op jit(solution)/shard_map/ppermute | solution.py:400
  (17 other events, 68.6 us)

commit v4 on v3

--- a/solution.py
+++ b/solution.py
@@ -35,29 +35,27 @@
 
 
 def route_kernel(owner_ref, row_ref, req_ref, slot_ref):
+    blocks = TOK // 128
     upper = (iota((128, 128), 0) < iota((128, 128), 1)).astype(BF)
-    ones = jnp.ones((128, 128), BF)
-    scan = jnp.concatenate([upper, ones], axis=1)
+    scan = jnp.concatenate([upper, jnp.ones((128, 128), BF)], axis=1)
+    hots = [(iota((NOWN, 128), 0) == owner_ref[b : b + 1, :]).astype(F32) for b in range(blocks)]
+    sums = dot(jnp.concatenate(hots, axis=0).astype(BF), scan, 1, 0)
     carry = jnp.zeros((NOWN, 128), F32)
-    high = jnp.zeros((NOWN, 128), F32)
-    low = jnp.zeros((NOWN, 128), F32)
-    for b in range(TOK // 128):
-        own = owner_ref[b : b + 1, :]
+    highs, lows = [], []
+    for b in range(blocks):
+        part = sums[b * NOWN : (b + 1) * NOWN, :]
+        rank = jnp.sum(hots[b] * (part[:, :128] + carry), axis=0, keepdims=True).astype(I32)
+        carry = carry + part[:, 128:]
         row = row_ref[b : b + 1, :]
-        hot = iota((NOWN, 128), 0) == own
-        hot_f = hot.astype(F32)
-        hot_b = hot_f.astype(BF)
-        sums = dot(hot_b, scan, 1, 0)
-        rank = jnp.sum(hot_f * (sums[:, :128] + carry), axis=0, keepdims=True)
-        carry = carry + sums[:, 128:]
-        rank_i = rank.astype(I32)
-        slot_ref[b : b + 1, :] = own * CAP + rank_i
-        place = iota((128, 128), 0) == rank_i
-        row_hi = jnp.where(place, (row >> 6).astype(F32), 0.0).astype(BF)
-        row_lo = jnp.where(place, (row & 63).astype(F32), 0.0).astype(BF)
-        high = high + dot(hot_b, row_hi, 1, 1)
-        low = low + dot(hot_b, row_lo, 1, 1)
-    req_ref[...] = high.astype(I32) * 64 + low.astype(I32)
+        slot_ref[b : b + 1, :] = owner_ref[b : b + 1, :] * CAP + rank
+        here = iota((32, 128), 0) == rank
+        highs.append(jnp.where(here, (row >> 6).astype(F32), 0.0))
+        lows.append(jnp.where(here, (row & 63).astype(F32), 0.0))
+    hot = jnp.concatenate(hots, axis=1).astype(BF)
+    high = dot(hot, jnp.concatenate(highs, axis=1).astype(BF), 1, 1)
+    low = dot(hot, jnp.concatenate(lows, axis=1).astype(BF), 1, 1)
+    req_ref[...] = jnp.zeros((NOWN, 128), I32)
+    req_ref[:, 0:32] = (high * 64.0 + low).astype(I32)
 
 
 def route(owner, row):
@@ -143,12 +141,13 @@
 
 
 def layer_kernel(
-    pos_ref, seg_ref, x0, x1, x2, x3, g0, g1, g2, g3, win_ref, wout_ref,
-    dx0, dx1, dx2, dx3, u_ref, y_ref, dp_ref,
-    w, wo, pre, act, segc, aw, dsil, dout, dkv, du,
+    pos_ref, core_ref, seg_ref, x0, x1, x2, x3, g0, g1, g2, g3, win_ref, wout_ref,
+    mine_ref, other_ref, dx0, dx1, dx2, dx3, z0, z1, z2, z3,
+    w, wo, pre, act, segc, aw, dsil, dkv, du, u_ref, y_ref, dp_ref, dw_ref,
 ):
-    xs, gs, dxs = (x0, x1, x2, x3), (g0, g1, g2, g3), (dx0, dx1, dx2, dx3)
-    me = pos_ref[0]
+    xs, gs = (x0, x1, x2, x3), (g0, g1, g2, g3)
+    dxs, zs = (dx0, dx1, dx2, dx3), (z0, z1, z2, z3)
+    me, core = pos_ref[0], core_ref[0]
     for k in range(NT):
         at = pl.multiple_of(lax.rem(me + k, NT) * 128, 128)
         for c in range(4):
@@ -248,15 +247,25 @@
             for k in range(NT):
                 dxs[k][lo + r : lo + r + step, :] = ((d[k] - m1 - n[k] * m2) * scale).astype(BF)
 
-
-def layer(pos, seg, xs, gs, w_in, w_out):
+    for k in range(NT):
+        at = pl.multiple_of(lax.rem(me + k, NT) * 128, 128)
+        dw = dot(u_ref[:, k * 128 : (k + 1) * 128], dp_ref[...], 0, 0)
+        for c in range(4):
+            dw_ref[pl.ds(pl.multiple_of(c * 512 + at, 128), 128), :] = dw[:, c * 128 : (c + 1) * 128]
+        dw_ref[pl.ds(pl.multiple_of(2048 + at, 128), 128), :] = dot(y_ref[...], gs[k][...], 0, 0)
+        zs[k][...] = dot(y_ref[...], wo[:, k * 128 : (k + 1) * 128], 1, 0).astype(BF)
+    mine_ref[...] = dw_ref[pl.ds(pl.multiple_of(core * 1280, 1280), 1280), :]
+    other_ref[...] = dw_ref[pl.ds(pl.multiple_of(1280 - core * 1280, 1280), 1280), :].astype(BF)
+
+
+def layer(pos, core, seg, xs, gs, w_in, w_out):
     piece = jax.ShapeDtypeStruct((TOK, 128), BF)
-    wide = jax.ShapeDtypeStruct((TOK, D), BF)
     return pl.pallas_call(
         layer_kernel,
-        out_shape=(piece,) * 4 + (wide, piece, wide),
-        in_specs=[SM] + [VM] * 11,
-        out_specs=(VM,) * 7,
+        out_shape=(jax.ShapeDtypeStruct((1280, 128), F32), jax.ShapeDtypeStruct((1280, 128), BF))
+        + (piece,) * 8,
+        in_specs=[SM, SM] + [VM] * 11,
+        out_specs=(VM,) * 10,
         scratch_shapes=[
             pltpu.VMEM((D, 512), BF),
             pltpu.VMEM((HD, D), BF),
@@ -265,43 +274,16 @@
             pltpu.VMEM((TOK, 128), F32),
             pltpu.VMEM((QB, 768), BF),
             pltpu.VMEM((QB, 768), F32),
-            pltpu.VMEM((QB, 128), BF),
             pltpu.VMEM((TOK, 256), F32),
             pltpu.VMEM((QB, 512), F32),
+            pltpu.VMEM((TOK, D), BF),
+            pltpu.VMEM((TOK, HD), BF),
+            pltpu.VMEM((TOK, 512), BF),
+            pltpu.VMEM((2560, 128), F32),
         ],
         compiler_params=PARAMS,
         name="layer",
-    )(pos, seg, *xs, *gs, w_in, w_out)
-
-
-def proj_kernel(
-    pos_ref, y_ref, u_ref, dp_ref, g0, g1, g2, g3, wout_ref, mine_ref, other_ref, z0, z1, z2, z3, dw_ref
-):
-    me, core = pos_ref[0], pos_ref[1]
-    gs, zs = (g0, g1, g2, g3), (z0, z1, z2, z3)
-    for k in range(NT):
-        at = pl.multiple_of(lax.rem(me + k, NT) * 128, 128)
-        dw = dot(u_ref[:, k * 128 : (k + 1) * 128], dp_ref[...], 0, 0)
-        for c in range(4):
-            dw_ref[pl.ds(pl.multiple_of(c * 512 + at, 128), 128), :] = dw[:, c * 128 : (c + 1) * 128]
-        dw_ref[pl.ds(pl.multiple_of(2048 + at, 128), 128), :] = dot(y_ref[...], gs[k][...], 0, 0)
-        zs[k][...] = dot(y_ref[...], wout_ref[:, pl.ds(at, 128)], 1, 0).astype(BF)
-    mine_ref[...] = dw_ref[pl.ds(pl.multiple_of(core * 1280, 1280), 1280), :]
-    other_ref[...] = dw_ref[pl.ds(pl.multiple_of(1280 - core * 1280, 1280), 1280), :].astype(BF)
-
-
-def project(pos, y, u, dp, gs, w_out):
-    piece = jax.ShapeDtypeStruct((TOK, 128), BF)
-    return pl.pallas_call(
-        proj_kernel,
-        out_shape=(jax.ShapeDtypeStruct((1280, 128), F32), jax.ShapeDtypeStruct((1280, 128), BF))
-        + (piece,) * 4,
-        in_specs=[SM] + [VM] * 8,
-        out_specs=(VM,) * 6,
-        scratch_shapes=[pltpu.VMEM((2560, 128), F32)],
-        compiler_params=PARAMS,
-        name="project",
-    )(pos, y, u, dp, *gs, w_out)
+    )(pos, core, seg, *xs, *gs, w_in, w_out)
 
 
 def spread(at_ref, blocks, size, values):
@@ -361,39 +343,27 @@
     )(req, arrived)
 
 
-def join_kernel(y_ref, p0, p1, p2, p3, out_ref):
+def unpack_kernel(y_ref, p0, p1, p2, p3, in_ref, out_ref, whole):
     for k, p in enumerate((p0, p1, p2, p3)):
-        at = pl.multiple_of(lax.rem(y_ref[0] + k, 4) * 320, 320)
-        out_ref[pl.ds(at, 320), :] = p[...]
-
-
-def join(y, parts):
-    return pl.pallas_call(
-        join_kernel,
-        out_shape=jax.ShapeDtypeStruct((1280, 128), BF),
+        half, quarter = y_place(lax.rem(y_ref[0] + k, 4))
+        for core in range(2):
+            at = pl.multiple_of(half * 640 + quarter * 320 + core * 1280, 320)
+            whole[pl.ds(at, 320), :] = p[core * 320 : (core + 1) * 320, :].astype(F32)
+    in_ref[...] = whole[0:2048, :]
+    for k in range(NT):
+        out_ref[:, k * 128 : (k + 1) * 128] = whole[2048 + k * 128 : 2176 + k * 128, :]
+
+
+def unpack(y, parts):
+    return pl.pallas_call(
+        unpack_kernel,
+        out_shape=(jax.ShapeDtypeStruct((2048, 128), F32), jax.ShapeDtypeStruct((HD, D), F32)),
         in_specs=[SM] + [VM] * 4,
-        out_specs=VM,
-        compiler_params=PARAMS,
-        name="join",
+        out_specs=(VM, VM),
+        scratch_shapes=[pltpu.VMEM((2560, 128), F32)],
+        compiler_params=PARAMS,
+        name="unpack",
     )(y, *parts)
-
-
-def unpack_kernel(whole_ref, in_ref, out_ref):
-    for c in range(4):
-        in_ref[c, :, :] = whole_ref[c * 512 : (c + 1) * 512, :].astype(F32)
-    for k in range(NT):
-        out_ref[:, k * 128 : (k + 1) * 128] = whole_ref[2048 + k * 128 : 2176 + k * 128, :].astype(F32)
-
-
-def unpack(whole):
-    return pl.pallas_call(
-        unpack_kernel,
-        out_shape=(jax.ShapeDtypeStruct((4, D, 128), F32), jax.ShapeDtypeStruct((HD, D), F32)),
-        in_specs=[VM],
-        out_specs=(VM, VM),
-        compiler_params=PARAMS,
-        name="unpack",
-    )(whole)
 
 
 def shift(x, axis, fn, n):
@@ -417,66 +387,63 @@
     return lax.dynamic_index_in_dim(x, i, 0, keepdims=False)
 
 
-def reduce_weights(mine, other, grads):
-    at = lax.axis_index("table")
-    core, y = at % 2, at // 2
+def y_place(y):
+    return ((y == 1) | (y == 2)).astype(I32), (y >= 2).astype(I32)
+
+
+def reduce_over_chips(mine, other):
+    half, quarter = y_place(lax.axis_index("table") // 2)
     other = shift(other, "table", lambda i: i ^ 1, 8)
-    mine = (mine + other.astype(F32)).reshape(4, 320, 128)
-    total = pick(mine, y)
-    got = [
-        shift(pick(mine, (y + k) % 4).astype(BF), "table", lambda i, k=k: (i + 2 * k) % 8, 8)
-        for k in range(1, 4)
-    ]
-    for v in got:
-        total = total + v.astype(F32)
-    total, grads = lax.optimization_barrier((total.astype(BF), grads))
-    for bit in (1, 2, 4):
-        total = total.astype(F32) + shift(total, "seq", lambda i, b=bit: i ^ b, 8).astype(F32)
-        total = total.astype(BF)
-    return total, grads
+    mine = (mine + other.astype(F32)).reshape(2, 640, 128)
+    got = shift(pick(mine, 1 - half).astype(BF), "table", lambda i: i ^ 2, 8)
+    mine = (pick(mine, half) + got.astype(F32)).reshape(2, 320, 128)
+    got = shift(pick(mine, 1 - quarter).astype(BF), "table", lambda i: 6 - (i & 6) + (i & 1), 8)
+    return pick(mine, quarter), got
+
+
+def add_step(total, mask):
+    return (total.astype(F32) + shift(total, "seq", lambda i: i ^ mask, 8).astype(F32)).astype(BF)
 
 
 def gather_weights(total):
-    y = lax.axis_index("table") // 2
-    parts = [total] + [
-        shift(total, "table", lambda i, k=k: (i - 2 * k) % 8, 8) for k in range(1, 4)
-    ]
-    whole = lax.all_gather(
-        join(y.astype(I32).reshape(1), parts),
-        "table",
-        axis=0,
-        tiled=True,
-        axis_index_groups=[[2 * i, 2 * i + 1] for i in range(4)],
-    )
-    return unpack(whole)
+    y = (lax.axis_index("table") // 2).astype(I32).reshape(1)
+    pairs = [[2 * i, 2 * i + 1] for i in range(4)]
+    both = lax.all_gather(total, "table", axis=0, tiled=True, axis_index_groups=pairs)
+    parts = [both] + [shift(both, "table", lambda i, k=k: (i - 2 * k) % 8, 8) for k in range(1, 4)]
+    return unpack(y, parts)
 
 
 def body(table, owner, local_row, segment_ids, proj_in, proj_out, grad_out):
-    pos = jnp.stack([lax.axis_index("tensor"), lax.axis_index("table") % 2]).astype(I32)
+    pos = lax.axis_index("tensor").astype(I32).reshape(1)
+    core = (lax.axis_index("table") % 2).astype(I32).reshape(1)
     requests, slot = route(owner.reshape(8, 128), local_row.reshape(8, 128))
-    requests, pos = lax.optimization_barrier((requests, pos))
     gs = order(gather_pieces(grad_out))
     received = lax.all_to_all(requests, BOTH, split_axis=0, concat_axis=0, tiled=True)
     rows = fetch(received, table)
     back = lax.all_to_all(rows.reshape(NOWN, CAP, 128), BOTH, split_axis=0, concat_axis=0, tiled=True)
     x = place(slot, back.reshape(SLOTS, 128))
     xs = order(gather_pieces(x))
-    d0, d1, d2, d3, u, y, dp = layer(pos, segment_ids, xs, gs, proj_in, proj_out)
+    mine, other, d0, d1, d2, d3, z0, z1, z2, z3 = layer(
+        pos, core, segment_ids, xs, gs, proj_in, proj_out
+    )
     dparts = scatter_pieces([d0, d1, d2, d3])
-    mine, other, z0, z1, z2, z3 = project(pos, y, u, dp, gs, proj_out)
+    own, got = reduce_over_chips(mine, other)
+    dparts, got = lax.optimization_barrier((dparts, got))
     grads = to_slots(slot, grad_out, dparts)
-    total, grads = reduce_weights(mine, other, grads)
+    total = add_step(add_step((own + got.astype(F32)).astype(BF), 1), 2)
     arrived = lax.all_to_all(grads.reshape(NOWN, CAP, 128), BOTH, split_axis=0, concat_axis=0, tiled=True)
-    zparts = scatter_pieces([z0, z1, z2, z3])
+    total, zs = lax.optimization_barrier((total, [z0, z1, z2, z3]))
+    total = add_step(total, 7)
+    zparts = scatter_pieces(zs)
+    flat = received[:, :CAP].reshape(SLOTS // 128, 128)
+    total, arrived, zparts, flat = lax.optimization_barrier((total, arrived, zparts, flat))
+    table_grad = add_rows(flat, arrived.reshape(SLOTS, 128))
+    grad_in, grad_outw = gather_weights(total)
     layer_out = (
         x.astype(F32)
         + (zparts[0].astype(F32) + zparts[1].astype(F32) + zparts[2].astype(F32) + zparts[3].astype(F32))
     ).astype(BF)
-    flat = received[:, :CAP].reshape(SLOTS // 128, 128)
-    total, arrived, layer_out = lax.optimization_barrier((total, arrived, layer_out))
-    table_grad = add_rows(flat, arrived.reshape(SLOTS, 128))
-    grad_in, grad_outw = gather_weights(total)
-    return layer_out, table_grad, grad_in, grad_outw
+    return layer_out, table_grad, grad_in.reshape(4, D, 128), grad_outw
 
 
 def solution(mesh):

time: 159 us -> 160 us (level)
  waiting for transfers between devices: 35.2 us -> 55.3 us
  starting transfers between devices: 52.3 us -> 45.3 us
  Pallas kernels: 33.8 us -> 27.1 us
  blocking collectives: 28.8 us -> 25.9 us
    ppermute x22 -> x21, waiting for transfers between devices: 25.2 us -> 45.4 us  [shift(): return lax.ppermute(x, axis, [(i, fn(i)) for i in range(n)])]
    pallas_call x4 -> x2, Pallas kernels: 19.8 us -> 14.1 us  [the longest x1 11.7 us: layer(): pl.pallas_call(layer_kernel, out_shape=(jax.ShapeDtypeStruct((1280, 128),...]
    all_to_all x1, starting transfers between devices: 12.4 us -> 7.37 us  [body(): lax.all_to_all(grads.reshape(NOWN, CAP, 128), BOTH, split_axis=0, concat_...]
    all_gather x1, blocking collectives: 6.41 us -> 3.63 us  [gather_weights(): lax.all_gather(total, 'table', axis=0, tiled=True, axis_index_groups=pairs)]
    ppermute x22 -> x21, starting transfers between devices: 34.9 us -> 32.6 us  [shift(): return lax.ppermute(x, axis, [(i, fn(i)) for i in range(n)])]
  transfers between devices with their start and end apart: 24 -> 23, of which waited for: 9 -> 12; matrix products, arithmetic and copies ran while one was open for 2% -> 1% of each run, Pallas kernels for 5% -> 5%
where the time goes in v4:
time: 160 us
  waiting for transfers between devices  55.3 us (35%)
  starting transfers between devices  45.3 us (28%)
  Pallas kernels  27.1 us (17%)
  blocking collectives  25.9 us (16%)
  local copies, waits for them, and re-layouts  2.96 us (2%)
  other arithmetic  2.21 us (1%)
    ppermute x21, waiting for transfers between devices, shift(): return lax.ppermute(x, axis, [(i, fn(i)) for i in range(n)])  45.4 us
    ppermute x21, starting transfers between devices, shift(): return lax.ppermute(x, axis, [(i, fn(i)) for i in range(n)])  32.6 us
    all_to_all x1, blocking collectives, body(): lax.all_to_all(requests, BOTH, split_axis=0, concat_axis=0, tiled=True)  22.3 us
    pallas_call x1, Pallas kernels, layer(): pl.pallas_call(layer_kernel, out_shape=(jax.ShapeDtypeStruct((1280, 128),...  11.7 us
    all_to_all x1, waiting for transfers between devices, body(): lax.all_to_all(rows.reshape(NOWN, CAP, 128), BOTH, split_axis=0, concat_a...  9.98 us
    all_to_all x1, starting transfers between devices, body(): lax.all_to_all(grads.reshape(NOWN, CAP, 128), BOTH, split_axis=0, concat_...  7.37 us
    all_to_all x1, starting transfers between devices, body(): lax.all_to_all(rows.reshape(NOWN, CAP, 128), BOTH, split_axis=0, concat_a...  5.29 us
    all_gather x1, blocking collectives, gather_weights(): lax.all_gather(total, 'table', axis=0, tiled=True, axis_index_groups=pairs)  3.63 us
  transfers between devices with their start and end apart: 23, of which 12 were waited for; matrix products, arithmetic and copies ran while one was open for 1% of the time, Pallas kernels for 5%

profile of v4, /device:TPU:1, one launch (start us, length us, event | category | flops | bytes accessed | tf_op | source)
XLA Modules:
  0.0 159.5 jit_solution(10754680434623735106)
XLA Ops:
  0.6 1.8 %route.1 = (s32[64,128]{1,0:T(8,128)}, s32[8,128]{1,0:T(8,128)}) custom-call(s32[8,128]{1,0:T(8,128)} %bitcast.38, s32[8,128]{1,0:T(8,128)} %bitcast.39), custom_call_target="tpu_custom_call" | custom-call | tf_op jit(solution)/shard_map/route/pallas_call | solution.py:62
  2.5 22.3 %all_to_all.21 = s32[64,1,128]{2,1,0:T(1,128)} all-to-all(s32[64,1,128]{2,1,0:T(1,128)} %bitcast.37), channel_id=1, replica_groups=mesh['table'=8,'seq'=8,'tensor'=4] {'table','seq'}, dimensions={0} | all-to-all | bytes 65536 | tf_op jit(solution)/shard_map/all_to_all | solution.py:421
  24.7 2.9 %fetch.1 = bf16[1536,128]{1,0:T(8,128)(2,1)} custom-call(s32[64,128]{1,0:T(8,128)} %bitcast.35, bf16[2048,128]{1,0:T(8,128)(2,1)} %table_ref.1), custom_call_target="tpu_custom_call" | custom-call | tf_op jit(solution)/shard_map/fetch/pallas_call | solution.py:98
  27.6 5.3 %all-to-all-start.1 = ((bf16[64,24,128]{2,1,0:T(8,128)(2,1)}), bf16[64,24,128]{2,1,0:T(8,128)(2,1)S(1)}, u32[]{:S(2)}, u32[]{:S(2)}) async-start(bf16[64,24,128]{2,1,0:T(8,128)(2,1)} %bitcast.31), calls=%async_computation.1 | async-start | bytes 786432 | tf_op jit(solution)/shard_map/all_to_all | solution.py:423
  32.9 1.3 collective-permute-start.5
  34.2 2.5 %collective-permute-start.4 = (bf16[1024,128]{1,0:T(8,128)(2,1)S(1)}, bf16[1024,128]{1,0:T(8,128)(2,1)S(1)}, u32[]{:S(2)}, u32[]{:S(2)}) collective-permute-start(bf16[1024,128]{1,0:T(8,128)(2,1)S(1)} %copy-done.3), channel_id=1, source_target_pairs={{0,2},{1,3},{2,0},{3,1},{4,6},{5,7},{6,4},{7,5},{8,10},{9,11},{10,... | collective-permute-start | bytes 786440 | tf_op jit(solution)/shard_map/ppermute | solution.py:370
  37.8 10.0 %all-to-all-done.1 = bf16[64,24,128]{2,1,0:T(8,128)(2,1)S(1)} async-done(((bf16[64,24,128]{2,1,0:T(8,128)(2,1)}), bf16[64,24,128]{2,1,0:T(8,128)(2,1)S(1)}, u32[]{:S(2)}, u32[]{:S(2)}) %all-to-all-start.1) | async-done | bytes 393248 | tf_op jit(solution)/shard_map/all_to_all | solution.py:423
  48.5 2.4 %place.1.x0 = bf16[1024,128]{1,0:T(8,128)(2,1)} custom-call(s32[8,128]{1,0:T(8,128)} %get-tuple-element.35.slot_ref, bf16[1536,128]{1,0:T(8,128)(2,1)} %bitcast.29), custom_call_target="tpu_custom_call" | custom-call | tf_op jit(solution)/shard_map/place/pallas_call | solution.py:133
  52.1 2.5 %collective-permute-start.1 = (bf16[1024,128]{1,0:T(8,128)(2,1)}, bf16[1024,128]{1,0:T(8,128)(2,1)S(1)}, u32[]{:S(2)}, u32[]{:S(2)}) collective-permute-start(bf16[1024,128]{1,0:T(8,128)(2,1)} %place.1.x0), channel_id=1, source_target_pairs={{0,2},{1,3},{2,0},{3,1},{4,6},{5,7},{6,4},{7,5},{8,10},{9,11},{10,... | collective-permute-start | bytes 786440 | tf_op jit(solution)/shard_map/ppermute | solution.py:370
  55.7 3.4 %collective-permute-done.2.x3 = bf16[1024,128]{1,0:T(8,128)(2,1)S(1)} collective-permute-done((bf16[1024,128]{1,0:T(8,128)(2,1)}, bf16[1024,128]{1,0:T(8,128)(2,1)S(1)}, u32[]{:S(2)}, u32[]{:S(2)}) %collective-permute-start.2) | collective-permute-done | bytes 262176 | tf_op jit(solution)/shard_map/ppermute | solution.py:370
  59.1 6.6 %collective-permute-done.1.x2 = bf16[1024,128]{1,0:T(8,128)(2,1)S(1)} collective-permute-done((bf16[1024,128]{1,0:T(8,128)(2,1)}, bf16[1024,128]{1,0:T(8,128)(2,1)S(1)}, u32[]{:S(2)}, u32[]{:S(2)}) %collective-permute-start.1) | collective-permute-done | bytes 262176 | tf_op jit(solution)/shard_map/ppermute | solution.py:370
  66.5 11.7 %layer.1 = (f32[1280,128]{1,0:T(8,128)}, bf16[1280,128]{1,0:T(8,128)(2,1)}, bf16[1024,128]{1,0:T(8,128)(2,1)}, bf16[1024,128]{1,0:T(8,128)(2,1)}, bf16[1024,128]...) custom-call(s32[1]{0:T(128)} %bitcast.7.pos_ref, ...), custom_call_target="tpu_custom_call" | custom-call | tf_op jit(solution)/shard_map/layer/pallas_call | solution.py:263
  78.2 2.0 %collective-permute-start.6 = (bf16[1280,128]{1,0:T(8,128)(2,1)}, bf16[1280,128]{1,0:T(8,128)(2,1)S(1)}, u32[]{:S(2)}, u32[]{:S(2)}) collective-permute-start(bf16[1280,128]{1,0:T(8,128)(2,1)} %get-tuple-element.38), channel_id=1, source_target_pairs={{0,32},{32,0},{64,96},{96,64},{128,160},{160,128},{192,224},{224,1... | collective-permute-start | bytes 983048 | tf_op jit(solution)/shard_map/ppermute | solution.py:370
  80.2 1.5 collective-permute-done.6
  84.7 1.7 %collective-permute-start.9 = (bf16[1024,128]{1,0:T(8,128)(2,1)S(1)}, bf16[1024,128]{1,0:T(8,128)(2,1)S(1)}, u32[]{:S(2)}, u32[]{:S(2)}) collective-permute-start(bf16[1024,128]{1,0:T(8,128)(2,1)S(1)} %copy-done.23), channel_id=1, source_target_pairs={{0,3},{1,0},{2,1},{3,2},{4,7},{5,4},{6,5},{7,6},{8,11},{9,8},{10,9... | collective-permute-start | bytes 786440 | tf_op jit(solution)/shard_map/ppermute | solution.py:370
  88.5 1.5 collective-permute-start.11
  90.0 2.2 %collective-permute-done.8.d1 = bf16[1024,128]{1,0:T(8,128)(2,1)S(1)} collective-permute-done((bf16[1024,128]{1,0:T(8,128)(2,1)S(1)}, bf16[1024,128]{1,0:T(8,128)(2,1)S(1)}, u32[]{:S(2)}, u32[]{:S(2)}) %collective-permute-start.8) | collective-permute-done | bytes 262176 | tf_op jit(solution)/shard_map/ppermute | solution.py:370
  92.2 6.0 %collective-permute-done.10.d3 = bf16[1024,128]{1,0:T(8,128)(2,1)S(1)} collective-permute-done((bf16[1024,128]{1,0:T(8,128)(2,1)S(1)}, bf16[1024,128]{1,0:T(8,128)(2,1)S(1)}, u32[]{:S(2)}, u32[]{:S(2)}) %collective-permute-start.10) | collective-permute-done | bytes 262176 | tf_op jit(solution)/shard_map/ppermute | solution.py:370
  98.2 1.5 collective-permute-start.12
  99.7 2.8 %to_slots.1 = bf16[1536,128]{1,0:T(8,128)(2,1)} custom-call(s32[8,128]{1,0:T(8,128)} %get-tuple-element.35.slot_ref, bf16[1024,128]{1,0:T(8,128)(2,1)} %grad_ref.1, bf16[1024,128]{1,0:T(8,128)(2,1)} %get-tuple-element.49.d0, bf16[1024,128]{1,0:T(8,128)(2,1)} %copy-done.13, bf16[1024,128]{1,0:T(8,128)(2,1)} %copy-done.14, bf16[1024,128]{1,0:T(8,128)(2,1)} %copy-done.15), custom_call_target="tpu_custom_call" | custom-call | tf_op jit(solution)/shard_map/to_slots/pallas_call | solution.py:318
  102.5 7.4 %all-to-all-start.2 = ((bf16[64,24,128]{2,1,0:T(8,128)(2,1)}), bf16[64,24,128]{2,1,0:T(8,128)(2,1)S(1)}, u32[]{:S(2)}, u32[]{:S(2)}) async-start(bf16[64,24,128]{2,1,0:T(8,128)(2,1)} %bitcast.32), calls=%async_computation.2 | async-start | bytes 786432 | tf_op jit(solution)/shard_map/all_to_all | solution.py:434
  109.9 2.4 %collective-permute-start.13 = (bf16[320,128]{1,0:T(8,128)(2,1)S(1)}, bf16[320,128]{1,0:T(8,128)(2,1)S(1)}, u32[]{:S(2)}, u32[]{:S(2)}) collective-permute-start(bf16[320,128]{1,0:T(8,128)(2,1)S(1)} %add_convert_fusion.3), channel_id=1, source_target_pairs={{0,8},{4,12},{8,0},{12,4},{16,24},{20,28},{24,16},{28,20},{1,9},{5... | collective-permute-start | bytes 245768 | tf_op jit(solution)/shard_map/ppermute | solution.py:370
  112.3 12.4 %collective-permute-done.13 = bf16[320,128]{1,0:T(8,128)(2,1)S(1)} collective-permute-done((bf16[320,128]{1,0:T(8,128)(2,1)S(1)}, bf16[320,128]{1,0:T(8,128)(2,1)S(1)}, u32[]{:S(2)}, u32[]{:S(2)}) %collective-permute-start.13) | collective-permute-done | bytes 81952 | tf_op jit(solution)/shard_map/ppermute | solution.py:370
  124.7 2.5 %collective-permute-start.14 = (bf16[320,128]{1,0:T(8,128)(2,1)S(1)}, bf16[320,128]{1,0:T(8,128)(2,1)S(1)}, u32[]{:S(2)}, u32[]{:S(2)}) collective-permute-start(bf16[320,128]{1,0:T(8,128)(2,1)S(1)} %add_convert_fusion.2), channel_id=1, source_target_pairs={{0,28},{4,24},{8,20},{12,16},{16,12},{20,8},{24,4},{28,0},{1,29},{... | collective-permute-start | bytes 245768 | tf_op jit(solution)/shard_map/ppermute | solution.py:370
  128.1 1.8 %collective-permute-start.16 = (bf16[1024,128]{1,0:T(8,128)(2,1)S(1)}, bf16[1024,128]{1,0:T(8,128)(2,1)S(1)}, u32[]{:S(2)}, u32[]{:S(2)}) collective-permute-start(bf16[1024,128]{1,0:T(8,128)(2,1)S(1)} %copy-done.20), channel_id=1, source_target_pairs={{0,3},{1,0},{2,1},{3,2},{4,7},{5,4},{6,5},{7,6},{8,11},{9,8},{10,9... | collective-permute-start | bytes 786440 | tf_op jit(solution)/shard_map/ppermute | solution.py:370
  131.5 3.6 %collective-permute-done.15 = bf16[1024,128]{1,0:T(8,128)(2,1)S(1)} collective-permute-done((bf16[1024,128]{1,0:T(8,128)(2,1)S(1)}, bf16[1024,128]{1,0:T(8,128)(2,1)S(1)}, u32[]{:S(2)}, u32[]{:S(2)}) %collective-permute-start.15) | collective-permute-done | bytes 262176 | tf_op jit(solution)/shard_map/ppermute | solution.py:370
  135.1 6.4 %collective-permute-done.17 = bf16[1024,128]{1,0:T(8,128)(2,1)S(1)} collective-permute-done((bf16[1024,128]{1,0:T(8,128)(2,1)S(1)}, bf16[1024,128]{1,0:T(8,128)(2,1)S(1)}, u32[]{:S(2)}, u32[]{:S(2)}) %collective-permute-start.17) | collective-permute-done | bytes 262176 | tf_op jit(solution)/shard_map/ppermute | solution.py:370
  141.5 3.6 %all_gather.3.p0 = bf16[640,128]{1,0:T(8,128)(2,1)S(1)} all-gather(bf16[320,128]{1,0:T(8,128)(2,1)S(1)} %add_convert_fusion.1), channel_id=1, replica_groups={{0,32},{64,96},{128,160},{192,224},{1,33},{65,97},{129,161},{193,225},{..., dimensions={0}, use_global_device_ids=true | all-gather | bytes 245760 | tf_op jit(solution)/shard_map/all_gather | solution.py:411
  146.4 2.6 %collective-permute-start.19 = (bf16[640,128]{1,0:T(8,128)(2,1)S(1)}, bf16[640,128]{1,0:T(8,128)(2,1)S(1)}, u32[]{:S(2)}, u32[]{:S(2)}) collective-permute-start(bf16[640,128]{1,0:T(8,128)(2,1)S(1)} %all_gather.3.p0), channel_id=1, source_target_pairs={{0,128},{32,160},{64,192},{96,224},{128,0},{160,32},{192,64},{224,... | collective-permute-start | bytes 491528 | tf_op jit(solution)/shard_map/ppermute | solution.py:370
  150.1 3.2 %add_rows.1 = f32[2048,128]{1,0:T(8,128)} custom-call(s32[12,128]{1,0:T(8,128)} %reshape.60.req_ref, bf16[1536,128]{1,0:T(8,128)(2,1)} %bitcast.30), custom_call_target="tpu_custom_call" | custom-call | tf_op jit(solution)/shard_map/add_rows/pallas_call | solution.py:336
  154.1 2.3 %collective-permute-done.19.p2 = bf16[640,128]{1,0:T(8,128)(2,1)S(1)} collective-permute-done((bf16[640,128]{1,0:T(8,128)(2,1)S(1)}, bf16[640,128]{1,0:T(8,128)(2,1)S(1)}, u32[]{:S(2)}, u32[]{:S(2)}) %collective-permute-start.19) | collective-permute-done | bytes 163872 | tf_op jit(solution)/shard_map/ppermute | solution.py:370
  157.2 2.4 %unpack.1 = (f32[2048,128]{1,0:T(8,128)}, f32[128,512]{1,0:T(8,128)}) custom-call(s32[1]{0:T(128)} %bitcast.17.y_ref, bf16[640,128]{1,0:T(8,128)(2,1)} %copy-done.4, bf16[640,128]{1,0:T(8,128)(2,1)} %copy-done.18, bf16[640,128]{1,0:T(8,128)(2,1)} %copy-done.17, bf16[640,128]{1,0:T(8,128)(2,1)} %copy-done.16), custom_call_target="tpu_custom_call" | custom-call | tf_op jit(solution)/shard_map/unpack/pallas_call | solution.py:358
  (83 shorter events, 16.7 us)
Async XLA Ops:
  27.6 20.2 %all-to-all-start.1 = ((bf16[64,24,128]{2,1,0:T(8,128)(2,1)}), bf16[64,24,128]{2,1,0:T(8,128)(2,1)S(1)}, u32[]{:S(2)}, u32[]{:S(2)}) async-start(bf16[64,24,128]{2,1,0:T(8,128)(2,1)} %bitcast.31), calls=%async_computation.1 | async-start | bytes 786432 | tf_op jit(solution)/shard_map/all_to_all | solution.py:423
  32.9 21.6 %collective-permute-start.5 = (bf16[1024,128]{1,0:T(8,128)(2,1)S(1)}, bf16[1024,128]{1,0:T(8,128)(2,1)S(1)}, u32[]{:S(2)}, u32[]{:S(2)}) collective-permute-start(bf16[1024,128]{1,0:T(8,128)(2,1)S(1)} %copy-done.3), channel_id=1, source_target_pairs={{0,1},{1,2},{2,3},{3,0},{4,5},{5,6},{6,7},{7,4},{8,9},{9,10},{10,1... | collective-permute-start | bytes 786440 | tf_op jit(solution)/shard_map/ppermute | solution.py:370
  34.2 21.5 %collective-permute-start.4 = (bf16[1024,128]{1,0:T(8,128)(2,1)S(1)}, bf16[1024,128]{1,0:T(8,128)(2,1)S(1)}, u32[]{:S(2)}, u32[]{:S(2)}) collective-permute-start(bf16[1024,128]{1,0:T(8,128)(2,1)S(1)} %copy-done.3), channel_id=1, source_target_pairs={{0,2},{1,3},{2,0},{3,1},{4,6},{5,7},{6,4},{7,5},{8,10},{9,11},{10,... | collective-permute-start | bytes 786440 | tf_op jit(solution)/shard_map/ppermute | solution.py:370
  36.6 19.1 %collective-permute-start.3 = (bf16[1024,128]{1,0:T(8,128)(2,1)S(1)}, bf16[1024,128]{1,0:T(8,128)(2,1)S(1)}, u32[]{:S(2)}, u32[]{:S(2)}) collective-permute-start(bf16[1024,128]{1,0:T(8,128)(2,1)S(1)} %copy-done.3), channel_id=1, source_target_pairs={{0,3},{1,0},{2,1},{3,2},{4,7},{5,4},{6,5},{7,6},{8,11},{9,8},{10,9... | collective-permute-start | bytes 786440 | tf_op jit(solution)/shard_map/ppermute | solution.py:370
  50.9 8.2 %collective-permute-start.2 = (bf16[1024,128]{1,0:T(8,128)(2,1)}, bf16[1024,128]{1,0:T(8,128)(2,1)S(1)}, u32[]{:S(2)}, u32[]{:S(2)}) collective-permute-start(bf16[1024,128]{1,0:T(8,128)(2,1)} %place.1.x0), channel_id=1, source_target_pairs={{0,1},{1,2},{2,3},{3,0},{4,5},{5,6},{6,7},{7,4},{8,9},{9,10},{10,1... | collective-permute-start | bytes 786440 | tf_op jit(solution)/shard_map/ppermute | solution.py:370
  52.1 13.6 %collective-permute-start.1 = (bf16[1024,128]{1,0:T(8,128)(2,1)}, bf16[1024,128]{1,0:T(8,128)(2,1)S(1)}, u32[]{:S(2)}, u32[]{:S(2)}) collective-permute-start(bf16[1024,128]{1,0:T(8,128)(2,1)} %place.1.x0), channel_id=1, source_target_pairs={{0,2},{1,3},{2,0},{3,1},{4,6},{5,7},{6,4},{7,5},{8,10},{9,11},{10,... | collective-permute-start | bytes 786440 | tf_op jit(solution)/shard_map/ppermute | solution.py:370
  54.6 11.3 %copy-start.6 = (bf16[1024,128]{1,0:T(8,128)(2,1)}, bf16[1024,128]{1,0:T(8,128)(2,1)S(1)}, u32[]{:S(2)}) copy-start(bf16[1024,128]{1,0:T(8,128)(2,1)S(1)} %collective-permute-done.5.g3) | copy-start | bytes 786436
  54.6 11.3 %collective-permute-start = (bf16[1024,128]{1,0:T(8,128)(2,1)}, bf16[1024,128]{1,0:T(8,128)(2,1)S(1)}, u32[]{:S(2)}, u32[]{:S(2)}) collective-permute-start(bf16[1024,128]{1,0:T(8,128)(2,1)} %place.1.x0), channel_id=1, source_target_pairs={{0,3},{1,0},{2,1},{3,2},{4,7},{5,4},{6,5},{7,6},{8,11},{9,8},{10,9... | collective-permute-start | bytes 786440 | tf_op jit(solution)/shard_map/ppermute | solution.py:370
  55.7 10.1 %copy-start.7 = (bf16[1024,128]{1,0:T(8,128)(2,1)}, bf16[1024,128]{1,0:T(8,128)(2,1)S(1)}, u32[]{:S(2)}) copy-start(bf16[1024,128]{1,0:T(8,128)(2,1)S(1)} %collective-permute-done.4.g2) | copy-start | bytes 786436
  55.7 10.1 %copy-start.8 = (bf16[1024,128]{1,0:T(8,128)(2,1)}, bf16[1024,128]{1,0:T(8,128)(2,1)S(1)}, u32[]{:S(2)}) copy-start(bf16[1024,128]{1,0:T(8,128)(2,1)S(1)} %collective-permute-done.3.g1) | copy-start | bytes 786436
  78.2 3.5 %collective-permute-start.6 = (bf16[1280,128]{1,0:T(8,128)(2,1)}, bf16[1280,128]{1,0:T(8,128)(2,1)S(1)}, u32[]{:S(2)}, u32[]{:S(2)}) collective-permute-start(bf16[1280,128]{1,0:T(8,128)(2,1)} %get-tuple-element.38), channel_id=1, source_target_pairs={{0,32},{32,0},{64,96},{96,64},{128,160},{160,128},{192,224},{224,1... | collective-permute-start | bytes 983048 | tf_op jit(solution)/shard_map/ppermute | solution.py:370
  82.9 5.5 %collective-permute-start.7 = (bf16[640,128]{1,0:T(8,128)(2,1)S(1)}, bf16[640,128]{1,0:T(8,128)(2,1)S(1)}, u32[]{:S(2)}, u32[]{:S(2)}) collective-permute-start(bf16[640,128]{1,0:T(8,128)(2,1)S(1)} %fusion), channel_id=1, source_target_pairs={{0,64},{32,96},{64,0},{96,32},{128,192},{160,224},{192,128},{224,1... | collective-permute-start | bytes 491528 | tf_op jit(solution)/shard_map/ppermute | solution.py:370
  83.8 8.4 %collective-permute-start.8 = (bf16[1024,128]{1,0:T(8,128)(2,1)S(1)}, bf16[1024,128]{1,0:T(8,128)(2,1)S(1)}, u32[]{:S(2)}, u32[]{:S(2)}) collective-permute-start(bf16[1024,128]{1,0:T(8,128)(2,1)S(1)} %copy-done.24), channel_id=1, source_target_pairs={{0,1},{1,2},{2,3},{3,0},{4,5},{5,6},{6,7},{7,4},{8,9},{9,10},{10,1... | collective-permute-start | bytes 786440 | tf_op jit(solution)/shard_map/ppermute | solution.py:370
  84.7 7.4 %collective-permute-start.9 = (bf16[1024,128]{1,0:T(8,128)(2,1)S(1)}, bf16[1024,128]{1,0:T(8,128)(2,1)S(1)}, u32[]{:S(2)}, u32[]{:S(2)}) collective-permute-start(bf16[1024,128]{1,0:T(8,128)(2,1)S(1)} %copy-done.23), channel_id=1, source_target_pairs={{0,3},{1,0},{2,1},{3,2},{4,7},{5,4},{6,5},{7,6},{8,11},{9,8},{10,9... | collective-permute-start | bytes 786440 | tf_op jit(solution)/shard_map/ppermute | solution.py:370
  86.4 11.7 %collective-permute-start.10 = (bf16[1024,128]{1,0:T(8,128)(2,1)S(1)}, bf16[1024,128]{1,0:T(8,128)(2,1)S(1)}, u32[]{:S(2)}, u32[]{:S(2)}) collective-permute-start(bf16[1024,128]{1,0:T(8,128)(2,1)S(1)} %copy-done.22), channel_id=1, source_target_pairs={{0,2},{1,3},{2,0},{3,1},{4,6},{5,7},{6,4},{7,5},{8,10},{9,11},{10,... | collective-permute-start | bytes 786440 | tf_op jit(solution)/shard_map/ppermute | solution.py:370
  88.5 9.7 %collective-permute-start.11 = (bf16[320,128]{1,0:T(8,128)(2,1)S(1)}, bf16[320,128]{1,0:T(8,128)(2,1)S(1)}, u32[]{:S(2)}, u32[]{:S(2)}) collective-permute-start(bf16[320,128]{1,0:T(8,128)(2,1)S(1)} %fusion.2), channel_id=1, source_target_pairs={{0,192},{32,224},{64,128},{96,160},{128,64},{160,96},{192,0},{224,... | collective-permute-start | bytes 245768 | tf_op jit(solution)/shard_map/ppermute | solution.py:370
  98.2 11.6 %collective-permute-start.12 = (bf16[320,128]{1,0:T(8,128)(2,1)S(1)}, bf16[320,128]{1,0:T(8,128)(2,1)S(1)}, u32[]{:S(2)}, u32[]{:S(2)}) collective-permute-start(bf16[320,128]{1,0:T(8,128)(2,1)S(1)} %fusion.1), channel_id=1, source_target_pairs={{0,4},{4,0},{8,12},{12,8},{16,20},{20,16},{24,28},{28,24},{1,5},{5... | collective-permute-start | bytes 245768 | tf_op jit(solution)/shard_map/ppermute | solution.py:370
  102.5 24.7 %copy-start.21 = (bf16[1024,128]{1,0:T(8,128)(2,1)S(1)}, bf16[1024,128]{1,0:T(8,128)(2,1)}, u32[]{:S(2)}) copy-start(bf16[1024,128]{1,0:T(8,128)(2,1)} %get-tuple-element.54) | copy-start | bytes 786436
  102.5 25.6 %copy-start.20 = (bf16[1024,128]{1,0:T(8,128)(2,1)S(1)}, bf16[1024,128]{1,0:T(8,128)(2,1)}, u32[]{:S(2)}) copy-start(bf16[1024,128]{1,0:T(8,128)(2,1)} %get-tuple-element.55) | copy-start | bytes 786436
  102.5 39.0 %all-to-all-start.2 = ((bf16[64,24,128]{2,1,0:T(8,128)(2,1)}), bf16[64,24,128]{2,1,0:T(8,128)(2,1)S(1)}, u32[]{:S(2)}, u32[]{:S(2)}) async-start(bf16[64,24,128]{2,1,0:T(8,128)(2,1)} %bitcast.32), calls=%async_computation.2 | async-start | bytes 786432 | tf_op jit(solution)/shard_map/all_to_all | solution.py:434
  109.9 20.0 %copy-start.19 = (bf16[1024,128]{1,0:T(8,128)(2,1)S(1)}, bf16[1024,128]{1,0:T(8,128)(2,1)}, u32[]{:S(2)}) copy-start(bf16[1024,128]{1,0:T(8,128)(2,1)} %get-tuple-element.56) | copy-start | bytes 786436
  109.9 20.9 %copy-start.5 = (s32[64,1,128]{2,1,0:T(1,128)S(1)}, s32[64,1,128]{2,1,0:T(1,128)}, u32[]{:S(2)}) copy-start(s32[64,1,128]{2,1,0:T(1,128)} %all_to_all.21) | copy-start | bytes 98308
  109.9 14.8 %collective-permute-start.13 = (bf16[320,128]{1,0:T(8,128)(2,1)S(1)}, bf16[320,128]{1,0:T(8,128)(2,1)S(1)}, u32[]{:S(2)}, u32[]{:S(2)}) collective-permute-start(bf16[320,128]{1,0:T(8,128)(2,1)S(1)} %add_convert_fusion.3), channel_id=1, source_target_pairs={{0,8},{4,12},{8,0},{12,4},{16,24},{20,28},{24,16},{28,20},{1,9},{5... | collective-permute-start | bytes 245768 | tf_op jit(solution)/shard_map/ppermute | solution.py:370
  124.7 6.7 %collective-permute-start.14 = (bf16[320,128]{1,0:T(8,128)(2,1)S(1)}, bf16[320,128]{1,0:T(8,128)(2,1)S(1)}, u32[]{:S(2)}, u32[]{:S(2)}) collective-permute-start(bf16[320,128]{1,0:T(8,128)(2,1)S(1)} %add_convert_fusion.2), channel_id=1, source_target_pairs={{0,28},{4,24},{8,20},{12,16},{16,12},{20,8},{24,4},{28,0},{1,29},{... | collective-permute-start | bytes 245768 | tf_op jit(solution)/shard_map/ppermute | solution.py:370
  127.2 7.9 %collective-permute-start.15 = (bf16[1024,128]{1,0:T(8,128)(2,1)S(1)}, bf16[1024,128]{1,0:T(8,128)(2,1)S(1)}, u32[]{:S(2)}, u32[]{:S(2)}) collective-permute-start(bf16[1024,128]{1,0:T(8,128)(2,1)S(1)} %copy-done.21), channel_id=1, source_target_pairs={{0,1},{1,2},{2,3},{3,0},{4,5},{5,6},{6,7},{7,4},{8,9},{9,10},{10,1... | collective-permute-start | bytes 786440 | tf_op jit(solution)/shard_map/ppermute | solution.py:370
  128.1 7.0 %collective-permute-start.16 = (bf16[1024,128]{1,0:T(8,128)(2,1)S(1)}, bf16[1024,128]{1,0:T(8,128)(2,1)S(1)}, u32[]{:S(2)}, u32[]{:S(2)}) collective-permute-start(bf16[1024,128]{1,0:T(8,128)(2,1)S(1)} %copy-done.20), channel_id=1, source_target_pairs={{0,3},{1,0},{2,1},{3,2},{4,7},{5,4},{6,5},{7,6},{8,11},{9,8},{10,9... | collective-permute-start | bytes 786440 | tf_op jit(solution)/shard_map/ppermute | solution.py:370
  129.9 11.6 %collective-permute-start.17 = (bf16[1024,128]{1,0:T(8,128)(2,1)S(1)}, bf16[1024,128]{1,0:T(8,128)(2,1)S(1)}, u32[]{:S(2)}, u32[]{:S(2)}) collective-permute-start(bf16[1024,128]{1,0:T(8,128)(2,1)S(1)} %copy-done.19), channel_id=1, source_target_pairs={{0,2},{1,3},{2,0},{3,1},{4,6},{5,7},{6,4},{7,5},{8,10},{9,11},{10,... | collective-permute-start | bytes 786440 | tf_op jit(solution)/shard_map/ppermute | solution.py:370
  141.5 8.6 %copy-start.2 = (bf16[64,24,128]{2,1,0:T(8,128)(2,1)}, bf16[64,24,128]{2,1,0:T(8,128)(2,1)S(1)}, u32[]{:S(2)}) copy-start(bf16[64,24,128]{2,1,0:T(8,128)(2,1)S(1)} %all-to-all-done.2) | copy-start | bytes 1179652
  145.1 8.1 %copy-start.4 = (bf16[640,128]{1,0:T(8,128)(2,1)}, bf16[640,128]{1,0:T(8,128)(2,1)S(1)}, u32[]{:S(2)}) copy-start(bf16[640,128]{1,0:T(8,128)(2,1)S(1)} %all_gather.3.p0) | copy-start | bytes 491524
  145.1 9.0 %collective-permute-start.20 = (bf16[640,128]{1,0:T(8,128)(2,1)S(1)}, bf16[640,128]{1,0:T(8,128)(2,1)S(1)}, u32[]{:S(2)}, u32[]{:S(2)}) collective-permute-start(bf16[640,128]{1,0:T(8,128)(2,1)S(1)} %all_gather.3.p0), channel_id=1, source_target_pairs={{0,64},{32,96},{64,128},{96,160},{128,192},{160,224},{192,0},{224,... | collective-permute-start | bytes 491528 | tf_op jit(solution)/shard_map/ppermute | solution.py:370
  146.4 10.1 %collective-permute-start.19 = (bf16[640,128]{1,0:T(8,128)(2,1)S(1)}, bf16[640,128]{1,0:T(8,128)(2,1)S(1)}, u32[]{:S(2)}, u32[]{:S(2)}) collective-permute-start(bf16[640,128]{1,0:T(8,128)(2,1)S(1)} %all_gather.3.p0), channel_id=1, source_target_pairs={{0,128},{32,160},{64,192},{96,224},{128,0},{160,32},{192,64},{224,... | collective-permute-start | bytes 491528 | tf_op jit(solution)/shard_map/ppermute | solution.py:370
  149.0 7.5 %collective-permute-start.18 = (bf16[640,128]{1,0:T(8,128)(2,1)S(1)}, bf16[640,128]{1,0:T(8,128)(2,1)S(1)}, u32[]{:S(2)}, u32[]{:S(2)}) collective-permute-start(bf16[640,128]{1,0:T(8,128)(2,1)S(1)} %all_gather.3.p0), channel_id=1, source_target_pairs={{0,192},{32,224},{64,0},{96,32},{128,64},{160,96},{192,128},{224,1... | collective-permute-start | bytes 491528 | tf_op jit(solution)/shard_map/ppermute | solution.py:370
  (16 other events, 49.5 us)

commit v5 on v4

--- a/solution.py
+++ b/solution.py
@@ -428,17 +428,16 @@
     )
     dparts = scatter_pieces([d0, d1, d2, d3])
     own, got = reduce_over_chips(mine, other)
-    dparts, got = lax.optimization_barrier((dparts, got))
+    flat = received[:, :CAP].reshape(SLOTS // 128, 128)
+    total = add_step((own + got.astype(F32)).astype(BF), 1)
+    dparts, total, flat = lax.optimization_barrier((dparts, total, flat))
     grads = to_slots(slot, grad_out, dparts)
-    total = add_step(add_step((own + got.astype(F32)).astype(BF), 1), 2)
+    total = add_step(add_step(total, 2), 7)
+    grads, total, zs = lax.optimization_barrier((grads, total, [z0, z1, z2, z3]))
     arrived = lax.all_to_all(grads.reshape(NOWN, CAP, 128), BOTH, split_axis=0, concat_axis=0, tiled=True)
-    total, zs = lax.optimization_barrier((total, [z0, z1, z2, z3]))
-    total = add_step(total, 7)
+    grad_in, grad_outw = gather_weights(total)
     zparts = scatter_pieces(zs)
-    flat = received[:, :CAP].reshape(SLOTS // 128, 128)
-    total, arrived, zparts, flat = lax.optimization_barrier((total, arrived, zparts, flat))
     table_grad = add_rows(flat, arrived.reshape(SLOTS, 128))
-    grad_in, grad_outw = gather_weights(total)
     layer_out = (
         x.astype(F32)
         + (zparts[0].astype(F32) + zparts[1].astype(F32) + zparts[2].astype(F32) + zparts[3].astype(F32))

time: 160 us -> 156 us (0.975)
  waiting for transfers between devices: 55.3 us -> 47.6 us
  starting transfers between devices: 45.3 us -> 48.4 us
    ppermute x21, waiting for transfers between devices: 45.4 us -> 37.6 us  [shift(): return lax.ppermute(x, axis, [(i, fn(i)) for i in range(n)])]
    all_to_all x1, starting transfers between devices: 7.37 us -> 11.5 us  [body(): lax.all_to_all(grads.reshape(NOWN, CAP, 128), BOTH, split_axis=0, concat_...]
    all_gather x1, blocking collectives: 3.63 us -> 2.02 us  [gather_weights(): lax.all_gather(total, 'table', axis=0, tiled=True, axis_index_groups=pairs)]
  transfers between devices with their start and end apart: 23 -> 23, of which waited for: 12 -> 15; matrix products, arithmetic and copies ran while one was open for 1% -> 1% of each run, Pallas kernels for 5% -> 5%
where the time goes in v5:
time: 156 us; the launch traced here: 154 us
  starting transfers between devices  48.4 us (31%)
  waiting for transfers between devices  47.6 us (31%)
  Pallas kernels  27.1 us (17%)
  blocking collectives  24.3 us (16%)
  local copies, waits for them, and re-layouts  3.64 us (2%)
  other arithmetic  2.15 us (1%)
    ppermute x21, waiting for transfers between devices, shift(): return lax.ppermute(x, axis, [(i, fn(i)) for i in range(n)])  37.6 us
    ppermute x21, starting transfers between devices, shift(): return lax.ppermute(x, axis, [(i, fn(i)) for i in range(n)])  31.7 us
    all_to_all x1, blocking collectives, body(): lax.all_to_all(requests, BOTH, split_axis=0, concat_axis=0, tiled=True)  22.3 us
    pallas_call x1, Pallas kernels, layer(): pl.pallas_call(layer_kernel, out_shape=(jax.ShapeDtypeStruct((1280, 128),...  11.7 us
    all_to_all x1, starting transfers between devices, body(): lax.all_to_all(grads.reshape(NOWN, CAP, 128), BOTH, split_axis=0, concat_...  11.5 us
    all_to_all x1, waiting for transfers between devices, body(): lax.all_to_all(rows.reshape(NOWN, CAP, 128), BOTH, split_axis=0, concat_a...  9.98 us
    all_to_all x1, starting transfers between devices, body(): lax.all_to_all(rows.reshape(NOWN, CAP, 128), BOTH, split_axis=0, concat_a...  5.29 us
  transfers between devices with their start and end apart: 23, of which 15 were waited for; matrix products, arithmetic and copies ran while one was open for 1% of the time, Pallas kernels for 5%

profile of v5, /device:TPU:1, one launch (start us, length us, event | category | flops | bytes accessed | tf_op | source)
XLA Modules:
  0.0 154.0 jit_solution(5369694678823572450)
XLA Ops:
  0.6 1.8 %route.1 = (s32[64,128]{1,0:T(8,128)}, s32[8,128]{1,0:T(8,128)}) custom-call(s32[8,128]{1,0:T(8,128)} %bitcast.38, s32[8,128]{1,0:T(8,128)} %bitcast.39), custom_call_target="tpu_custom_call" | custom-call | tf_op jit(solution)/shard_map/route/pallas_call | solution.py:62
  2.5 22.3 %all_to_all.21 = s32[64,1,128]{2,1,0:T(1,128)} all-to-all(s32[64,1,128]{2,1,0:T(1,128)} %bitcast.37), channel_id=1, replica_groups=mesh['table'=8,'seq'=8,'tensor'=4] {'table','seq'}, dimensions={0} | all-to-all | bytes 65536 | tf_op jit(solution)/shard_map/all_to_all | solution.py:421
  24.7 2.9 %fetch.1 = bf16[1536,128]{1,0:T(8,128)(2,1)} custom-call(s32[64,128]{1,0:T(8,128)} %bitcast.35, bf16[2048,128]{1,0:T(8,128)(2,1)} %table_ref.1), custom_call_target="tpu_custom_call" | custom-call | tf_op jit(solution)/shard_map/fetch/pallas_call | solution.py:98
  27.6 5.3 %all-to-all-start.1 = ((bf16[64,24,128]{2,1,0:T(8,128)(2,1)}), bf16[64,24,128]{2,1,0:T(8,128)(2,1)S(1)}, u32[]{:S(2)}, u32[]{:S(2)}) async-start(bf16[64,24,128]{2,1,0:T(8,128)(2,1)} %bitcast.31), calls=%async_computation.1 | async-start | bytes 786432 | tf_op jit(solution)/shard_map/all_to_all | solution.py:423
  34.2 2.5 %collective-permute-start.4 = (bf16[1024,128]{1,0:T(8,128)(2,1)S(1)}, bf16[1024,128]{1,0:T(8,128)(2,1)S(1)}, u32[]{:S(2)}, u32[]{:S(2)}) collective-permute-start(bf16[1024,128]{1,0:T(8,128)(2,1)S(1)} %copy-done.3), channel_id=1, source_target_pairs={{0,2},{1,3},{2,0},{3,1},{4,6},{5,7},{6,4},{7,5},{8,10},{9,11},{10,... | collective-permute-start | bytes 786440 | tf_op jit(solution)/shard_map/ppermute | solution.py:370
  37.8 10.0 %all-to-all-done.1 = bf16[64,24,128]{2,1,0:T(8,128)(2,1)S(1)} async-done(((bf16[64,24,128]{2,1,0:T(8,128)(2,1)}), bf16[64,24,128]{2,1,0:T(8,128)(2,1)S(1)}, u32[]{:S(2)}, u32[]{:S(2)}) %all-to-all-start.1) | async-done | bytes 393248 | tf_op jit(solution)/shard_map/all_to_all | solution.py:423
  48.5 2.4 %place.1.x0 = bf16[1024,128]{1,0:T(8,128)(2,1)} custom-call(s32[8,128]{1,0:T(8,128)} %get-tuple-element.30.slot_ref, bf16[1536,128]{1,0:T(8,128)(2,1)} %bitcast.29), custom_call_target="tpu_custom_call" | custom-call | tf_op jit(solution)/shard_map/place/pallas_call | solution.py:133
  52.1 2.5 %collective-permute-start.1 = (bf16[1024,128]{1,0:T(8,128)(2,1)}, bf16[1024,128]{1,0:T(8,128)(2,1)S(1)}, u32[]{:S(2)}, u32[]{:S(2)}) collective-permute-start(bf16[1024,128]{1,0:T(8,128)(2,1)} %place.1.x0), channel_id=1, source_target_pairs={{0,2},{1,3},{2,0},{3,1},{4,6},{5,7},{6,4},{7,5},{8,10},{9,11},{10,... | collective-permute-start | bytes 786440 | tf_op jit(solution)/shard_map/ppermute | solution.py:370
  55.7 3.4 %collective-permute-done.2.x3 = bf16[1024,128]{1,0:T(8,128)(2,1)S(1)} collective-permute-done((bf16[1024,128]{1,0:T(8,128)(2,1)}, bf16[1024,128]{1,0:T(8,128)(2,1)S(1)}, u32[]{:S(2)}, u32[]{:S(2)}) %collective-permute-start.2) | collective-permute-done | bytes 262176 | tf_op jit(solution)/shard_map/ppermute | solution.py:370
  59.1 6.6 %collective-permute-done.1.x2 = bf16[1024,128]{1,0:T(8,128)(2,1)S(1)} collective-permute-done((bf16[1024,128]{1,0:T(8,128)(2,1)}, bf16[1024,128]{1,0:T(8,128)(2,1)S(1)}, u32[]{:S(2)}, u32[]{:S(2)}) %collective-permute-start.1) | collective-permute-done | bytes 262176 | tf_op jit(solution)/shard_map/ppermute | solution.py:370
  66.5 11.7 %layer.1 = (f32[1280,128]{1,0:T(8,128)}, bf16[1280,128]{1,0:T(8,128)(2,1)}, bf16[1024,128]{1,0:T(8,128)(2,1)}, bf16[1024,128]{1,0:T(8,128)(2,1)}, bf16[1024,128]...) custom-call(s32[1]{0:T(128)} %bitcast.7.pos_ref, ...), custom_call_target="tpu_custom_call" | custom-call | tf_op jit(solution)/shard_map/layer/pallas_call | solution.py:263
  78.2 2.0 %collective-permute-start.9 = (bf16[1280,128]{1,0:T(8,128)(2,1)}, bf16[1280,128]{1,0:T(8,128)(2,1)S(1)}, u32[]{:S(2)}, u32[]{:S(2)}) collective-permute-start(bf16[1280,128]{1,0:T(8,128)(2,1)} %get-tuple-element.37), channel_id=1, source_target_pairs={{0,32},{32,0},{64,96},{96,64},{128,160},{160,128},{192,224},{224,1... | collective-permute-start | bytes 983048 | tf_op jit(solution)/shard_map/ppermute | solution.py:370
  80.2 1.5 collective-permute-done.9
  83.7 4.7 %collective-permute-done.10 = bf16[640,128]{1,0:T(8,128)(2,1)S(1)} collective-permute-done((bf16[640,128]{1,0:T(8,128)(2,1)S(1)}, bf16[640,128]{1,0:T(8,128)(2,1)S(1)}, u32[]{:S(2)}, u32[]{:S(2)}) %collective-permute-start.10) | collective-permute-done | bytes 163872 | tf_op jit(solution)/shard_map/ppermute | solution.py:370
  88.4 1.3 collective-permute-start.11
  89.7 3.3 %collective-permute-done.11 = bf16[320,128]{1,0:T(8,128)(2,1)S(1)} collective-permute-done((bf16[320,128]{1,0:T(8,128)(2,1)S(1)}, bf16[320,128]{1,0:T(8,128)(2,1)S(1)}, u32[]{:S(2)}, u32[]{:S(2)}) %collective-permute-start.11) | collective-permute-done | bytes 81952 | tf_op jit(solution)/shard_map/ppermute | solution.py:370
  95.2 1.7 %collective-permute-start.7 = (bf16[1024,128]{1,0:T(8,128)(2,1)S(1)}, bf16[1024,128]{1,0:T(8,128)(2,1)S(1)}, u32[]{:S(2)}, u32[]{:S(2)}) collective-permute-start(bf16[1024,128]{1,0:T(8,128)(2,1)S(1)} %copy-done.23), channel_id=1, source_target_pairs={{0,3},{1,0},{2,1},{3,2},{4,7},{5,4},{6,5},{7,6},{8,11},{9,8},{10,9... | collective-permute-start | bytes 786440 | tf_op jit(solution)/shard_map/ppermute | solution.py:370
  98.7 2.0 %collective-permute-done.6.d1 = bf16[1024,128]{1,0:T(8,128)(2,1)S(1)} collective-permute-done((bf16[1024,128]{1,0:T(8,128)(2,1)S(1)}, bf16[1024,128]{1,0:T(8,128)(2,1)S(1)}, u32[]{:S(2)}, u32[]{:S(2)}) %collective-permute-start.6) | collective-permute-done | bytes 262176 | tf_op jit(solution)/shard_map/ppermute | solution.py:370
  101.3 5.0 %collective-permute-done.8.d3 = bf16[1024,128]{1,0:T(8,128)(2,1)S(1)} collective-permute-done((bf16[1024,128]{1,0:T(8,128)(2,1)S(1)}, bf16[1024,128]{1,0:T(8,128)(2,1)S(1)}, u32[]{:S(2)}, u32[]{:S(2)}) %collective-permute-start.8) | collective-permute-done | bytes 262176 | tf_op jit(solution)/shard_map/ppermute | solution.py:370
  107.5 3.9 %collective-permute-done.13 = bf16[320,128]{1,0:T(8,128)(2,1)S(1)} collective-permute-done((bf16[320,128]{1,0:T(8,128)(2,1)S(1)}, bf16[320,128]{1,0:T(8,128)(2,1)S(1)}, u32[]{:S(2)}, u32[]{:S(2)}) %collective-permute-start.13) | collective-permute-done | bytes 81952 | tf_op jit(solution)/shard_map/ppermute | solution.py:370
  111.4 1.7 %collective-permute-start.14 = (bf16[320,128]{1,0:T(8,128)(2,1)S(1)}, bf16[320,128]{1,0:T(8,128)(2,1)S(1)}, u32[]{:S(2)}, u32[]{:S(2)}) collective-permute-start(bf16[320,128]{1,0:T(8,128)(2,1)S(1)} %add_convert_fusion.2), channel_id=1, source_target_pairs={{0,28},{4,24},{8,20},{12,16},{16,12},{20,8},{24,4},{28,0},{1,29},{... | collective-permute-start | bytes 245768 | tf_op jit(solution)/shard_map/ppermute | solution.py:370
  113.1 2.8 %to_slots.1 = bf16[1536,128]{1,0:T(8,128)(2,1)} custom-call(s32[8,128]{1,0:T(8,128)} %get-tuple-element.30.slot_ref, bf16[1024,128]{1,0:T(8,128)(2,1)} %grad_ref.1, bf16[1024,128]{1,0:T(8,128)(2,1)} %get-tuple-element.38.d0, bf16[1024,128]{1,0:T(8,128)(2,1)} %copy-done.13, bf16[1024,128]{1,0:T(8,128)(2,1)} %copy-done.14, bf16[1024,128]{1,0:T(8,128)(2,1)} %copy-done.15), custom_call_target="tpu_custom_call" | custom-call | tf_op jit(solution)/shard_map/to_slots/pallas_call | solution.py:318
  117.0 11.5 %all-to-all-start.2 = ((bf16[64,24,128]{2,1,0:T(8,128)(2,1)}), bf16[64,24,128]{2,1,0:T(8,128)(2,1)S(1)}, u32[]{:S(2)}, u32[]{:S(2)}) async-start(bf16[64,24,128]{2,1,0:T(8,128)(2,1)} %bitcast.32), calls=%async_computation.2 | async-start | bytes 786432 | tf_op jit(solution)/shard_map/all_to_all | solution.py:437
  128.4 2.0 %all_gather.3.p0 = bf16[640,128]{1,0:T(8,128)(2,1)S(1)} all-gather(bf16[320,128]{1,0:T(8,128)(2,1)S(1)} %add_convert_fusion.1), channel_id=1, replica_groups={{0,32},{64,96},{128,160},{192,224},{1,33},{65,97},{129,161},{193,225},{..., dimensions={0}, use_global_device_ids=true | all-gather | bytes 245760 | tf_op jit(solution)/shard_map/all_gather | solution.py:411
  130.4 1.3 collective-permute-start.20
  132.7 1.8 %collective-permute-start.16 = (bf16[1024,128]{1,0:T(8,128)(2,1)S(1)}, bf16[1024,128]{1,0:T(8,128)(2,1)S(1)}, u32[]{:S(2)}, u32[]{:S(2)}) collective-permute-start(bf16[1024,128]{1,0:T(8,128)(2,1)S(1)} %copy-done.20), channel_id=1, source_target_pairs={{0,3},{1,0},{2,1},{3,2},{4,7},{5,4},{6,5},{7,6},{8,11},{9,8},{10,9... | collective-permute-start | bytes 786440 | tf_op jit(solution)/shard_map/ppermute | solution.py:370
  135.4 2.6 %collective-permute-start.19 = (bf16[640,128]{1,0:T(8,128)(2,1)S(1)}, bf16[640,128]{1,0:T(8,128)(2,1)S(1)}, u32[]{:S(2)}, u32[]{:S(2)}) collective-permute-start(bf16[640,128]{1,0:T(8,128)(2,1)S(1)} %all_gather.3.p0), channel_id=1, source_target_pairs={{0,128},{32,160},{64,192},{96,224},{128,0},{160,32},{192,64},{224,... | collective-permute-start | bytes 491528 | tf_op jit(solution)/shard_map/ppermute | solution.py:370
  138.0 1.3 collective-permute-done.20.p3
  139.4 2.5 %collective-permute-start.18 = (bf16[640,128]{1,0:T(8,128)(2,1)S(1)}, bf16[640,128]{1,0:T(8,128)(2,1)S(1)}, u32[]{:S(2)}, u32[]{:S(2)}) collective-permute-start(bf16[640,128]{1,0:T(8,128)(2,1)S(1)} %all_gather.3.p0), channel_id=1, source_target_pairs={{0,192},{32,224},{64,0},{96,32},{128,64},{160,96},{192,128},{224,1... | collective-permute-start | bytes 491528 | tf_op jit(solution)/shard_map/ppermute | solution.py:370
  141.9 3.6 %collective-permute-done.19.p2 = bf16[640,128]{1,0:T(8,128)(2,1)S(1)} collective-permute-done((bf16[640,128]{1,0:T(8,128)(2,1)S(1)}, bf16[640,128]{1,0:T(8,128)(2,1)S(1)}, u32[]{:S(2)}, u32[]{:S(2)}) %collective-permute-start.19) | collective-permute-done | bytes 163872 | tf_op jit(solution)/shard_map/ppermute | solution.py:370
  146.8 2.4 %unpack.1 = (f32[2048,128]{1,0:T(8,128)}, f32[128,512]{1,0:T(8,128)}) custom-call(s32[1]{0:T(128)} %bitcast.17.y_ref, bf16[640,128]{1,0:T(8,128)(2,1)} %copy-done.4, bf16[640,128]{1,0:T(8,128)(2,1)} %copy-done.18, bf16[640,128]{1,0:T(8,128)(2,1)} %copy-done.17, bf16[640,128]{1,0:T(8,128)(2,1)} %copy-done.16), custom_call_target="tpu_custom_call" | custom-call | tf_op jit(solution)/shard_map/unpack/pallas_call | solution.py:358
  150.9 3.1 %add_rows.1 = f32[2048,128]{1,0:T(8,128)} custom-call(s32[12,128]{1,0:T(8,128)} %reshape.59.req_ref, bf16[1536,128]{1,0:T(8,128)(2,1)} %bitcast.30), custom_call_target="tpu_custom_call" | custom-call | tf_op jit(solution)/shard_map/add_rows/pallas_call | solution.py:336
  (83 shorter events, 20.0 us)
Async XLA Ops:
  27.6 20.2 %all-to-all-start.1 = ((bf16[64,24,128]{2,1,0:T(8,128)(2,1)}), bf16[64,24,128]{2,1,0:T(8,128)(2,1)S(1)}, u32[]{:S(2)}, u32[]{:S(2)}) async-start(bf16[64,24,128]{2,1,0:T(8,128)(2,1)} %bitcast.31), calls=%async_computation.1 | async-start | bytes 786432 | tf_op jit(solution)/shard_map/all_to_all | solution.py:423
  32.9 21.6 %collective-permute-start.5 = (bf16[1024,128]{1,0:T(8,128)(2,1)S(1)}, bf16[1024,128]{1,0:T(8,128)(2,1)S(1)}, u32[]{:S(2)}, u32[]{:S(2)}) collective-permute-start(bf16[1024,128]{1,0:T(8,128)(2,1)S(1)} %copy-done.3), channel_id=1, source_target_pairs={{0,1},{1,2},{2,3},{3,0},{4,5},{5,6},{6,7},{7,4},{8,9},{9,10},{10,1... | collective-permute-start | bytes 786440 | tf_op jit(solution)/shard_map/ppermute | solution.py:370
  34.2 21.5 %collective-permute-start.4 = (bf16[1024,128]{1,0:T(8,128)(2,1)S(1)}, bf16[1024,128]{1,0:T(8,128)(2,1)S(1)}, u32[]{:S(2)}, u32[]{:S(2)}) collective-permute-start(bf16[1024,128]{1,0:T(8,128)(2,1)S(1)} %copy-done.3), channel_id=1, source_target_pairs={{0,2},{1,3},{2,0},{3,1},{4,6},{5,7},{6,4},{7,5},{8,10},{9,11},{10,... | collective-permute-start | bytes 786440 | tf_op jit(solution)/shard_map/ppermute | solution.py:370
  36.6 19.1 %collective-permute-start.3 = (bf16[1024,128]{1,0:T(8,128)(2,1)S(1)}, bf16[1024,128]{1,0:T(8,128)(2,1)S(1)}, u32[]{:S(2)}, u32[]{:S(2)}) collective-permute-start(bf16[1024,128]{1,0:T(8,128)(2,1)S(1)} %copy-done.3), channel_id=1, source_target_pairs={{0,3},{1,0},{2,1},{3,2},{4,7},{5,4},{6,5},{7,6},{8,11},{9,8},{10,9... | collective-permute-start | bytes 786440 | tf_op jit(solution)/shard_map/ppermute | solution.py:370
  50.9 8.2 %collective-permute-start.2 = (bf16[1024,128]{1,0:T(8,128)(2,1)}, bf16[1024,128]{1,0:T(8,128)(2,1)S(1)}, u32[]{:S(2)}, u32[]{:S(2)}) collective-permute-start(bf16[1024,128]{1,0:T(8,128)(2,1)} %place.1.x0), channel_id=1, source_target_pairs={{0,1},{1,2},{2,3},{3,0},{4,5},{5,6},{6,7},{7,4},{8,9},{9,10},{10,1... | collective-permute-start | bytes 786440 | tf_op jit(solution)/shard_map/ppermute | solution.py:370
  52.1 13.6 %collective-permute-start.1 = (bf16[1024,128]{1,0:T(8,128)(2,1)}, bf16[1024,128]{1,0:T(8,128)(2,1)S(1)}, u32[]{:S(2)}, u32[]{:S(2)}) collective-permute-start(bf16[1024,128]{1,0:T(8,128)(2,1)} %place.1.x0), channel_id=1, source_target_pairs={{0,2},{1,3},{2,0},{3,1},{4,6},{5,7},{6,4},{7,5},{8,10},{9,11},{10,... | collective-permute-start | bytes 786440 | tf_op jit(solution)/shard_map/ppermute | solution.py:370
  54.6 11.3 %copy-start.6 = (bf16[1024,128]{1,0:T(8,128)(2,1)}, bf16[1024,128]{1,0:T(8,128)(2,1)S(1)}, u32[]{:S(2)}) copy-start(bf16[1024,128]{1,0:T(8,128)(2,1)S(1)} %collective-permute-done.5.g3) | copy-start | bytes 786436
  54.6 11.3 %collective-permute-start = (bf16[1024,128]{1,0:T(8,128)(2,1)}, bf16[1024,128]{1,0:T(8,128)(2,1)S(1)}, u32[]{:S(2)}, u32[]{:S(2)}) collective-permute-start(bf16[1024,128]{1,0:T(8,128)(2,1)} %place.1.x0), channel_id=1, source_target_pairs={{0,3},{1,0},{2,1},{3,2},{4,7},{5,4},{6,5},{7,6},{8,11},{9,8},{10,9... | collective-permute-start | bytes 786440 | tf_op jit(solution)/shard_map/ppermute | solution.py:370
  55.7 10.1 %copy-start.7 = (bf16[1024,128]{1,0:T(8,128)(2,1)}, bf16[1024,128]{1,0:T(8,128)(2,1)S(1)}, u32[]{:S(2)}) copy-start(bf16[1024,128]{1,0:T(8,128)(2,1)S(1)} %collective-permute-done.4.g2) | copy-start | bytes 786436
  55.7 10.1 %copy-start.8 = (bf16[1024,128]{1,0:T(8,128)(2,1)}, bf16[1024,128]{1,0:T(8,128)(2,1)S(1)}, u32[]{:S(2)}) copy-start(bf16[1024,128]{1,0:T(8,128)(2,1)S(1)} %collective-permute-done.3.g1) | copy-start | bytes 786436
  78.2 3.5 %collective-permute-start.9 = (bf16[1280,128]{1,0:T(8,128)(2,1)}, bf16[1280,128]{1,0:T(8,128)(2,1)S(1)}, u32[]{:S(2)}, u32[]{:S(2)}) collective-permute-start(bf16[1280,128]{1,0:T(8,128)(2,1)} %get-tuple-element.37), channel_id=1, source_target_pairs={{0,32},{32,0},{64,96},{96,64},{128,160},{160,128},{192,224},{224,1... | collective-permute-start | bytes 983048 | tf_op jit(solution)/shard_map/ppermute | solution.py:370
  82.9 5.5 %collective-permute-start.10 = (bf16[640,128]{1,0:T(8,128)(2,1)S(1)}, bf16[640,128]{1,0:T(8,128)(2,1)S(1)}, u32[]{:S(2)}, u32[]{:S(2)}) collective-permute-start(bf16[640,128]{1,0:T(8,128)(2,1)S(1)} %fusion), channel_id=1, source_target_pairs={{0,64},{32,96},{64,0},{96,32},{128,192},{160,224},{192,128},{224,1... | collective-permute-start | bytes 491528 | tf_op jit(solution)/shard_map/ppermute | solution.py:370
  88.4 4.6 %collective-permute-start.11 = (bf16[320,128]{1,0:T(8,128)(2,1)S(1)}, bf16[320,128]{1,0:T(8,128)(2,1)S(1)}, u32[]{:S(2)}, u32[]{:S(2)}) collective-permute-start(bf16[320,128]{1,0:T(8,128)(2,1)S(1)} %fusion.2), channel_id=1, source_target_pairs={{0,192},{32,224},{64,128},{96,160},{128,64},{160,96},{192,0},{224,... | collective-permute-start | bytes 245768 | tf_op jit(solution)/shard_map/ppermute | solution.py:370
  93.1 5.6 %collective-permute-start.12 = (bf16[320,128]{1,0:T(8,128)(2,1)S(1)}, bf16[320,128]{1,0:T(8,128)(2,1)S(1)}, u32[]{:S(2)}, u32[]{:S(2)}) collective-permute-start(bf16[320,128]{1,0:T(8,128)(2,1)S(1)} %fusion.1), channel_id=1, source_target_pairs={{0,4},{4,0},{8,12},{12,8},{16,20},{20,16},{24,28},{28,24},{1,5},{5... | collective-permute-start | bytes 245768 | tf_op jit(solution)/shard_map/ppermute | solution.py:370
  94.2 6.4 %collective-permute-start.6 = (bf16[1024,128]{1,0:T(8,128)(2,1)S(1)}, bf16[1024,128]{1,0:T(8,128)(2,1)S(1)}, u32[]{:S(2)}, u32[]{:S(2)}) collective-permute-start(bf16[1024,128]{1,0:T(8,128)(2,1)S(1)} %copy-done.24), channel_id=1, source_target_pairs={{0,1},{1,2},{2,3},{3,0},{4,5},{5,6},{6,7},{7,4},{8,9},{9,10},{10,1... | collective-permute-start | bytes 786440 | tf_op jit(solution)/shard_map/ppermute | solution.py:370
  95.2 6.1 %collective-permute-start.7 = (bf16[1024,128]{1,0:T(8,128)(2,1)S(1)}, bf16[1024,128]{1,0:T(8,128)(2,1)S(1)}, u32[]{:S(2)}, u32[]{:S(2)}) collective-permute-start(bf16[1024,128]{1,0:T(8,128)(2,1)S(1)} %copy-done.23), channel_id=1, source_target_pairs={{0,3},{1,0},{2,1},{3,2},{4,7},{5,4},{6,5},{7,6},{8,11},{9,8},{10,9... | collective-permute-start | bytes 786440 | tf_op jit(solution)/shard_map/ppermute | solution.py:370
  96.9 9.4 %collective-permute-start.8 = (bf16[1024,128]{1,0:T(8,128)(2,1)S(1)}, bf16[1024,128]{1,0:T(8,128)(2,1)S(1)}, u32[]{:S(2)}, u32[]{:S(2)}) collective-permute-start(bf16[1024,128]{1,0:T(8,128)(2,1)S(1)} %copy-done.22), channel_id=1, source_target_pairs={{0,2},{1,3},{2,0},{3,1},{4,6},{5,7},{6,4},{7,5},{8,10},{9,11},{10,... | collective-permute-start | bytes 786440 | tf_op jit(solution)/shard_map/ppermute | solution.py:370
  100.7 12.4 %copy-start.13 = (bf16[1024,128]{1,0:T(8,128)(2,1)}, bf16[1024,128]{1,0:T(8,128)(2,1)S(1)}, u32[]{:S(2)}) copy-start(bf16[1024,128]{1,0:T(8,128)(2,1)S(1)} %collective-permute-done.6.d1) | copy-start | bytes 786436
  101.3 11.8 %copy-start.14 = (bf16[1024,128]{1,0:T(8,128)(2,1)}, bf16[1024,128]{1,0:T(8,128)(2,1)S(1)}, u32[]{:S(2)}) copy-start(bf16[1024,128]{1,0:T(8,128)(2,1)S(1)} %collective-permute-done.7.d2) | copy-start | bytes 786436
  106.3 5.1 %collective-permute-start.13 = (bf16[320,128]{1,0:T(8,128)(2,1)S(1)}, bf16[320,128]{1,0:T(8,128)(2,1)S(1)}, u32[]{:S(2)}, u32[]{:S(2)}) collective-permute-start(bf16[320,128]{1,0:T(8,128)(2,1)S(1)} %add_convert_fusion.3), channel_id=1, source_target_pairs={{0,8},{4,12},{8,0},{12,4},{16,24},{20,28},{24,16},{28,20},{1,9},{5... | collective-permute-start | bytes 245768 | tf_op jit(solution)/shard_map/ppermute | solution.py:370
  111.4 5.5 %collective-permute-start.14 = (bf16[320,128]{1,0:T(8,128)(2,1)S(1)}, bf16[320,128]{1,0:T(8,128)(2,1)S(1)}, u32[]{:S(2)}, u32[]{:S(2)}) collective-permute-start(bf16[320,128]{1,0:T(8,128)(2,1)S(1)} %add_convert_fusion.2), channel_id=1, source_target_pairs={{0,28},{4,24},{8,20},{12,16},{16,12},{20,8},{24,4},{28,0},{1,29},{... | collective-permute-start | bytes 245768 | tf_op jit(solution)/shard_map/ppermute | solution.py:370
  116.9 14.8 %copy-start.21 = (bf16[1024,128]{1,0:T(8,128)(2,1)S(1)}, bf16[1024,128]{1,0:T(8,128)(2,1)}, u32[]{:S(2)}) copy-start(bf16[1024,128]{1,0:T(8,128)(2,1)} %get-tuple-element.48) | copy-start | bytes 786436
  116.9 15.7 %copy-start.20 = (bf16[1024,128]{1,0:T(8,128)(2,1)S(1)}, bf16[1024,128]{1,0:T(8,128)(2,1)}, u32[]{:S(2)}) copy-start(bf16[1024,128]{1,0:T(8,128)(2,1)} %get-tuple-element.49) | copy-start | bytes 786436
  116.9 17.5 %copy-start.19 = (bf16[1024,128]{1,0:T(8,128)(2,1)S(1)}, bf16[1024,128]{1,0:T(8,128)(2,1)}, u32[]{:S(2)}) copy-start(bf16[1024,128]{1,0:T(8,128)(2,1)} %get-tuple-element.50) | copy-start | bytes 786436
  117.0 33.2 %all-to-all-start.2 = ((bf16[64,24,128]{2,1,0:T(8,128)(2,1)}), bf16[64,24,128]{2,1,0:T(8,128)(2,1)S(1)}, u32[]{:S(2)}, u32[]{:S(2)}) async-start(bf16[64,24,128]{2,1,0:T(8,128)(2,1)} %bitcast.32), calls=%async_computation.2 | async-start | bytes 786432 | tf_op jit(solution)/shard_map/all_to_all | solution.py:437
  130.4 15.7 %copy-start.4 = (bf16[640,128]{1,0:T(8,128)(2,1)}, bf16[640,128]{1,0:T(8,128)(2,1)S(1)}, u32[]{:S(2)}) copy-start(bf16[640,128]{1,0:T(8,128)(2,1)S(1)} %all_gather.3.p0) | copy-start | bytes 491524
  130.4 8.9 %collective-permute-start.20 = (bf16[640,128]{1,0:T(8,128)(2,1)S(1)}, bf16[640,128]{1,0:T(8,128)(2,1)S(1)}, u32[]{:S(2)}, u32[]{:S(2)}) collective-permute-start(bf16[640,128]{1,0:T(8,128)(2,1)S(1)} %all_gather.3.p0), channel_id=1, source_target_pairs={{0,64},{32,96},{64,128},{96,160},{128,192},{160,224},{192,0},{224,... | collective-permute-start | bytes 491528 | tf_op jit(solution)/shard_map/ppermute | solution.py:370
  131.8 17.4 %collective-permute-start.15 = (bf16[1024,128]{1,0:T(8,128)(2,1)S(1)}, bf16[1024,128]{1,0:T(8,128)(2,1)S(1)}, u32[]{:S(2)}, u32[]{:S(2)}) collective-permute-start(bf16[1024,128]{1,0:T(8,128)(2,1)S(1)} %copy-done.21), channel_id=1, source_target_pairs={{0,1},{1,2},{2,3},{3,0},{4,5},{5,6},{6,7},{7,4},{8,9},{9,10},{10,1... | collective-permute-start | bytes 786440 | tf_op jit(solution)/shard_map/ppermute | solution.py:370
  132.7 16.6 %collective-permute-start.16 = (bf16[1024,128]{1,0:T(8,128)(2,1)S(1)}, bf16[1024,128]{1,0:T(8,128)(2,1)S(1)}, u32[]{:S(2)}, u32[]{:S(2)}) collective-permute-start(bf16[1024,128]{1,0:T(8,128)(2,1)S(1)} %copy-done.20), channel_id=1, source_target_pairs={{0,3},{1,0},{2,1},{3,2},{4,7},{5,4},{6,5},{7,6},{8,11},{9,8},{10,9... | collective-permute-start | bytes 786440 | tf_op jit(solution)/shard_map/ppermute | solution.py:370
  134.5 14.8 %collective-permute-start.17 = (bf16[1024,128]{1,0:T(8,128)(2,1)S(1)}, bf16[1024,128]{1,0:T(8,128)(2,1)S(1)}, u32[]{:S(2)}, u32[]{:S(2)}) collective-permute-start(bf16[1024,128]{1,0:T(8,128)(2,1)S(1)} %copy-done.19), channel_id=1, source_target_pairs={{0,2},{1,3},{2,0},{3,1},{4,6},{5,7},{6,4},{7,5},{8,10},{9,11},{10,... | collective-permute-start | bytes 786440 | tf_op jit(solution)/shard_map/ppermute | solution.py:370
  135.4 10.1 %collective-permute-start.19 = (bf16[640,128]{1,0:T(8,128)(2,1)S(1)}, bf16[640,128]{1,0:T(8,128)(2,1)S(1)}, u32[]{:S(2)}, u32[]{:S(2)}) collective-permute-start(bf16[640,128]{1,0:T(8,128)(2,1)S(1)} %all_gather.3.p0), channel_id=1, source_target_pairs={{0,128},{32,160},{64,192},{96,224},{128,0},{160,32},{192,64},{224,... | collective-permute-start | bytes 491528 | tf_op jit(solution)/shard_map/ppermute | solution.py:370
  139.4 6.8 %collective-permute-start.18 = (bf16[640,128]{1,0:T(8,128)(2,1)S(1)}, bf16[640,128]{1,0:T(8,128)(2,1)S(1)}, u32[]{:S(2)}, u32[]{:S(2)}) collective-permute-start(bf16[640,128]{1,0:T(8,128)(2,1)S(1)} %all_gather.3.p0), channel_id=1, source_target_pairs={{0,192},{32,224},{64,0},{96,32},{128,64},{160,96},{192,128},{224,1... | collective-permute-start | bytes 491528 | tf_op jit(solution)/shard_map/ppermute | solution.py:370
  (16 other events, 64.2 us)

commit v6 on v5

--- a/solution.py
+++ b/solution.py
@@ -429,14 +429,15 @@
     dparts = scatter_pieces([d0, d1, d2, d3])
     own, got = reduce_over_chips(mine, other)
     flat = received[:, :CAP].reshape(SLOTS // 128, 128)
+    dparts, got, flat = lax.optimization_barrier((dparts, got, flat))
+    grads = to_slots(slot, grad_out, dparts)
     total = add_step((own + got.astype(F32)).astype(BF), 1)
-    dparts, total, flat = lax.optimization_barrier((dparts, total, flat))
-    grads = to_slots(slot, grad_out, dparts)
     total = add_step(add_step(total, 2), 7)
     grads, total, zs = lax.optimization_barrier((grads, total, [z0, z1, z2, z3]))
     arrived = lax.all_to_all(grads.reshape(NOWN, CAP, 128), BOTH, split_axis=0, concat_axis=0, tiled=True)
     grad_in, grad_outw = gather_weights(total)
     zparts = scatter_pieces(zs)
+    arrived, zparts = lax.optimization_barrier((arrived, zparts))
     table_grad = add_rows(flat, arrived.reshape(SLOTS, 128))
     layer_out = (
         x.astype(F32)

time: 156 us -> 151 us (0.968)
  waiting for transfers between devices: 47.6 us -> 40.9 us
    ppermute x21, waiting for transfers between devices: 37.6 us -> 30.9 us  [shift(): return lax.ppermute(x, axis, [(i, fn(i)) for i in range(n)])]
  transfers between devices with their start and end apart: 23 -> 23, of which waited for: 15 -> 13; matrix products, arithmetic and copies ran while one was open for 1% -> 0% of each run, Pallas kernels for 5% -> 5%
where the time goes in v6:
time: 151 us; the launch traced here: 149 us
  starting transfers between devices  49.4 us (33%)
  waiting for transfers between devices  40.9 us (27%)
  Pallas kernels  27.1 us (18%)
  blocking collectives  24.4 us (16%)
  local copies, waits for them, and re-layouts  3.64 us (2%)
  other arithmetic  2.2 us (1%)
    ppermute x21, starting transfers between devices, shift(): return lax.ppermute(x, axis, [(i, fn(i)) for i in range(n)])  32.5 us
    ppermute x21, waiting for transfers between devices, shift(): return lax.ppermute(x, axis, [(i, fn(i)) for i in range(n)])  30.9 us
    all_to_all x1, blocking collectives, body(): lax.all_to_all(requests, BOTH, split_axis=0, concat_axis=0, tiled=True)  22.4 us
    all_to_all x1, starting transfers between devices, body(): lax.all_to_all(grads.reshape(NOWN, CAP, 128), BOTH, split_axis=0, concat_...  11.9 us
    pallas_call x1, Pallas kernels, layer(): pl.pallas_call(layer_kernel, out_shape=(jax.ShapeDtypeStruct((1280, 128),...  11.7 us
    all_to_all x1, waiting for transfers between devices, body(): lax.all_to_all(rows.reshape(NOWN, CAP, 128), BOTH, split_axis=0, concat_a...  9.98 us
    all_to_all x1, starting transfers between devices, body(): lax.all_to_all(rows.reshape(NOWN, CAP, 128), BOTH, split_axis=0, concat_a...  4.98 us
    pallas_call x1, Pallas kernels, add_rows(): pl.pallas_call(add_rows_kernel, out_shape=jax.ShapeDtypeStruct((ROWS, 128...  3.16 us
  transfers between devices with their start and end apart: 23, of which 13 were waited for; matrix products, arithmetic and copies ran while one was open for 0% of the time, Pallas kernels for 5%

profile of v6, /device:TPU:1, one launch (start us, length us, event | category | flops | bytes accessed | tf_op | source)
XLA Modules:
  0.0 148.6 jit_solution(1353993019090350607)
XLA Ops:
  0.6 1.8 %route.1 = (s32[64,128]{1,0:T(8,128)}, s32[8,128]{1,0:T(8,128)}) custom-call(s32[8,128]{1,0:T(8,128)} %bitcast.38, s32[8,128]{1,0:T(8,128)} %bitcast.39), custom_call_target="tpu_custom_call" | custom-call | tf_op jit(solution)/shard_map/route/pallas_call | solution.py:62
  2.5 22.4 %all_to_all.21 = s32[64,1,128]{2,1,0:T(1,128)} all-to-all(s32[64,1,128]{2,1,0:T(1,128)} %bitcast.37), channel_id=1, replica_groups=mesh['table'=8,'seq'=8,'tensor'=4] {'table','seq'}, dimensions={0} | all-to-all | bytes 65536 | tf_op jit(solution)/shard_map/all_to_all | solution.py:421
  24.9 2.9 %fetch.1 = bf16[1536,128]{1,0:T(8,128)(2,1)} custom-call(s32[64,128]{1,0:T(8,128)} %bitcast.35, bf16[2048,128]{1,0:T(8,128)(2,1)} %table_ref.1), custom_call_target="tpu_custom_call" | custom-call | tf_op jit(solution)/shard_map/fetch/pallas_call | solution.py:98
  27.8 5.0 %all-to-all-start.1 = ((bf16[64,24,128]{2,1,0:T(8,128)(2,1)}), bf16[64,24,128]{2,1,0:T(8,128)(2,1)S(1)}, u32[]{:S(2)}, u32[]{:S(2)}) async-start(bf16[64,24,128]{2,1,0:T(8,128)(2,1)} %bitcast.31), calls=%async_computation.1 | async-start | bytes 786432 | tf_op jit(solution)/shard_map/all_to_all | solution.py:423
  34.0 2.5 %collective-permute-start.4 = (bf16[1024,128]{1,0:T(8,128)(2,1)S(1)}, bf16[1024,128]{1,0:T(8,128)(2,1)S(1)}, u32[]{:S(2)}, u32[]{:S(2)}) collective-permute-start(bf16[1024,128]{1,0:T(8,128)(2,1)S(1)} %copy-done.3), channel_id=1, source_target_pairs={{0,2},{1,3},{2,0},{3,1},{4,6},{5,7},{6,4},{7,5},{8,10},{9,11},{10,... | collective-permute-start | bytes 786440 | tf_op jit(solution)/shard_map/ppermute | solution.py:370
  37.7 10.0 %all-to-all-done.1 = bf16[64,24,128]{2,1,0:T(8,128)(2,1)S(1)} async-done(((bf16[64,24,128]{2,1,0:T(8,128)(2,1)}), bf16[64,24,128]{2,1,0:T(8,128)(2,1)S(1)}, u32[]{:S(2)}, u32[]{:S(2)}) %all-to-all-start.1) | async-done | bytes 393248 | tf_op jit(solution)/shard_map/all_to_all | solution.py:423
  48.4 2.4 %place.1.x0 = bf16[1024,128]{1,0:T(8,128)(2,1)} custom-call(s32[8,128]{1,0:T(8,128)} %get-tuple-element.35.slot_ref, bf16[1536,128]{1,0:T(8,128)(2,1)} %bitcast.29), custom_call_target="tpu_custom_call" | custom-call | tf_op jit(solution)/shard_map/place/pallas_call | solution.py:133
  51.9 2.5 %collective-permute-start.1 = (bf16[1024,128]{1,0:T(8,128)(2,1)}, bf16[1024,128]{1,0:T(8,128)(2,1)S(1)}, u32[]{:S(2)}, u32[]{:S(2)}) collective-permute-start(bf16[1024,128]{1,0:T(8,128)(2,1)} %place.1.x0), channel_id=1, source_target_pairs={{0,2},{1,3},{2,0},{3,1},{4,6},{5,7},{6,4},{7,5},{8,10},{9,11},{10,... | collective-permute-start | bytes 786440 | tf_op jit(solution)/shard_map/ppermute | solution.py:370
  55.6 3.4 %collective-permute-done.2.x3 = bf16[1024,128]{1,0:T(8,128)(2,1)S(1)} collective-permute-done((bf16[1024,128]{1,0:T(8,128)(2,1)}, bf16[1024,128]{1,0:T(8,128)(2,1)S(1)}, u32[]{:S(2)}, u32[]{:S(2)}) %collective-permute-start.2) | collective-permute-done | bytes 262176 | tf_op jit(solution)/shard_map/ppermute | solution.py:370
  59.0 6.6 %collective-permute-done.1.x2 = bf16[1024,128]{1,0:T(8,128)(2,1)S(1)} collective-permute-done((bf16[1024,128]{1,0:T(8,128)(2,1)}, bf16[1024,128]{1,0:T(8,128)(2,1)S(1)}, u32[]{:S(2)}, u32[]{:S(2)}) %collective-permute-start.1) | collective-permute-done | bytes 262176 | tf_op jit(solution)/shard_map/ppermute | solution.py:370
  66.4 11.7 %layer.1 = (f32[1280,128]{1,0:T(8,128)}, bf16[1280,128]{1,0:T(8,128)(2,1)}, bf16[1024,128]{1,0:T(8,128)(2,1)}, bf16[1024,128]{1,0:T(8,128)(2,1)}, bf16[1024,128]...) custom-call(s32[1]{0:T(128)} %bitcast.7.pos_ref, ...), custom_call_target="tpu_custom_call" | custom-call | tf_op jit(solution)/shard_map/layer/pallas_call | solution.py:263
  78.1 2.0 %collective-permute-start.9 = (bf16[1280,128]{1,0:T(8,128)(2,1)}, bf16[1280,128]{1,0:T(8,128)(2,1)S(1)}, u32[]{:S(2)}, u32[]{:S(2)}) collective-permute-start(bf16[1280,128]{1,0:T(8,128)(2,1)} %get-tuple-element.42), channel_id=1, source_target_pairs={{0,32},{32,0},{64,96},{96,64},{128,160},{160,128},{192,224},{224,1... | collective-permute-start | bytes 983048 | tf_op jit(solution)/shard_map/ppermute | solution.py:370
  80.1 1.5 collective-permute-done.9
  84.6 1.7 %collective-permute-start.7 = (bf16[1024,128]{1,0:T(8,128)(2,1)S(1)}, bf16[1024,128]{1,0:T(8,128)(2,1)S(1)}, u32[]{:S(2)}, u32[]{:S(2)}) collective-permute-start(bf16[1024,128]{1,0:T(8,128)(2,1)S(1)} %copy-done.23), channel_id=1, source_target_pairs={{0,3},{1,0},{2,1},{3,2},{4,7},{5,4},{6,5},{7,6},{8,11},{9,8},{10,9... | collective-permute-start | bytes 786440 | tf_op jit(solution)/shard_map/ppermute | solution.py:370
  88.4 1.5 %collective-permute-start.11 = (bf16[320,128]{1,0:T(8,128)(2,1)S(1)}, bf16[320,128]{1,0:T(8,128)(2,1)S(1)}, u32[]{:S(2)}, u32[]{:S(2)}) collective-permute-start(bf16[320,128]{1,0:T(8,128)(2,1)S(1)} %fusion.2), channel_id=1, source_target_pairs={{0,192},{32,224},{64,128},{96,160},{128,64},{160,96},{192,0},{224,... | collective-permute-start | bytes 245768 | tf_op jit(solution)/shard_map/ppermute | solution.py:370
  90.5 1.5 collective-permute-done.6.d1
  92.0 6.0 %collective-permute-done.8.d3 = bf16[1024,128]{1,0:T(8,128)(2,1)S(1)} collective-permute-done((bf16[1024,128]{1,0:T(8,128)(2,1)S(1)}, bf16[1024,128]{1,0:T(8,128)(2,1)S(1)}, u32[]{:S(2)}, u32[]{:S(2)}) %collective-permute-start.8) | collective-permute-done | bytes 262176 | tf_op jit(solution)/shard_map/ppermute | solution.py:370
  98.1 1.5 collective-permute-start.12
  99.5 1.9 %collective-permute-done.12 = bf16[320,128]{1,0:T(8,128)(2,1)S(1)} collective-permute-done((bf16[320,128]{1,0:T(8,128)(2,1)S(1)}, bf16[320,128]{1,0:T(8,128)(2,1)S(1)}, u32[]{:S(2)}, u32[]{:S(2)}) %collective-permute-start.12) | collective-permute-done | bytes 81952 | tf_op jit(solution)/shard_map/ppermute | solution.py:370
  102.2 3.5 %collective-permute-done.13 = bf16[320,128]{1,0:T(8,128)(2,1)S(1)} collective-permute-done((bf16[320,128]{1,0:T(8,128)(2,1)S(1)}, bf16[320,128]{1,0:T(8,128)(2,1)S(1)}, u32[]{:S(2)}, u32[]{:S(2)}) %collective-permute-start.13) | collective-permute-done | bytes 81952 | tf_op jit(solution)/shard_map/ppermute | solution.py:370
  105.8 2.4 %collective-permute-start.14 = (bf16[320,128]{1,0:T(8,128)(2,1)S(1)}, bf16[320,128]{1,0:T(8,128)(2,1)S(1)}, u32[]{:S(2)}, u32[]{:S(2)}) collective-permute-start(bf16[320,128]{1,0:T(8,128)(2,1)S(1)} %add_convert_fusion.2), channel_id=1, source_target_pairs={{0,28},{4,24},{8,20},{12,16},{16,12},{20,8},{24,4},{28,0},{1,29},{... | collective-permute-start | bytes 245768 | tf_op jit(solution)/shard_map/ppermute | solution.py:370
  108.2 2.8 %to_slots.1 = bf16[1536,128]{1,0:T(8,128)(2,1)} custom-call(s32[8,128]{1,0:T(8,128)} %get-tuple-element.35.slot_ref, bf16[1024,128]{1,0:T(8,128)(2,1)} %grad_ref.1, bf16[1024,128]{1,0:T(8,128)(2,1)} %get-tuple-element.43.d0, bf16[1024,128]{1,0:T(8,128)(2,1)} %copy-done.13, bf16[1024,128]{1,0:T(8,128)(2,1)} %copy-done.14, bf16[1024,128]{1,0:T(8,128)(2,1)} %copy-done.15), custom_call_target="tpu_custom_call" | custom-call | tf_op jit(solution)/shard_map/to_slots/pallas_call | solution.py:318
  111.1 11.9 %all-to-all-start.2 = ((bf16[64,24,128]{2,1,0:T(8,128)(2,1)}), bf16[64,24,128]{2,1,0:T(8,128)(2,1)S(1)}, u32[]{:S(2)}, u32[]{:S(2)}) async-start(bf16[64,24,128]{2,1,0:T(8,128)(2,1)} %bitcast.32), calls=%async_computation.2 | async-start | bytes 786432 | tf_op jit(solution)/shard_map/all_to_all | solution.py:437
  123.0 2.0 %all_gather.3.p0 = bf16[640,128]{1,0:T(8,128)(2,1)S(1)} all-gather(bf16[320,128]{1,0:T(8,128)(2,1)S(1)} %add_convert_fusion.1), channel_id=1, replica_groups={{0,32},{64,96},{128,160},{192,224},{1,33},{65,97},{129,161},{193,225},{..., dimensions={0}, use_global_device_ids=true | all-gather | bytes 245760 | tf_op jit(solution)/shard_map/all_gather | solution.py:411
  125.0 1.3 collective-permute-start.20
  127.2 1.8 %collective-permute-start.16 = (bf16[1024,128]{1,0:T(8,128)(2,1)S(1)}, bf16[1024,128]{1,0:T(8,128)(2,1)S(1)}, u32[]{:S(2)}, u32[]{:S(2)}) collective-permute-start(bf16[1024,128]{1,0:T(8,128)(2,1)S(1)} %copy-done.20), channel_id=1, source_target_pairs={{0,3},{1,0},{2,1},{3,2},{4,7},{5,4},{6,5},{7,6},{8,11},{9,8},{10,9... | collective-permute-start | bytes 786440 | tf_op jit(solution)/shard_map/ppermute | solution.py:370
  130.0 2.6 %collective-permute-start.19 = (bf16[640,128]{1,0:T(8,128)(2,1)S(1)}, bf16[640,128]{1,0:T(8,128)(2,1)S(1)}, u32[]{:S(2)}, u32[]{:S(2)}) collective-permute-start(bf16[640,128]{1,0:T(8,128)(2,1)S(1)} %all_gather.3.p0), channel_id=1, source_target_pairs={{0,128},{32,160},{64,192},{96,224},{128,0},{160,32},{192,64},{224,... | collective-permute-start | bytes 491528 | tf_op jit(solution)/shard_map/ppermute | solution.py:370
  132.6 1.3 collective-permute-done.20.p3
  133.9 2.5 %collective-permute-start.18 = (bf16[640,128]{1,0:T(8,128)(2,1)S(1)}, bf16[640,128]{1,0:T(8,128)(2,1)S(1)}, u32[]{:S(2)}, u32[]{:S(2)}) collective-permute-start(bf16[640,128]{1,0:T(8,128)(2,1)S(1)} %all_gather.3.p0), channel_id=1, source_target_pairs={{0,192},{32,224},{64,0},{96,32},{128,64},{160,96},{192,128},{224,1... | collective-permute-start | bytes 491528 | tf_op jit(solution)/shard_map/ppermute | solution.py:370
  136.5 3.6 %collective-permute-done.19.p2 = bf16[640,128]{1,0:T(8,128)(2,1)S(1)} collective-permute-done((bf16[640,128]{1,0:T(8,128)(2,1)S(1)}, bf16[640,128]{1,0:T(8,128)(2,1)S(1)}, u32[]{:S(2)}, u32[]{:S(2)}) %collective-permute-start.19) | collective-permute-done | bytes 163872 | tf_op jit(solution)/shard_map/ppermute | solution.py:370
  141.4 2.4 %unpack.1 = (f32[2048,128]{1,0:T(8,128)}, f32[128,512]{1,0:T(8,128)}) custom-call(s32[1]{0:T(128)} %bitcast.17.y_ref, bf16[640,128]{1,0:T(8,128)(2,1)} %copy-done.4, bf16[640,128]{1,0:T(8,128)(2,1)} %copy-done.18, bf16[640,128]{1,0:T(8,128)(2,1)} %copy-done.17, bf16[640,128]{1,0:T(8,128)(2,1)} %copy-done.16), custom_call_target="tpu_custom_call" | custom-call | tf_op jit(solution)/shard_map/unpack/pallas_call | solution.py:358
  144.5 3.2 %add_rows.1 = f32[2048,128]{1,0:T(8,128)} custom-call(s32[12,128]{1,0:T(8,128)} %reshape.59.req_ref, bf16[1536,128]{1,0:T(8,128)(2,1)} %bitcast.30), custom_call_target="tpu_custom_call" | custom-call | tf_op jit(solution)/shard_map/add_rows/pallas_call | solution.py:336
  (83 shorter events, 17.7 us)
Async XLA Ops:
  27.8 19.9 %all-to-all-start.1 = ((bf16[64,24,128]{2,1,0:T(8,128)(2,1)}), bf16[64,24,128]{2,1,0:T(8,128)(2,1)S(1)}, u32[]{:S(2)}, u32[]{:S(2)}) async-start(bf16[64,24,128]{2,1,0:T(8,128)(2,1)} %bitcast.31), calls=%async_computation.1 | async-start | bytes 786432 | tf_op jit(solution)/shard_map/all_to_all | solution.py:423
  32.8 21.6 %collective-permute-start.5 = (bf16[1024,128]{1,0:T(8,128)(2,1)S(1)}, bf16[1024,128]{1,0:T(8,128)(2,1)S(1)}, u32[]{:S(2)}, u32[]{:S(2)}) collective-permute-start(bf16[1024,128]{1,0:T(8,128)(2,1)S(1)} %copy-done.3), channel_id=1, source_target_pairs={{0,1},{1,2},{2,3},{3,0},{4,5},{5,6},{6,7},{7,4},{8,9},{9,10},{10,1... | collective-permute-start | bytes 786440 | tf_op jit(solution)/shard_map/ppermute | solution.py:370
  34.0 21.5 %collective-permute-start.4 = (bf16[1024,128]{1,0:T(8,128)(2,1)S(1)}, bf16[1024,128]{1,0:T(8,128)(2,1)S(1)}, u32[]{:S(2)}, u32[]{:S(2)}) collective-permute-start(bf16[1024,128]{1,0:T(8,128)(2,1)S(1)} %copy-done.3), channel_id=1, source_target_pairs={{0,2},{1,3},{2,0},{3,1},{4,6},{5,7},{6,4},{7,5},{8,10},{9,11},{10,... | collective-permute-start | bytes 786440 | tf_op jit(solution)/shard_map/ppermute | solution.py:370
  36.5 19.1 %collective-permute-start.3 = (bf16[1024,128]{1,0:T(8,128)(2,1)S(1)}, bf16[1024,128]{1,0:T(8,128)(2,1)S(1)}, u32[]{:S(2)}, u32[]{:S(2)}) collective-permute-start(bf16[1024,128]{1,0:T(8,128)(2,1)S(1)} %copy-done.3), channel_id=1, source_target_pairs={{0,3},{1,0},{2,1},{3,2},{4,7},{5,4},{6,5},{7,6},{8,11},{9,8},{10,9... | collective-permute-start | bytes 786440 | tf_op jit(solution)/shard_map/ppermute | solution.py:370
  50.7 8.2 %collective-permute-start.2 = (bf16[1024,128]{1,0:T(8,128)(2,1)}, bf16[1024,128]{1,0:T(8,128)(2,1)S(1)}, u32[]{:S(2)}, u32[]{:S(2)}) collective-permute-start(bf16[1024,128]{1,0:T(8,128)(2,1)} %place.1.x0), channel_id=1, source_target_pairs={{0,1},{1,2},{2,3},{3,0},{4,5},{5,6},{6,7},{7,4},{8,9},{9,10},{10,1... | collective-permute-start | bytes 786440 | tf_op jit(solution)/shard_map/ppermute | solution.py:370
  51.9 13.6 %collective-permute-start.1 = (bf16[1024,128]{1,0:T(8,128)(2,1)}, bf16[1024,128]{1,0:T(8,128)(2,1)S(1)}, u32[]{:S(2)}, u32[]{:S(2)}) collective-permute-start(bf16[1024,128]{1,0:T(8,128)(2,1)} %place.1.x0), channel_id=1, source_target_pairs={{0,2},{1,3},{2,0},{3,1},{4,6},{5,7},{6,4},{7,5},{8,10},{9,11},{10,... | collective-permute-start | bytes 786440 | tf_op jit(solution)/shard_map/ppermute | solution.py:370
  54.4 11.3 %copy-start.6 = (bf16[1024,128]{1,0:T(8,128)(2,1)}, bf16[1024,128]{1,0:T(8,128)(2,1)S(1)}, u32[]{:S(2)}) copy-start(bf16[1024,128]{1,0:T(8,128)(2,1)S(1)} %collective-permute-done.5.g3) | copy-start | bytes 786436
  54.4 11.3 %collective-permute-start = (bf16[1024,128]{1,0:T(8,128)(2,1)}, bf16[1024,128]{1,0:T(8,128)(2,1)S(1)}, u32[]{:S(2)}, u32[]{:S(2)}) collective-permute-start(bf16[1024,128]{1,0:T(8,128)(2,1)} %place.1.x0), channel_id=1, source_target_pairs={{0,3},{1,0},{2,1},{3,2},{4,7},{5,4},{6,5},{7,6},{8,11},{9,8},{10,9... | collective-permute-start | bytes 786440 | tf_op jit(solution)/shard_map/ppermute | solution.py:370
  55.6 10.1 %copy-start.7 = (bf16[1024,128]{1,0:T(8,128)(2,1)}, bf16[1024,128]{1,0:T(8,128)(2,1)S(1)}, u32[]{:S(2)}) copy-start(bf16[1024,128]{1,0:T(8,128)(2,1)S(1)} %collective-permute-done.4.g2) | copy-start | bytes 786436
  55.6 10.1 %copy-start.8 = (bf16[1024,128]{1,0:T(8,128)(2,1)}, bf16[1024,128]{1,0:T(8,128)(2,1)S(1)}, u32[]{:S(2)}) copy-start(bf16[1024,128]{1,0:T(8,128)(2,1)S(1)} %collective-permute-done.3.g1) | copy-start | bytes 786436
  78.1 3.5 %collective-permute-start.9 = (bf16[1280,128]{1,0:T(8,128)(2,1)}, bf16[1280,128]{1,0:T(8,128)(2,1)S(1)}, u32[]{:S(2)}, u32[]{:S(2)}) collective-permute-start(bf16[1280,128]{1,0:T(8,128)(2,1)} %get-tuple-element.42), channel_id=1, source_target_pairs={{0,32},{32,0},{64,96},{96,64},{128,160},{160,128},{192,224},{224,1... | collective-permute-start | bytes 983048 | tf_op jit(solution)/shard_map/ppermute | solution.py:370
  82.8 5.5 %collective-permute-start.10 = (bf16[640,128]{1,0:T(8,128)(2,1)S(1)}, bf16[640,128]{1,0:T(8,128)(2,1)S(1)}, u32[]{:S(2)}, u32[]{:S(2)}) collective-permute-start(bf16[640,128]{1,0:T(8,128)(2,1)S(1)} %fusion), channel_id=1, source_target_pairs={{0,64},{32,96},{64,0},{96,32},{128,192},{160,224},{192,128},{224,1... | collective-permute-start | bytes 491528 | tf_op jit(solution)/shard_map/ppermute | solution.py:370
  83.6 8.4 %collective-permute-start.6 = (bf16[1024,128]{1,0:T(8,128)(2,1)S(1)}, bf16[1024,128]{1,0:T(8,128)(2,1)S(1)}, u32[]{:S(2)}, u32[]{:S(2)}) collective-permute-start(bf16[1024,128]{1,0:T(8,128)(2,1)S(1)} %copy-done.24), channel_id=1, source_target_pairs={{0,1},{1,2},{2,3},{3,0},{4,5},{5,6},{6,7},{7,4},{8,9},{9,10},{10,1... | collective-permute-start | bytes 786440 | tf_op jit(solution)/shard_map/ppermute | solution.py:370
  84.6 7.4 %collective-permute-start.7 = (bf16[1024,128]{1,0:T(8,128)(2,1)S(1)}, bf16[1024,128]{1,0:T(8,128)(2,1)S(1)}, u32[]{:S(2)}, u32[]{:S(2)}) collective-permute-start(bf16[1024,128]{1,0:T(8,128)(2,1)S(1)} %copy-done.23), channel_id=1, source_target_pairs={{0,3},{1,0},{2,1},{3,2},{4,7},{5,4},{6,5},{7,6},{8,11},{9,8},{10,9... | collective-permute-start | bytes 786440 | tf_op jit(solution)/shard_map/ppermute | solution.py:370
  86.3 11.7 %collective-permute-start.8 = (bf16[1024,128]{1,0:T(8,128)(2,1)S(1)}, bf16[1024,128]{1,0:T(8,128)(2,1)S(1)}, u32[]{:S(2)}, u32[]{:S(2)}) collective-permute-start(bf16[1024,128]{1,0:T(8,128)(2,1)S(1)} %copy-done.22), channel_id=1, source_target_pairs={{0,2},{1,3},{2,0},{3,1},{4,6},{5,7},{6,4},{7,5},{8,10},{9,11},{10,... | collective-permute-start | bytes 786440 | tf_op jit(solution)/shard_map/ppermute | solution.py:370
  88.4 9.7 %collective-permute-start.11 = (bf16[320,128]{1,0:T(8,128)(2,1)S(1)}, bf16[320,128]{1,0:T(8,128)(2,1)S(1)}, u32[]{:S(2)}, u32[]{:S(2)}) collective-permute-start(bf16[320,128]{1,0:T(8,128)(2,1)S(1)} %fusion.2), channel_id=1, source_target_pairs={{0,192},{32,224},{64,128},{96,160},{128,64},{160,96},{192,0},{224,... | collective-permute-start | bytes 245768 | tf_op jit(solution)/shard_map/ppermute | solution.py:370
  92.0 9.5 %copy-start.14 = (bf16[1024,128]{1,0:T(8,128)(2,1)}, bf16[1024,128]{1,0:T(8,128)(2,1)S(1)}, u32[]{:S(2)}) copy-start(bf16[1024,128]{1,0:T(8,128)(2,1)S(1)} %collective-permute-done.7.d2) | copy-start | bytes 786436
  98.0 10.2 %copy-start.15 = (bf16[1024,128]{1,0:T(8,128)(2,1)}, bf16[1024,128]{1,0:T(8,128)(2,1)S(1)}, u32[]{:S(2)}) copy-start(bf16[1024,128]{1,0:T(8,128)(2,1)S(1)} %collective-permute-done.8.d3) | copy-start | bytes 786436
  98.1 3.4 %collective-permute-start.12 = (bf16[320,128]{1,0:T(8,128)(2,1)S(1)}, bf16[320,128]{1,0:T(8,128)(2,1)S(1)}, u32[]{:S(2)}, u32[]{:S(2)}) collective-permute-start(bf16[320,128]{1,0:T(8,128)(2,1)S(1)} %fusion.1), channel_id=1, source_target_pairs={{0,4},{4,0},{8,12},{12,8},{16,20},{20,16},{24,28},{28,24},{1,5},{5... | collective-permute-start | bytes 245768 | tf_op jit(solution)/shard_map/ppermute | solution.py:370
  101.5 4.3 %collective-permute-start.13 = (bf16[320,128]{1,0:T(8,128)(2,1)S(1)}, bf16[320,128]{1,0:T(8,128)(2,1)S(1)}, u32[]{:S(2)}, u32[]{:S(2)}) collective-permute-start(bf16[320,128]{1,0:T(8,128)(2,1)S(1)} %add_convert_fusion.3), channel_id=1, source_target_pairs={{0,8},{4,12},{8,0},{12,4},{16,24},{20,28},{24,16},{28,20},{1,9},{5... | collective-permute-start | bytes 245768 | tf_op jit(solution)/shard_map/ppermute | solution.py:370
  105.8 5.2 %collective-permute-start.14 = (bf16[320,128]{1,0:T(8,128)(2,1)S(1)}, bf16[320,128]{1,0:T(8,128)(2,1)S(1)}, u32[]{:S(2)}, u32[]{:S(2)}) collective-permute-start(bf16[320,128]{1,0:T(8,128)(2,1)S(1)} %add_convert_fusion.2), channel_id=1, source_target_pairs={{0,28},{4,24},{8,20},{12,16},{16,12},{20,8},{24,4},{28,0},{1,29},{... | collective-permute-start | bytes 245768 | tf_op jit(solution)/shard_map/ppermute | solution.py:370
  111.0 15.3 %copy-start.21 = (bf16[1024,128]{1,0:T(8,128)(2,1)S(1)}, bf16[1024,128]{1,0:T(8,128)(2,1)}, u32[]{:S(2)}) copy-start(bf16[1024,128]{1,0:T(8,128)(2,1)} %get-tuple-element.54) | copy-start | bytes 786436
  111.0 16.2 %copy-start.20 = (bf16[1024,128]{1,0:T(8,128)(2,1)S(1)}, bf16[1024,128]{1,0:T(8,128)(2,1)}, u32[]{:S(2)}) copy-start(bf16[1024,128]{1,0:T(8,128)(2,1)} %get-tuple-element.55) | copy-start | bytes 786436
  111.1 18.0 %copy-start.19 = (bf16[1024,128]{1,0:T(8,128)(2,1)S(1)}, bf16[1024,128]{1,0:T(8,128)(2,1)}, u32[]{:S(2)}) copy-start(bf16[1024,128]{1,0:T(8,128)(2,1)} %get-tuple-element.56) | copy-start | bytes 786436
  111.1 32.7 %all-to-all-start.2 = ((bf16[64,24,128]{2,1,0:T(8,128)(2,1)}), bf16[64,24,128]{2,1,0:T(8,128)(2,1)S(1)}, u32[]{:S(2)}, u32[]{:S(2)}) async-start(bf16[64,24,128]{2,1,0:T(8,128)(2,1)} %bitcast.32), calls=%async_computation.2 | async-start | bytes 786432 | tf_op jit(solution)/shard_map/all_to_all | solution.py:437
  125.0 15.7 %copy-start.4 = (bf16[640,128]{1,0:T(8,128)(2,1)}, bf16[640,128]{1,0:T(8,128)(2,1)S(1)}, u32[]{:S(2)}) copy-start(bf16[640,128]{1,0:T(8,128)(2,1)S(1)} %all_gather.3.p0) | copy-start | bytes 491524
  125.0 8.9 %collective-permute-start.20 = (bf16[640,128]{1,0:T(8,128)(2,1)S(1)}, bf16[640,128]{1,0:T(8,128)(2,1)S(1)}, u32[]{:S(2)}, u32[]{:S(2)}) collective-permute-start(bf16[640,128]{1,0:T(8,128)(2,1)S(1)} %all_gather.3.p0), channel_id=1, source_target_pairs={{0,64},{32,96},{64,128},{96,160},{128,192},{160,224},{192,0},{224,... | collective-permute-start | bytes 491528 | tf_op jit(solution)/shard_map/ppermute | solution.py:370
  126.4 17.4 %collective-permute-start.15 = (bf16[1024,128]{1,0:T(8,128)(2,1)S(1)}, bf16[1024,128]{1,0:T(8,128)(2,1)S(1)}, u32[]{:S(2)}, u32[]{:S(2)}) collective-permute-start(bf16[1024,128]{1,0:T(8,128)(2,1)S(1)} %copy-done.21), channel_id=1, source_target_pairs={{0,1},{1,2},{2,3},{3,0},{4,5},{5,6},{6,7},{7,4},{8,9},{9,10},{10,1... | collective-permute-start | bytes 786440 | tf_op jit(solution)/shard_map/ppermute | solution.py:370
  127.2 16.5 %collective-permute-start.16 = (bf16[1024,128]{1,0:T(8,128)(2,1)S(1)}, bf16[1024,128]{1,0:T(8,128)(2,1)S(1)}, u32[]{:S(2)}, u32[]{:S(2)}) collective-permute-start(bf16[1024,128]{1,0:T(8,128)(2,1)S(1)} %copy-done.20), channel_id=1, source_target_pairs={{0,3},{1,0},{2,1},{3,2},{4,7},{5,4},{6,5},{7,6},{8,11},{9,8},{10,9... | collective-permute-start | bytes 786440 | tf_op jit(solution)/shard_map/ppermute | solution.py:370
  129.0 14.7 %collective-permute-start.17 = (bf16[1024,128]{1,0:T(8,128)(2,1)S(1)}, bf16[1024,128]{1,0:T(8,128)(2,1)S(1)}, u32[]{:S(2)}, u32[]{:S(2)}) collective-permute-start(bf16[1024,128]{1,0:T(8,128)(2,1)S(1)} %copy-done.19), channel_id=1, source_target_pairs={{0,2},{1,3},{2,0},{3,1},{4,6},{5,7},{6,4},{7,5},{8,10},{9,11},{10,... | collective-permute-start | bytes 786440 | tf_op jit(solution)/shard_map/ppermute | solution.py:370
  130.0 10.1 %collective-permute-start.19 = (bf16[640,128]{1,0:T(8,128)(2,1)S(1)}, bf16[640,128]{1,0:T(8,128)(2,1)S(1)}, u32[]{:S(2)}, u32[]{:S(2)}) collective-permute-start(bf16[640,128]{1,0:T(8,128)(2,1)S(1)} %all_gather.3.p0), channel_id=1, source_target_pairs={{0,128},{32,160},{64,192},{96,224},{128,0},{160,32},{192,64},{224,... | collective-permute-start | bytes 491528 | tf_op jit(solution)/shard_map/ppermute | solution.py:370
  133.9 6.7 %collective-permute-start.18 = (bf16[640,128]{1,0:T(8,128)(2,1)S(1)}, bf16[640,128]{1,0:T(8,128)(2,1)S(1)}, u32[]{:S(2)}, u32[]{:S(2)}) collective-permute-start(bf16[640,128]{1,0:T(8,128)(2,1)S(1)} %all_gather.3.p0), channel_id=1, source_target_pairs={{0,192},{32,224},{64,0},{96,32},{128,64},{160,96},{192,128},{224,1... | collective-permute-start | bytes 491528 | tf_op jit(solution)/shard_map/ppermute | solution.py:370
  (16 other events, 48.8 us)

commit v7 on v5

--- a/solution.py
+++ b/solution.py
@@ -142,12 +142,25 @@
 
 def layer_kernel(
     pos_ref, core_ref, seg_ref, x0, x1, x2, x3, g0, g1, g2, g3, win_ref, wout_ref,
-    mine_ref, other_ref, dx0, dx1, dx2, dx3, z0, z1, z2, z3,
+    mine_ref, other_ref, own_ref, right_ref, left_ref, near_right, near_left,
     w, wo, pre, act, segc, aw, dsil, dkv, du, u_ref, y_ref, dp_ref, dw_ref,
 ):
     xs, gs = (x0, x1, x2, x3), (g0, g1, g2, g3)
-    dxs, zs = (dx0, dx1, dx2, dx3), (z0, z1, z2, z3)
     me, core = pos_ref[0], core_ref[0]
+
+    def keep(k, kind, row, value):
+        late = row >= TOK // 2
+        at = kind * (TOK // 2) + row % (TOK // 2)
+        if k == 0:
+            ref, at = own_ref, at + (TOK if late else 0)
+        elif k == 1:
+            ref, at = (right_ref, at + TOK) if late else (near_right, at)
+        elif k == 2:
+            ref = left_ref if late else right_ref
+        else:
+            ref, at = (near_left, at) if late else (left_ref, at + TOK)
+        ref[at : at + value.shape[0], :] = value.astype(BF)
+
     for k in range(NT):
         at = pl.multiple_of(lax.rem(me + k, NT) * 128, 128)
         for c in range(4):
@@ -245,7 +258,7 @@
                 d[0] * n[0] + d[1] * n[1] + d[2] * n[2] + d[3] * n[3], axis=1, keepdims=True
             ) * (1.0 / D)
             for k in range(NT):
-                dxs[k][lo + r : lo + r + step, :] = ((d[k] - m1 - n[k] * m2) * scale).astype(BF)
+                keep(k, 0, lo + r, (d[k] - m1 - n[k] * m2) * scale)
 
     for k in range(NT):
         at = pl.multiple_of(lax.rem(me + k, NT) * 128, 128)
@@ -253,19 +266,22 @@
         for c in range(4):
             dw_ref[pl.ds(pl.multiple_of(c * 512 + at, 128), 128), :] = dw[:, c * 128 : (c + 1) * 128]
         dw_ref[pl.ds(pl.multiple_of(2048 + at, 128), 128), :] = dot(y_ref[...], gs[k][...], 0, 0)
-        zs[k][...] = dot(y_ref[...], wo[:, k * 128 : (k + 1) * 128], 1, 0).astype(BF)
+        for row in (0, TOK // 2):
+            keep(k, 1, row, dot(y_ref[row : row + TOK // 2, :], wo[:, k * 128 : (k + 1) * 128], 1, 0))
     mine_ref[...] = dw_ref[pl.ds(pl.multiple_of(core * 1280, 1280), 1280), :]
     other_ref[...] = dw_ref[pl.ds(pl.multiple_of(1280 - core * 1280, 1280), 1280), :].astype(BF)
 
 
 def layer(pos, core, seg, xs, gs, w_in, w_out):
     piece = jax.ShapeDtypeStruct((TOK, 128), BF)
+    pair = jax.ShapeDtypeStruct((2 * TOK, 128), BF)
     return pl.pallas_call(
         layer_kernel,
         out_shape=(jax.ShapeDtypeStruct((1280, 128), F32), jax.ShapeDtypeStruct((1280, 128), BF))
-        + (piece,) * 8,
+        + (pair,) * 3
+        + (piece,) * 2,
         in_specs=[SM, SM] + [VM] * 11,
-        out_specs=(VM,) * 10,
+        out_specs=(VM,) * 7,
         scratch_shapes=[
             pltpu.VMEM((D, 512), BF),
             pltpu.VMEM((HD, D), BF),
@@ -304,9 +320,21 @@
     return [dot(hot_where(high, s, low), pair, 1, 0) for s in range(size // 128)]
 
 
-def slots_kernel(slot_ref, grad_ref, d0, d1, d2, d3, out_ref):
-    dx = grad_ref[...].astype(F32) + (
-        d0[...].astype(F32) + d1[...].astype(F32) + d2[...].astype(F32) + d3[...].astype(F32)
+def summed(first, kind, own, from_left, from_right, via_left, via_right):
+    half = TOK // 2
+    at = kind * half
+    early = own[at : at + half, :].astype(F32) + (
+        via_left[at : at + half, :].astype(F32) + from_right[TOK + at : TOK + at + half, :].astype(F32)
+    )
+    late = own[TOK + at : TOK + at + half, :].astype(F32) + (
+        via_right[at : at + half, :].astype(F32) + from_left[TOK + at : TOK + at + half, :].astype(F32)
+    )
+    return first.astype(F32) + jnp.concatenate([early, late], axis=0)
+
+
+def slots_kernel(slot_ref, grad_ref, own, from_left, from_right, via_left, via_right, out_ref):
+    dx = summed(
+        grad_ref[...], 0, own[...], from_left[...], from_right[...], via_left[...], via_right[...]
     )
     half = SLOTS // 2
     for s, both in enumerate(spread(slot_ref, TOK // 128, half, dx)):
@@ -318,7 +346,7 @@
     return pl.pallas_call(
         slots_kernel,
         out_shape=jax.ShapeDtypeStruct((SLOTS, 128), BF),
-        in_specs=[VM] * 6,
+        in_specs=[VM] * 7,
         out_specs=VM,
         compiler_params=PARAMS,
         name="to_slots",
@@ -379,8 +407,12 @@
     return [own, one, two, three]
 
 
-def scatter_pieces(parts):
-    return [parts[0]] + [shift(parts[k], "tensor", lambda i, k=k: (i + k) % NT, NT) for k in (1, 3, 2)]
+def to_right(x):
+    return shift(x, "tensor", lambda i: (i + 1) % NT, NT)
+
+
+def to_left(x):
+    return shift(x, "tensor", lambda i: (i - 1) % NT, NT)
 
 
 def pick(x, i):
@@ -423,25 +455,26 @@
     back = lax.all_to_all(rows.reshape(NOWN, CAP, 128), BOTH, split_axis=0, concat_axis=0, tiled=True)
     x = place(slot, back.reshape(SLOTS, 128))
     xs = order(gather_pieces(x))
-    mine, other, d0, d1, d2, d3, z0, z1, z2, z3 = layer(
+    mine, other, own, right, left, near_right, near_left = layer(
         pos, core, segment_ids, xs, gs, proj_in, proj_out
     )
-    dparts = scatter_pieces([d0, d1, d2, d3])
-    own, got = reduce_over_chips(mine, other)
+    from_left, from_right = to_right(right), to_left(left)
+    kept, got = reduce_over_chips(mine, other)
     flat = received[:, :CAP].reshape(SLOTS // 128, 128)
-    total = add_step((own + got.astype(F32)).astype(BF), 1)
-    dparts, total, flat = lax.optimization_barrier((dparts, total, flat))
-    grads = to_slots(slot, grad_out, dparts)
-    total = add_step(add_step(total, 2), 7)
-    grads, total, zs = lax.optimization_barrier((grads, total, [z0, z1, z2, z3]))
+    from_left, from_right, got, flat = lax.optimization_barrier((from_left, from_right, got, flat))
+    via_left = to_right((near_right.astype(F32) + from_left[:TOK].astype(F32)).astype(BF))
+    via_right = to_left((near_left.astype(F32) + from_right[:TOK].astype(F32)).astype(BF))
+    total = add_step((kept + got.astype(F32)).astype(BF), 1)
+    total = add_step(total, 2)
+    via_left, via_right, total = lax.optimization_barrier((via_left, via_right, total))
+    parts = [own, from_left, from_right, via_left, via_right]
+    grads = to_slots(slot, grad_out, parts)
+    total = add_step(total, 7)
+    grads, total = lax.optimization_barrier((grads, total))
     arrived = lax.all_to_all(grads.reshape(NOWN, CAP, 128), BOTH, split_axis=0, concat_axis=0, tiled=True)
     grad_in, grad_outw = gather_weights(total)
-    zparts = scatter_pieces(zs)
+    layer_out = summed(x, 1, *parts).astype(BF)
     table_grad = add_rows(flat, arrived.reshape(SLOTS, 128))
-    layer_out = (
-        x.astype(F32)
-        + (zparts[0].astype(F32) + zparts[1].astype(F32) + zparts[2].astype(F32) + zparts[3].astype(F32))
-    ).astype(BF)
     return layer_out, table_grad, grad_in.reshape(4, D, 128), grad_outw
 
 

time: 156 us -> 152 us (0.974); the launches traced: 154 us -> 152 us
  starting transfers between devices: 48.4 us -> 45.8 us
    ppermute x21 -> x19, starting transfers between devices: 31.7 us -> 27.6 us  [shift(): return lax.ppermute(x, axis, [(i, fn(i)) for i in range(n)])]
    ppermute x21 -> x19, waiting for transfers between devices: 37.6 us -> 36.3 us  [shift(): return lax.ppermute(x, axis, [(i, fn(i)) for i in range(n)])]
  transfers between devices with their start and end apart: 23 -> 21, of which waited for: 15 -> 11; matrix products, arithmetic and copies ran while one was open for 1% -> 2% of each run, Pallas kernels for 5% -> 5%
where the time goes in v7:
time: 152 us
  waiting for transfers between devices  46.2 us (30%)
  starting transfers between devices  45.8 us (30%)
  Pallas kernels  27.6 us (18%)
  blocking collectives  24.3 us (16%)
  local copies, waits for them, and re-layouts  3.68 us (2%)
  other arithmetic  3.42 us (2%)
    ppermute x19, waiting for transfers between devices, shift(): return lax.ppermute(x, axis, [(i, fn(i)) for i in range(n)])  36.3 us
    ppermute x19, starting transfers between devices, shift(): return lax.ppermute(x, axis, [(i, fn(i)) for i in range(n)])  27.6 us
    all_to_all x1, blocking collectives, body(): lax.all_to_all(requests, BOTH, split_axis=0, concat_axis=0, tiled=True)  22.3 us
    all_to_all x1, starting transfers between devices, body(): lax.all_to_all(grads.reshape(NOWN, CAP, 128), BOTH, split_axis=0, concat_...  12.9 us
    pallas_call x1, Pallas kernels, layer(): pl.pallas_call(layer_kernel, out_shape=(jax.ShapeDtypeStruct((1280, 128),...  12 us
    all_to_all x1, waiting for transfers between devices, body(): lax.all_to_all(rows.reshape(NOWN, CAP, 128), BOTH, split_axis=0, concat_a...  9.98 us
    all_to_all x1, starting transfers between devices, body(): lax.all_to_all(rows.reshape(NOWN, CAP, 128), BOTH, split_axis=0, concat_a...  5.29 us
    pallas_call x1, Pallas kernels, add_rows(): pl.pallas_call(add_rows_kernel, out_shape=jax.ShapeDtypeStruct((ROWS, 128...  3.1 us
  transfers between devices with their start and end apart: 21, of which 11 were waited for; matrix products, arithmetic and copies ran while one was open for 2% of the time, Pallas kernels for 5%

profile of v7, /device:TPU:1, one launch (start us, length us, event | category | flops | bytes accessed | tf_op | source)
XLA Modules:
  0.0 151.9 jit_solution(16881592602201652755)
XLA Ops:
  0.6 1.8 %route.1 = (s32[64,128]{1,0:T(8,128)}, s32[8,128]{1,0:T(8,128)}) custom-call(s32[8,128]{1,0:T(8,128)} %bitcast.38, s32[8,128]{1,0:T(8,128)} %bitcast.39), custom_call_target="tpu_custom_call" | custom-call | tf_op jit(solution)/shard_map/route/pallas_call | solution.py:62
  2.5 22.3 %all_to_all.21 = s32[64,1,128]{2,1,0:T(1,128)} all-to-all(s32[64,1,128]{2,1,0:T(1,128)} %bitcast.37), channel_id=1, replica_groups=mesh['table'=8,'seq'=8,'tensor'=4] {'table','seq'}, dimensions={0} | all-to-all | bytes 65536 | tf_op jit(solution)/shard_map/all_to_all | solution.py:453
  24.7 2.9 %fetch.1 = bf16[1536,128]{1,0:T(8,128)(2,1)} custom-call(s32[64,128]{1,0:T(8,128)} %bitcast.35, bf16[2048,128]{1,0:T(8,128)(2,1)} %table_ref.1), custom_call_target="tpu_custom_call" | custom-call | tf_op jit(solution)/shard_map/fetch/pallas_call | solution.py:98
  27.6 5.3 %all-to-all-start.1 = ((bf16[64,24,128]{2,1,0:T(8,128)(2,1)}), bf16[64,24,128]{2,1,0:T(8,128)(2,1)S(1)}, u32[]{:S(2)}, u32[]{:S(2)}) async-start(bf16[64,24,128]{2,1,0:T(8,128)(2,1)} %bitcast.31), calls=%async_computation.1 | async-start | bytes 786432 | tf_op jit(solution)/shard_map/all_to_all | solution.py:455
  32.9 1.3 collective-permute-start.5
  34.2 2.5 %collective-permute-start.4 = (bf16[1024,128]{1,0:T(8,128)(2,1)S(1)}, bf16[1024,128]{1,0:T(8,128)(2,1)S(1)}, u32[]{:S(2)}, u32[]{:S(2)}) collective-permute-start(bf16[1024,128]{1,0:T(8,128)(2,1)S(1)} %copy-done.6), channel_id=1, source_target_pairs={{0,2},{1,3},{2,0},{3,1},{4,6},{5,7},{6,4},{7,5},{8,10},{9,11},{10,... | collective-permute-start | bytes 786440 | tf_op jit(solution)/shard_map/ppermute | solution.py:398
  37.8 10.0 %all-to-all-done.1 = bf16[64,24,128]{2,1,0:T(8,128)(2,1)S(1)} async-done(((bf16[64,24,128]{2,1,0:T(8,128)(2,1)}), bf16[64,24,128]{2,1,0:T(8,128)(2,1)S(1)}, u32[]{:S(2)}, u32[]{:S(2)}) %all-to-all-start.1) | async-done | bytes 393248 | tf_op jit(solution)/shard_map/all_to_all | solution.py:455
  48.5 2.4 %place.1.x0 = bf16[1024,128]{1,0:T(8,128)(2,1)} custom-call(s32[8,128]{1,0:T(8,128)} %get-tuple-element.24.slot_ref, bf16[1536,128]{1,0:T(8,128)(2,1)} %bitcast.29), custom_call_target="tpu_custom_call" | custom-call | tf_op jit(solution)/shard_map/place/pallas_call | solution.py:133
  52.1 2.5 %collective-permute-start.1 = (bf16[1024,128]{1,0:T(8,128)(2,1)}, bf16[1024,128]{1,0:T(8,128)(2,1)S(1)}, u32[]{:S(2)}, u32[]{:S(2)}) collective-permute-start(bf16[1024,128]{1,0:T(8,128)(2,1)} %place.1.x0), channel_id=1, source_target_pairs={{0,2},{1,3},{2,0},{3,1},{4,6},{5,7},{6,4},{7,5},{8,10},{9,11},{10,... | collective-permute-start | bytes 786440 | tf_op jit(solution)/shard_map/ppermute | solution.py:398
  55.7 3.4 %collective-permute-done.2.x3 = bf16[1024,128]{1,0:T(8,128)(2,1)S(1)} collective-permute-done((bf16[1024,128]{1,0:T(8,128)(2,1)}, bf16[1024,128]{1,0:T(8,128)(2,1)S(1)}, u32[]{:S(2)}, u32[]{:S(2)}) %collective-permute-start.2) | collective-permute-done | bytes 262176 | tf_op jit(solution)/shard_map/ppermute | solution.py:398
  59.1 6.6 %collective-permute-done.1.x2 = bf16[1024,128]{1,0:T(8,128)(2,1)S(1)} collective-permute-done((bf16[1024,128]{1,0:T(8,128)(2,1)}, bf16[1024,128]{1,0:T(8,128)(2,1)S(1)}, u32[]{:S(2)}, u32[]{:S(2)}) %collective-permute-start.1) | collective-permute-done | bytes 262176 | tf_op jit(solution)/shard_map/ppermute | solution.py:398
  66.5 12.0 %layer.1 = (f32[1280,128]{1,0:T(8,128)}, bf16[1280,128]{1,0:T(8,128)(2,1)}, bf16[2048,128]{1,0:T(8,128)(2,1)}, bf16[2048,128]{1,0:T(8,128)(2,1)}, bf16[2048,128]...) custom-call(s32[1]{0:T(128)} %bitcast.7.pos_ref, s32[1]{0:T(128)} %bitcast.8.core_ref, ...), custom_call_target="tpu_custom_call" | custom-call | tf_op jit(solution)/shard_map/layer/pallas_call | solution.py:278
  78.5 1.9 %collective-permute-start.8 = (bf16[1280,128]{1,0:T(8,128)(2,1)}, bf16[1280,128]{1,0:T(8,128)(2,1)S(1)}, u32[]{:S(2)}, u32[]{:S(2)}) collective-permute-start(bf16[1280,128]{1,0:T(8,128)(2,1)} %get-tuple-element.31), channel_id=1, source_target_pairs={{0,32},{32,0},{64,96},{96,64},{128,160},{160,128},{192,224},{224,1... | collective-permute-start | bytes 983048 | tf_op jit(solution)/shard_map/ppermute | solution.py:398
  80.4 1.5 collective-permute-done.8
  85.0 1.7 %collective-permute-start.7 = (bf16[2048,128]{1,0:T(8,128)(2,1)S(1)}, bf16[2048,128]{1,0:T(8,128)(2,1)S(1)}, u32[]{:S(2)}, u32[]{:S(2)}) collective-permute-start(bf16[2048,128]{1,0:T(8,128)(2,1)S(1)} %copy-done.23), channel_id=1, source_target_pairs={{0,3},{1,0},{2,1},{3,2},{4,7},{5,4},{6,5},{7,6},{8,11},{9,8},{10,9... | collective-permute-start | bytes 1572872 | tf_op jit(solution)/shard_map/ppermute | solution.py:398
  86.7 2.0 %collective-permute-done.9 = bf16[640,128]{1,0:T(8,128)(2,1)S(1)} collective-permute-done((bf16[640,128]{1,0:T(8,128)(2,1)S(1)}, bf16[640,128]{1,0:T(8,128)(2,1)S(1)}, u32[]{:S(2)}, u32[]{:S(2)}) %collective-permute-start.9) | collective-permute-done | bytes 163872 | tf_op jit(solution)/shard_map/ppermute | solution.py:398
  88.7 1.3 collective-permute-start.10
  90.7 7.3 %collective-permute-done.6.from_left = bf16[2048,128]{1,0:T(8,128)(2,1)S(1)} collective-permute-done((bf16[2048,128]{1,0:T(8,128)(2,1)S(1)}, bf16[2048,128]{1,0:T(8,128)(2,1)S(1)}, u32[]{:S(2)}, u32[]{:S(2)}) %collective-permute-start.6) | collective-permute-done | bytes 524320 | tf_op jit(solution)/shard_map/ppermute | solution.py:398
  98.1 1.7 %collective-permute-start.13 = (bf16[320,128]{1,0:T(8,128)(2,1)S(1)}, bf16[320,128]{1,0:T(8,128)(2,1)S(1)}, u32[]{:S(2)}, u32[]{:S(2)}) collective-permute-start(bf16[320,128]{1,0:T(8,128)(2,1)S(1)} %fusion.2), channel_id=1, source_target_pairs={{0,4},{4,0},{8,12},{12,8},{16,20},{20,16},{24,28},{28,24},{1,5},{5... | collective-permute-start | bytes 245768 | tf_op jit(solution)/shard_map/ppermute | solution.py:398
  99.8 2.4 %collective-permute-start.12 = (bf16[1024,128]{1,0:T(8,128)(2,1)S(1)}, bf16[1024,128]{1,0:T(8,128)(2,1)S(1)}, u32[]{:S(2)}, u32[]{:S(2)}) collective-permute-start(bf16[1024,128]{1,0:T(8,128)(2,1)S(1)} %add_convert_fusion), channel_id=1, source_target_pairs={{0,3},{1,0},{2,1},{3,2},{4,7},{5,4},{6,5},{7,6},{8,11},{9,8},{10,9... | collective-permute-start | bytes 786440 | tf_op jit(solution)/shard_map/ppermute | solution.py:398
  103.0 4.4 %collective-permute-done.14 = bf16[320,128]{1,0:T(8,128)(2,1)S(1)} collective-permute-done((bf16[320,128]{1,0:T(8,128)(2,1)S(1)}, bf16[320,128]{1,0:T(8,128)(2,1)S(1)}, u32[]{:S(2)}, u32[]{:S(2)}) %collective-permute-start.14) | collective-permute-done | bytes 81952 | tf_op jit(solution)/shard_map/ppermute | solution.py:398
  107.5 2.0 %collective-permute-done.11.via_left = bf16[1024,128]{1,0:T(8,128)(2,1)S(1)} collective-permute-done((bf16[1024,128]{1,0:T(8,128)(2,1)S(1)}, bf16[1024,128]{1,0:T(8,128)(2,1)S(1)}, u32[]{:S(2)}, u32[]{:S(2)}) %collective-permute-start.11) | collective-permute-done | bytes 262176 | tf_op jit(solution)/shard_map/ppermute | solution.py:398
  109.5 1.5 collective-permute-start.15
  111.0 3.1 %to_slots.1 = bf16[1536,128]{1,0:T(8,128)(2,1)} custom-call(s32[8,128]{1,0:T(8,128)} %get-tuple-element.24.slot_ref, bf16[1024,128]{1,0:T(8,128)(2,1)} %grad_ref.1, bf16[2048,128]{1,0:T(8,128)(2,1)} %get-tuple-element.26.own, bf16[2048,128]{1,0:T(8,128)(2,1)} %copy-done.1, bf16[2048,128]{1,0:T(8,128)(2,1)} %copy-done.2, bf16[1024,128]{1,0:T(8,128)(2,1)} %copy-done.10, ...), custom_call_target="tpu_custom_call" | custom-call | tf_op jit(solution)/shard_map/to_slots/pallas_call | solution.py:346
  114.1 12.9 %all-to-all-start.2 = ((bf16[64,24,128]{2,1,0:T(8,128)(2,1)}), bf16[64,24,128]{2,1,0:T(8,128)(2,1)S(1)}, u32[]{:S(2)}, u32[]{:S(2)}) async-start(bf16[64,24,128]{2,1,0:T(8,128)(2,1)} %bitcast.32), calls=%async_computation.2 | async-start | bytes 786432 | tf_op jit(solution)/shard_map/all_to_all | solution.py:474
  128.3 2.0 %all_gather.3.p0 = bf16[640,128]{1,0:T(8,128)(2,1)S(1)} all-gather(bf16[320,128]{1,0:T(8,128)(2,1)S(1)} %add_convert_fusion.2), channel_id=1, replica_groups={{0,32},{64,96},{128,160},{192,224},{1,33},{65,97},{129,161},{193,225},{..., dimensions={0}, use_global_device_ids=true | all-gather | bytes 245760 | tf_op jit(solution)/shard_map/all_gather | solution.py:443
  130.3 1.3 collective-permute-start.18
  131.6 2.6 %collective-permute-start.17 = (bf16[640,128]{1,0:T(8,128)(2,1)S(1)}, bf16[640,128]{1,0:T(8,128)(2,1)S(1)}, u32[]{:S(2)}, u32[]{:S(2)}) collective-permute-start(bf16[640,128]{1,0:T(8,128)(2,1)S(1)} %all_gather.3.p0), channel_id=1, source_target_pairs={{0,128},{32,160},{64,192},{96,224},{128,0},{160,32},{192,64},{224,... | collective-permute-start | bytes 491528 | tf_op jit(solution)/shard_map/ppermute | solution.py:398
  136.0 4.3 %collective-permute-done.18.p3 = bf16[640,128]{1,0:T(8,128)(2,1)S(1)} collective-permute-done((bf16[640,128]{1,0:T(8,128)(2,1)S(1)}, bf16[640,128]{1,0:T(8,128)(2,1)S(1)}, u32[]{:S(2)}, u32[]{:S(2)}) %collective-permute-start.18) | collective-permute-done | bytes 163872 | tf_op jit(solution)/shard_map/ppermute | solution.py:398
  140.4 4.6 %collective-permute-done.17.p2 = bf16[640,128]{1,0:T(8,128)(2,1)S(1)} collective-permute-done((bf16[640,128]{1,0:T(8,128)(2,1)S(1)}, bf16[640,128]{1,0:T(8,128)(2,1)S(1)}, u32[]{:S(2)}, u32[]{:S(2)}) %collective-permute-start.17) | collective-permute-done | bytes 163872 | tf_op jit(solution)/shard_map/ppermute | solution.py:398
  145.7 2.4 %unpack.1 = (f32[2048,128]{1,0:T(8,128)}, f32[128,512]{1,0:T(8,128)}) custom-call(s32[1]{0:T(128)} %bitcast.17.y_ref, bf16[640,128]{1,0:T(8,128)(2,1)} %copy-done.7, bf16[640,128]{1,0:T(8,128)(2,1)} %copy-done.22, bf16[640,128]{1,0:T(8,128)(2,1)} %copy-done.21, bf16[640,128]{1,0:T(8,128)(2,1)} %copy-done.20), custom_call_target="tpu_custom_call" | custom-call | tf_op jit(solution)/shard_map/unpack/pallas_call | solution.py:386
  148.8 3.1 %add_rows.1 = f32[2048,128]{1,0:T(8,128)} custom-call(s32[12,128]{1,0:T(8,128)} %reshape.59.req_ref, bf16[1536,128]{1,0:T(8,128)(2,1)} %bitcast.30), custom_call_target="tpu_custom_call" | custom-call | tf_op jit(solution)/shard_map/add_rows/pallas_call | solution.py:364
  (82 shorter events, 14.3 us)
Async XLA Ops:
  27.6 5.3 %copy-start.6 = (bf16[1024,128]{1,0:T(8,128)(2,1)S(1)}, bf16[1024,128]{1,0:T(8,128)(2,1)}, u32[]{:S(2)}) copy-start(bf16[1024,128]{1,0:T(8,128)(2,1)} %grad_ref.1) | copy-start | bytes 786436
  27.6 20.2 %all-to-all-start.1 = ((bf16[64,24,128]{2,1,0:T(8,128)(2,1)}), bf16[64,24,128]{2,1,0:T(8,128)(2,1)S(1)}, u32[]{:S(2)}, u32[]{:S(2)}) async-start(bf16[64,24,128]{2,1,0:T(8,128)(2,1)} %bitcast.31), calls=%async_computation.1 | async-start | bytes 786432 | tf_op jit(solution)/shard_map/all_to_all | solution.py:455
  32.9 21.6 %collective-permute-start.5 = (bf16[1024,128]{1,0:T(8,128)(2,1)S(1)}, bf16[1024,128]{1,0:T(8,128)(2,1)S(1)}, u32[]{:S(2)}, u32[]{:S(2)}) collective-permute-start(bf16[1024,128]{1,0:T(8,128)(2,1)S(1)} %copy-done.6), channel_id=1, source_target_pairs={{0,1},{1,2},{2,3},{3,0},{4,5},{5,6},{6,7},{7,4},{8,9},{9,10},{10,1... | collective-permute-start | bytes 786440 | tf_op jit(solution)/shard_map/ppermute | solution.py:398
  34.2 21.5 %collective-permute-start.4 = (bf16[1024,128]{1,0:T(8,128)(2,1)S(1)}, bf16[1024,128]{1,0:T(8,128)(2,1)S(1)}, u32[]{:S(2)}, u32[]{:S(2)}) collective-permute-start(bf16[1024,128]{1,0:T(8,128)(2,1)S(1)} %copy-done.6), channel_id=1, source_target_pairs={{0,2},{1,3},{2,0},{3,1},{4,6},{5,7},{6,4},{7,5},{8,10},{9,11},{10,... | collective-permute-start | bytes 786440 | tf_op jit(solution)/shard_map/ppermute | solution.py:398
  36.6 19.1 %collective-permute-start.3 = (bf16[1024,128]{1,0:T(8,128)(2,1)S(1)}, bf16[1024,128]{1,0:T(8,128)(2,1)S(1)}, u32[]{:S(2)}, u32[]{:S(2)}) collective-permute-start(bf16[1024,128]{1,0:T(8,128)(2,1)S(1)} %copy-done.6), channel_id=1, source_target_pairs={{0,3},{1,0},{2,1},{3,2},{4,7},{5,4},{6,5},{7,6},{8,11},{9,8},{10,9... | collective-permute-start | bytes 786440 | tf_op jit(solution)/shard_map/ppermute | solution.py:398
  50.9 8.2 %collective-permute-start.2 = (bf16[1024,128]{1,0:T(8,128)(2,1)}, bf16[1024,128]{1,0:T(8,128)(2,1)S(1)}, u32[]{:S(2)}, u32[]{:S(2)}) collective-permute-start(bf16[1024,128]{1,0:T(8,128)(2,1)} %place.1.x0), channel_id=1, source_target_pairs={{0,1},{1,2},{2,3},{3,0},{4,5},{5,6},{6,7},{7,4},{8,9},{9,10},{10,1... | collective-permute-start | bytes 786440 | tf_op jit(solution)/shard_map/ppermute | solution.py:398
  52.1 13.6 %collective-permute-start.1 = (bf16[1024,128]{1,0:T(8,128)(2,1)}, bf16[1024,128]{1,0:T(8,128)(2,1)S(1)}, u32[]{:S(2)}, u32[]{:S(2)}) collective-permute-start(bf16[1024,128]{1,0:T(8,128)(2,1)} %place.1.x0), channel_id=1, source_target_pairs={{0,2},{1,3},{2,0},{3,1},{4,6},{5,7},{6,4},{7,5},{8,10},{9,11},{10,... | collective-permute-start | bytes 786440 | tf_op jit(solution)/shard_map/ppermute | solution.py:398
  54.6 11.3 %copy-start.14 = (bf16[1024,128]{1,0:T(8,128)(2,1)}, bf16[1024,128]{1,0:T(8,128)(2,1)S(1)}, u32[]{:S(2)}) copy-start(bf16[1024,128]{1,0:T(8,128)(2,1)S(1)} %collective-permute-done.5.g3) | copy-start | bytes 786436
  54.6 11.3 %collective-permute-start = (bf16[1024,128]{1,0:T(8,128)(2,1)}, bf16[1024,128]{1,0:T(8,128)(2,1)S(1)}, u32[]{:S(2)}, u32[]{:S(2)}) collective-permute-start(bf16[1024,128]{1,0:T(8,128)(2,1)} %place.1.x0), channel_id=1, source_target_pairs={{0,3},{1,0},{2,1},{3,2},{4,7},{5,4},{6,5},{7,6},{8,11},{9,8},{10,9... | collective-permute-start | bytes 786440 | tf_op jit(solution)/shard_map/ppermute | solution.py:398
  55.7 10.1 %copy-start.15 = (bf16[1024,128]{1,0:T(8,128)(2,1)}, bf16[1024,128]{1,0:T(8,128)(2,1)S(1)}, u32[]{:S(2)}) copy-start(bf16[1024,128]{1,0:T(8,128)(2,1)S(1)} %collective-permute-done.4.g2) | copy-start | bytes 786436
  55.7 10.1 %copy-start.16 = (bf16[1024,128]{1,0:T(8,128)(2,1)}, bf16[1024,128]{1,0:T(8,128)(2,1)S(1)}, u32[]{:S(2)}) copy-start(bf16[1024,128]{1,0:T(8,128)(2,1)S(1)} %collective-permute-done.3.g1) | copy-start | bytes 786436
  59.1 6.7 %copy-start.17 = (bf16[1024,128]{1,0:T(8,128)(2,1)}, bf16[1024,128]{1,0:T(8,128)(2,1)S(1)}, u32[]{:S(2)}) copy-start(bf16[1024,128]{1,0:T(8,128)(2,1)S(1)} %collective-permute-done.2.x3) | copy-start | bytes 786436
  78.5 3.4 %collective-permute-start.8 = (bf16[1280,128]{1,0:T(8,128)(2,1)}, bf16[1280,128]{1,0:T(8,128)(2,1)S(1)}, u32[]{:S(2)}, u32[]{:S(2)}) collective-permute-start(bf16[1280,128]{1,0:T(8,128)(2,1)} %get-tuple-element.31), channel_id=1, source_target_pairs={{0,32},{32,0},{64,96},{96,64},{128,160},{160,128},{192,224},{224,1... | collective-permute-start | bytes 983048 | tf_op jit(solution)/shard_map/ppermute | solution.py:398
  83.2 5.5 %collective-permute-start.9 = (bf16[640,128]{1,0:T(8,128)(2,1)S(1)}, bf16[640,128]{1,0:T(8,128)(2,1)S(1)}, u32[]{:S(2)}, u32[]{:S(2)}) collective-permute-start(bf16[640,128]{1,0:T(8,128)(2,1)S(1)} %fusion.1), channel_id=1, source_target_pairs={{0,64},{32,96},{64,0},{96,32},{128,192},{160,224},{192,128},{224,1... | collective-permute-start | bytes 491528 | tf_op jit(solution)/shard_map/ppermute | solution.py:398
  84.0 14.0 %collective-permute-start.6 = (bf16[2048,128]{1,0:T(8,128)(2,1)S(1)}, bf16[2048,128]{1,0:T(8,128)(2,1)S(1)}, u32[]{:S(2)}, u32[]{:S(2)}) collective-permute-start(bf16[2048,128]{1,0:T(8,128)(2,1)S(1)} %copy-done.24), channel_id=1, source_target_pairs={{0,1},{1,2},{2,3},{3,0},{4,5},{5,6},{6,7},{7,4},{8,9},{9,10},{10,1... | collective-permute-start | bytes 1572872 | tf_op jit(solution)/shard_map/ppermute | solution.py:398
  85.0 13.1 %collective-permute-start.7 = (bf16[2048,128]{1,0:T(8,128)(2,1)S(1)}, bf16[2048,128]{1,0:T(8,128)(2,1)S(1)}, u32[]{:S(2)}, u32[]{:S(2)}) collective-permute-start(bf16[2048,128]{1,0:T(8,128)(2,1)S(1)} %copy-done.23), channel_id=1, source_target_pairs={{0,3},{1,0},{2,1},{3,2},{4,7},{5,4},{6,5},{7,6},{8,11},{9,8},{10,9... | collective-permute-start | bytes 1572872 | tf_op jit(solution)/shard_map/ppermute | solution.py:398
  88.7 11.0 %copy-start.13 = (bf16[1024,128]{1,0:T(8,128)(2,1)S(1)}, bf16[1024,128]{1,0:T(8,128)(2,1)}, u32[]{:S(2)}) copy-start(bf16[1024,128]{1,0:T(8,128)(2,1)} %get-tuple-element.33) | copy-start | bytes 786436
  88.7 9.3 %collective-permute-start.10 = (bf16[320,128]{1,0:T(8,128)(2,1)S(1)}, bf16[320,128]{1,0:T(8,128)(2,1)S(1)}, u32[]{:S(2)}, u32[]{:S(2)}) collective-permute-start(bf16[320,128]{1,0:T(8,128)(2,1)S(1)} %fusion.3), channel_id=1, source_target_pairs={{0,192},{32,224},{64,128},{96,160},{128,64},{160,96},{192,0},{224,... | collective-permute-start | bytes 245768 | tf_op jit(solution)/shard_map/ppermute | solution.py:398
  98.0 4.8 %copy-start.1 = (bf16[2048,128]{1,0:T(8,128)(2,1)}, bf16[2048,128]{1,0:T(8,128)(2,1)S(1)}, u32[]{:S(2)}) copy-start(bf16[2048,128]{1,0:T(8,128)(2,1)S(1)} %collective-permute-done.6.from_left) | copy-start | bytes 1572868
  98.1 4.2 %collective-permute-start.13 = (bf16[320,128]{1,0:T(8,128)(2,1)S(1)}, bf16[320,128]{1,0:T(8,128)(2,1)S(1)}, u32[]{:S(2)}, u32[]{:S(2)}) collective-permute-start(bf16[320,128]{1,0:T(8,128)(2,1)S(1)} %fusion.2), channel_id=1, source_target_pairs={{0,4},{4,0},{8,12},{12,8},{16,20},{20,16},{24,28},{28,24},{1,5},{5... | collective-permute-start | bytes 245768 | tf_op jit(solution)/shard_map/ppermute | solution.py:398
  99.8 7.6 %collective-permute-start.12 = (bf16[1024,128]{1,0:T(8,128)(2,1)S(1)}, bf16[1024,128]{1,0:T(8,128)(2,1)S(1)}, u32[]{:S(2)}, u32[]{:S(2)}) collective-permute-start(bf16[1024,128]{1,0:T(8,128)(2,1)S(1)} %add_convert_fusion), channel_id=1, source_target_pairs={{0,3},{1,0},{2,1},{3,2},{4,7},{5,4},{6,5},{7,6},{8,11},{9,8},{10,9... | collective-permute-start | bytes 786440 | tf_op jit(solution)/shard_map/ppermute | solution.py:398
  102.3 5.2 %collective-permute-start.14 = (bf16[320,128]{1,0:T(8,128)(2,1)S(1)}, bf16[320,128]{1,0:T(8,128)(2,1)S(1)}, u32[]{:S(2)}, u32[]{:S(2)}) collective-permute-start(bf16[320,128]{1,0:T(8,128)(2,1)S(1)} %add_convert_fusion.4), channel_id=1, source_target_pairs={{0,8},{4,12},{8,0},{12,4},{16,24},{20,28},{24,16},{28,20},{1,9},{5... | collective-permute-start | bytes 245768 | tf_op jit(solution)/shard_map/ppermute | solution.py:398
  102.9 6.6 %collective-permute-start.11 = (bf16[1024,128]{1,0:T(8,128)(2,1)S(1)}, bf16[1024,128]{1,0:T(8,128)(2,1)S(1)}, u32[]{:S(2)}, u32[]{:S(2)}) collective-permute-start(bf16[1024,128]{1,0:T(8,128)(2,1)S(1)} %add_convert_fusion.1), channel_id=1, source_target_pairs={{0,1},{1,2},{2,3},{3,0},{4,5},{5,6},{6,7},{7,4},{8,9},{9,10},{10,1... | collective-permute-start | bytes 786440 | tf_op jit(solution)/shard_map/ppermute | solution.py:398
  109.5 4.6 %collective-permute-start.15 = (bf16[320,128]{1,0:T(8,128)(2,1)S(1)}, bf16[320,128]{1,0:T(8,128)(2,1)S(1)}, u32[]{:S(2)}, u32[]{:S(2)}) collective-permute-start(bf16[320,128]{1,0:T(8,128)(2,1)S(1)} %add_convert_fusion.3), channel_id=1, source_target_pairs={{0,28},{4,24},{8,20},{12,16},{16,12},{20,8},{24,4},{28,0},{1,29},{... | collective-permute-start | bytes 245768 | tf_op jit(solution)/shard_map/ppermute | solution.py:398
  114.1 13.0 %copy-start.5 = (bf16[2048,128]{1,0:T(8,128)(2,1)S(1)}, bf16[2048,128]{1,0:T(8,128)(2,1)}, u32[]{:S(2)}) copy-start(bf16[2048,128]{1,0:T(8,128)(2,1)} %get-tuple-element.26.own) | copy-start | bytes 1572868
  114.1 13.0 %copy-start.9 = (bf16[1024,128]{1,0:T(8,128)(2,1)S(1)}, bf16[1024,128]{1,0:T(8,128)(2,1)}, u32[]{:S(2)}) copy-start(bf16[1024,128]{1,0:T(8,128)(2,1)} %copy-done.8) | copy-start | bytes 786436
  114.1 34.0 %all-to-all-start.2 = ((bf16[64,24,128]{2,1,0:T(8,128)(2,1)}), bf16[64,24,128]{2,1,0:T(8,128)(2,1)S(1)}, u32[]{:S(2)}, u32[]{:S(2)}) async-start(bf16[64,24,128]{2,1,0:T(8,128)(2,1)} %bitcast.32), calls=%async_computation.2 | async-start | bytes 786432 | tf_op jit(solution)/shard_map/all_to_all | solution.py:474
  127.1 8.2 %copy-start = (bf16[1024,128]{1,0:T(8,128)(2,1)S(1)}, bf16[1024,128]{1,0:T(8,128)(2,1)}, u32[]{:S(2)}) copy-start(bf16[1024,128]{1,0:T(8,128)(2,1)} %place.1.x0) | copy-start | bytes 786436
  130.3 5.8 %copy-start.7 = (bf16[640,128]{1,0:T(8,128)(2,1)}, bf16[640,128]{1,0:T(8,128)(2,1)S(1)}, u32[]{:S(2)}) copy-start(bf16[640,128]{1,0:T(8,128)(2,1)S(1)} %all_gather.3.p0) | copy-start | bytes 491524
  130.3 10.1 %collective-permute-start.18 = (bf16[640,128]{1,0:T(8,128)(2,1)S(1)}, bf16[640,128]{1,0:T(8,128)(2,1)S(1)}, u32[]{:S(2)}, u32[]{:S(2)}) collective-permute-start(bf16[640,128]{1,0:T(8,128)(2,1)S(1)} %all_gather.3.p0), channel_id=1, source_target_pairs={{0,64},{32,96},{64,128},{96,160},{128,192},{160,224},{192,0},{224,... | collective-permute-start | bytes 491528 | tf_op jit(solution)/shard_map/ppermute | solution.py:398
  131.6 13.4 %collective-permute-start.17 = (bf16[640,128]{1,0:T(8,128)(2,1)S(1)}, bf16[640,128]{1,0:T(8,128)(2,1)S(1)}, u32[]{:S(2)}, u32[]{:S(2)}) collective-permute-start(bf16[640,128]{1,0:T(8,128)(2,1)S(1)} %all_gather.3.p0), channel_id=1, source_target_pairs={{0,128},{32,160},{64,192},{96,224},{128,0},{160,32},{192,64},{224,... | collective-permute-start | bytes 491528 | tf_op jit(solution)/shard_map/ppermute | solution.py:398
  134.2 10.8 %collective-permute-start.16 = (bf16[640,128]{1,0:T(8,128)(2,1)S(1)}, bf16[640,128]{1,0:T(8,128)(2,1)S(1)}, u32[]{:S(2)}, u32[]{:S(2)}) collective-permute-start(bf16[640,128]{1,0:T(8,128)(2,1)S(1)} %all_gather.3.p0), channel_id=1, source_target_pairs={{0,192},{32,224},{64,0},{96,32},{128,64},{160,96},{192,128},{224,1... | collective-permute-start | bytes 491528 | tf_op jit(solution)/shard_map/ppermute | solution.py:398
  (14 other events, 25.2 us)

commit v8 on v5

--- a/solution.py
+++ b/solution.py
@@ -142,11 +142,11 @@
 
 def layer_kernel(
     pos_ref, core_ref, seg_ref, x0, x1, x2, x3, g0, g1, g2, g3, win_ref, wout_ref,
-    mine_ref, other_ref, dx0, dx1, dx2, dx3, z0, z1, z2, z3,
+    mine_ref, other_ref, c0, c1, c2, c3,
     w, wo, pre, act, segc, aw, dsil, dkv, du, u_ref, y_ref, dp_ref, dw_ref,
 ):
     xs, gs = (x0, x1, x2, x3), (g0, g1, g2, g3)
-    dxs, zs = (dx0, dx1, dx2, dx3), (z0, z1, z2, z3)
+    both = (c0, c1, c2, c3)
     me, core = pos_ref[0], core_ref[0]
     for k in range(NT):
         at = pl.multiple_of(lax.rem(me + k, NT) * 128, 128)
@@ -245,7 +245,7 @@
                 d[0] * n[0] + d[1] * n[1] + d[2] * n[2] + d[3] * n[3], axis=1, keepdims=True
             ) * (1.0 / D)
             for k in range(NT):
-                dxs[k][lo + r : lo + r + step, :] = ((d[k] - m1 - n[k] * m2) * scale).astype(BF)
+                both[k][lo + r : lo + r + step, :] = ((d[k] - m1 - n[k] * m2) * scale).astype(BF)
 
     for k in range(NT):
         at = pl.multiple_of(lax.rem(me + k, NT) * 128, 128)
@@ -253,19 +253,19 @@
         for c in range(4):
             dw_ref[pl.ds(pl.multiple_of(c * 512 + at, 128), 128), :] = dw[:, c * 128 : (c + 1) * 128]
         dw_ref[pl.ds(pl.multiple_of(2048 + at, 128), 128), :] = dot(y_ref[...], gs[k][...], 0, 0)
-        zs[k][...] = dot(y_ref[...], wo[:, k * 128 : (k + 1) * 128], 1, 0).astype(BF)
+        both[k][TOK:, :] = dot(y_ref[...], wo[:, k * 128 : (k + 1) * 128], 1, 0).astype(BF)
     mine_ref[...] = dw_ref[pl.ds(pl.multiple_of(core * 1280, 1280), 1280), :]
     other_ref[...] = dw_ref[pl.ds(pl.multiple_of(1280 - core * 1280, 1280), 1280), :].astype(BF)
 
 
 def layer(pos, core, seg, xs, gs, w_in, w_out):
-    piece = jax.ShapeDtypeStruct((TOK, 128), BF)
+    pair = jax.ShapeDtypeStruct((2 * TOK, 128), BF)
     return pl.pallas_call(
         layer_kernel,
         out_shape=(jax.ShapeDtypeStruct((1280, 128), F32), jax.ShapeDtypeStruct((1280, 128), BF))
-        + (piece,) * 8,
+        + (pair,) * 4,
         in_specs=[SM, SM] + [VM] * 11,
-        out_specs=(VM,) * 10,
+        out_specs=(VM,) * 6,
         scratch_shapes=[
             pltpu.VMEM((D, 512), BF),
             pltpu.VMEM((HD, D), BF),
@@ -315,11 +315,13 @@
 
 
 def to_slots(slot, grad, parts):
+    top = pl.BlockSpec((TOK, 128), lambda i: (0, 0))
     return pl.pallas_call(
         slots_kernel,
         out_shape=jax.ShapeDtypeStruct((SLOTS, 128), BF),
-        in_specs=[VM] * 6,
-        out_specs=VM,
+        grid=(1,),
+        in_specs=[pl.BlockSpec((TOK // 128, 128), lambda i: (0, 0))] + [top] * 5,
+        out_specs=pl.BlockSpec((SLOTS, 128), lambda i: (0, 0)),
         compiler_params=PARAMS,
         name="to_slots",
     )(slot, grad, *parts)
@@ -403,6 +405,13 @@
 
 def add_step(total, mask):
     return (total.astype(F32) + shift(total, "seq", lambda i: i ^ mask, 8).astype(F32)).astype(BF)
+
+
+def add_group(total):
+    got = [shift(total, "seq", lambda i, k=k: i ^ k, 8) for k in (1, 2, 3)]
+    for other in got:
+        total = total.astype(F32) + other.astype(F32)
+    return total.astype(BF)
 
 
 def gather_weights(total):
@@ -423,25 +432,28 @@
     back = lax.all_to_all(rows.reshape(NOWN, CAP, 128), BOTH, split_axis=0, concat_axis=0, tiled=True)
     x = place(slot, back.reshape(SLOTS, 128))
     xs = order(gather_pieces(x))
-    mine, other, d0, d1, d2, d3, z0, z1, z2, z3 = layer(
-        pos, core, segment_ids, xs, gs, proj_in, proj_out
-    )
-    dparts = scatter_pieces([d0, d1, d2, d3])
+    mine, other, c0, c1, c2, c3 = layer(pos, core, segment_ids, xs, gs, proj_in, proj_out)
+    cparts = scatter_pieces([c0, c1, c2, c3])
     own, got = reduce_over_chips(mine, other)
     flat = received[:, :CAP].reshape(SLOTS // 128, 128)
-    total = add_step((own + got.astype(F32)).astype(BF), 1)
-    dparts, total, flat = lax.optimization_barrier((dparts, total, flat))
-    grads = to_slots(slot, grad_out, dparts)
-    total = add_step(add_step(total, 2), 7)
-    grads, total, zs = lax.optimization_barrier((grads, total, [z0, z1, z2, z3]))
+    got, cparts[3] = lax.optimization_barrier((got, cparts[3]))
+    total = add_group((own + got.astype(F32)).astype(BF))
+    cparts, _, flat = lax.optimization_barrier((cparts, total, flat))
+    grads = to_slots(slot, grad_out, cparts)
+    total = add_step(total, 7)
+    grads, total = lax.optimization_barrier((grads, total))
     arrived = lax.all_to_all(grads.reshape(NOWN, CAP, 128), BOTH, split_axis=0, concat_axis=0, tiled=True)
     grad_in, grad_outw = gather_weights(total)
-    zparts = scatter_pieces(zs)
-    table_grad = add_rows(flat, arrived.reshape(SLOTS, 128))
     layer_out = (
         x.astype(F32)
-        + (zparts[0].astype(F32) + zparts[1].astype(F32) + zparts[2].astype(F32) + zparts[3].astype(F32))
+        + (
+            cparts[0][TOK:].astype(F32)
+            + cparts[1][TOK:].astype(F32)
+            + cparts[2][TOK:].astype(F32)
+            + cparts[3][TOK:].astype(F32)
+        )
     ).astype(BF)
+    table_grad = add_rows(flat, arrived.reshape(SLOTS, 128))
     return layer_out, table_grad, grad_in.reshape(4, D, 128), grad_outw
 
 

time: 156 us -> 147 us (0.942)
  starting transfers between devices: 48.4 us -> 41.5 us
  waiting for transfers between devices: 47.6 us -> 44.7 us
    all_to_all x1, starting transfers between devices: 11.5 us -> 7.75 us  [body(): lax.all_to_all(grads.reshape(NOWN, CAP, 128), BOTH, split_axis=0, concat_...]
    ppermute x21 -> x19, starting transfers between devices: 31.7 us -> 28.5 us  [shift(): return lax.ppermute(x, axis, [(i, fn(i)) for i in range(n)])]
    ppermute x21 -> x19, waiting for transfers between devices: 37.6 us -> 34.7 us  [shift(): return lax.ppermute(x, axis, [(i, fn(i)) for i in range(n)])]
    unnamed x50 -> x40, local copies, waits for them, and re-layouts: 2.91 us -> 3.89 us
  transfers between devices with their start and end apart: 23 -> 21, of which waited for: 15 -> 12; matrix products, arithmetic and copies ran while one was open for 1% -> 2% of each run, Pallas kernels for 5% -> 5%
where the time goes in v8:
time: 147 us; the launch traced here: 146 us
  waiting for transfers between devices  44.7 us (30%)
  starting transfers between devices  41.5 us (28%)
  Pallas kernels  27.1 us (18%)
  blocking collectives  24.3 us (17%)
  local copies, waits for them, and re-layouts  4.62 us (3%)
  other arithmetic  3.25 us (2%)
    ppermute x19, waiting for transfers between devices, shift(): return lax.ppermute(x, axis, [(i, fn(i)) for i in range(n)])  34.7 us
    ppermute x19, starting transfers between devices, shift(): return lax.ppermute(x, axis, [(i, fn(i)) for i in range(n)])  28.5 us
    all_to_all x1, blocking collectives, body(): lax.all_to_all(requests, BOTH, split_axis=0, concat_axis=0, tiled=True)  22.3 us
    pallas_call x1, Pallas kernels, layer(): pl.pallas_call(layer_kernel, out_shape=(jax.ShapeDtypeStruct((1280, 128),...  11.8 us
    all_to_all x1, waiting for transfers between devices, body(): lax.all_to_all(rows.reshape(NOWN, CAP, 128), BOTH, split_axis=0, concat_a...  9.98 us
    all_to_all x1, starting transfers between devices, body(): lax.all_to_all(grads.reshape(NOWN, CAP, 128), BOTH, split_axis=0, concat_...  7.75 us
    all_to_all x1, starting transfers between devices, body(): lax.all_to_all(rows.reshape(NOWN, CAP, 128), BOTH, split_axis=0, concat_a...  5.29 us
    unnamed x40, local copies, waits for them, and re-layouts  3.89 us
  transfers between devices with their start and end apart: 21, of which 12 were waited for; matrix products, arithmetic and copies ran while one was open for 2% of the time, Pallas kernels for 5%

profile of v8, /device:TPU:1, one launch (start us, length us, event | category | flops | bytes accessed | tf_op | source)
XLA Modules:
  0.0 146.2 jit_solution(1667238813836305904)
XLA Ops:
  0.6 1.8 %route.1 = (s32[64,128]{1,0:T(8,128)}, s32[8,128]{1,0:T(8,128)}) custom-call(s32[8,128]{1,0:T(8,128)} %bitcast.38, s32[8,128]{1,0:T(8,128)} %bitcast.39), custom_call_target="tpu_custom_call" | custom-call | tf_op jit(solution)/shard_map/route/pallas_call | solution.py:62
  2.5 22.3 %all_to_all.21 = s32[64,1,128]{2,1,0:T(1,128)} all-to-all(s32[64,1,128]{2,1,0:T(1,128)} %bitcast.37), channel_id=1, replica_groups=mesh['table'=8,'seq'=8,'tensor'=4] {'table','seq'}, dimensions={0} | all-to-all | bytes 65536 | tf_op jit(solution)/shard_map/all_to_all | solution.py:430
  24.7 2.9 %fetch.1 = bf16[1536,128]{1,0:T(8,128)(2,1)} custom-call(s32[64,128]{1,0:T(8,128)} %bitcast.35, bf16[2048,128]{1,0:T(8,128)(2,1)} %table_ref.1), custom_call_target="tpu_custom_call" | custom-call | tf_op jit(solution)/shard_map/fetch/pallas_call | solution.py:98
  27.6 5.3 %all-to-all-start.1 = ((bf16[64,24,128]{2,1,0:T(8,128)(2,1)}), bf16[64,24,128]{2,1,0:T(8,128)(2,1)S(1)}, u32[]{:S(2)}, u32[]{:S(2)}) async-start(bf16[64,24,128]{2,1,0:T(8,128)(2,1)} %bitcast.31), calls=%async_computation.1 | async-start | bytes 786432 | tf_op jit(solution)/shard_map/all_to_all | solution.py:432
  34.2 2.5 %collective-permute-start.4 = (bf16[1024,128]{1,0:T(8,128)(2,1)S(1)}, bf16[1024,128]{1,0:T(8,128)(2,1)S(1)}, u32[]{:S(2)}, u32[]{:S(2)}) collective-permute-start(bf16[1024,128]{1,0:T(8,128)(2,1)S(1)} %copy-done.7), channel_id=1, source_target_pairs={{0,2},{1,3},{2,0},{3,1},{4,6},{5,7},{6,4},{7,5},{8,10},{9,11},{10,... | collective-permute-start | bytes 786440 | tf_op jit(solution)/shard_map/ppermute | solution.py:372
  37.8 10.0 %all-to-all-done.1 = bf16[64,24,128]{2,1,0:T(8,128)(2,1)S(1)} async-done(((bf16[64,24,128]{2,1,0:T(8,128)(2,1)}), bf16[64,24,128]{2,1,0:T(8,128)(2,1)S(1)}, u32[]{:S(2)}, u32[]{:S(2)}) %all-to-all-start.1) | async-done | bytes 393248 | tf_op jit(solution)/shard_map/all_to_all | solution.py:432
  48.5 2.4 %place.1.x0 = bf16[1024,128]{1,0:T(8,128)(2,1)} custom-call(s32[8,128]{1,0:T(8,128)} %get-tuple-element.23.slot_ref, bf16[1536,128]{1,0:T(8,128)(2,1)} %bitcast.29), custom_call_target="tpu_custom_call" | custom-call | tf_op jit(solution)/shard_map/place/pallas_call | solution.py:133
  52.1 2.5 %collective-permute-start.1 = (bf16[1024,128]{1,0:T(8,128)(2,1)}, bf16[1024,128]{1,0:T(8,128)(2,1)S(1)}, u32[]{:S(2)}, u32[]{:S(2)}) collective-permute-start(bf16[1024,128]{1,0:T(8,128)(2,1)} %place.1.x0), channel_id=1, source_target_pairs={{0,2},{1,3},{2,0},{3,1},{4,6},{5,7},{6,4},{7,5},{8,10},{9,11},{10,... | collective-permute-start | bytes 786440 | tf_op jit(solution)/shard_map/ppermute | solution.py:372
  55.7 3.4 %collective-permute-done.2.x3 = bf16[1024,128]{1,0:T(8,128)(2,1)S(1)} collective-permute-done((bf16[1024,128]{1,0:T(8,128)(2,1)}, bf16[1024,128]{1,0:T(8,128)(2,1)S(1)}, u32[]{:S(2)}, u32[]{:S(2)}) %collective-permute-start.2) | collective-permute-done | bytes 262176 | tf_op jit(solution)/shard_map/ppermute | solution.py:372
  59.1 6.6 %collective-permute-done.1.x2 = bf16[1024,128]{1,0:T(8,128)(2,1)S(1)} collective-permute-done((bf16[1024,128]{1,0:T(8,128)(2,1)}, bf16[1024,128]{1,0:T(8,128)(2,1)S(1)}, u32[]{:S(2)}, u32[]{:S(2)}) %collective-permute-start.1) | collective-permute-done | bytes 262176 | tf_op jit(solution)/shard_map/ppermute | solution.py:372
  66.5 11.8 %layer.1 = (f32[1280,128]{1,0:T(8,128)}, bf16[1280,128]{1,0:T(8,128)(2,1)}, bf16[2048,128]{1,0:T(8,128)(2,1)}, bf16[2048,128]{1,0:T(8,128)(2,1)}, bf16[2048,128]{1,0:T(8,128)(2,1)}, /*index=5*/bf16[2048,128]{1,0:T(8,128)(2,1)}) custom-call(s32[1]{0:T(128)} %bitcast.7.pos_ref, s32[1]{0:T(128)} %bitcast.8.core_ref, s32[1,1024]{1,0:T(1,128)} %seg_ref.1, ...), custom_call_target="tpu_custom_call" | custom-call | tf_op jit(solution)/shard_map/layer/pallas_call | solution.py:263
  78.3 2.0 %collective-permute-start.8 = (bf16[1280,128]{1,0:T(8,128)(2,1)}, bf16[1280,128]{1,0:T(8,128)(2,1)S(1)}, u32[]{:S(2)}, u32[]{:S(2)}) collective-permute-start(bf16[1280,128]{1,0:T(8,128)(2,1)} %get-tuple-element.29), channel_id=1, source_target_pairs={{0,32},{32,0},{64,96},{96,64},{128,160},{160,128},{192,224},{224,1... | collective-permute-start | bytes 983048 | tf_op jit(solution)/shard_map/ppermute | solution.py:372
  80.3 1.5 %collective-permute-done.8 = bf16[1280,128]{1,0:T(8,128)(2,1)S(1)} collective-permute-done((bf16[1280,128]{1,0:T(8,128)(2,1)}, bf16[1280,128]{1,0:T(8,128)(2,1)S(1)}, u32[]{:S(2)}, u32[]{:S(2)}) %collective-permute-start.8) | collective-permute-done | bytes 327712 | tf_op jit(solution)/shard_map/ppermute | solution.py:372
  83.8 2.3 %collective-permute-start.11 = (bf16[2048,128]{1,0:T(8,128)(2,1)}, bf16[2048,128]{1,0:T(8,128)(2,1)S(1)}, u32[]{:S(2)}, u32[]{:S(2)}) collective-permute-start(bf16[2048,128]{1,0:T(8,128)(2,1)} %get-tuple-element.30), channel_id=1, source_target_pairs={{0,2},{1,3},{2,0},{3,1},{4,6},{5,7},{6,4},{7,5},{8,10},{9,11},{10,... | collective-permute-start | bytes 1572872 | tf_op jit(solution)/shard_map/ppermute | solution.py:372
  86.1 2.4 %collective-permute-done.9 = bf16[640,128]{1,0:T(8,128)(2,1)S(1)} collective-permute-done((bf16[640,128]{1,0:T(8,128)(2,1)S(1)}, bf16[640,128]{1,0:T(8,128)(2,1)S(1)}, u32[]{:S(2)}, u32[]{:S(2)}) %collective-permute-start.9) | collective-permute-done | bytes 163872 | tf_op jit(solution)/shard_map/ppermute | solution.py:372
  88.5 1.3 collective-permute-start.10
  90.8 1.7 %collective-permute-start.7 = (bf16[2048,128]{1,0:T(8,128)(2,1)S(1)}, bf16[2048,128]{1,0:T(8,128)(2,1)S(1)}, u32[]{:S(2)}, u32[]{:S(2)}) collective-permute-start(bf16[2048,128]{1,0:T(8,128)(2,1)S(1)} %copy-done.19), channel_id=1, source_target_pairs={{0,3},{1,0},{2,1},{3,2},{4,7},{5,4},{6,5},{7,6},{8,11},{9,8},{10,9... | collective-permute-start | bytes 1572872 | tf_op jit(solution)/shard_map/ppermute | solution.py:372
  92.5 5.9 %collective-permute-done.11.d3 = bf16[2048,128]{1,0:T(8,128)(2,1)S(1)} collective-permute-done((bf16[2048,128]{1,0:T(8,128)(2,1)}, bf16[2048,128]{1,0:T(8,128)(2,1)S(1)}, u32[]{:S(2)}, u32[]{:S(2)}) %collective-permute-start.11) | collective-permute-done | bytes 524320 | tf_op jit(solution)/shard_map/ppermute | solution.py:372
  98.4 1.6 %collective-permute-start.14 = (bf16[320,128]{1,0:T(8,128)(2,1)S(1)}, bf16[320,128]{1,0:T(8,128)(2,1)S(1)}, u32[]{:S(2)}, u32[]{:S(2)}) collective-permute-start(bf16[320,128]{1,0:T(8,128)(2,1)S(1)} %fusion.1), channel_id=1, source_target_pairs={{0,12},{4,8},{8,4},{12,0},{16,28},{20,24},{24,20},{28,16},{1,13},{... | collective-permute-start | bytes 245768 | tf_op jit(solution)/shard_map/ppermute | solution.py:372
  102.0 1.7 %collective-permute-done.14 = bf16[320,128]{1,0:T(8,128)(2,1)S(1)} collective-permute-done((bf16[320,128]{1,0:T(8,128)(2,1)S(1)}, bf16[320,128]{1,0:T(8,128)(2,1)S(1)}, u32[]{:S(2)}, u32[]{:S(2)}) %collective-permute-start.14) | collective-permute-done | bytes 81952 | tf_op jit(solution)/shard_map/ppermute | solution.py:372
  103.7 2.4 %collective-permute-done.13 = bf16[320,128]{1,0:T(8,128)(2,1)S(1)} collective-permute-done((bf16[320,128]{1,0:T(8,128)(2,1)S(1)}, bf16[320,128]{1,0:T(8,128)(2,1)S(1)}, u32[]{:S(2)}, u32[]{:S(2)}) %collective-permute-start.13) | collective-permute-done | bytes 81952 | tf_op jit(solution)/shard_map/ppermute | solution.py:372
  107.9 2.7 %collective-permute-done.6.d1 = bf16[2048,128]{1,0:T(8,128)(2,1)S(1)} collective-permute-done((bf16[2048,128]{1,0:T(8,128)(2,1)}, bf16[2048,128]{1,0:T(8,128)(2,1)S(1)}, u32[]{:S(2)}, u32[]{:S(2)}) %collective-permute-start.6) | collective-permute-done | bytes 524320 | tf_op jit(solution)/shard_map/ppermute | solution.py:372
  111.5 2.8 %to_slots.1 = bf16[1536,128]{1,0:T(8,128)(2,1)} custom-call(s32[8,128]{1,0:T(8,128)} %get-tuple-element.23.slot_ref, bf16[1024,128]{1,0:T(8,128)(2,1)} %grad_ref.1, bf16[2048,128]{1,0:T(8,128)(2,1)} %get-tuple-element.33.d0, bf16[2048,128]{1,0:T(8,128)(2,1)} %copy-done.5, bf16[2048,128]{1,0:T(8,128)(2,1)} %copy-done.6, bf16[2048,128]{1,0:T(8,128)(2,1)} %copy-done.4), custom_call_target="tpu_custom_call" | custom-call | tf_op jit(solution)/shard_map/to_slots/pallas_call | solution.py:319
  114.4 7.8 %all-to-all-start.2 = ((bf16[64,24,128]{2,1,0:T(8,128)(2,1)}), bf16[64,24,128]{2,1,0:T(8,128)(2,1)S(1)}, u32[]{:S(2)}, u32[]{:S(2)}) async-start(bf16[64,24,128]{2,1,0:T(8,128)(2,1)} %bitcast.32), calls=%async_computation.2 | async-start | bytes 786432 | tf_op jit(solution)/shard_map/all_to_all | solution.py:445
  122.1 2.0 %all_gather.3.p0 = bf16[640,128]{1,0:T(8,128)(2,1)S(1)} all-gather(bf16[320,128]{1,0:T(8,128)(2,1)S(1)} %add_convert_fusion.1), channel_id=1, replica_groups={{0,32},{64,96},{128,160},{192,224},{1,33},{65,97},{129,161},{193,225},{..., dimensions={0}, use_global_device_ids=true | all-gather | bytes 245760 | tf_op jit(solution)/shard_map/all_gather | solution.py:420
  124.2 1.3 collective-permute-start.18
  125.5 2.6 %collective-permute-start.17 = (bf16[640,128]{1,0:T(8,128)(2,1)S(1)}, bf16[640,128]{1,0:T(8,128)(2,1)S(1)}, u32[]{:S(2)}, u32[]{:S(2)}) collective-permute-start(bf16[640,128]{1,0:T(8,128)(2,1)S(1)} %all_gather.3.p0), channel_id=1, source_target_pairs={{0,128},{32,160},{64,192},{96,224},{128,0},{160,32},{192,64},{224,... | collective-permute-start | bytes 491528 | tf_op jit(solution)/shard_map/ppermute | solution.py:372
  129.2 2.0 %add_convert_fusion = bf16[1024,128]{1,0:T(8,128)(2,1)} fusion(bf16[1024,128]{1,0:T(8,128)(2,1)S(1)} %copy-done, bf16[2048,128]{1,0:T(8,128)(2,1)} %copy-done.4, bf16[2048,128]{1,0:T(8,128)(2,1)} %copy-done.6, bf16[2048,128]{1,0:T(8,128)(2,1)} %copy-done.5, bf16[2048,128]{1,0:T(8,128)(2,1)S(1)} %copy-done.3), kind=kLoop, calls=%fused_computation.1 | loop fusion | flops 1310720 | bytes 1572864 | tf_op jit(solution)/shard_map/convert_element_type | solution.py:455
  131.1 1.9 %collective-permute-done.18.p3 = bf16[640,128]{1,0:T(8,128)(2,1)S(1)} collective-permute-done((bf16[640,128]{1,0:T(8,128)(2,1)S(1)}, bf16[640,128]{1,0:T(8,128)(2,1)S(1)}, u32[]{:S(2)}, u32[]{:S(2)}) %collective-permute-start.18) | collective-permute-done | bytes 163872 | tf_op jit(solution)/shard_map/ppermute | solution.py:372
  133.1 6.2 %collective-permute-done.17.p2 = bf16[640,128]{1,0:T(8,128)(2,1)S(1)} collective-permute-done((bf16[640,128]{1,0:T(8,128)(2,1)S(1)}, bf16[640,128]{1,0:T(8,128)(2,1)S(1)}, u32[]{:S(2)}, u32[]{:S(2)}) %collective-permute-start.17) | collective-permute-done | bytes 163872 | tf_op jit(solution)/shard_map/ppermute | solution.py:372
  140.0 2.4 %unpack.1 = (f32[2048,128]{1,0:T(8,128)}, f32[128,512]{1,0:T(8,128)}) custom-call(s32[1]{0:T(128)} %bitcast.17.y_ref, bf16[640,128]{1,0:T(8,128)(2,1)} %copy-done.8, bf16[640,128]{1,0:T(8,128)(2,1)} %copy-done.18, bf16[640,128]{1,0:T(8,128)(2,1)} %copy-done.17, bf16[640,128]{1,0:T(8,128)(2,1)} %copy-done.16), custom_call_target="tpu_custom_call" | custom-call | tf_op jit(solution)/shard_map/unpack/pallas_call | solution.py:360
  143.1 3.1 %add_rows.1 = f32[2048,128]{1,0:T(8,128)} custom-call(s32[12,128]{1,0:T(8,128)} %reshape.59.req_ref, bf16[1536,128]{1,0:T(8,128)(2,1)} %bitcast.30), custom_call_target="tpu_custom_call" | custom-call | tf_op jit(solution)/shard_map/add_rows/pallas_call | solution.py:338
  (68 shorter events, 16.8 us)
Async XLA Ops:
  27.6 20.2 %all-to-all-start.1 = ((bf16[64,24,128]{2,1,0:T(8,128)(2,1)}), bf16[64,24,128]{2,1,0:T(8,128)(2,1)S(1)}, u32[]{:S(2)}, u32[]{:S(2)}) async-start(bf16[64,24,128]{2,1,0:T(8,128)(2,1)} %bitcast.31), calls=%async_computation.1 | async-start | bytes 786432 | tf_op jit(solution)/shard_map/all_to_all | solution.py:432
  32.9 21.6 %collective-permute-start.5 = (bf16[1024,128]{1,0:T(8,128)(2,1)S(1)}, bf16[1024,128]{1,0:T(8,128)(2,1)S(1)}, u32[]{:S(2)}, u32[]{:S(2)}) collective-permute-start(bf16[1024,128]{1,0:T(8,128)(2,1)S(1)} %copy-done.7), channel_id=1, source_target_pairs={{0,1},{1,2},{2,3},{3,0},{4,5},{5,6},{6,7},{7,4},{8,9},{9,10},{10,1... | collective-permute-start | bytes 786440 | tf_op jit(solution)/shard_map/ppermute | solution.py:372
  34.2 21.5 %collective-permute-start.4 = (bf16[1024,128]{1,0:T(8,128)(2,1)S(1)}, bf16[1024,128]{1,0:T(8,128)(2,1)S(1)}, u32[]{:S(2)}, u32[]{:S(2)}) collective-permute-start(bf16[1024,128]{1,0:T(8,128)(2,1)S(1)} %copy-done.7), channel_id=1, source_target_pairs={{0,2},{1,3},{2,0},{3,1},{4,6},{5,7},{6,4},{7,5},{8,10},{9,11},{10,... | collective-permute-start | bytes 786440 | tf_op jit(solution)/shard_map/ppermute | solution.py:372
  36.6 19.1 %collective-permute-start.3 = (bf16[1024,128]{1,0:T(8,128)(2,1)S(1)}, bf16[1024,128]{1,0:T(8,128)(2,1)S(1)}, u32[]{:S(2)}, u32[]{:S(2)}) collective-permute-start(bf16[1024,128]{1,0:T(8,128)(2,1)S(1)} %copy-done.7), channel_id=1, source_target_pairs={{0,3},{1,0},{2,1},{3,2},{4,7},{5,4},{6,5},{7,6},{8,11},{9,8},{10,9... | collective-permute-start | bytes 786440 | tf_op jit(solution)/shard_map/ppermute | solution.py:372
  50.9 8.2 %collective-permute-start.2 = (bf16[1024,128]{1,0:T(8,128)(2,1)}, bf16[1024,128]{1,0:T(8,128)(2,1)S(1)}, u32[]{:S(2)}, u32[]{:S(2)}) collective-permute-start(bf16[1024,128]{1,0:T(8,128)(2,1)} %place.1.x0), channel_id=1, source_target_pairs={{0,1},{1,2},{2,3},{3,0},{4,5},{5,6},{6,7},{7,4},{8,9},{9,10},{10,1... | collective-permute-start | bytes 786440 | tf_op jit(solution)/shard_map/ppermute | solution.py:372
  52.1 13.6 %collective-permute-start.1 = (bf16[1024,128]{1,0:T(8,128)(2,1)}, bf16[1024,128]{1,0:T(8,128)(2,1)S(1)}, u32[]{:S(2)}, u32[]{:S(2)}) collective-permute-start(bf16[1024,128]{1,0:T(8,128)(2,1)} %place.1.x0), channel_id=1, source_target_pairs={{0,2},{1,3},{2,0},{3,1},{4,6},{5,7},{6,4},{7,5},{8,10},{9,11},{10,... | collective-permute-start | bytes 786440 | tf_op jit(solution)/shard_map/ppermute | solution.py:372
  54.6 11.3 %copy-start.10 = (bf16[1024,128]{1,0:T(8,128)(2,1)}, bf16[1024,128]{1,0:T(8,128)(2,1)S(1)}, u32[]{:S(2)}) copy-start(bf16[1024,128]{1,0:T(8,128)(2,1)S(1)} %collective-permute-done.5.g3) | copy-start | bytes 786436
  54.6 11.3 %collective-permute-start = (bf16[1024,128]{1,0:T(8,128)(2,1)}, bf16[1024,128]{1,0:T(8,128)(2,1)S(1)}, u32[]{:S(2)}, u32[]{:S(2)}) collective-permute-start(bf16[1024,128]{1,0:T(8,128)(2,1)} %place.1.x0), channel_id=1, source_target_pairs={{0,3},{1,0},{2,1},{3,2},{4,7},{5,4},{6,5},{7,6},{8,11},{9,8},{10,9... | collective-permute-start | bytes 786440 | tf_op jit(solution)/shard_map/ppermute | solution.py:372
  55.7 10.1 %copy-start.11 = (bf16[1024,128]{1,0:T(8,128)(2,1)}, bf16[1024,128]{1,0:T(8,128)(2,1)S(1)}, u32[]{:S(2)}) copy-start(bf16[1024,128]{1,0:T(8,128)(2,1)S(1)} %collective-permute-done.4.g2) | copy-start | bytes 786436
  55.7 10.1 %copy-start.12 = (bf16[1024,128]{1,0:T(8,128)(2,1)}, bf16[1024,128]{1,0:T(8,128)(2,1)S(1)}, u32[]{:S(2)}) copy-start(bf16[1024,128]{1,0:T(8,128)(2,1)S(1)} %collective-permute-done.3.g1) | copy-start | bytes 786436
  59.1 6.7 %copy-start.13 = (bf16[1024,128]{1,0:T(8,128)(2,1)}, bf16[1024,128]{1,0:T(8,128)(2,1)S(1)}, u32[]{:S(2)}) copy-start(bf16[1024,128]{1,0:T(8,128)(2,1)S(1)} %collective-permute-done.2.x3) | copy-start | bytes 786436
  78.3 3.4 %collective-permute-start.8 = (bf16[1280,128]{1,0:T(8,128)(2,1)}, bf16[1280,128]{1,0:T(8,128)(2,1)S(1)}, u32[]{:S(2)}, u32[]{:S(2)}) collective-permute-start(bf16[1280,128]{1,0:T(8,128)(2,1)} %get-tuple-element.29), channel_id=1, source_target_pairs={{0,32},{32,0},{64,96},{96,64},{128,160},{160,128},{192,224},{224,1... | collective-permute-start | bytes 983048 | tf_op jit(solution)/shard_map/ppermute | solution.py:372
  82.9 7.8 %copy-start.19 = (bf16[2048,128]{1,0:T(8,128)(2,1)S(1)}, bf16[2048,128]{1,0:T(8,128)(2,1)}, u32[]{:S(2)}) copy-start(bf16[2048,128]{1,0:T(8,128)(2,1)} %get-tuple-element.27) | copy-start | bytes 1572868
  82.9 5.5 %collective-permute-start.9 = (bf16[640,128]{1,0:T(8,128)(2,1)S(1)}, bf16[640,128]{1,0:T(8,128)(2,1)S(1)}, u32[]{:S(2)}, u32[]{:S(2)}) collective-permute-start(bf16[640,128]{1,0:T(8,128)(2,1)S(1)} %fusion), channel_id=1, source_target_pairs={{0,64},{32,96},{64,0},{96,32},{128,192},{160,224},{192,128},{224,1... | collective-permute-start | bytes 491528 | tf_op jit(solution)/shard_map/ppermute | solution.py:372
  83.8 14.6 %collective-permute-start.11 = (bf16[2048,128]{1,0:T(8,128)(2,1)}, bf16[2048,128]{1,0:T(8,128)(2,1)S(1)}, u32[]{:S(2)}, u32[]{:S(2)}) collective-permute-start(bf16[2048,128]{1,0:T(8,128)(2,1)} %get-tuple-element.30), channel_id=1, source_target_pairs={{0,2},{1,3},{2,0},{3,1},{4,6},{5,7},{6,4},{7,5},{8,10},{9,11},{10,... | collective-permute-start | bytes 1572872 | tf_op jit(solution)/shard_map/ppermute | solution.py:372
  88.5 9.8 %collective-permute-start.10 = (bf16[320,128]{1,0:T(8,128)(2,1)S(1)}, bf16[320,128]{1,0:T(8,128)(2,1)S(1)}, u32[]{:S(2)}, u32[]{:S(2)}) collective-permute-start(bf16[320,128]{1,0:T(8,128)(2,1)S(1)} %fusion.2), channel_id=1, source_target_pairs={{0,192},{32,224},{64,128},{96,160},{128,64},{160,96},{192,0},{224,... | collective-permute-start | bytes 245768 | tf_op jit(solution)/shard_map/ppermute | solution.py:372
  89.8 20.8 %collective-permute-start.6 = (bf16[2048,128]{1,0:T(8,128)(2,1)}, bf16[2048,128]{1,0:T(8,128)(2,1)S(1)}, u32[]{:S(2)}, u32[]{:S(2)}) collective-permute-start(bf16[2048,128]{1,0:T(8,128)(2,1)} %get-tuple-element.26), channel_id=1, source_target_pairs={{0,1},{1,2},{2,3},{3,0},{4,5},{5,6},{6,7},{7,4},{8,9},{9,10},{10,1... | collective-permute-start | bytes 1572872 | tf_op jit(solution)/shard_map/ppermute | solution.py:372
  90.8 19.8 %collective-permute-start.7 = (bf16[2048,128]{1,0:T(8,128)(2,1)S(1)}, bf16[2048,128]{1,0:T(8,128)(2,1)S(1)}, u32[]{:S(2)}, u32[]{:S(2)}) collective-permute-start(bf16[2048,128]{1,0:T(8,128)(2,1)S(1)} %copy-done.19), channel_id=1, source_target_pairs={{0,3},{1,0},{2,1},{3,2},{4,7},{5,4},{6,5},{7,6},{8,11},{9,8},{10,9... | collective-permute-start | bytes 1572872 | tf_op jit(solution)/shard_map/ppermute | solution.py:372
  98.3 12.2 %copy-start.4 = (bf16[2048,128]{1,0:T(8,128)(2,1)}, bf16[2048,128]{1,0:T(8,128)(2,1)S(1)}, u32[]{:S(2)}) copy-start(bf16[2048,128]{1,0:T(8,128)(2,1)S(1)} %collective-permute-done.11.d3) | copy-start | bytes 1572868
  98.4 8.9 %copy-start.9 = (s32[64,1,128]{2,1,0:T(1,128)S(1)}, s32[64,1,128]{2,1,0:T(1,128)}, u32[]{:S(2)}) copy-start(s32[64,1,128]{2,1,0:T(1,128)} %all_to_all.21) | copy-start | bytes 98308
  98.4 5.3 %collective-permute-start.14 = (bf16[320,128]{1,0:T(8,128)(2,1)S(1)}, bf16[320,128]{1,0:T(8,128)(2,1)S(1)}, u32[]{:S(2)}, u32[]{:S(2)}) collective-permute-start(bf16[320,128]{1,0:T(8,128)(2,1)S(1)} %fusion.1), channel_id=1, source_target_pairs={{0,12},{4,8},{8,4},{12,0},{16,28},{20,24},{24,20},{28,16},{1,13},{... | collective-permute-start | bytes 245768 | tf_op jit(solution)/shard_map/ppermute | solution.py:372
  100.0 6.1 %collective-permute-start.13 = (bf16[320,128]{1,0:T(8,128)(2,1)S(1)}, bf16[320,128]{1,0:T(8,128)(2,1)S(1)}, u32[]{:S(2)}, u32[]{:S(2)}) collective-permute-start(bf16[320,128]{1,0:T(8,128)(2,1)S(1)} %fusion.1), channel_id=1, source_target_pairs={{0,8},{4,12},{8,0},{12,4},{16,24},{20,28},{24,16},{28,20},{1,9},{5... | collective-permute-start | bytes 245768 | tf_op jit(solution)/shard_map/ppermute | solution.py:372
  101.0 5.1 %collective-permute-start.12 = (bf16[320,128]{1,0:T(8,128)(2,1)S(1)}, bf16[320,128]{1,0:T(8,128)(2,1)S(1)}, u32[]{:S(2)}, u32[]{:S(2)}) collective-permute-start(bf16[320,128]{1,0:T(8,128)(2,1)S(1)} %fusion.1), channel_id=1, source_target_pairs={{0,4},{4,0},{8,12},{12,8},{16,20},{20,16},{24,28},{28,24},{1,5},{5... | collective-permute-start | bytes 245768 | tf_op jit(solution)/shard_map/ppermute | solution.py:372
  106.2 8.1 %collective-permute-start.15 = (bf16[320,128]{1,0:T(8,128)(2,1)S(1)}, bf16[320,128]{1,0:T(8,128)(2,1)S(1)}, u32[]{:S(2)}, u32[]{:S(2)}) collective-permute-start(bf16[320,128]{1,0:T(8,128)(2,1)S(1)} %add_convert_fusion.2), channel_id=1, source_target_pairs={{0,28},{4,24},{8,20},{12,16},{16,12},{20,8},{24,4},{28,0},{1,29},{... | collective-permute-start | bytes 245768 | tf_op jit(solution)/shard_map/ppermute | solution.py:372
  114.3 14.8 %copy-start.3 = (bf16[2048,128]{1,0:T(8,128)(2,1)S(1)}, bf16[2048,128]{1,0:T(8,128)(2,1)}, u32[]{:S(2)}) copy-start(bf16[2048,128]{1,0:T(8,128)(2,1)} %get-tuple-element.33.d0) | copy-start | bytes 1572868
  114.4 14.8 %copy-start = (bf16[1024,128]{1,0:T(8,128)(2,1)S(1)}, bf16[1024,128]{1,0:T(8,128)(2,1)}, u32[]{:S(2)}) copy-start(bf16[1024,128]{1,0:T(8,128)(2,1)} %place.1.x0) | copy-start | bytes 786436
  114.4 28.0 %all-to-all-start.2 = ((bf16[64,24,128]{2,1,0:T(8,128)(2,1)}), bf16[64,24,128]{2,1,0:T(8,128)(2,1)S(1)}, u32[]{:S(2)}, u32[]{:S(2)}) async-start(bf16[64,24,128]{2,1,0:T(8,128)(2,1)} %bitcast.32), calls=%async_computation.2 | async-start | bytes 786432 | tf_op jit(solution)/shard_map/all_to_all | solution.py:445
  124.2 7.0 %copy-start.8 = (bf16[640,128]{1,0:T(8,128)(2,1)}, bf16[640,128]{1,0:T(8,128)(2,1)S(1)}, u32[]{:S(2)}) copy-start(bf16[640,128]{1,0:T(8,128)(2,1)S(1)} %all_gather.3.p0) | copy-start | bytes 491524
  124.2 8.9 %collective-permute-start.18 = (bf16[640,128]{1,0:T(8,128)(2,1)S(1)}, bf16[640,128]{1,0:T(8,128)(2,1)S(1)}, u32[]{:S(2)}, u32[]{:S(2)}) collective-permute-start(bf16[640,128]{1,0:T(8,128)(2,1)S(1)} %all_gather.3.p0), channel_id=1, source_target_pairs={{0,64},{32,96},{64,128},{96,160},{128,192},{160,224},{192,0},{224,... | collective-permute-start | bytes 491528 | tf_op jit(solution)/shard_map/ppermute | solution.py:372
  125.5 13.8 %collective-permute-start.17 = (bf16[640,128]{1,0:T(8,128)(2,1)S(1)}, bf16[640,128]{1,0:T(8,128)(2,1)S(1)}, u32[]{:S(2)}, u32[]{:S(2)}) collective-permute-start(bf16[640,128]{1,0:T(8,128)(2,1)S(1)} %all_gather.3.p0), channel_id=1, source_target_pairs={{0,128},{32,160},{64,192},{96,224},{128,0},{160,32},{192,64},{224,... | collective-permute-start | bytes 491528 | tf_op jit(solution)/shard_map/ppermute | solution.py:372
  128.1 11.2 %collective-permute-start.16 = (bf16[640,128]{1,0:T(8,128)(2,1)S(1)}, bf16[640,128]{1,0:T(8,128)(2,1)S(1)}, u32[]{:S(2)}, u32[]{:S(2)}) collective-permute-start(bf16[640,128]{1,0:T(8,128)(2,1)S(1)} %all_gather.3.p0), channel_id=1, source_target_pairs={{0,192},{32,224},{64,0},{96,32},{128,64},{160,96},{192,128},{224,1... | collective-permute-start | bytes 491528 | tf_op jit(solution)/shard_map/ppermute | solution.py:372
  133.1 6.2 %copy-start.16 = (bf16[640,128]{1,0:T(8,128)(2,1)}, bf16[640,128]{1,0:T(8,128)(2,1)S(1)}, u32[]{:S(2)}) copy-start(bf16[640,128]{1,0:T(8,128)(2,1)S(1)} %collective-permute-done.18.p3) | copy-start | bytes 491524
  (9 other events, 11.4 us)

commit v9 on v8

--- a/solution.py
+++ b/solution.py
@@ -23,11 +23,24 @@
 I32 = jnp.int32
 VM = pl.BlockSpec(memory_space=pltpu.VMEM)
 SM = pl.BlockSpec(memory_space=pltpu.SMEM)
+ANY = pl.BlockSpec(memory_space=pl.ANY)
 PARAMS = pltpu.CompilerParams(vmem_limit_bytes=56 * 1024 * 1024)
 
 
 def iota(shape, dim):
     return lax.broadcasted_iota(I32, shape, dim)
+
+
+def begin(pairs, sems):
+    copies = [pltpu.make_async_copy(a, b, sems.at[i]) for i, (a, b) in enumerate(pairs)]
+    for copy in copies:
+        copy.start()
+    return copies
+
+
+def finish(copies):
+    for copy in copies:
+        copy.wait()
 
 
 def dot(a, b, ca, cb):
@@ -111,8 +124,9 @@
     return jnp.transpose(wide)
 
 
-def place_kernel(slot_ref, back_ref, x_ref):
+def place_kernel(slot_ref, back_any, x_ref, back_ref, sems):
     half = SLOTS // 2
+    finish(begin([(back_any, back_ref)], sems))
     both = jnp.concatenate([back_ref[:half, :], back_ref[half:, :]], axis=1)
     for b0 in range(0, TOK // 128, 2):
         hots, uppers = [], []
@@ -133,20 +147,24 @@
     return pl.pallas_call(
         place_kernel,
         out_shape=jax.ShapeDtypeStruct((TOK, 128), BF),
-        in_specs=[VM, VM],
+        in_specs=[VM, ANY],
         out_specs=VM,
+        scratch_shapes=[pltpu.VMEM((SLOTS, 128), BF), pltpu.SemaphoreType.DMA((1,))],
         compiler_params=PARAMS,
         name="place",
     )(slot, back)
 
 
 def layer_kernel(
-    pos_ref, core_ref, seg_ref, x0, x1, x2, x3, g0, g1, g2, g3, win_ref, wout_ref,
-    mine_ref, other_ref, c0, c1, c2, c3,
+    pos_ref, core_ref, seg_ref, xa0, xa1, xa2, xa3, ga0, ga1, ga2, ga3, win_ref, wout_ref,
+    mine_ref, other_ref, ca0, ca1, ca2, ca3,
     w, wo, pre, act, segc, aw, dsil, dkv, du, u_ref, y_ref, dp_ref, dw_ref,
+    x_in, g_in, c_out, x_sems, g_sems, d_sems, z_sems,
 ):
-    xs, gs = (x0, x1, x2, x3), (g0, g1, g2, g3)
-    both = (c0, c1, c2, c3)
+    xs, gs, both = ([ref.at[k] for k in range(NT)] for ref in (x_in, g_in, c_out))
+    targets = (ca0, ca1, ca2, ca3)
+    x_copies = begin(list(zip((xa0, xa1, xa2, xa3), xs)), x_sems)
+    g_copies = begin(list(zip((ga0, ga1, ga2, ga3), gs)), g_sems)
     me, core = pos_ref[0], core_ref[0]
     for k in range(NT):
         at = pl.multiple_of(lax.rem(me + k, NT) * 128, 128)
@@ -166,6 +184,7 @@
         scale = lax.rsqrt(var * (1.0 / D) + 1e-05)
         return [v * scale for v in x], scale
 
+    finish(x_copies)
     step = 64
     for q in range(TOK // QB):
         lo = q * QB
@@ -181,6 +200,7 @@
             act[r0 : r0 + step, :] = ps.astype(BF)
             pre[r0 : r0 + step, :] = s + ps * (1.0 - s)
 
+    finish(g_copies)
     dkv[...] = jnp.zeros((TOK, 256), F32)
     for q in range(TOK // QB):
         lo = q * QB
@@ -247,15 +267,19 @@
             for k in range(NT):
                 both[k][lo + r : lo + r + step, :] = ((d[k] - m1 - n[k] * m2) * scale).astype(BF)
 
+    out_copies = begin([(both[k].at[0:TOK], targets[k].at[0:TOK]) for k in range(NT)], d_sems)
+    for k in range(NT):
+        both[k][TOK:, :] = dot(y_ref[...], wo[:, k * 128 : (k + 1) * 128], 1, 0).astype(BF)
+    out_copies += begin([(both[k].at[TOK : 2 * TOK], targets[k].at[TOK : 2 * TOK]) for k in range(NT)], z_sems)
     for k in range(NT):
         at = pl.multiple_of(lax.rem(me + k, NT) * 128, 128)
         dw = dot(u_ref[:, k * 128 : (k + 1) * 128], dp_ref[...], 0, 0)
         for c in range(4):
             dw_ref[pl.ds(pl.multiple_of(c * 512 + at, 128), 128), :] = dw[:, c * 128 : (c + 1) * 128]
         dw_ref[pl.ds(pl.multiple_of(2048 + at, 128), 128), :] = dot(y_ref[...], gs[k][...], 0, 0)
-        both[k][TOK:, :] = dot(y_ref[...], wo[:, k * 128 : (k + 1) * 128], 1, 0).astype(BF)
     mine_ref[...] = dw_ref[pl.ds(pl.multiple_of(core * 1280, 1280), 1280), :]
     other_ref[...] = dw_ref[pl.ds(pl.multiple_of(1280 - core * 1280, 1280), 1280), :].astype(BF)
+    finish(out_copies)
 
 
 def layer(pos, core, seg, xs, gs, w_in, w_out):
@@ -264,8 +288,8 @@
         layer_kernel,
         out_shape=(jax.ShapeDtypeStruct((1280, 128), F32), jax.ShapeDtypeStruct((1280, 128), BF))
         + (pair,) * 4,
-        in_specs=[SM, SM] + [VM] * 11,
-        out_specs=(VM,) * 6,
+        in_specs=[SM, SM, VM] + [ANY] * 8 + [VM] * 2,
+        out_specs=(VM,) * 2 + (ANY,) * 4,
         scratch_shapes=[
             pltpu.VMEM((D, 512), BF),
             pltpu.VMEM((HD, D), BF),
@@ -280,6 +304,13 @@
             pltpu.VMEM((TOK, HD), BF),
             pltpu.VMEM((TOK, 512), BF),
             pltpu.VMEM((2560, 128), F32),
+            pltpu.VMEM((NT, TOK, 128), BF),
+            pltpu.VMEM((NT, TOK, 128), BF),
+            pltpu.VMEM((NT, 2 * TOK, 128), BF),
+            pltpu.SemaphoreType.DMA((NT,)),
+            pltpu.SemaphoreType.DMA((NT,)),
+            pltpu.SemaphoreType.DMA((NT,)),
+            pltpu.SemaphoreType.DMA((NT,)),
         ],
         compiler_params=PARAMS,
         name="layer",
@@ -304,7 +335,9 @@
     return [dot(hot_where(high, s, low), pair, 1, 0) for s in range(size // 128)]
 
 
-def slots_kernel(slot_ref, grad_ref, d0, d1, d2, d3, out_ref):
+def slots_kernel(slot_ref, grad_ref, c0, c1, c2, c3, out_ref, parts, sems):
+    finish(begin([(c.at[0:TOK], parts.at[k]) for k, c in enumerate((c0, c1, c2, c3))], sems))
+    d0, d1, d2, d3 = (parts.at[k] for k in range(NT))
     dx = grad_ref[...].astype(F32) + (
         d0[...].astype(F32) + d1[...].astype(F32) + d2[...].astype(F32) + d3[...].astype(F32)
     )
@@ -315,20 +348,20 @@
 
 
 def to_slots(slot, grad, parts):
-    top = pl.BlockSpec((TOK, 128), lambda i: (0, 0))
     return pl.pallas_call(
         slots_kernel,
         out_shape=jax.ShapeDtypeStruct((SLOTS, 128), BF),
-        grid=(1,),
-        in_specs=[pl.BlockSpec((TOK // 128, 128), lambda i: (0, 0))] + [top] * 5,
-        out_specs=pl.BlockSpec((SLOTS, 128), lambda i: (0, 0)),
+        in_specs=[VM, VM] + [ANY] * 4,
+        out_specs=VM,
+        scratch_shapes=[pltpu.VMEM((NT, TOK, 128), BF), pltpu.SemaphoreType.DMA((NT,))],
         compiler_params=PARAMS,
         name="to_slots",
     )(slot, grad, *parts)
 
 
-def add_rows_kernel(req_ref, arrived_ref, out_ref):
+def add_rows_kernel(req_ref, arrived_any, out_ref, arrived_ref, sems):
     half = ROWS // 2
+    finish(begin([(arrived_any, arrived_ref)], sems))
     for s, both in enumerate(spread(req_ref, SLOTS // 128, half, arrived_ref[...].astype(F32))):
         out_ref[s * 128 : (s + 1) * 128, :] = both[:, :128]
         out_ref[half + s * 128 : half + (s + 1) * 128, :] = both[:, 128:]
@@ -338,15 +371,19 @@
     return pl.pallas_call(
         add_rows_kernel,
         out_shape=jax.ShapeDtypeStruct((ROWS, 128), F32),
-        in_specs=[VM, VM],
+        in_specs=[VM, ANY],
         out_specs=VM,
+        scratch_shapes=[pltpu.VMEM((SLOTS, 128), BF), pltpu.SemaphoreType.DMA((1,))],
         compiler_params=PARAMS,
         name="add_rows",
     )(req, arrived)
 
 
-def unpack_kernel(y_ref, p0, p1, p2, p3, in_ref, out_ref, whole):
-    for k, p in enumerate((p0, p1, p2, p3)):
+def unpack_kernel(y_ref, p0, p1, p2, p3, in_ref, out_ref, whole, parts, sems):
+    copies = begin([(p, parts.at[k]) for k, p in enumerate((p0, p1, p2, p3))], sems)
+    for k in range(NT):
+        copies[k].wait()
+        p = parts.at[k]
         half, quarter = y_place(lax.rem(y_ref[0] + k, 4))
         for core in range(2):
             at = pl.multiple_of(half * 640 + quarter * 320 + core * 1280, 320)
@@ -360,9 +397,13 @@
     return pl.pallas_call(
         unpack_kernel,
         out_shape=(jax.ShapeDtypeStruct((2048, 128), F32), jax.ShapeDtypeStruct((HD, D), F32)),
-        in_specs=[SM] + [VM] * 4,
+        in_specs=[SM] + [ANY] * 4,
         out_specs=(VM, VM),
-        scratch_shapes=[pltpu.VMEM((2560, 128), F32)],
+        scratch_shapes=[
+            pltpu.VMEM((2560, 128), F32),
+            pltpu.VMEM((NT, 640, 128), BF),
+            pltpu.SemaphoreType.DMA((NT,)),
+        ],
         compiler_params=PARAMS,
         name="unpack",
     )(y, *parts)
@@ -414,12 +455,14 @@
     return total.astype(BF)
 
 
-def gather_weights(total):
+def gather_weights(total, add):
     y = (lax.axis_index("table") // 2).astype(I32).reshape(1)
     pairs = [[2 * i, 2 * i + 1] for i in range(4)]
     both = lax.all_gather(total, "table", axis=0, tiled=True, axis_index_groups=pairs)
     parts = [both] + [shift(both, "table", lambda i, k=k: (i - 2 * k) % 8, 8) for k in range(1, 4)]
-    return unpack(y, parts)
+    table_grad = add()
+    parts, table_grad = lax.optimization_barrier((parts, table_grad))
+    return unpack(y, parts), table_grad
 
 
 def body(table, owner, local_row, segment_ids, proj_in, proj_out, grad_out):
@@ -443,7 +486,9 @@
     total = add_step(total, 7)
     grads, total = lax.optimization_barrier((grads, total))
     arrived = lax.all_to_all(grads.reshape(NOWN, CAP, 128), BOTH, split_axis=0, concat_axis=0, tiled=True)
-    grad_in, grad_outw = gather_weights(total)
+    (grad_in, grad_outw), table_grad = gather_weights(
+        total, lambda: add_rows(flat, arrived.reshape(SLOTS, 128))
+    )
     layer_out = (
         x.astype(F32)
         + (
@@ -453,7 +498,6 @@
             + cparts[3][TOK:].astype(F32)
         )
     ).astype(BF)
-    table_grad = add_rows(flat, arrived.reshape(SLOTS, 128))
     return layer_out, table_grad, grad_in.reshape(4, D, 128), grad_outw
 
 

time: 147 us -> 149 us (1.014)
  Pallas kernels: 27.1 us -> 31.6 us
  waiting for transfers between devices: 44.7 us -> 42.4 us
    ppermute x19, waiting for transfers between devices: 34.7 us -> 26.6 us  [shift(): return lax.ppermute(x, axis, [(i, fn(i)) for i in range(n)])]
    all_to_all x1, waiting for transfers between devices: 0.01 us -> 5.81 us  [body(): lax.all_to_all(grads.reshape(NOWN, CAP, 128), BOTH, split_axis=0, concat_...]
    pallas_call x1, Pallas kernels: 11.8 us -> 14 us  [layer(): pl.pallas_call(layer_kernel, out_shape=(jax.ShapeDtypeStruct((1280, 128),...]
  transfers between devices with their start and end apart: 21 -> 21, of which waited for: 12 -> 11; matrix products, arithmetic and copies ran while one was open for 2% -> 2% of each run, Pallas kernels for 5% -> 7%
where the time goes in v9:
time: 149 us
  waiting for transfers between devices  42.4 us (28%)
  starting transfers between devices  41.6 us (28%)
  Pallas kernels  31.6 us (21%)
  blocking collectives  24.3 us (16%)
  local copies, waits for them, and re-layouts  4.64 us (3%)
  other arithmetic  3.25 us (2%)
    ppermute x19, starting transfers between devices, shift(): return lax.ppermute(x, axis, [(i, fn(i)) for i in range(n)])  28.5 us
    ppermute x19, waiting for transfers between devices, shift(): return lax.ppermute(x, axis, [(i, fn(i)) for i in range(n)])  26.6 us
    all_to_all x1, blocking collectives, body(): lax.all_to_all(requests, BOTH, split_axis=0, concat_axis=0, tiled=True)  22.3 us
    pallas_call x1, Pallas kernels, layer(): pl.pallas_call(layer_kernel, out_shape=(jax.ShapeDtypeStruct((1280, 128),...  14 us
    all_to_all x1, waiting for transfers between devices, body(): lax.all_to_all(rows.reshape(NOWN, CAP, 128), BOTH, split_axis=0, concat_a...  9.98 us
    all_to_all x1, starting transfers between devices, body(): lax.all_to_all(grads.reshape(NOWN, CAP, 128), BOTH, split_axis=0, concat_...  7.73 us
    all_to_all x1, waiting for transfers between devices, body(): lax.all_to_all(grads.reshape(NOWN, CAP, 128), BOTH, split_axis=0, concat_...  5.81 us
    all_to_all x1, starting transfers between devices, body(): lax.all_to_all(rows.reshape(NOWN, CAP, 128), BOTH, split_axis=0, concat_a...  5.29 us
  transfers between devices with their start and end apart: 21, of which 11 were waited for; matrix products, arithmetic and copies ran while one was open for 2% of the time, Pallas kernels for 7%

profile of v9, /device:TPU:1, one launch (start us, length us, event | category | flops | bytes accessed | tf_op | source)
XLA Modules:
  0.0 148.7 jit_solution(3389680862567525496)
XLA Ops:
  0.6 1.8 %route.1 = (s32[64,128]{1,0:T(8,128)}, s32[8,128]{1,0:T(8,128)}) custom-call(s32[8,128]{1,0:T(8,128)} %bitcast.38, s32[8,128]{1,0:T(8,128)} %bitcast.39), custom_call_target="tpu_custom_call" | custom-call | tf_op jit(solution)/shard_map/route/pallas_call | solution.py:75
  2.5 22.3 %all_to_all.21 = s32[64,1,128]{2,1,0:T(1,128)} all-to-all(s32[64,1,128]{2,1,0:T(1,128)} %bitcast.37), channel_id=1, replica_groups=mesh['table'=8,'seq'=8,'tensor'=4] {'table','seq'}, dimensions={0} | all-to-all | bytes 65536 | tf_op jit(solution)/shard_map/all_to_all | solution.py:473
  24.7 2.9 %fetch.1 = bf16[1536,128]{1,0:T(8,128)(2,1)} custom-call(s32[64,128]{1,0:T(8,128)} %bitcast.35, bf16[2048,128]{1,0:T(8,128)(2,1)} %table_ref.1), custom_call_target="tpu_custom_call" | custom-call | tf_op jit(solution)/shard_map/fetch/pallas_call | solution.py:111
  27.6 5.3 %all-to-all-start.1 = ((bf16[64,24,128]{2,1,0:T(8,128)(2,1)}), bf16[64,24,128]{2,1,0:T(8,128)(2,1)S(1)}, u32[]{:S(2)}, u32[]{:S(2)}) async-start(bf16[64,24,128]{2,1,0:T(8,128)(2,1)} %bitcast.31), calls=%async_computation.1 | async-start | bytes 786432 | tf_op jit(solution)/shard_map/all_to_all | solution.py:475
  34.2 2.5 %collective-permute-start.4 = (bf16[1024,128]{1,0:T(8,128)(2,1)S(1)}, bf16[1024,128]{1,0:T(8,128)(2,1)S(1)}, u32[]{:S(2)}, u32[]{:S(2)}) collective-permute-start(bf16[1024,128]{1,0:T(8,128)(2,1)S(1)} %copy-done.7), channel_id=1, source_target_pairs={{0,2},{1,3},{2,0},{3,1},{4,6},{5,7},{6,4},{7,5},{8,10},{9,11},{10,... | collective-permute-start | bytes 786440 | tf_op jit(solution)/shard_map/ppermute | solution.py:413
  37.8 10.0 %all-to-all-done.1 = bf16[64,24,128]{2,1,0:T(8,128)(2,1)S(1)} async-done(((bf16[64,24,128]{2,1,0:T(8,128)(2,1)}), bf16[64,24,128]{2,1,0:T(8,128)(2,1)S(1)}, u32[]{:S(2)}, u32[]{:S(2)}) %all-to-all-start.1) | async-done | bytes 393248 | tf_op jit(solution)/shard_map/all_to_all | solution.py:475
  48.5 3.0 %place.1.xa0 = bf16[1024,128]{1,0:T(8,128)(2,1)} custom-call(s32[8,128]{1,0:T(8,128)} %get-tuple-element.28.slot_ref, bf16[1536,128]{1,0:T(8,128)(2,1)} %bitcast.29), custom_call_target="tpu_custom_call" | custom-call | tf_op jit(solution)/shard_map/place/pallas_call | solution.py:147
  51.6 1.3 collective-permute-start.2
  52.9 2.5 %collective-permute-start.1 = (bf16[1024,128]{1,0:T(8,128)(2,1)}, bf16[1024,128]{1,0:T(8,128)(2,1)S(1)}, u32[]{:S(2)}, u32[]{:S(2)}) collective-permute-start(bf16[1024,128]{1,0:T(8,128)(2,1)} %place.1.xa0), channel_id=1, source_target_pairs={{0,2},{1,3},{2,0},{3,1},{4,6},{5,7},{6,4},{7,5},{8,10},{9,11},{10,... | collective-permute-start | bytes 786440 | tf_op jit(solution)/shard_map/ppermute | solution.py:413
  56.5 3.4 %collective-permute-done.2.xa3 = bf16[1024,128]{1,0:T(8,128)(2,1)S(1)} collective-permute-done((bf16[1024,128]{1,0:T(8,128)(2,1)}, bf16[1024,128]{1,0:T(8,128)(2,1)S(1)}, u32[]{:S(2)}, u32[]{:S(2)}) %collective-permute-start.2) | collective-permute-done | bytes 262176 | tf_op jit(solution)/shard_map/ppermute | solution.py:413
  59.9 6.6 %collective-permute-done.1.xa2 = bf16[1024,128]{1,0:T(8,128)(2,1)S(1)} collective-permute-done((bf16[1024,128]{1,0:T(8,128)(2,1)}, bf16[1024,128]{1,0:T(8,128)(2,1)S(1)}, u32[]{:S(2)}, u32[]{:S(2)}) %collective-permute-start.1) | collective-permute-done | bytes 262176 | tf_op jit(solution)/shard_map/ppermute | solution.py:413
  67.3 14.0 %layer.1 = (f32[1280,128]{1,0:T(8,128)}, bf16[1280,128]{1,0:T(8,128)(2,1)}, bf16[2048,128]{1,0:T(8,128)(2,1)}, bf16[2048,128]{1,0:T(8,128)(2,1)}, bf16[2048,128]{1,0:T(8,128)(2,1)}, /*index=5*/bf16[2048,128]{1,0:T(8,128)(2,1)}) custom-call(s32[1]{0:T(128)} %bitcast.7.pos_ref, s32[1]{0:T(128)} %bitcast.8.core_ref, s32[1,1024]{1,0:T(1,128)} %seg_ref.1, ...), custom_call_target="tpu_custom_call" | custom-call | tf_op jit(solution)/shard_map/layer/pallas_call | solution.py:287
  81.3 2.0 %collective-permute-start.8 = (bf16[1280,128]{1,0:T(8,128)(2,1)}, bf16[1280,128]{1,0:T(8,128)(2,1)S(1)}, u32[]{:S(2)}, u32[]{:S(2)}) collective-permute-start(bf16[1280,128]{1,0:T(8,128)(2,1)} %get-tuple-element.34), channel_id=1, source_target_pairs={{0,32},{32,0},{64,96},{96,64},{128,160},{160,128},{192,224},{224,1... | collective-permute-start | bytes 983048 | tf_op jit(solution)/shard_map/ppermute | solution.py:413
  83.3 1.5 collective-permute-done.8
  86.8 2.3 %collective-permute-start.11 = (bf16[2048,128]{1,0:T(8,128)(2,1)}, bf16[2048,128]{1,0:T(8,128)(2,1)S(1)}, u32[]{:S(2)}, u32[]{:S(2)}) collective-permute-start(bf16[2048,128]{1,0:T(8,128)(2,1)} %get-tuple-element.35), channel_id=1, source_target_pairs={{0,2},{1,3},{2,0},{3,1},{4,6},{5,7},{6,4},{7,5},{8,10},{9,11},{10,... | collective-permute-start | bytes 1572872 | tf_op jit(solution)/shard_map/ppermute | solution.py:413
  89.1 2.4 %collective-permute-done.9 = bf16[640,128]{1,0:T(8,128)(2,1)S(1)} collective-permute-done((bf16[640,128]{1,0:T(8,128)(2,1)S(1)}, bf16[640,128]{1,0:T(8,128)(2,1)S(1)}, u32[]{:S(2)}, u32[]{:S(2)}) %collective-permute-start.9) | collective-permute-done | bytes 163872 | tf_op jit(solution)/shard_map/ppermute | solution.py:413
  91.5 1.3 collective-permute-start.10
  93.8 1.7 %collective-permute-start.7 = (bf16[2048,128]{1,0:T(8,128)(2,1)S(1)}, bf16[2048,128]{1,0:T(8,128)(2,1)S(1)}, u32[]{:S(2)}, u32[]{:S(2)}) collective-permute-start(bf16[2048,128]{1,0:T(8,128)(2,1)S(1)} %copy-done.19), channel_id=1, source_target_pairs={{0,3},{1,0},{2,1},{3,2},{4,7},{5,4},{6,5},{7,6},{8,11},{9,8},{10,9... | collective-permute-start | bytes 1572872 | tf_op jit(solution)/shard_map/ppermute | solution.py:413
  95.5 5.9 %collective-permute-done.11.c3 = bf16[2048,128]{1,0:T(8,128)(2,1)S(1)} collective-permute-done((bf16[2048,128]{1,0:T(8,128)(2,1)}, bf16[2048,128]{1,0:T(8,128)(2,1)S(1)}, u32[]{:S(2)}, u32[]{:S(2)}) %collective-permute-start.11) | collective-permute-done | bytes 524320 | tf_op jit(solution)/shard_map/ppermute | solution.py:413
  101.4 1.6 %collective-permute-start.14 = (bf16[320,128]{1,0:T(8,128)(2,1)S(1)}, bf16[320,128]{1,0:T(8,128)(2,1)S(1)}, u32[]{:S(2)}, u32[]{:S(2)}) collective-permute-start(bf16[320,128]{1,0:T(8,128)(2,1)S(1)} %fusion.1), channel_id=1, source_target_pairs={{0,12},{4,8},{8,4},{12,0},{16,28},{20,24},{24,20},{28,16},{1,13},{... | collective-permute-start | bytes 245768 | tf_op jit(solution)/shard_map/ppermute | solution.py:413
  105.0 1.7 %collective-permute-done.14 = bf16[320,128]{1,0:T(8,128)(2,1)S(1)} collective-permute-done((bf16[320,128]{1,0:T(8,128)(2,1)S(1)}, bf16[320,128]{1,0:T(8,128)(2,1)S(1)}, u32[]{:S(2)}, u32[]{:S(2)}) %collective-permute-start.14) | collective-permute-done | bytes 81952 | tf_op jit(solution)/shard_map/ppermute | solution.py:413
  106.7 2.4 %collective-permute-done.13 = bf16[320,128]{1,0:T(8,128)(2,1)S(1)} collective-permute-done((bf16[320,128]{1,0:T(8,128)(2,1)S(1)}, bf16[320,128]{1,0:T(8,128)(2,1)S(1)}, u32[]{:S(2)}, u32[]{:S(2)}) %collective-permute-start.13) | collective-permute-done | bytes 81952 | tf_op jit(solution)/shard_map/ppermute | solution.py:413
  110.9 2.7 %collective-permute-done.6.c1 = bf16[2048,128]{1,0:T(8,128)(2,1)S(1)} collective-permute-done((bf16[2048,128]{1,0:T(8,128)(2,1)}, bf16[2048,128]{1,0:T(8,128)(2,1)S(1)}, u32[]{:S(2)}, u32[]{:S(2)}) %collective-permute-start.6) | collective-permute-done | bytes 524320 | tf_op jit(solution)/shard_map/ppermute | solution.py:413
  114.6 3.7 %to_slots.1 = bf16[1536,128]{1,0:T(8,128)(2,1)} custom-call(s32[8,128]{1,0:T(8,128)} %get-tuple-element.28.slot_ref, bf16[1024,128]{1,0:T(8,128)(2,1)} %grad_ref.1, bf16[2048,128]{1,0:T(8,128)(2,1)} %get-tuple-element.38.c0, bf16[2048,128]{1,0:T(8,128)(2,1)} %copy-done.5, bf16[2048,128]{1,0:T(8,128)(2,1)} %copy-done.6, bf16[2048,128]{1,0:T(8,128)(2,1)} %copy-done.4), custom_call_target="tpu_custom_call" | custom-call | tf_op jit(solution)/shard_map/to_slots/pallas_call | solution.py:351
  118.3 7.7 %all-to-all-start.2 = ((bf16[64,24,128]{2,1,0:T(8,128)(2,1)}), bf16[64,24,128]{2,1,0:T(8,128)(2,1)S(1)}, u32[]{:S(2)}, u32[]{:S(2)}) async-start(bf16[64,24,128]{2,1,0:T(8,128)(2,1)} %bitcast.32), calls=%async_computation.2 | async-start | bytes 786432 | tf_op jit(solution)/shard_map/all_to_all | solution.py:488
  126.1 2.0 %all_gather.3.p0 = bf16[640,128]{1,0:T(8,128)(2,1)S(1)} all-gather(bf16[320,128]{1,0:T(8,128)(2,1)S(1)} %add_convert_fusion.1), channel_id=1, replica_groups={{0,32},{64,96},{128,160},{192,224},{1,33},{65,97},{129,161},{193,225},{..., dimensions={0}, use_global_device_ids=true | all-gather | bytes 245760 | tf_op jit(solution)/shard_map/all_gather | solution.py:461
  128.1 1.3 collective-permute-start.18
  129.4 2.6 %collective-permute-start.17 = (bf16[640,128]{1,0:T(8,128)(2,1)S(1)}, bf16[640,128]{1,0:T(8,128)(2,1)S(1)}, u32[]{:S(2)}, u32[]{:S(2)}) collective-permute-start(bf16[640,128]{1,0:T(8,128)(2,1)S(1)} %all_gather.3.p0), channel_id=1, source_target_pairs={{0,128},{32,160},{64,192},{96,224},{128,0},{160,32},{192,64},{224,... | collective-permute-start | bytes 491528 | tf_op jit(solution)/shard_map/ppermute | solution.py:413
  133.1 2.0 %add_convert_fusion = bf16[1024,128]{1,0:T(8,128)(2,1)} fusion(bf16[1024,128]{1,0:T(8,128)(2,1)S(1)} %copy-done, bf16[2048,128]{1,0:T(8,128)(2,1)} %copy-done.4, bf16[2048,128]{1,0:T(8,128)(2,1)} %copy-done.6, bf16[2048,128]{1,0:T(8,128)(2,1)} %copy-done.5, bf16[2048,128]{1,0:T(8,128)(2,1)S(1)} %copy-done.3), kind=kLoop, calls=%fused_computation.1 | loop fusion | flops 1310720 | bytes 1572864 | tf_op jit(solution)/shard_map/convert_element_type | solution.py:500
  135.1 5.8 %all-to-all-done.2 = bf16[64,24,128]{2,1,0:T(8,128)(2,1)S(1)} async-done(((bf16[64,24,128]{2,1,0:T(8,128)(2,1)}), bf16[64,24,128]{2,1,0:T(8,128)(2,1)S(1)}, u32[]{:S(2)}, u32[]{:S(2)}) %all-to-all-start.2) | async-done | bytes 393248 | tf_op jit(solution)/shard_map/all_to_all | solution.py:488
  141.6 3.8 %add_rows.1 = f32[2048,128]{1,0:T(8,128)} custom-call(s32[12,128]{1,0:T(8,128)} %reshape.59.req_ref, bf16[1536,128]{1,0:T(8,128)(2,1)} %bitcast.30), custom_call_target="tpu_custom_call" | custom-call | tf_op jit(solution)/shard_map/add_rows/pallas_call | solution.py:371
  146.2 2.3 %unpack.1 = (f32[2048,128]{1,0:T(8,128)}, f32[128,512]{1,0:T(8,128)}) custom-call(s32[1]{0:T(128)} %bitcast.17.y_ref, bf16[640,128]{1,0:T(8,128)(2,1)} %copy-done.8, bf16[640,128]{1,0:T(8,128)(2,1)} %copy-done.18, bf16[640,128]{1,0:T(8,128)(2,1)} %copy-done.17, bf16[640,128]{1,0:T(8,128)(2,1)} %copy-done.16), custom_call_target="tpu_custom_call" | custom-call | tf_op jit(solution)/shard_map/unpack/pallas_call | solution.py:397
  (68 shorter events, 15.6 us)
Async XLA Ops:
  27.6 5.3 %copy-start.7 = (bf16[1024,128]{1,0:T(8,128)(2,1)S(1)}, bf16[1024,128]{1,0:T(8,128)(2,1)}, u32[]{:S(2)}) copy-start(bf16[1024,128]{1,0:T(8,128)(2,1)} %grad_ref.1) | copy-start | bytes 786436
  27.6 20.2 %all-to-all-start.1 = ((bf16[64,24,128]{2,1,0:T(8,128)(2,1)}), bf16[64,24,128]{2,1,0:T(8,128)(2,1)S(1)}, u32[]{:S(2)}, u32[]{:S(2)}) async-start(bf16[64,24,128]{2,1,0:T(8,128)(2,1)} %bitcast.31), calls=%async_computation.1 | async-start | bytes 786432 | tf_op jit(solution)/shard_map/all_to_all | solution.py:475
  32.9 22.4 %collective-permute-start.5 = (bf16[1024,128]{1,0:T(8,128)(2,1)S(1)}, bf16[1024,128]{1,0:T(8,128)(2,1)S(1)}, u32[]{:S(2)}, u32[]{:S(2)}) collective-permute-start(bf16[1024,128]{1,0:T(8,128)(2,1)S(1)} %copy-done.7), channel_id=1, source_target_pairs={{0,1},{1,2},{2,3},{3,0},{4,5},{5,6},{6,7},{7,4},{8,9},{9,10},{10,1... | collective-permute-start | bytes 786440 | tf_op jit(solution)/shard_map/ppermute | solution.py:413
  34.2 22.3 %collective-permute-start.4 = (bf16[1024,128]{1,0:T(8,128)(2,1)S(1)}, bf16[1024,128]{1,0:T(8,128)(2,1)S(1)}, u32[]{:S(2)}, u32[]{:S(2)}) collective-permute-start(bf16[1024,128]{1,0:T(8,128)(2,1)S(1)} %copy-done.7), channel_id=1, source_target_pairs={{0,2},{1,3},{2,0},{3,1},{4,6},{5,7},{6,4},{7,5},{8,10},{9,11},{10,... | collective-permute-start | bytes 786440 | tf_op jit(solution)/shard_map/ppermute | solution.py:413
  36.6 19.8 %collective-permute-start.3 = (bf16[1024,128]{1,0:T(8,128)(2,1)S(1)}, bf16[1024,128]{1,0:T(8,128)(2,1)S(1)}, u32[]{:S(2)}, u32[]{:S(2)}) collective-permute-start(bf16[1024,128]{1,0:T(8,128)(2,1)S(1)} %copy-done.7), channel_id=1, source_target_pairs={{0,3},{1,0},{2,1},{3,2},{4,7},{5,4},{6,5},{7,6},{8,11},{9,8},{10,9... | collective-permute-start | bytes 786440 | tf_op jit(solution)/shard_map/ppermute | solution.py:413
  51.6 8.3 %collective-permute-start.2 = (bf16[1024,128]{1,0:T(8,128)(2,1)}, bf16[1024,128]{1,0:T(8,128)(2,1)S(1)}, u32[]{:S(2)}, u32[]{:S(2)}) collective-permute-start(bf16[1024,128]{1,0:T(8,128)(2,1)} %place.1.xa0), channel_id=1, source_target_pairs={{0,1},{1,2},{2,3},{3,0},{4,5},{5,6},{6,7},{7,4},{8,9},{9,10},{10,1... | collective-permute-start | bytes 786440 | tf_op jit(solution)/shard_map/ppermute | solution.py:413
  52.9 13.6 %collective-permute-start.1 = (bf16[1024,128]{1,0:T(8,128)(2,1)}, bf16[1024,128]{1,0:T(8,128)(2,1)S(1)}, u32[]{:S(2)}, u32[]{:S(2)}) collective-permute-start(bf16[1024,128]{1,0:T(8,128)(2,1)} %place.1.xa0), channel_id=1, source_target_pairs={{0,2},{1,3},{2,0},{3,1},{4,6},{5,7},{6,4},{7,5},{8,10},{9,11},{10,... | collective-permute-start | bytes 786440 | tf_op jit(solution)/shard_map/ppermute | solution.py:413
  55.3 11.3 %copy-start.10 = (bf16[1024,128]{1,0:T(8,128)(2,1)}, bf16[1024,128]{1,0:T(8,128)(2,1)S(1)}, u32[]{:S(2)}) copy-start(bf16[1024,128]{1,0:T(8,128)(2,1)S(1)} %collective-permute-done.5.ga3) | copy-start | bytes 786436
  55.3 11.3 %collective-permute-start = (bf16[1024,128]{1,0:T(8,128)(2,1)}, bf16[1024,128]{1,0:T(8,128)(2,1)S(1)}, u32[]{:S(2)}, u32[]{:S(2)}) collective-permute-start(bf16[1024,128]{1,0:T(8,128)(2,1)} %place.1.xa0), channel_id=1, source_target_pairs={{0,3},{1,0},{2,1},{3,2},{4,7},{5,4},{6,5},{7,6},{8,11},{9,8},{10,9... | collective-permute-start | bytes 786440 | tf_op jit(solution)/shard_map/ppermute | solution.py:413
  56.5 10.1 %copy-start.11 = (bf16[1024,128]{1,0:T(8,128)(2,1)}, bf16[1024,128]{1,0:T(8,128)(2,1)S(1)}, u32[]{:S(2)}) copy-start(bf16[1024,128]{1,0:T(8,128)(2,1)S(1)} %collective-permute-done.4.ga2) | copy-start | bytes 786436
  56.5 10.1 %copy-start.12 = (bf16[1024,128]{1,0:T(8,128)(2,1)}, bf16[1024,128]{1,0:T(8,128)(2,1)S(1)}, u32[]{:S(2)}) copy-start(bf16[1024,128]{1,0:T(8,128)(2,1)S(1)} %collective-permute-done.3.ga1) | copy-start | bytes 786436
  59.9 6.7 %copy-start.13 = (bf16[1024,128]{1,0:T(8,128)(2,1)}, bf16[1024,128]{1,0:T(8,128)(2,1)S(1)}, u32[]{:S(2)}) copy-start(bf16[1024,128]{1,0:T(8,128)(2,1)S(1)} %collective-permute-done.2.xa3) | copy-start | bytes 786436
  81.3 3.5 %collective-permute-start.8 = (bf16[1280,128]{1,0:T(8,128)(2,1)}, bf16[1280,128]{1,0:T(8,128)(2,1)S(1)}, u32[]{:S(2)}, u32[]{:S(2)}) collective-permute-start(bf16[1280,128]{1,0:T(8,128)(2,1)} %get-tuple-element.34), channel_id=1, source_target_pairs={{0,32},{32,0},{64,96},{96,64},{128,160},{160,128},{192,224},{224,1... | collective-permute-start | bytes 983048 | tf_op jit(solution)/shard_map/ppermute | solution.py:413
  86.0 7.8 %copy-start.19 = (bf16[2048,128]{1,0:T(8,128)(2,1)S(1)}, bf16[2048,128]{1,0:T(8,128)(2,1)}, u32[]{:S(2)}) copy-start(bf16[2048,128]{1,0:T(8,128)(2,1)} %get-tuple-element.32) | copy-start | bytes 1572868
  86.0 5.5 %collective-permute-start.9 = (bf16[640,128]{1,0:T(8,128)(2,1)S(1)}, bf16[640,128]{1,0:T(8,128)(2,1)S(1)}, u32[]{:S(2)}, u32[]{:S(2)}) collective-permute-start(bf16[640,128]{1,0:T(8,128)(2,1)S(1)} %fusion), channel_id=1, source_target_pairs={{0,64},{32,96},{64,0},{96,32},{128,192},{160,224},{192,128},{224,1... | collective-permute-start | bytes 491528 | tf_op jit(solution)/shard_map/ppermute | solution.py:413
  86.8 14.6 %collective-permute-start.11 = (bf16[2048,128]{1,0:T(8,128)(2,1)}, bf16[2048,128]{1,0:T(8,128)(2,1)S(1)}, u32[]{:S(2)}, u32[]{:S(2)}) collective-permute-start(bf16[2048,128]{1,0:T(8,128)(2,1)} %get-tuple-element.35), channel_id=1, source_target_pairs={{0,2},{1,3},{2,0},{3,1},{4,6},{5,7},{6,4},{7,5},{8,10},{9,11},{10,... | collective-permute-start | bytes 1572872 | tf_op jit(solution)/shard_map/ppermute | solution.py:413
  91.5 9.8 %collective-permute-start.10 = (bf16[320,128]{1,0:T(8,128)(2,1)S(1)}, bf16[320,128]{1,0:T(8,128)(2,1)S(1)}, u32[]{:S(2)}, u32[]{:S(2)}) collective-permute-start(bf16[320,128]{1,0:T(8,128)(2,1)S(1)} %fusion.2), channel_id=1, source_target_pairs={{0,192},{32,224},{64,128},{96,160},{128,64},{160,96},{192,0},{224,... | collective-permute-start | bytes 245768 | tf_op jit(solution)/shard_map/ppermute | solution.py:413
  92.8 20.8 %collective-permute-start.6 = (bf16[2048,128]{1,0:T(8,128)(2,1)}, bf16[2048,128]{1,0:T(8,128)(2,1)S(1)}, u32[]{:S(2)}, u32[]{:S(2)}) collective-permute-start(bf16[2048,128]{1,0:T(8,128)(2,1)} %get-tuple-element.31), channel_id=1, source_target_pairs={{0,1},{1,2},{2,3},{3,0},{4,5},{5,6},{6,7},{7,4},{8,9},{9,10},{10,1... | collective-permute-start | bytes 1572872 | tf_op jit(solution)/shard_map/ppermute | solution.py:413
  93.8 19.8 %collective-permute-start.7 = (bf16[2048,128]{1,0:T(8,128)(2,1)S(1)}, bf16[2048,128]{1,0:T(8,128)(2,1)S(1)}, u32[]{:S(2)}, u32[]{:S(2)}) collective-permute-start(bf16[2048,128]{1,0:T(8,128)(2,1)S(1)} %copy-done.19), channel_id=1, source_target_pairs={{0,3},{1,0},{2,1},{3,2},{4,7},{5,4},{6,5},{7,6},{8,11},{9,8},{10,9... | collective-permute-start | bytes 1572872 | tf_op jit(solution)/shard_map/ppermute | solution.py:413
  101.4 12.2 %copy-start.4 = (bf16[2048,128]{1,0:T(8,128)(2,1)}, bf16[2048,128]{1,0:T(8,128)(2,1)S(1)}, u32[]{:S(2)}) copy-start(bf16[2048,128]{1,0:T(8,128)(2,1)S(1)} %collective-permute-done.11.c3) | copy-start | bytes 1572868
  101.4 8.9 %copy-start.9 = (s32[64,1,128]{2,1,0:T(1,128)S(1)}, s32[64,1,128]{2,1,0:T(1,128)}, u32[]{:S(2)}) copy-start(s32[64,1,128]{2,1,0:T(1,128)} %all_to_all.21) | copy-start | bytes 98308
  101.4 5.3 %collective-permute-start.14 = (bf16[320,128]{1,0:T(8,128)(2,1)S(1)}, bf16[320,128]{1,0:T(8,128)(2,1)S(1)}, u32[]{:S(2)}, u32[]{:S(2)}) collective-permute-start(bf16[320,128]{1,0:T(8,128)(2,1)S(1)} %fusion.1), channel_id=1, source_target_pairs={{0,12},{4,8},{8,4},{12,0},{16,28},{20,24},{24,20},{28,16},{1,13},{... | collective-permute-start | bytes 245768 | tf_op jit(solution)/shard_map/ppermute | solution.py:413
  103.0 6.2 %collective-permute-start.13 = (bf16[320,128]{1,0:T(8,128)(2,1)S(1)}, bf16[320,128]{1,0:T(8,128)(2,1)S(1)}, u32[]{:S(2)}, u32[]{:S(2)}) collective-permute-start(bf16[320,128]{1,0:T(8,128)(2,1)S(1)} %fusion.1), channel_id=1, source_target_pairs={{0,8},{4,12},{8,0},{12,4},{16,24},{20,28},{24,16},{28,20},{1,9},{5... | collective-permute-start | bytes 245768 | tf_op jit(solution)/shard_map/ppermute | solution.py:413
  104.0 5.1 %collective-permute-start.12 = (bf16[320,128]{1,0:T(8,128)(2,1)S(1)}, bf16[320,128]{1,0:T(8,128)(2,1)S(1)}, u32[]{:S(2)}, u32[]{:S(2)}) collective-permute-start(bf16[320,128]{1,0:T(8,128)(2,1)S(1)} %fusion.1), channel_id=1, source_target_pairs={{0,4},{4,0},{8,12},{12,8},{16,20},{20,16},{24,28},{28,24},{1,5},{5... | collective-permute-start | bytes 245768 | tf_op jit(solution)/shard_map/ppermute | solution.py:413
  109.2 9.1 %collective-permute-start.15 = (bf16[320,128]{1,0:T(8,128)(2,1)S(1)}, bf16[320,128]{1,0:T(8,128)(2,1)S(1)}, u32[]{:S(2)}, u32[]{:S(2)}) collective-permute-start(bf16[320,128]{1,0:T(8,128)(2,1)S(1)} %add_convert_fusion.2), channel_id=1, source_target_pairs={{0,28},{4,24},{8,20},{12,16},{16,12},{20,8},{24,4},{28,0},{1,29},{... | collective-permute-start | bytes 245768 | tf_op jit(solution)/shard_map/ppermute | solution.py:413
  118.3 14.8 %copy-start.3 = (bf16[2048,128]{1,0:T(8,128)(2,1)S(1)}, bf16[2048,128]{1,0:T(8,128)(2,1)}, u32[]{:S(2)}) copy-start(bf16[2048,128]{1,0:T(8,128)(2,1)} %get-tuple-element.38.c0) | copy-start | bytes 1572868
  118.3 14.8 %copy-start = (bf16[1024,128]{1,0:T(8,128)(2,1)S(1)}, bf16[1024,128]{1,0:T(8,128)(2,1)}, u32[]{:S(2)}) copy-start(bf16[1024,128]{1,0:T(8,128)(2,1)} %place.1.xa0) | copy-start | bytes 786436
  118.3 22.6 %all-to-all-start.2 = ((bf16[64,24,128]{2,1,0:T(8,128)(2,1)}), bf16[64,24,128]{2,1,0:T(8,128)(2,1)S(1)}, u32[]{:S(2)}, u32[]{:S(2)}) async-start(bf16[64,24,128]{2,1,0:T(8,128)(2,1)} %bitcast.32), calls=%async_computation.2 | async-start | bytes 786432 | tf_op jit(solution)/shard_map/all_to_all | solution.py:488
  128.1 7.0 %copy-start.8 = (bf16[640,128]{1,0:T(8,128)(2,1)}, bf16[640,128]{1,0:T(8,128)(2,1)S(1)}, u32[]{:S(2)}) copy-start(bf16[640,128]{1,0:T(8,128)(2,1)S(1)} %all_gather.3.p0) | copy-start | bytes 491524
  128.1 17.3 %collective-permute-start.18 = (bf16[640,128]{1,0:T(8,128)(2,1)S(1)}, bf16[640,128]{1,0:T(8,128)(2,1)S(1)}, u32[]{:S(2)}, u32[]{:S(2)}) collective-permute-start(bf16[640,128]{1,0:T(8,128)(2,1)S(1)} %all_gather.3.p0), channel_id=1, source_target_pairs={{0,64},{32,96},{64,128},{96,160},{128,192},{160,224},{192,0},{224,... | collective-permute-start | bytes 491528 | tf_op jit(solution)/shard_map/ppermute | solution.py:413
  129.4 16.0 %collective-permute-start.17 = (bf16[640,128]{1,0:T(8,128)(2,1)S(1)}, bf16[640,128]{1,0:T(8,128)(2,1)S(1)}, u32[]{:S(2)}, u32[]{:S(2)}) collective-permute-start(bf16[640,128]{1,0:T(8,128)(2,1)S(1)} %all_gather.3.p0), channel_id=1, source_target_pairs={{0,128},{32,160},{64,192},{96,224},{128,0},{160,32},{192,64},{224,... | collective-permute-start | bytes 491528 | tf_op jit(solution)/shard_map/ppermute | solution.py:413
  132.0 13.5 %collective-permute-start.16 = (bf16[640,128]{1,0:T(8,128)(2,1)S(1)}, bf16[640,128]{1,0:T(8,128)(2,1)S(1)}, u32[]{:S(2)}, u32[]{:S(2)}) collective-permute-start(bf16[640,128]{1,0:T(8,128)(2,1)S(1)} %all_gather.3.p0), channel_id=1, source_target_pairs={{0,192},{32,224},{64,0},{96,32},{128,64},{160,96},{192,128},{224,1... | collective-permute-start | bytes 491528 | tf_op jit(solution)/shard_map/ppermute | solution.py:413
  (9 other events, 6.8 us)

commit v10 on v8

--- a/solution.py
+++ b/solution.py
@@ -191,17 +191,30 @@
         for kb in range(k0, lo + QB, QB):
             sc = dot(queries, act[kb : kb + QB, 384:512], 1, 1) * (HD ** (-0.5))
             for j in range(0, QB, 128):
-                same = segc[lo : lo + QB, :] == seg_ref[0:1, kb + j : kb + j + 128].astype(F32)
+                at = kb - k0 + j
+                first, last = 0, QB
+                if kb == lo and j:
+                    first = j
+                if lo - kb == SEQ_MOST and j + 128 < QB:
+                    last = j + 128
+                rows = slice(first, last)
+                same = segc[lo + first : lo + last, :] == seg_ref[0:1, kb + j : kb + j + 128].astype(F32)
                 if kb == lo:
-                    same = same & (iota((QB, 128), 1) + j <= iota((QB, 128), 0))
-                v = sc[:, j : j + 128]
+                    shape = (last - first, 128)
+                    same = same & (iota(shape, 1) + j <= iota(shape, 0) + first)
+                v = sc[rows, j : j + 128]
                 s = 0.5 + 0.5 * jnp.tanh(0.5 * v)
                 vs = v * s
-                at = kb - k0 + j
-                aw[:, at : at + 128] = jnp.where(same, vs * (1.0 / SEQ_MOST), 0.0).astype(BF)
-                dsil[:, at : at + 128] = jnp.where(
+                aw[rows, at : at + 128] = jnp.where(same, vs * (1.0 / SEQ_MOST), 0.0).astype(BF)
+                dsil[rows, at : at + 128] = jnp.where(
                     same, (s + vs * (1.0 - s)) * (HD ** (-0.5) / SEQ_MOST), 0.0
                 )
+                if first:
+                    aw[0:first, at : at + 128] = jnp.zeros((first, 128), BF)
+                    dsil[0:first, at : at + 128] = jnp.zeros((first, 128), F32)
+                if last < QB:
+                    aw[last:QB, at : at + 128] = jnp.zeros((QB - last, 128), BF)
+                    dsil[last:QB, at : at + 128] = jnp.zeros((QB - last, 128), F32)
         o = dot(aw[:, 0:width], act[k0 : lo + QB, 128:256], 1, 0)
         gate = act[lo : lo + QB, 0:128].astype(F32)
         mean = jnp.sum(o, axis=1, keepdims=True) * (1.0 / HD)
@@ -414,12 +427,14 @@
     return total.astype(BF)
 
 
-def gather_weights(total):
+def gather_weights(total, add):
     y = (lax.axis_index("table") // 2).astype(I32).reshape(1)
     pairs = [[2 * i, 2 * i + 1] for i in range(4)]
     both = lax.all_gather(total, "table", axis=0, tiled=True, axis_index_groups=pairs)
     parts = [both] + [shift(both, "table", lambda i, k=k: (i - 2 * k) % 8, 8) for k in range(1, 4)]
-    return unpack(y, parts)
+    table_grad = add()
+    parts, table_grad = lax.optimization_barrier((parts, table_grad))
+    return unpack(y, parts), table_grad
 
 
 def body(table, owner, local_row, segment_ids, proj_in, proj_out, grad_out):
@@ -436,14 +451,16 @@
     cparts = scatter_pieces([c0, c1, c2, c3])
     own, got = reduce_over_chips(mine, other)
     flat = received[:, :CAP].reshape(SLOTS // 128, 128)
-    got, cparts[3] = lax.optimization_barrier((got, cparts[3]))
+    got, cparts[1] = lax.optimization_barrier((got, cparts[1]))
     total = add_group((own + got.astype(F32)).astype(BF))
     cparts, _, flat = lax.optimization_barrier((cparts, total, flat))
     grads = to_slots(slot, grad_out, cparts)
     total = add_step(total, 7)
     grads, total = lax.optimization_barrier((grads, total))
     arrived = lax.all_to_all(grads.reshape(NOWN, CAP, 128), BOTH, split_axis=0, concat_axis=0, tiled=True)
-    grad_in, grad_outw = gather_weights(total)
+    (grad_in, grad_outw), table_grad = gather_weights(
+        total, lambda: add_rows(flat, arrived.reshape(SLOTS, 128))
+    )
     layer_out = (
         x.astype(F32)
         + (
@@ -453,7 +470,6 @@
             + cparts[3][TOK:].astype(F32)
         )
     ).astype(BF)
-    table_grad = add_rows(flat, arrived.reshape(SLOTS, 128))
     return layer_out, table_grad, grad_in.reshape(4, D, 128), grad_outw
 
 

time: 147 us -> 148 us (level)
  starting transfers between devices: 41.5 us -> 44.1 us
  waiting for transfers between devices: 44.7 us -> 43 us
    ppermute x19, waiting for transfers between devices: 34.7 us -> 27.2 us  [shift(): return lax.ppermute(x, axis, [(i, fn(i)) for i in range(n)])]
    all_to_all x1, waiting for transfers between devices: 0.01 us -> 5.81 us  [body(): lax.all_to_all(grads.reshape(NOWN, CAP, 128), BOTH, split_axis=0, concat_...]
    all_to_all x1, starting transfers between devices: 7.75 us -> 11.9 us  [body(): lax.all_to_all(grads.reshape(NOWN, CAP, 128), BOTH, split_axis=0, concat_...]
    ppermute x19, starting transfers between devices: 28.5 us -> 26.9 us  [shift(): return lax.ppermute(x, axis, [(i, fn(i)) for i in range(n)])]
  transfers between devices with their start and end apart: 21 -> 21, of which waited for: 12 -> 11; matrix products, arithmetic and copies ran while one was open for 2% -> 2% of each run, Pallas kernels for 5% -> 6%
where the time goes in v10:
time: 148 us; the launch traced here: 147 us
  starting transfers between devices  44.1 us (30%)
  waiting for transfers between devices  43 us (29%)
  Pallas kernels  27.1 us (18%)
  blocking collectives  24.3 us (16%)
  local copies, waits for them, and re-layouts  4.48 us (3%)
  other arithmetic  3.25 us (2%)
    ppermute x19, waiting for transfers between devices, shift(): return lax.ppermute(x, axis, [(i, fn(i)) for i in range(n)])  27.2 us
    ppermute x19, starting transfers between devices, shift(): return lax.ppermute(x, axis, [(i, fn(i)) for i in range(n)])  26.9 us
    all_to_all x1, blocking collectives, body(): lax.all_to_all(requests, BOTH, split_axis=0, concat_axis=0, tiled=True)  22.3 us
    all_to_all x1, starting transfers between devices, body(): lax.all_to_all(grads.reshape(NOWN, CAP, 128), BOTH, split_axis=0, concat_...  11.9 us
    pallas_call x1, Pallas kernels, layer(): pl.pallas_call(layer_kernel, out_shape=(jax.ShapeDtypeStruct((1280, 128),...  11.7 us
    all_to_all x1, waiting for transfers between devices, body(): lax.all_to_all(rows.reshape(NOWN, CAP, 128), BOTH, split_axis=0, concat_a...  9.98 us
    all_to_all x1, waiting for transfers between devices, body(): lax.all_to_all(grads.reshape(NOWN, CAP, 128), BOTH, split_axis=0, concat_...  5.81 us
    all_to_all x1, starting transfers between devices, body(): lax.all_to_all(rows.reshape(NOWN, CAP, 128), BOTH, split_axis=0, concat_a...  5.29 us
  transfers between devices with their start and end apart: 21, of which 11 were waited for; matrix products, arithmetic and copies ran while one was open for 2% of the time, Pallas kernels for 6%

profile of v10, /device:TPU:1, one launch (start us, length us, event | category | flops | bytes accessed | tf_op | source)
XLA Modules:
  0.0 146.9 jit_solution(16628511075857076062)
XLA Ops:
  0.6 1.8 %route.1 = (s32[64,128]{1,0:T(8,128)}, s32[8,128]{1,0:T(8,128)}) custom-call(s32[8,128]{1,0:T(8,128)} %bitcast.38, s32[8,128]{1,0:T(8,128)} %bitcast.39), custom_call_target="tpu_custom_call" | custom-call | tf_op jit(solution)/shard_map/route/pallas_call | solution.py:62
  2.5 22.3 %all_to_all.21 = s32[64,1,128]{2,1,0:T(1,128)} all-to-all(s32[64,1,128]{2,1,0:T(1,128)} %bitcast.37), channel_id=1, replica_groups=mesh['table'=8,'seq'=8,'tensor'=4] {'table','seq'}, dimensions={0} | all-to-all | bytes 65536 | tf_op jit(solution)/shard_map/all_to_all | solution.py:445
  24.7 2.9 %fetch.1 = bf16[1536,128]{1,0:T(8,128)(2,1)} custom-call(s32[64,128]{1,0:T(8,128)} %bitcast.35, bf16[2048,128]{1,0:T(8,128)(2,1)} %table_ref.1), custom_call_target="tpu_custom_call" | custom-call | tf_op jit(solution)/shard_map/fetch/pallas_call | solution.py:98
  27.6 5.3 %all-to-all-start.1 = ((bf16[64,24,128]{2,1,0:T(8,128)(2,1)}), bf16[64,24,128]{2,1,0:T(8,128)(2,1)S(1)}, u32[]{:S(2)}, u32[]{:S(2)}) async-start(bf16[64,24,128]{2,1,0:T(8,128)(2,1)} %bitcast.31), calls=%async_computation.1 | async-start | bytes 786432 | tf_op jit(solution)/shard_map/all_to_all | solution.py:447
  32.9 1.3 collective-permute-start.5
  34.2 2.5 %collective-permute-start.4 = (bf16[1024,128]{1,0:T(8,128)(2,1)S(1)}, bf16[1024,128]{1,0:T(8,128)(2,1)S(1)}, u32[]{:S(2)}, u32[]{:S(2)}) collective-permute-start(bf16[1024,128]{1,0:T(8,128)(2,1)S(1)} %copy-done.7), channel_id=1, source_target_pairs={{0,2},{1,3},{2,0},{3,1},{4,6},{5,7},{6,4},{7,5},{8,10},{9,11},{10,... | collective-permute-start | bytes 786440 | tf_op jit(solution)/shard_map/ppermute | solution.py:385
  37.8 10.0 %all-to-all-done.1 = bf16[64,24,128]{2,1,0:T(8,128)(2,1)S(1)} async-done(((bf16[64,24,128]{2,1,0:T(8,128)(2,1)}), bf16[64,24,128]{2,1,0:T(8,128)(2,1)S(1)}, u32[]{:S(2)}, u32[]{:S(2)}) %all-to-all-start.1) | async-done | bytes 393248 | tf_op jit(solution)/shard_map/all_to_all | solution.py:447
  48.5 2.4 %place.1.x0 = bf16[1024,128]{1,0:T(8,128)(2,1)} custom-call(s32[8,128]{1,0:T(8,128)} %get-tuple-element.28.slot_ref, bf16[1536,128]{1,0:T(8,128)(2,1)} %bitcast.29), custom_call_target="tpu_custom_call" | custom-call | tf_op jit(solution)/shard_map/place/pallas_call | solution.py:133
  50.9 1.2 collective-permute-start.2
  52.1 2.5 %collective-permute-start.1 = (bf16[1024,128]{1,0:T(8,128)(2,1)}, bf16[1024,128]{1,0:T(8,128)(2,1)S(1)}, u32[]{:S(2)}, u32[]{:S(2)}) collective-permute-start(bf16[1024,128]{1,0:T(8,128)(2,1)} %place.1.x0), channel_id=1, source_target_pairs={{0,2},{1,3},{2,0},{3,1},{4,6},{5,7},{6,4},{7,5},{8,10},{9,11},{10,... | collective-permute-start | bytes 786440 | tf_op jit(solution)/shard_map/ppermute | solution.py:385
  54.6 1.2 collective-permute-start
  55.7 3.4 %collective-permute-done.2.x3 = bf16[1024,128]{1,0:T(8,128)(2,1)S(1)} collective-permute-done((bf16[1024,128]{1,0:T(8,128)(2,1)}, bf16[1024,128]{1,0:T(8,128)(2,1)S(1)}, u32[]{:S(2)}, u32[]{:S(2)}) %collective-permute-start.2) | collective-permute-done | bytes 262176 | tf_op jit(solution)/shard_map/ppermute | solution.py:385
  59.1 6.6 %collective-permute-done.1.x2 = bf16[1024,128]{1,0:T(8,128)(2,1)S(1)} collective-permute-done((bf16[1024,128]{1,0:T(8,128)(2,1)}, bf16[1024,128]{1,0:T(8,128)(2,1)S(1)}, u32[]{:S(2)}, u32[]{:S(2)}) %collective-permute-start.1) | collective-permute-done | bytes 262176 | tf_op jit(solution)/shard_map/ppermute | solution.py:385
  66.5 11.7 %layer.1 = (f32[1280,128]{1,0:T(8,128)}, bf16[1280,128]{1,0:T(8,128)(2,1)}, bf16[2048,128]{1,0:T(8,128)(2,1)}, bf16[2048,128]{1,0:T(8,128)(2,1)}, bf16[2048,128]{1,0:T(8,128)(2,1)}, /*index=5*/bf16[2048,128]{1,0:T(8,128)(2,1)}) custom-call(s32[1]{0:T(128)} %bitcast.7.pos_ref, s32[1]{0:T(128)} %bitcast.8.core_ref, s32[1,1024]{1,0:T(1,128)} %seg_ref.1, ...), custom_call_target="tpu_custom_call" | custom-call | tf_op jit(solution)/shard_map/layer/pallas_call | solution.py:276
  78.3 2.0 %collective-permute-start.6 = (bf16[1280,128]{1,0:T(8,128)(2,1)}, bf16[1280,128]{1,0:T(8,128)(2,1)S(1)}, u32[]{:S(2)}, u32[]{:S(2)}) collective-permute-start(bf16[1280,128]{1,0:T(8,128)(2,1)} %get-tuple-element.32), channel_id=1, source_target_pairs={{0,32},{32,0},{64,96},{96,64},{128,160},{160,128},{192,224},{224,1... | collective-permute-start | bytes 983048 | tf_op jit(solution)/shard_map/ppermute | solution.py:385
  80.2 1.5 collective-permute-done.6
  84.7 3.7 %collective-permute-done.7 = bf16[640,128]{1,0:T(8,128)(2,1)S(1)} collective-permute-done((bf16[640,128]{1,0:T(8,128)(2,1)S(1)}, bf16[640,128]{1,0:T(8,128)(2,1)S(1)}, u32[]{:S(2)}, u32[]{:S(2)}) %collective-permute-start.7) | collective-permute-done | bytes 163872 | tf_op jit(solution)/shard_map/ppermute | solution.py:385
  88.5 1.3 collective-permute-start.8
  89.8 1.9 %collective-permute-start.10 = (bf16[2048,128]{1,0:T(8,128)(2,1)}, bf16[2048,128]{1,0:T(8,128)(2,1)S(1)}, u32[]{:S(2)}, u32[]{:S(2)}) collective-permute-start(bf16[2048,128]{1,0:T(8,128)(2,1)} %get-tuple-element.35), channel_id=1, source_target_pairs={{0,3},{1,0},{2,1},{3,2},{4,7},{5,4},{6,5},{7,6},{8,11},{9,8},{10,9... | collective-permute-start | bytes 1572872 | tf_op jit(solution)/shard_map/ppermute | solution.py:385
  92.5 5.4 %collective-permute-done.9.d1 = bf16[2048,128]{1,0:T(8,128)(2,1)S(1)} collective-permute-done((bf16[2048,128]{1,0:T(8,128)(2,1)}, bf16[2048,128]{1,0:T(8,128)(2,1)S(1)}, u32[]{:S(2)}, u32[]{:S(2)}) %collective-permute-start.9) | collective-permute-done | bytes 524320 | tf_op jit(solution)/shard_map/ppermute | solution.py:385
  98.0 1.6 %collective-permute-start.14 = (bf16[320,128]{1,0:T(8,128)(2,1)S(1)}, bf16[320,128]{1,0:T(8,128)(2,1)S(1)}, u32[]{:S(2)}, u32[]{:S(2)}) collective-permute-start(bf16[320,128]{1,0:T(8,128)(2,1)S(1)} %fusion.1), channel_id=1, source_target_pairs={{0,12},{4,8},{8,4},{12,0},{16,28},{20,24},{24,20},{28,16},{1,13},{... | collective-permute-start | bytes 245768 | tf_op jit(solution)/shard_map/ppermute | solution.py:385
  101.6 1.8 %collective-permute-done.14 = bf16[320,128]{1,0:T(8,128)(2,1)S(1)} collective-permute-done((bf16[320,128]{1,0:T(8,128)(2,1)S(1)}, bf16[320,128]{1,0:T(8,128)(2,1)S(1)}, u32[]{:S(2)}, u32[]{:S(2)}) %collective-permute-start.14) | collective-permute-done | bytes 81952 | tf_op jit(solution)/shard_map/ppermute | solution.py:385
  103.5 4.4 %collective-permute-done.13 = bf16[320,128]{1,0:T(8,128)(2,1)S(1)} collective-permute-done((bf16[320,128]{1,0:T(8,128)(2,1)S(1)}, bf16[320,128]{1,0:T(8,128)(2,1)S(1)}, u32[]{:S(2)}, u32[]{:S(2)}) %collective-permute-start.13) | collective-permute-done | bytes 81952 | tf_op jit(solution)/shard_map/ppermute | solution.py:385
  110.4 2.8 %to_slots.1 = bf16[1536,128]{1,0:T(8,128)(2,1)} custom-call(s32[8,128]{1,0:T(8,128)} %get-tuple-element.28.slot_ref, bf16[1024,128]{1,0:T(8,128)(2,1)} %grad_ref.1, bf16[2048,128]{1,0:T(8,128)(2,1)} %get-tuple-element.38.d0, bf16[2048,128]{1,0:T(8,128)(2,1)} %copy-done.4, bf16[2048,128]{1,0:T(8,128)(2,1)} %copy-done.5, bf16[2048,128]{1,0:T(8,128)(2,1)} %copy-done.6), custom_call_target="tpu_custom_call" | custom-call | tf_op jit(solution)/shard_map/to_slots/pallas_call | solution.py:332
  113.2 11.9 %all-to-all-start.2 = ((bf16[64,24,128]{2,1,0:T(8,128)(2,1)}), bf16[64,24,128]{2,1,0:T(8,128)(2,1)S(1)}, u32[]{:S(2)}, u32[]{:S(2)}) async-start(bf16[64,24,128]{2,1,0:T(8,128)(2,1)} %bitcast.32), calls=%async_computation.2 | async-start | bytes 786432 | tf_op jit(solution)/shard_map/all_to_all | solution.py:460
  125.1 2.0 %all_gather.3.p0 = bf16[640,128]{1,0:T(8,128)(2,1)S(1)} all-gather(bf16[320,128]{1,0:T(8,128)(2,1)S(1)} %add_convert_fusion.1), channel_id=1, replica_groups={{0,32},{64,96},{128,160},{192,224},{1,33},{65,97},{129,161},{193,225},{..., dimensions={0}, use_global_device_ids=true | all-gather | bytes 245760 | tf_op jit(solution)/shard_map/all_gather | solution.py:433
  127.2 1.3 collective-permute-start.18
  128.5 2.6 %collective-permute-start.17 = (bf16[640,128]{1,0:T(8,128)(2,1)S(1)}, bf16[640,128]{1,0:T(8,128)(2,1)S(1)}, u32[]{:S(2)}, u32[]{:S(2)}) collective-permute-start(bf16[640,128]{1,0:T(8,128)(2,1)S(1)} %all_gather.3.p0), channel_id=1, source_target_pairs={{0,128},{32,160},{64,192},{96,224},{128,0},{160,32},{192,64},{224,... | collective-permute-start | bytes 491528 | tf_op jit(solution)/shard_map/ppermute | solution.py:385
  132.2 2.0 %add_convert_fusion = bf16[1024,128]{1,0:T(8,128)(2,1)} fusion(bf16[1024,128]{1,0:T(8,128)(2,1)S(1)} %copy-done, bf16[2048,128]{1,0:T(8,128)(2,1)} %copy-done.6, bf16[2048,128]{1,0:T(8,128)(2,1)} %copy-done.5, bf16[2048,128]{1,0:T(8,128)(2,1)} %copy-done.4, bf16[2048,128]{1,0:T(8,128)(2,1)S(1)} %copy-done.3), kind=kLoop, calls=%fused_computation.1 | loop fusion | flops 1310720 | bytes 1572864 | tf_op jit(solution)/shard_map/convert_element_type | solution.py:472
  134.1 5.8 %all-to-all-done.2 = bf16[64,24,128]{2,1,0:T(8,128)(2,1)S(1)} async-done(((bf16[64,24,128]{2,1,0:T(8,128)(2,1)}), bf16[64,24,128]{2,1,0:T(8,128)(2,1)S(1)}, u32[]{:S(2)}, u32[]{:S(2)}) %all-to-all-start.2) | async-done | bytes 393248 | tf_op jit(solution)/shard_map/all_to_all | solution.py:460
  140.7 3.1 %add_rows.1 = f32[2048,128]{1,0:T(8,128)} custom-call(s32[12,128]{1,0:T(8,128)} %reshape.59.req_ref, bf16[1536,128]{1,0:T(8,128)(2,1)} %bitcast.30), custom_call_target="tpu_custom_call" | custom-call | tf_op jit(solution)/shard_map/add_rows/pallas_call | solution.py:351
  144.6 2.4 %unpack.1 = (f32[2048,128]{1,0:T(8,128)}, f32[128,512]{1,0:T(8,128)}) custom-call(s32[1]{0:T(128)} %bitcast.17.y_ref, bf16[640,128]{1,0:T(8,128)(2,1)} %copy-done.8, bf16[640,128]{1,0:T(8,128)(2,1)} %copy-done.18, bf16[640,128]{1,0:T(8,128)(2,1)} %copy-done.17, bf16[640,128]{1,0:T(8,128)(2,1)} %copy-done.16), custom_call_target="tpu_custom_call" | custom-call | tf_op jit(solution)/shard_map/unpack/pallas_call | solution.py:373
  (68 shorter events, 13.8 us)
Async XLA Ops:
  27.6 5.3 %copy-start.7 = (bf16[1024,128]{1,0:T(8,128)(2,1)S(1)}, bf16[1024,128]{1,0:T(8,128)(2,1)}, u32[]{:S(2)}) copy-start(bf16[1024,128]{1,0:T(8,128)(2,1)} %grad_ref.1) | copy-start | bytes 786436
  27.6 20.2 %all-to-all-start.1 = ((bf16[64,24,128]{2,1,0:T(8,128)(2,1)}), bf16[64,24,128]{2,1,0:T(8,128)(2,1)S(1)}, u32[]{:S(2)}, u32[]{:S(2)}) async-start(bf16[64,24,128]{2,1,0:T(8,128)(2,1)} %bitcast.31), calls=%async_computation.1 | async-start | bytes 786432 | tf_op jit(solution)/shard_map/all_to_all | solution.py:447
  32.9 21.6 %collective-permute-start.5 = (bf16[1024,128]{1,0:T(8,128)(2,1)S(1)}, bf16[1024,128]{1,0:T(8,128)(2,1)S(1)}, u32[]{:S(2)}, u32[]{:S(2)}) collective-permute-start(bf16[1024,128]{1,0:T(8,128)(2,1)S(1)} %copy-done.7), channel_id=1, source_target_pairs={{0,1},{1,2},{2,3},{3,0},{4,5},{5,6},{6,7},{7,4},{8,9},{9,10},{10,1... | collective-permute-start | bytes 786440 | tf_op jit(solution)/shard_map/ppermute | solution.py:385
  34.2 21.5 %collective-permute-start.4 = (bf16[1024,128]{1,0:T(8,128)(2,1)S(1)}, bf16[1024,128]{1,0:T(8,128)(2,1)S(1)}, u32[]{:S(2)}, u32[]{:S(2)}) collective-permute-start(bf16[1024,128]{1,0:T(8,128)(2,1)S(1)} %copy-done.7), channel_id=1, source_target_pairs={{0,2},{1,3},{2,0},{3,1},{4,6},{5,7},{6,4},{7,5},{8,10},{9,11},{10,... | collective-permute-start | bytes 786440 | tf_op jit(solution)/shard_map/ppermute | solution.py:385
  36.6 19.1 %collective-permute-start.3 = (bf16[1024,128]{1,0:T(8,128)(2,1)S(1)}, bf16[1024,128]{1,0:T(8,128)(2,1)S(1)}, u32[]{:S(2)}, u32[]{:S(2)}) collective-permute-start(bf16[1024,128]{1,0:T(8,128)(2,1)S(1)} %copy-done.7), channel_id=1, source_target_pairs={{0,3},{1,0},{2,1},{3,2},{4,7},{5,4},{6,5},{7,6},{8,11},{9,8},{10,9... | collective-permute-start | bytes 786440 | tf_op jit(solution)/shard_map/ppermute | solution.py:385
  50.9 8.2 %collective-permute-start.2 = (bf16[1024,128]{1,0:T(8,128)(2,1)}, bf16[1024,128]{1,0:T(8,128)(2,1)S(1)}, u32[]{:S(2)}, u32[]{:S(2)}) collective-permute-start(bf16[1024,128]{1,0:T(8,128)(2,1)} %place.1.x0), channel_id=1, source_target_pairs={{0,1},{1,2},{2,3},{3,0},{4,5},{5,6},{6,7},{7,4},{8,9},{9,10},{10,1... | collective-permute-start | bytes 786440 | tf_op jit(solution)/shard_map/ppermute | solution.py:385
  52.1 13.6 %collective-permute-start.1 = (bf16[1024,128]{1,0:T(8,128)(2,1)}, bf16[1024,128]{1,0:T(8,128)(2,1)S(1)}, u32[]{:S(2)}, u32[]{:S(2)}) collective-permute-start(bf16[1024,128]{1,0:T(8,128)(2,1)} %place.1.x0), channel_id=1, source_target_pairs={{0,2},{1,3},{2,0},{3,1},{4,6},{5,7},{6,4},{7,5},{8,10},{9,11},{10,... | collective-permute-start | bytes 786440 | tf_op jit(solution)/shard_map/ppermute | solution.py:385
  54.6 11.3 %copy-start.10 = (bf16[1024,128]{1,0:T(8,128)(2,1)}, bf16[1024,128]{1,0:T(8,128)(2,1)S(1)}, u32[]{:S(2)}) copy-start(bf16[1024,128]{1,0:T(8,128)(2,1)S(1)} %collective-permute-done.5.g3) | copy-start | bytes 786436
  54.6 11.3 %collective-permute-start = (bf16[1024,128]{1,0:T(8,128)(2,1)}, bf16[1024,128]{1,0:T(8,128)(2,1)S(1)}, u32[]{:S(2)}, u32[]{:S(2)}) collective-permute-start(bf16[1024,128]{1,0:T(8,128)(2,1)} %place.1.x0), channel_id=1, source_target_pairs={{0,3},{1,0},{2,1},{3,2},{4,7},{5,4},{6,5},{7,6},{8,11},{9,8},{10,9... | collective-permute-start | bytes 786440 | tf_op jit(solution)/shard_map/ppermute | solution.py:385
  55.7 10.1 %copy-start.11 = (bf16[1024,128]{1,0:T(8,128)(2,1)}, bf16[1024,128]{1,0:T(8,128)(2,1)S(1)}, u32[]{:S(2)}) copy-start(bf16[1024,128]{1,0:T(8,128)(2,1)S(1)} %collective-permute-done.4.g2) | copy-start | bytes 786436
  55.7 10.1 %copy-start.12 = (bf16[1024,128]{1,0:T(8,128)(2,1)}, bf16[1024,128]{1,0:T(8,128)(2,1)S(1)}, u32[]{:S(2)}) copy-start(bf16[1024,128]{1,0:T(8,128)(2,1)S(1)} %collective-permute-done.3.g1) | copy-start | bytes 786436
  59.1 6.7 %copy-start.13 = (bf16[1024,128]{1,0:T(8,128)(2,1)}, bf16[1024,128]{1,0:T(8,128)(2,1)S(1)}, u32[]{:S(2)}) copy-start(bf16[1024,128]{1,0:T(8,128)(2,1)S(1)} %collective-permute-done.2.x3) | copy-start | bytes 786436
  78.3 3.4 %collective-permute-start.6 = (bf16[1280,128]{1,0:T(8,128)(2,1)}, bf16[1280,128]{1,0:T(8,128)(2,1)S(1)}, u32[]{:S(2)}, u32[]{:S(2)}) collective-permute-start(bf16[1280,128]{1,0:T(8,128)(2,1)} %get-tuple-element.32), channel_id=1, source_target_pairs={{0,32},{32,0},{64,96},{96,64},{128,160},{160,128},{192,224},{224,1... | collective-permute-start | bytes 983048 | tf_op jit(solution)/shard_map/ppermute | solution.py:385
  82.9 8.8 %copy-start.19 = (bf16[2048,128]{1,0:T(8,128)(2,1)S(1)}, bf16[2048,128]{1,0:T(8,128)(2,1)}, u32[]{:S(2)}) copy-start(bf16[2048,128]{1,0:T(8,128)(2,1)} %get-tuple-element.36) | copy-start | bytes 1572868
  82.9 5.5 %collective-permute-start.7 = (bf16[640,128]{1,0:T(8,128)(2,1)S(1)}, bf16[640,128]{1,0:T(8,128)(2,1)S(1)}, u32[]{:S(2)}, u32[]{:S(2)}) collective-permute-start(bf16[640,128]{1,0:T(8,128)(2,1)S(1)} %fusion), channel_id=1, source_target_pairs={{0,64},{32,96},{64,0},{96,32},{128,192},{160,224},{192,128},{224,1... | collective-permute-start | bytes 491528 | tf_op jit(solution)/shard_map/ppermute | solution.py:385
  83.7 14.2 %collective-permute-start.9 = (bf16[2048,128]{1,0:T(8,128)(2,1)}, bf16[2048,128]{1,0:T(8,128)(2,1)S(1)}, u32[]{:S(2)}, u32[]{:S(2)}) collective-permute-start(bf16[2048,128]{1,0:T(8,128)(2,1)} %get-tuple-element.33), channel_id=1, source_target_pairs={{0,1},{1,2},{2,3},{3,0},{4,5},{5,6},{6,7},{7,4},{8,9},{9,10},{10,1... | collective-permute-start | bytes 1572872 | tf_op jit(solution)/shard_map/ppermute | solution.py:385
  88.5 9.5 %collective-permute-start.8 = (bf16[320,128]{1,0:T(8,128)(2,1)S(1)}, bf16[320,128]{1,0:T(8,128)(2,1)S(1)}, u32[]{:S(2)}, u32[]{:S(2)}) collective-permute-start(bf16[320,128]{1,0:T(8,128)(2,1)S(1)} %fusion.2), channel_id=1, source_target_pairs={{0,192},{32,224},{64,128},{96,160},{128,64},{160,96},{192,0},{224,... | collective-permute-start | bytes 245768 | tf_op jit(solution)/shard_map/ppermute | solution.py:385
  89.8 19.6 %collective-permute-start.10 = (bf16[2048,128]{1,0:T(8,128)(2,1)}, bf16[2048,128]{1,0:T(8,128)(2,1)S(1)}, u32[]{:S(2)}, u32[]{:S(2)}) collective-permute-start(bf16[2048,128]{1,0:T(8,128)(2,1)} %get-tuple-element.35), channel_id=1, source_target_pairs={{0,3},{1,0},{2,1},{3,2},{4,7},{5,4},{6,5},{7,6},{8,11},{9,8},{10,9... | collective-permute-start | bytes 1572872 | tf_op jit(solution)/shard_map/ppermute | solution.py:385
  91.7 18.0 %collective-permute-start.11 = (bf16[2048,128]{1,0:T(8,128)(2,1)S(1)}, bf16[2048,128]{1,0:T(8,128)(2,1)S(1)}, u32[]{:S(2)}, u32[]{:S(2)}) collective-permute-start(bf16[2048,128]{1,0:T(8,128)(2,1)S(1)} %copy-done.19), channel_id=1, source_target_pairs={{0,2},{1,3},{2,0},{3,1},{4,6},{5,7},{6,4},{7,5},{8,10},{9,11},{10,... | collective-permute-start | bytes 1572872 | tf_op jit(solution)/shard_map/ppermute | solution.py:385
  98.0 11.7 %copy-start.4 = (bf16[2048,128]{1,0:T(8,128)(2,1)}, bf16[2048,128]{1,0:T(8,128)(2,1)S(1)}, u32[]{:S(2)}) copy-start(bf16[2048,128]{1,0:T(8,128)(2,1)S(1)} %collective-permute-done.9.d1) | copy-start | bytes 1572868
  98.0 10.7 %copy-start.9 = (s32[64,1,128]{2,1,0:T(1,128)S(1)}, s32[64,1,128]{2,1,0:T(1,128)}, u32[]{:S(2)}) copy-start(s32[64,1,128]{2,1,0:T(1,128)} %all_to_all.21) | copy-start | bytes 98308
  98.0 5.5 %collective-permute-start.14 = (bf16[320,128]{1,0:T(8,128)(2,1)S(1)}, bf16[320,128]{1,0:T(8,128)(2,1)S(1)}, u32[]{:S(2)}, u32[]{:S(2)}) collective-permute-start(bf16[320,128]{1,0:T(8,128)(2,1)S(1)} %fusion.1), channel_id=1, source_target_pairs={{0,12},{4,8},{8,4},{12,0},{16,28},{20,24},{24,20},{28,16},{1,13},{... | collective-permute-start | bytes 245768 | tf_op jit(solution)/shard_map/ppermute | solution.py:385
  99.6 8.3 %collective-permute-start.13 = (bf16[320,128]{1,0:T(8,128)(2,1)S(1)}, bf16[320,128]{1,0:T(8,128)(2,1)S(1)}, u32[]{:S(2)}, u32[]{:S(2)}) collective-permute-start(bf16[320,128]{1,0:T(8,128)(2,1)S(1)} %fusion.1), channel_id=1, source_target_pairs={{0,8},{4,12},{8,0},{12,4},{16,24},{20,28},{24,16},{28,20},{1,9},{5... | collective-permute-start | bytes 245768 | tf_op jit(solution)/shard_map/ppermute | solution.py:385
  100.6 7.3 %collective-permute-start.12 = (bf16[320,128]{1,0:T(8,128)(2,1)S(1)}, bf16[320,128]{1,0:T(8,128)(2,1)S(1)}, u32[]{:S(2)}, u32[]{:S(2)}) collective-permute-start(bf16[320,128]{1,0:T(8,128)(2,1)S(1)} %fusion.1), channel_id=1, source_target_pairs={{0,4},{4,0},{8,12},{12,8},{16,20},{20,16},{24,28},{28,24},{1,5},{5... | collective-permute-start | bytes 245768 | tf_op jit(solution)/shard_map/ppermute | solution.py:385
  107.9 5.2 %collective-permute-start.15 = (bf16[320,128]{1,0:T(8,128)(2,1)S(1)}, bf16[320,128]{1,0:T(8,128)(2,1)S(1)}, u32[]{:S(2)}, u32[]{:S(2)}) collective-permute-start(bf16[320,128]{1,0:T(8,128)(2,1)S(1)} %add_convert_fusion.2), channel_id=1, source_target_pairs={{0,28},{4,24},{8,20},{12,16},{16,12},{20,8},{24,4},{28,0},{1,29},{... | collective-permute-start | bytes 245768 | tf_op jit(solution)/shard_map/ppermute | solution.py:385
  113.2 18.9 %copy-start.3 = (bf16[2048,128]{1,0:T(8,128)(2,1)S(1)}, bf16[2048,128]{1,0:T(8,128)(2,1)}, u32[]{:S(2)}) copy-start(bf16[2048,128]{1,0:T(8,128)(2,1)} %get-tuple-element.38.d0) | copy-start | bytes 1572868
  113.2 18.9 %copy-start = (bf16[1024,128]{1,0:T(8,128)(2,1)S(1)}, bf16[1024,128]{1,0:T(8,128)(2,1)}, u32[]{:S(2)}) copy-start(bf16[1024,128]{1,0:T(8,128)(2,1)} %place.1.x0) | copy-start | bytes 786436
  113.2 26.7 %all-to-all-start.2 = ((bf16[64,24,128]{2,1,0:T(8,128)(2,1)}), bf16[64,24,128]{2,1,0:T(8,128)(2,1)S(1)}, u32[]{:S(2)}, u32[]{:S(2)}) async-start(bf16[64,24,128]{2,1,0:T(8,128)(2,1)} %bitcast.32), calls=%async_computation.2 | async-start | bytes 786432 | tf_op jit(solution)/shard_map/all_to_all | solution.py:460
  127.2 7.0 %copy-start.8 = (bf16[640,128]{1,0:T(8,128)(2,1)}, bf16[640,128]{1,0:T(8,128)(2,1)S(1)}, u32[]{:S(2)}) copy-start(bf16[640,128]{1,0:T(8,128)(2,1)S(1)} %all_gather.3.p0) | copy-start | bytes 491524
  127.2 16.6 %collective-permute-start.18 = (bf16[640,128]{1,0:T(8,128)(2,1)S(1)}, bf16[640,128]{1,0:T(8,128)(2,1)S(1)}, u32[]{:S(2)}, u32[]{:S(2)}) collective-permute-start(bf16[640,128]{1,0:T(8,128)(2,1)S(1)} %all_gather.3.p0), channel_id=1, source_target_pairs={{0,64},{32,96},{64,128},{96,160},{128,192},{160,224},{192,0},{224,... | collective-permute-start | bytes 491528 | tf_op jit(solution)/shard_map/ppermute | solution.py:385
  128.5 15.3 %collective-permute-start.17 = (bf16[640,128]{1,0:T(8,128)(2,1)S(1)}, bf16[640,128]{1,0:T(8,128)(2,1)S(1)}, u32[]{:S(2)}, u32[]{:S(2)}) collective-permute-start(bf16[640,128]{1,0:T(8,128)(2,1)S(1)} %all_gather.3.p0), channel_id=1, source_target_pairs={{0,128},{32,160},{64,192},{96,224},{128,0},{160,32},{192,64},{224,... | collective-permute-start | bytes 491528 | tf_op jit(solution)/shard_map/ppermute | solution.py:385
  131.1 12.7 %collective-permute-start.16 = (bf16[640,128]{1,0:T(8,128)(2,1)S(1)}, bf16[640,128]{1,0:T(8,128)(2,1)S(1)}, u32[]{:S(2)}, u32[]{:S(2)}) collective-permute-start(bf16[640,128]{1,0:T(8,128)(2,1)S(1)} %all_gather.3.p0), channel_id=1, source_target_pairs={{0,192},{32,224},{64,0},{96,32},{128,64},{160,96},{192,128},{224,1... | collective-permute-start | bytes 491528 | tf_op jit(solution)/shard_map/ppermute | solution.py:385
  (9 other events, 6.6 us)

commit v11 on v10

--- a/solution.py
+++ b/solution.py
@@ -18,6 +18,7 @@
 ROWS = 2048
 QB = 256
 BOTH = ("table", "seq")
+FAR = (0, 1, 3, 2)
 BF = jnp.bfloat16
 F32 = jnp.float32
 I32 = jnp.int32
@@ -149,7 +150,7 @@
     both = (c0, c1, c2, c3)
     me, core = pos_ref[0], core_ref[0]
     for k in range(NT):
-        at = pl.multiple_of(lax.rem(me + k, NT) * 128, 128)
+        at = pl.multiple_of(lax.rem(me + FAR[k], NT) * 128, 128)
         for c in range(4):
             w[k * 128 : (k + 1) * 128, c * 128 : (c + 1) * 128] = win_ref[c, pl.ds(at, 128), :]
         wo[:, k * 128 : (k + 1) * 128] = wout_ref[:, pl.ds(at, 128)]
@@ -261,7 +262,7 @@
                 both[k][lo + r : lo + r + step, :] = ((d[k] - m1 - n[k] * m2) * scale).astype(BF)
 
     for k in range(NT):
-        at = pl.multiple_of(lax.rem(me + k, NT) * 128, 128)
+        at = pl.multiple_of(lax.rem(me + FAR[k], NT) * 128, 128)
         dw = dot(u_ref[:, k * 128 : (k + 1) * 128], dp_ref[...], 0, 0)
         for c in range(4):
             dw_ref[pl.ds(pl.multiple_of(c * 512 + at, 128), 128), :] = dw[:, c * 128 : (c + 1) * 128]
@@ -360,7 +361,7 @@
 
 def unpack_kernel(y_ref, p0, p1, p2, p3, in_ref, out_ref, whole):
     for k, p in enumerate((p0, p1, p2, p3)):
-        half, quarter = y_place(lax.rem(y_ref[0] + k, 4))
+        half, quarter = y_place(lax.rem(y_ref[0] + FAR[k], 4))
         for core in range(2):
             at = pl.multiple_of(half * 640 + quarter * 320 + core * 1280, 320)
             whole[pl.ds(at, 320), :] = p[core * 320 : (core + 1) * 320, :].astype(F32)
@@ -386,16 +387,13 @@
 
 
 def gather_pieces(x):
-    return [x] + [shift(x, "tensor", lambda i, k=k: (i - k) % NT, NT) for k in (1, 3, 2)]
-
-
-def order(pieces):
-    own, one, three, two = pieces
-    return [own, one, two, three]
+    return [x] + [shift(x, "tensor", lambda i, k=k: (i - k) % NT, NT) for k in FAR[1:]]
 
 
 def scatter_pieces(parts):
-    return [parts[0]] + [shift(parts[k], "tensor", lambda i, k=k: (i + k) % NT, NT) for k in (1, 3, 2)]
+    return [parts[0]] + [
+        shift(parts[i], "tensor", lambda j, k=FAR[i]: (j + k) % NT, NT) for i in range(1, NT)
+    ]
 
 
 def pick(x, i):
@@ -431,7 +429,7 @@
     y = (lax.axis_index("table") // 2).astype(I32).reshape(1)
     pairs = [[2 * i, 2 * i + 1] for i in range(4)]
     both = lax.all_gather(total, "table", axis=0, tiled=True, axis_index_groups=pairs)
-    parts = [both] + [shift(both, "table", lambda i, k=k: (i - 2 * k) % 8, 8) for k in range(1, 4)]
+    parts = [both] + [shift(both, "table", lambda i, k=k: (i - 2 * k) % 8, 8) for k in FAR[1:]]
     table_grad = add()
     parts, table_grad = lax.optimization_barrier((parts, table_grad))
     return unpack(y, parts), table_grad
@@ -441,17 +439,17 @@
     pos = lax.axis_index("tensor").astype(I32).reshape(1)
     core = (lax.axis_index("table") % 2).astype(I32).reshape(1)
     requests, slot = route(owner.reshape(8, 128), local_row.reshape(8, 128))
-    gs = order(gather_pieces(grad_out))
+    gs = gather_pieces(grad_out)
     received = lax.all_to_all(requests, BOTH, split_axis=0, concat_axis=0, tiled=True)
     rows = fetch(received, table)
     back = lax.all_to_all(rows.reshape(NOWN, CAP, 128), BOTH, split_axis=0, concat_axis=0, tiled=True)
     x = place(slot, back.reshape(SLOTS, 128))
-    xs = order(gather_pieces(x))
+    xs = gather_pieces(x)
     mine, other, c0, c1, c2, c3 = layer(pos, core, segment_ids, xs, gs, proj_in, proj_out)
     cparts = scatter_pieces([c0, c1, c2, c3])
     own, got = reduce_over_chips(mine, other)
     flat = received[:, :CAP].reshape(SLOTS // 128, 128)
-    got, cparts[1] = lax.optimization_barrier((got, cparts[1]))
+    got, cparts[3] = lax.optimization_barrier((got, cparts[3]))
     total = add_group((own + got.astype(F32)).astype(BF))
     cparts, _, flat = lax.optimization_barrier((cparts, total, flat))
     grads = to_slots(slot, grad_out, cparts)

time: 148 us -> 144 us (0.973)
  starting transfers between devices: 44.1 us -> 41.6 us
  waiting for transfers between devices: 43 us -> 41.5 us
    all_to_all x1, starting transfers between devices: 11.9 us -> 7.8 us  [body(): lax.all_to_all(grads.reshape(NOWN, CAP, 128), BOTH, split_axis=0, concat_...]
    ppermute x19, starting transfers between devices: 26.9 us -> 28.5 us  [shift(): return lax.ppermute(x, axis, [(i, fn(i)) for i in range(n)])]
  transfers between devices with their start and end apart: 21 -> 21, of which waited for: 11 -> 10; matrix products, arithmetic and copies ran while one was open for 2% -> 2% of each run, Pallas kernels for 6% -> 6%
where the time goes in v11:
time: 144 us; the launch traced here: 143 us
  starting transfers between devices  41.6 us (29%)
  waiting for transfers between devices  41.5 us (29%)
  Pallas kernels  27.1 us (19%)
  blocking collectives  24.3 us (17%)
  local copies, waits for them, and re-layouts  4.71 us (3%)
  other arithmetic  3.25 us (2%)
    ppermute x19, starting transfers between devices, shift(): return lax.ppermute(x, axis, [(i, fn(i)) for i in range(n)])  28.5 us
    ppermute x19, waiting for transfers between devices, shift(): return lax.ppermute(x, axis, [(i, fn(i)) for i in range(n)])  27 us
    all_to_all x1, blocking collectives, body(): lax.all_to_all(requests, BOTH, split_axis=0, concat_axis=0, tiled=True)  22.3 us
    pallas_call x1, Pallas kernels, layer(): pl.pallas_call(layer_kernel, out_shape=(jax.ShapeDtypeStruct((1280, 128),...  11.7 us
    all_to_all x1, waiting for transfers between devices, body(): lax.all_to_all(rows.reshape(NOWN, CAP, 128), BOTH, split_axis=0, concat_a...  9.36 us
    all_to_all x1, starting transfers between devices, body(): lax.all_to_all(grads.reshape(NOWN, CAP, 128), BOTH, split_axis=0, concat_...  7.8 us
    all_to_all x1, starting transfers between devices, body(): lax.all_to_all(rows.reshape(NOWN, CAP, 128), BOTH, split_axis=0, concat_a...  5.29 us
    all_to_all x1, waiting for transfers between devices, body(): lax.all_to_all(grads.reshape(NOWN, CAP, 128), BOTH, split_axis=0, concat_...  5.19 us
  transfers between devices with their start and end apart: 21, of which 10 were waited for; matrix products, arithmetic and copies ran while one was open for 2% of the time, Pallas kernels for 6%

profile of v11, /device:TPU:1, one launch (start us, length us, event | category | flops | bytes accessed | tf_op | source)
XLA Modules:
  0.0 143.3 jit_solution(15712211856527064905)
XLA Ops:
  0.6 1.8 %route.1 = (s32[64,128]{1,0:T(8,128)}, s32[8,128]{1,0:T(8,128)}) custom-call(s32[8,128]{1,0:T(8,128)} %bitcast.38, s32[8,128]{1,0:T(8,128)} %bitcast.39), custom_call_target="tpu_custom_call" | custom-call | tf_op jit(solution)/shard_map/route/pallas_call | solution.py:63
  2.5 22.3 %all_to_all.21 = s32[64,1,128]{2,1,0:T(1,128)} all-to-all(s32[64,1,128]{2,1,0:T(1,128)} %bitcast.37), channel_id=1, replica_groups=mesh['table'=8,'seq'=8,'tensor'=4] {'table','seq'}, dimensions={0} | all-to-all | bytes 65536 | tf_op jit(solution)/shard_map/all_to_all | solution.py:443
  24.7 2.9 %fetch.1 = bf16[1536,128]{1,0:T(8,128)(2,1)} custom-call(s32[64,128]{1,0:T(8,128)} %bitcast.35, bf16[2048,128]{1,0:T(8,128)(2,1)} %table_ref.1), custom_call_target="tpu_custom_call" | custom-call | tf_op jit(solution)/shard_map/fetch/pallas_call | solution.py:99
  27.6 5.3 %all-to-all-start.1 = ((bf16[64,24,128]{2,1,0:T(8,128)(2,1)}), bf16[64,24,128]{2,1,0:T(8,128)(2,1)S(1)}, u32[]{:S(2)}, u32[]{:S(2)}) async-start(bf16[64,24,128]{2,1,0:T(8,128)(2,1)} %bitcast.31), calls=%async_computation.1 | async-start | bytes 786432 | tf_op jit(solution)/shard_map/all_to_all | solution.py:445
  32.9 2.8 %collective-permute-start.5 = (bf16[1024,128]{1,0:T(8,128)(2,1)S(1)}, bf16[1024,128]{1,0:T(8,128)(2,1)S(1)}, u32[]{:S(2)}, u32[]{:S(2)}) collective-permute-start(bf16[1024,128]{1,0:T(8,128)(2,1)S(1)} %copy-done.7), channel_id=1, source_target_pairs={{0,2},{1,3},{2,0},{3,1},{4,6},{5,7},{6,4},{7,5},{8,10},{9,11},{10,... | collective-permute-start | bytes 786440 | tf_op jit(solution)/shard_map/ppermute | solution.py:386
  36.1 2.4 %collective-permute-start.3 = (bf16[1024,128]{1,0:T(8,128)(2,1)S(1)}, bf16[1024,128]{1,0:T(8,128)(2,1)S(1)}, u32[]{:S(2)}, u32[]{:S(2)}) collective-permute-start(bf16[1024,128]{1,0:T(8,128)(2,1)S(1)} %copy-done.7), channel_id=1, source_target_pairs={{0,3},{1,0},{2,1},{3,2},{4,7},{5,4},{6,5},{7,6},{8,11},{9,8},{10,9... | collective-permute-start | bytes 786440 | tf_op jit(solution)/shard_map/ppermute | solution.py:386
  38.4 9.4 %all-to-all-done.1 = bf16[64,24,128]{2,1,0:T(8,128)(2,1)S(1)} async-done(((bf16[64,24,128]{2,1,0:T(8,128)(2,1)}), bf16[64,24,128]{2,1,0:T(8,128)(2,1)S(1)}, u32[]{:S(2)}, u32[]{:S(2)}) %all-to-all-start.1) | async-done | bytes 393248 | tf_op jit(solution)/shard_map/all_to_all | solution.py:445
  48.5 2.4 %place.1.x0 = bf16[1024,128]{1,0:T(8,128)(2,1)} custom-call(s32[8,128]{1,0:T(8,128)} %get-tuple-element.28.slot_ref, bf16[1536,128]{1,0:T(8,128)(2,1)} %bitcast.29), custom_call_target="tpu_custom_call" | custom-call | tf_op jit(solution)/shard_map/place/pallas_call | solution.py:134
  50.9 2.7 %collective-permute-start.2 = (bf16[1024,128]{1,0:T(8,128)(2,1)}, bf16[1024,128]{1,0:T(8,128)(2,1)S(1)}, u32[]{:S(2)}, u32[]{:S(2)}) collective-permute-start(bf16[1024,128]{1,0:T(8,128)(2,1)} %place.1.x0), channel_id=1, source_target_pairs={{0,2},{1,3},{2,0},{3,1},{4,6},{5,7},{6,4},{7,5},{8,10},{9,11},{10,... | collective-permute-start | bytes 786440 | tf_op jit(solution)/shard_map/ppermute | solution.py:386
  54.0 2.4 %collective-permute-start = (bf16[1024,128]{1,0:T(8,128)(2,1)}, bf16[1024,128]{1,0:T(8,128)(2,1)S(1)}, u32[]{:S(2)}, u32[]{:S(2)}) collective-permute-start(bf16[1024,128]{1,0:T(8,128)(2,1)} %place.1.x0), channel_id=1, source_target_pairs={{0,3},{1,0},{2,1},{3,2},{4,7},{5,4},{6,5},{7,6},{8,11},{9,8},{10,9... | collective-permute-start | bytes 786440 | tf_op jit(solution)/shard_map/ppermute | solution.py:386
  56.3 3.1 %collective-permute-done.2.x3 = bf16[1024,128]{1,0:T(8,128)(2,1)S(1)} collective-permute-done((bf16[1024,128]{1,0:T(8,128)(2,1)}, bf16[1024,128]{1,0:T(8,128)(2,1)S(1)}, u32[]{:S(2)}, u32[]{:S(2)}) %collective-permute-start.2) | collective-permute-done | bytes 262176 | tf_op jit(solution)/shard_map/ppermute | solution.py:386
  59.4 7.0 %collective-permute-done.1.x2 = bf16[1024,128]{1,0:T(8,128)(2,1)S(1)} collective-permute-done((bf16[1024,128]{1,0:T(8,128)(2,1)}, bf16[1024,128]{1,0:T(8,128)(2,1)S(1)}, u32[]{:S(2)}, u32[]{:S(2)}) %collective-permute-start.1) | collective-permute-done | bytes 262176 | tf_op jit(solution)/shard_map/ppermute | solution.py:386
  67.2 11.7 %layer.1 = (f32[1280,128]{1,0:T(8,128)}, bf16[1280,128]{1,0:T(8,128)(2,1)}, bf16[2048,128]{1,0:T(8,128)(2,1)}, bf16[2048,128]{1,0:T(8,128)(2,1)}, bf16[2048,128]{1,0:T(8,128)(2,1)}, /*index=5*/bf16[2048,128]{1,0:T(8,128)(2,1)}) custom-call(s32[1]{0:T(128)} %bitcast.7.pos_ref, s32[1]{0:T(128)} %bitcast.8.core_ref, s32[1,1024]{1,0:T(1,128)} %seg_ref.1, ...), custom_call_target="tpu_custom_call" | custom-call | tf_op jit(solution)/shard_map/layer/pallas_call | solution.py:277
  79.6 1.5 %collective-permute-done.8 = bf16[1280,128]{1,0:T(8,128)(2,1)S(1)} collective-permute-done((bf16[1280,128]{1,0:T(8,128)(2,1)}, bf16[1280,128]{1,0:T(8,128)(2,1)S(1)}, u32[]{:S(2)}, u32[]{:S(2)}) %collective-permute-start.8) | collective-permute-done | bytes 327712 | tf_op jit(solution)/shard_map/ppermute | solution.py:386
  83.0 1.9 %collective-permute-start.11 = (bf16[2048,128]{1,0:T(8,128)(2,1)}, bf16[2048,128]{1,0:T(8,128)(2,1)S(1)}, u32[]{:S(2)}, u32[]{:S(2)}) collective-permute-start(bf16[2048,128]{1,0:T(8,128)(2,1)} %get-tuple-element.35), channel_id=1, source_target_pairs={{0,2},{1,3},{2,0},{3,1},{4,6},{5,7},{6,4},{7,5},{8,10},{9,11},{10,... | collective-permute-start | bytes 1572872 | tf_op jit(solution)/shard_map/ppermute | solution.py:386
  84.9 2.8 %collective-permute-done.9 = bf16[640,128]{1,0:T(8,128)(2,1)S(1)} collective-permute-done((bf16[640,128]{1,0:T(8,128)(2,1)S(1)}, bf16[640,128]{1,0:T(8,128)(2,1)S(1)}, u32[]{:S(2)}, u32[]{:S(2)}) %collective-permute-start.9) | collective-permute-done | bytes 163872 | tf_op jit(solution)/shard_map/ppermute | solution.py:386
  89.1 1.3 collective-permute-start.6
  90.3 1.4 collective-permute-start.7
  91.7 5.9 %collective-permute-done.11.d3 = bf16[2048,128]{1,0:T(8,128)(2,1)S(1)} collective-permute-done((bf16[2048,128]{1,0:T(8,128)(2,1)}, bf16[2048,128]{1,0:T(8,128)(2,1)S(1)}, u32[]{:S(2)}, u32[]{:S(2)}) %collective-permute-start.11) | collective-permute-done | bytes 524320 | tf_op jit(solution)/shard_map/ppermute | solution.py:386
  97.6 1.6 %collective-permute-start.14 = (bf16[320,128]{1,0:T(8,128)(2,1)S(1)}, bf16[320,128]{1,0:T(8,128)(2,1)S(1)}, u32[]{:S(2)}, u32[]{:S(2)}) collective-permute-start(bf16[320,128]{1,0:T(8,128)(2,1)S(1)} %fusion.1), channel_id=1, source_target_pairs={{0,12},{4,8},{8,4},{12,0},{16,28},{20,24},{24,20},{28,16},{1,13},{... | collective-permute-start | bytes 245768 | tf_op jit(solution)/shard_map/ppermute | solution.py:386
  101.3 1.7 %collective-permute-done.14 = bf16[320,128]{1,0:T(8,128)(2,1)S(1)} collective-permute-done((bf16[320,128]{1,0:T(8,128)(2,1)S(1)}, bf16[320,128]{1,0:T(8,128)(2,1)S(1)}, u32[]{:S(2)}, u32[]{:S(2)}) %collective-permute-start.14) | collective-permute-done | bytes 81952 | tf_op jit(solution)/shard_map/ppermute | solution.py:386
  102.9 2.5 %collective-permute-done.13 = bf16[320,128]{1,0:T(8,128)(2,1)S(1)} collective-permute-done((bf16[320,128]{1,0:T(8,128)(2,1)S(1)}, bf16[320,128]{1,0:T(8,128)(2,1)S(1)}, u32[]{:S(2)}, u32[]{:S(2)}) %collective-permute-start.13) | collective-permute-done | bytes 81952 | tf_op jit(solution)/shard_map/ppermute | solution.py:386
  107.2 2.6 %collective-permute-done.6.d1 = bf16[2048,128]{1,0:T(8,128)(2,1)S(1)} collective-permute-done((bf16[2048,128]{1,0:T(8,128)(2,1)}, bf16[2048,128]{1,0:T(8,128)(2,1)S(1)}, u32[]{:S(2)}, u32[]{:S(2)}) %collective-permute-start.6) | collective-permute-done | bytes 524320 | tf_op jit(solution)/shard_map/ppermute | solution.py:386
  110.8 2.8 %to_slots.1 = bf16[1536,128]{1,0:T(8,128)(2,1)} custom-call(s32[8,128]{1,0:T(8,128)} %get-tuple-element.28.slot_ref, bf16[1024,128]{1,0:T(8,128)(2,1)} %grad_ref.1, bf16[2048,128]{1,0:T(8,128)(2,1)} %get-tuple-element.38.d0, bf16[2048,128]{1,0:T(8,128)(2,1)} %copy-done.5, bf16[2048,128]{1,0:T(8,128)(2,1)} %copy-done.6, bf16[2048,128]{1,0:T(8,128)(2,1)} %copy-done.4), custom_call_target="tpu_custom_call" | custom-call | tf_op jit(solution)/shard_map/to_slots/pallas_call | solution.py:333
  113.6 7.8 %all-to-all-start.2 = ((bf16[64,24,128]{2,1,0:T(8,128)(2,1)}), bf16[64,24,128]{2,1,0:T(8,128)(2,1)S(1)}, u32[]{:S(2)}, u32[]{:S(2)}) async-start(bf16[64,24,128]{2,1,0:T(8,128)(2,1)} %bitcast.32), calls=%async_computation.2 | async-start | bytes 786432 | tf_op jit(solution)/shard_map/all_to_all | solution.py:458
  121.4 2.0 %all_gather.3.p0 = bf16[640,128]{1,0:T(8,128)(2,1)S(1)} all-gather(bf16[320,128]{1,0:T(8,128)(2,1)S(1)} %add_convert_fusion.1), channel_id=1, replica_groups={{0,32},{64,96},{128,160},{192,224},{1,33},{65,97},{129,161},{193,225},{..., dimensions={0}, use_global_device_ids=true | all-gather | bytes 245760 | tf_op jit(solution)/shard_map/all_gather | solution.py:431
  123.5 2.9 %collective-permute-start.18 = (bf16[640,128]{1,0:T(8,128)(2,1)S(1)}, bf16[640,128]{1,0:T(8,128)(2,1)S(1)}, u32[]{:S(2)}, u32[]{:S(2)}) collective-permute-start(bf16[640,128]{1,0:T(8,128)(2,1)S(1)} %all_gather.3.p0), channel_id=1, source_target_pairs={{0,128},{32,160},{64,192},{96,224},{128,0},{160,32},{192,64},{224,... | collective-permute-start | bytes 491528 | tf_op jit(solution)/shard_map/ppermute | solution.py:386
  126.8 2.3 %collective-permute-start.16 = (bf16[640,128]{1,0:T(8,128)(2,1)S(1)}, bf16[640,128]{1,0:T(8,128)(2,1)S(1)}, u32[]{:S(2)}, u32[]{:S(2)}) collective-permute-start(bf16[640,128]{1,0:T(8,128)(2,1)S(1)} %all_gather.3.p0), channel_id=1, source_target_pairs={{0,192},{32,224},{64,0},{96,32},{128,64},{160,96},{192,128},{224,1... | collective-permute-start | bytes 491528 | tf_op jit(solution)/shard_map/ppermute | solution.py:386
  129.1 2.0 %add_convert_fusion = bf16[1024,128]{1,0:T(8,128)(2,1)} fusion(bf16[1024,128]{1,0:T(8,128)(2,1)S(1)} %copy-done, bf16[2048,128]{1,0:T(8,128)(2,1)} %copy-done.4, bf16[2048,128]{1,0:T(8,128)(2,1)} %copy-done.6, bf16[2048,128]{1,0:T(8,128)(2,1)} %copy-done.5, bf16[2048,128]{1,0:T(8,128)(2,1)S(1)} %copy-done.3), kind=kLoop, calls=%fused_computation.1 | loop fusion | flops 1310720 | bytes 1572864 | tf_op jit(solution)/shard_map/convert_element_type | solution.py:470
  131.1 5.2 %all-to-all-done.2 = bf16[64,24,128]{2,1,0:T(8,128)(2,1)S(1)} async-done(((bf16[64,24,128]{2,1,0:T(8,128)(2,1)}), bf16[64,24,128]{2,1,0:T(8,128)(2,1)S(1)}, u32[]{:S(2)}, u32[]{:S(2)}) %all-to-all-start.2) | async-done | bytes 393248 | tf_op jit(solution)/shard_map/all_to_all | solution.py:458
  137.0 3.1 %add_rows.1 = f32[2048,128]{1,0:T(8,128)} custom-call(s32[12,128]{1,0:T(8,128)} %reshape.59.req_ref, bf16[1536,128]{1,0:T(8,128)(2,1)} %bitcast.30), custom_call_target="tpu_custom_call" | custom-call | tf_op jit(solution)/shard_map/add_rows/pallas_call | solution.py:352
  140.9 2.4 %unpack.1 = (f32[2048,128]{1,0:T(8,128)}, f32[128,512]{1,0:T(8,128)}) custom-call(s32[1]{0:T(128)} %bitcast.17.y_ref, bf16[640,128]{1,0:T(8,128)(2,1)} %copy-done.8, bf16[640,128]{1,0:T(8,128)(2,1)} %copy-done.18, bf16[640,128]{1,0:T(8,128)(2,1)} %copy-done.17, bf16[640,128]{1,0:T(8,128)(2,1)} %copy-done.16), custom_call_target="tpu_custom_call" | custom-call | tf_op jit(solution)/shard_map/unpack/pallas_call | solution.py:374
  (68 shorter events, 12.8 us)
Async XLA Ops:
  27.6 5.3 %copy-start.7 = (bf16[1024,128]{1,0:T(8,128)(2,1)S(1)}, bf16[1024,128]{1,0:T(8,128)(2,1)}, u32[]{:S(2)}) copy-start(bf16[1024,128]{1,0:T(8,128)(2,1)} %grad_ref.1) | copy-start | bytes 786436
  27.6 20.2 %all-to-all-start.1 = ((bf16[64,24,128]{2,1,0:T(8,128)(2,1)}), bf16[64,24,128]{2,1,0:T(8,128)(2,1)S(1)}, u32[]{:S(2)}, u32[]{:S(2)}) async-start(bf16[64,24,128]{2,1,0:T(8,128)(2,1)} %bitcast.31), calls=%async_computation.1 | async-start | bytes 786432 | tf_op jit(solution)/shard_map/all_to_all | solution.py:445
  32.9 21.0 %collective-permute-start.5 = (bf16[1024,128]{1,0:T(8,128)(2,1)S(1)}, bf16[1024,128]{1,0:T(8,128)(2,1)S(1)}, u32[]{:S(2)}, u32[]{:S(2)}) collective-permute-start(bf16[1024,128]{1,0:T(8,128)(2,1)S(1)} %copy-done.7), channel_id=1, source_target_pairs={{0,2},{1,3},{2,0},{3,1},{4,6},{5,7},{6,4},{7,5},{8,10},{9,11},{10,... | collective-permute-start | bytes 786440 | tf_op jit(solution)/shard_map/ppermute | solution.py:386
  35.7 20.6 %collective-permute-start.4 = (bf16[1024,128]{1,0:T(8,128)(2,1)S(1)}, bf16[1024,128]{1,0:T(8,128)(2,1)S(1)}, u32[]{:S(2)}, u32[]{:S(2)}) collective-permute-start(bf16[1024,128]{1,0:T(8,128)(2,1)S(1)} %copy-done.7), channel_id=1, source_target_pairs={{0,1},{1,2},{2,3},{3,0},{4,5},{5,6},{6,7},{7,4},{8,9},{9,10},{10,1... | collective-permute-start | bytes 786440 | tf_op jit(solution)/shard_map/ppermute | solution.py:386
  36.1 20.3 %collective-permute-start.3 = (bf16[1024,128]{1,0:T(8,128)(2,1)S(1)}, bf16[1024,128]{1,0:T(8,128)(2,1)S(1)}, u32[]{:S(2)}, u32[]{:S(2)}) collective-permute-start(bf16[1024,128]{1,0:T(8,128)(2,1)S(1)} %copy-done.7), channel_id=1, source_target_pairs={{0,3},{1,0},{2,1},{3,2},{4,7},{5,4},{6,5},{7,6},{8,11},{9,8},{10,9... | collective-permute-start | bytes 786440 | tf_op jit(solution)/shard_map/ppermute | solution.py:386
  50.9 8.5 %collective-permute-start.2 = (bf16[1024,128]{1,0:T(8,128)(2,1)}, bf16[1024,128]{1,0:T(8,128)(2,1)S(1)}, u32[]{:S(2)}, u32[]{:S(2)}) collective-permute-start(bf16[1024,128]{1,0:T(8,128)(2,1)} %place.1.x0), channel_id=1, source_target_pairs={{0,2},{1,3},{2,0},{3,1},{4,6},{5,7},{6,4},{7,5},{8,10},{9,11},{10,... | collective-permute-start | bytes 786440 | tf_op jit(solution)/shard_map/ppermute | solution.py:386
  53.6 12.8 %collective-permute-start.1 = (bf16[1024,128]{1,0:T(8,128)(2,1)}, bf16[1024,128]{1,0:T(8,128)(2,1)S(1)}, u32[]{:S(2)}, u32[]{:S(2)}) collective-permute-start(bf16[1024,128]{1,0:T(8,128)(2,1)} %place.1.x0), channel_id=1, source_target_pairs={{0,1},{1,2},{2,3},{3,0},{4,5},{5,6},{6,7},{7,4},{8,9},{9,10},{10,1... | collective-permute-start | bytes 786440 | tf_op jit(solution)/shard_map/ppermute | solution.py:386
  53.9 12.5 %copy-start.10 = (bf16[1024,128]{1,0:T(8,128)(2,1)}, bf16[1024,128]{1,0:T(8,128)(2,1)S(1)}, u32[]{:S(2)}) copy-start(bf16[1024,128]{1,0:T(8,128)(2,1)S(1)} %collective-permute-done.5.g3) | copy-start | bytes 786436
  54.0 12.5 %collective-permute-start = (bf16[1024,128]{1,0:T(8,128)(2,1)}, bf16[1024,128]{1,0:T(8,128)(2,1)S(1)}, u32[]{:S(2)}, u32[]{:S(2)}) collective-permute-start(bf16[1024,128]{1,0:T(8,128)(2,1)} %place.1.x0), channel_id=1, source_target_pairs={{0,3},{1,0},{2,1},{3,2},{4,7},{5,4},{6,5},{7,6},{8,11},{9,8},{10,9... | collective-permute-start | bytes 786440 | tf_op jit(solution)/shard_map/ppermute | solution.py:386
  56.3 10.1 %copy-start.11 = (bf16[1024,128]{1,0:T(8,128)(2,1)}, bf16[1024,128]{1,0:T(8,128)(2,1)S(1)}, u32[]{:S(2)}) copy-start(bf16[1024,128]{1,0:T(8,128)(2,1)S(1)} %collective-permute-done.4.g2) | copy-start | bytes 786436
  56.3 10.1 %copy-start.12 = (bf16[1024,128]{1,0:T(8,128)(2,1)}, bf16[1024,128]{1,0:T(8,128)(2,1)S(1)}, u32[]{:S(2)}) copy-start(bf16[1024,128]{1,0:T(8,128)(2,1)S(1)} %collective-permute-done.3.g1) | copy-start | bytes 786436
  59.4 7.1 %copy-start.13 = (bf16[1024,128]{1,0:T(8,128)(2,1)}, bf16[1024,128]{1,0:T(8,128)(2,1)S(1)}, u32[]{:S(2)}) copy-start(bf16[1024,128]{1,0:T(8,128)(2,1)S(1)} %collective-permute-done.2.x3) | copy-start | bytes 786436
  79.0 2.0 %collective-permute-start.8 = (bf16[1280,128]{1,0:T(8,128)(2,1)}, bf16[1280,128]{1,0:T(8,128)(2,1)S(1)}, u32[]{:S(2)}, u32[]{:S(2)}) collective-permute-start(bf16[1280,128]{1,0:T(8,128)(2,1)} %get-tuple-element.34), channel_id=1, source_target_pairs={{0,32},{32,0},{64,96},{96,64},{128,160},{160,128},{192,224},{224,1... | collective-permute-start | bytes 983048 | tf_op jit(solution)/shard_map/ppermute | solution.py:386
  82.2 8.1 %copy-start.19 = (bf16[2048,128]{1,0:T(8,128)(2,1)S(1)}, bf16[2048,128]{1,0:T(8,128)(2,1)}, u32[]{:S(2)}) copy-start(bf16[2048,128]{1,0:T(8,128)(2,1)} %get-tuple-element.32) | copy-start | bytes 1572868
  82.2 5.5 %collective-permute-start.9 = (bf16[640,128]{1,0:T(8,128)(2,1)S(1)}, bf16[640,128]{1,0:T(8,128)(2,1)S(1)}, u32[]{:S(2)}, u32[]{:S(2)}) collective-permute-start(bf16[640,128]{1,0:T(8,128)(2,1)S(1)} %fusion), channel_id=1, source_target_pairs={{0,64},{32,96},{64,0},{96,32},{128,192},{160,224},{192,128},{224,1... | collective-permute-start | bytes 491528 | tf_op jit(solution)/shard_map/ppermute | solution.py:386
  83.0 14.6 %collective-permute-start.11 = (bf16[2048,128]{1,0:T(8,128)(2,1)}, bf16[2048,128]{1,0:T(8,128)(2,1)S(1)}, u32[]{:S(2)}, u32[]{:S(2)}) collective-permute-start(bf16[2048,128]{1,0:T(8,128)(2,1)} %get-tuple-element.35), channel_id=1, source_target_pairs={{0,2},{1,3},{2,0},{3,1},{4,6},{5,7},{6,4},{7,5},{8,10},{9,11},{10,... | collective-permute-start | bytes 1572872 | tf_op jit(solution)/shard_map/ppermute | solution.py:386
  87.8 9.8 %collective-permute-start.10 = (bf16[320,128]{1,0:T(8,128)(2,1)S(1)}, bf16[320,128]{1,0:T(8,128)(2,1)S(1)}, u32[]{:S(2)}, u32[]{:S(2)}) collective-permute-start(bf16[320,128]{1,0:T(8,128)(2,1)S(1)} %fusion.2), channel_id=1, source_target_pairs={{0,192},{32,224},{64,128},{96,160},{128,64},{160,96},{192,0},{224,... | collective-permute-start | bytes 245768 | tf_op jit(solution)/shard_map/ppermute | solution.py:386
  89.1 20.8 %collective-permute-start.6 = (bf16[2048,128]{1,0:T(8,128)(2,1)}, bf16[2048,128]{1,0:T(8,128)(2,1)S(1)}, u32[]{:S(2)}, u32[]{:S(2)}) collective-permute-start(bf16[2048,128]{1,0:T(8,128)(2,1)} %get-tuple-element.31), channel_id=1, source_target_pairs={{0,1},{1,2},{2,3},{3,0},{4,5},{5,6},{6,7},{7,4},{8,9},{9,10},{10,1... | collective-permute-start | bytes 1572872 | tf_op jit(solution)/shard_map/ppermute | solution.py:386
  90.3 19.5 %collective-permute-start.7 = (bf16[2048,128]{1,0:T(8,128)(2,1)S(1)}, bf16[2048,128]{1,0:T(8,128)(2,1)S(1)}, u32[]{:S(2)}, u32[]{:S(2)}) collective-permute-start(bf16[2048,128]{1,0:T(8,128)(2,1)S(1)} %copy-done.19), channel_id=1, source_target_pairs={{0,3},{1,0},{2,1},{3,2},{4,7},{5,4},{6,5},{7,6},{8,11},{9,8},{10,9... | collective-permute-start | bytes 1572872 | tf_op jit(solution)/shard_map/ppermute | solution.py:386
  97.6 12.2 %copy-start.4 = (bf16[2048,128]{1,0:T(8,128)(2,1)}, bf16[2048,128]{1,0:T(8,128)(2,1)S(1)}, u32[]{:S(2)}) copy-start(bf16[2048,128]{1,0:T(8,128)(2,1)S(1)} %collective-permute-done.11.d3) | copy-start | bytes 1572868
  97.6 8.9 %copy-start.9 = (s32[64,1,128]{2,1,0:T(1,128)S(1)}, s32[64,1,128]{2,1,0:T(1,128)}, u32[]{:S(2)}) copy-start(s32[64,1,128]{2,1,0:T(1,128)} %all_to_all.21) | copy-start | bytes 98308
  97.6 5.3 %collective-permute-start.14 = (bf16[320,128]{1,0:T(8,128)(2,1)S(1)}, bf16[320,128]{1,0:T(8,128)(2,1)S(1)}, u32[]{:S(2)}, u32[]{:S(2)}) collective-permute-start(bf16[320,128]{1,0:T(8,128)(2,1)S(1)} %fusion.1), channel_id=1, source_target_pairs={{0,12},{4,8},{8,4},{12,0},{16,28},{20,24},{24,20},{28,16},{1,13},{... | collective-permute-start | bytes 245768 | tf_op jit(solution)/shard_map/ppermute | solution.py:386
  99.2 6.2 %collective-permute-start.13 = (bf16[320,128]{1,0:T(8,128)(2,1)S(1)}, bf16[320,128]{1,0:T(8,128)(2,1)S(1)}, u32[]{:S(2)}, u32[]{:S(2)}) collective-permute-start(bf16[320,128]{1,0:T(8,128)(2,1)S(1)} %fusion.1), channel_id=1, source_target_pairs={{0,8},{4,12},{8,0},{12,4},{16,24},{20,28},{24,16},{28,20},{1,9},{5... | collective-permute-start | bytes 245768 | tf_op jit(solution)/shard_map/ppermute | solution.py:386
  100.3 5.1 %collective-permute-start.12 = (bf16[320,128]{1,0:T(8,128)(2,1)S(1)}, bf16[320,128]{1,0:T(8,128)(2,1)S(1)}, u32[]{:S(2)}, u32[]{:S(2)}) collective-permute-start(bf16[320,128]{1,0:T(8,128)(2,1)S(1)} %fusion.1), channel_id=1, source_target_pairs={{0,4},{4,0},{8,12},{12,8},{16,20},{20,16},{24,28},{28,24},{1,5},{5... | collective-permute-start | bytes 245768 | tf_op jit(solution)/shard_map/ppermute | solution.py:386
  105.5 8.1 %collective-permute-start.15 = (bf16[320,128]{1,0:T(8,128)(2,1)S(1)}, bf16[320,128]{1,0:T(8,128)(2,1)S(1)}, u32[]{:S(2)}, u32[]{:S(2)}) collective-permute-start(bf16[320,128]{1,0:T(8,128)(2,1)S(1)} %add_convert_fusion.2), channel_id=1, source_target_pairs={{0,28},{4,24},{8,20},{12,16},{16,12},{20,8},{24,4},{28,0},{1,29},{... | collective-permute-start | bytes 245768 | tf_op jit(solution)/shard_map/ppermute | solution.py:386
  113.6 15.5 %copy-start.3 = (bf16[2048,128]{1,0:T(8,128)(2,1)S(1)}, bf16[2048,128]{1,0:T(8,128)(2,1)}, u32[]{:S(2)}) copy-start(bf16[2048,128]{1,0:T(8,128)(2,1)} %get-tuple-element.38.d0) | copy-start | bytes 1572868
  113.6 15.5 %copy-start = (bf16[1024,128]{1,0:T(8,128)(2,1)S(1)}, bf16[1024,128]{1,0:T(8,128)(2,1)}, u32[]{:S(2)}) copy-start(bf16[1024,128]{1,0:T(8,128)(2,1)} %place.1.x0) | copy-start | bytes 786436
  113.6 22.6 %all-to-all-start.2 = ((bf16[64,24,128]{2,1,0:T(8,128)(2,1)}), bf16[64,24,128]{2,1,0:T(8,128)(2,1)S(1)}, u32[]{:S(2)}, u32[]{:S(2)}) async-start(bf16[64,24,128]{2,1,0:T(8,128)(2,1)} %bitcast.32), calls=%async_computation.2 | async-start | bytes 786432 | tf_op jit(solution)/shard_map/all_to_all | solution.py:458
  123.5 7.6 %copy-start.8 = (bf16[640,128]{1,0:T(8,128)(2,1)}, bf16[640,128]{1,0:T(8,128)(2,1)S(1)}, u32[]{:S(2)}) copy-start(bf16[640,128]{1,0:T(8,128)(2,1)S(1)} %all_gather.3.p0) | copy-start | bytes 491524
  123.5 16.6 %collective-permute-start.18 = (bf16[640,128]{1,0:T(8,128)(2,1)S(1)}, bf16[640,128]{1,0:T(8,128)(2,1)S(1)}, u32[]{:S(2)}, u32[]{:S(2)}) collective-permute-start(bf16[640,128]{1,0:T(8,128)(2,1)S(1)} %all_gather.3.p0), channel_id=1, source_target_pairs={{0,128},{32,160},{64,192},{96,224},{128,0},{160,32},{192,64},{224,... | collective-permute-start | bytes 491528 | tf_op jit(solution)/shard_map/ppermute | solution.py:386
  126.4 13.7 %collective-permute-start.17 = (bf16[640,128]{1,0:T(8,128)(2,1)S(1)}, bf16[640,128]{1,0:T(8,128)(2,1)S(1)}, u32[]{:S(2)}, u32[]{:S(2)}) collective-permute-start(bf16[640,128]{1,0:T(8,128)(2,1)S(1)} %all_gather.3.p0), channel_id=1, source_target_pairs={{0,64},{32,96},{64,128},{96,160},{128,192},{160,224},{192,0},{224,... | collective-permute-start | bytes 491528 | tf_op jit(solution)/shard_map/ppermute | solution.py:386
  126.8 13.3 %collective-permute-start.16 = (bf16[640,128]{1,0:T(8,128)(2,1)S(1)}, bf16[640,128]{1,0:T(8,128)(2,1)S(1)}, u32[]{:S(2)}, u32[]{:S(2)}) collective-permute-start(bf16[640,128]{1,0:T(8,128)(2,1)S(1)} %all_gather.3.p0), channel_id=1, source_target_pairs={{0,192},{32,224},{64,0},{96,32},{128,64},{160,96},{192,128},{224,1... | collective-permute-start | bytes 491528 | tf_op jit(solution)/shard_map/ppermute | solution.py:386
  (9 other events, 6.9 us)

commit v12 on v11

--- a/solution.py
+++ b/solution.py
@@ -404,14 +404,15 @@
     return ((y == 1) | (y == 2)).astype(I32), (y >= 2).astype(I32)
 
 
-def reduce_over_chips(mine, other):
+def reduce_over_chips(mine, other, far):
     half, quarter = y_place(lax.axis_index("table") // 2)
     other = shift(other, "table", lambda i: i ^ 1, 8)
     mine = (mine + other.astype(F32)).reshape(2, 640, 128)
     got = shift(pick(mine, 1 - half).astype(BF), "table", lambda i: i ^ 2, 8)
+    got, far = lax.optimization_barrier((got, far))
     mine = (pick(mine, half) + got.astype(F32)).reshape(2, 320, 128)
     got = shift(pick(mine, 1 - quarter).astype(BF), "table", lambda i: 6 - (i & 6) + (i & 1), 8)
-    return pick(mine, quarter), got
+    return pick(mine, quarter), got, far
 
 
 def add_step(total, mask):
@@ -447,9 +448,8 @@
     xs = gather_pieces(x)
     mine, other, c0, c1, c2, c3 = layer(pos, core, segment_ids, xs, gs, proj_in, proj_out)
     cparts = scatter_pieces([c0, c1, c2, c3])
-    own, got = reduce_over_chips(mine, other)
+    own, got, cparts[3] = reduce_over_chips(mine, other, cparts[3])
     flat = received[:, :CAP].reshape(SLOTS // 128, 128)
-    got, cparts[3] = lax.optimization_barrier((got, cparts[3]))
     total = add_group((own + got.astype(F32)).astype(BF))
     cparts, _, flat = lax.optimization_barrier((cparts, total, flat))
     grads = to_slots(slot, grad_out, cparts)

time: 144 us -> 145 us (level)
  waiting for transfers between devices: 41.5 us -> 43.2 us
    ppermute x19, waiting for transfers between devices: 27 us -> 28.6 us  [shift(): return lax.ppermute(x, axis, [(i, fn(i)) for i in range(n)])]
    unnamed x40 -> x42, local copies, waits for them, and re-layouts: 3.99 us -> 4.02 us
  transfers between devices with their start and end apart: 21 -> 21, of which waited for: 10 -> 10; matrix products, arithmetic and copies ran while one was open for 2% -> 3% of each run, Pallas kernels for 6% -> 6%
where the time goes in v12:
time: 145 us; the launch traced here: 144 us
  waiting for transfers between devices  43.2 us (30%)
  starting transfers between devices  40.9 us (28%)
  Pallas kernels  27.1 us (19%)
  blocking collectives  24.4 us (17%)
  local copies, waits for them, and re-layouts  4.74 us (3%)
  other arithmetic  3.17 us (2%)
    ppermute x19, waiting for transfers between devices, shift(): return lax.ppermute(x, axis, [(i, fn(i)) for i in range(n)])  28.6 us
    ppermute x19, starting transfers between devices, shift(): return lax.ppermute(x, axis, [(i, fn(i)) for i in range(n)])  27.5 us
    all_to_all x1, blocking collectives, body(): lax.all_to_all(requests, BOTH, split_axis=0, concat_axis=0, tiled=True)  22.4 us
    pallas_call x1, Pallas kernels, layer(): pl.pallas_call(layer_kernel, out_shape=(jax.ShapeDtypeStruct((1280, 128),...  11.7 us
    all_to_all x1, waiting for transfers between devices, body(): lax.all_to_all(rows.reshape(NOWN, CAP, 128), BOTH, split_axis=0, concat_a...  9.36 us
    all_to_all x1, starting transfers between devices, body(): lax.all_to_all(grads.reshape(NOWN, CAP, 128), BOTH, split_axis=0, concat_...  8.41 us
    all_to_all x1, waiting for transfers between devices, body(): lax.all_to_all(grads.reshape(NOWN, CAP, 128), BOTH, split_axis=0, concat_...  5.27 us
    all_to_all x1, starting transfers between devices, body(): lax.all_to_all(rows.reshape(NOWN, CAP, 128), BOTH, split_axis=0, concat_a...  4.98 us
  transfers between devices with their start and end apart: 21, of which 10 were waited for; matrix products, arithmetic and copies ran while one was open for 3% of the time, Pallas kernels for 6%

profile of v12, /device:TPU:1, one launch (start us, length us, event | category | flops | bytes accessed | tf_op | source)
XLA Modules:
  0.0 144.4 jit_solution(12841186784492347915)
XLA Ops:
  0.6 1.8 %route.1 = (s32[64,128]{1,0:T(8,128)}, s32[8,128]{1,0:T(8,128)}) custom-call(s32[8,128]{1,0:T(8,128)} %bitcast.38, s32[8,128]{1,0:T(8,128)} %bitcast.39), custom_call_target="tpu_custom_call" | custom-call | tf_op jit(solution)/shard_map/route/pallas_call | solution.py:63
  2.5 22.4 %all_to_all.21 = s32[64,1,128]{2,1,0:T(1,128)} all-to-all(s32[64,1,128]{2,1,0:T(1,128)} %bitcast.37), channel_id=1, replica_groups=mesh['table'=8,'seq'=8,'tensor'=4] {'table','seq'}, dimensions={0} | all-to-all | bytes 65536 | tf_op jit(solution)/shard_map/all_to_all | solution.py:444
  24.9 2.9 %fetch.1 = bf16[1536,128]{1,0:T(8,128)(2,1)} custom-call(s32[64,128]{1,0:T(8,128)} %bitcast.35, bf16[2048,128]{1,0:T(8,128)(2,1)} %table_ref.1), custom_call_target="tpu_custom_call" | custom-call | tf_op jit(solution)/shard_map/fetch/pallas_call | solution.py:99
  27.8 5.0 %all-to-all-start.1 = ((bf16[64,24,128]{2,1,0:T(8,128)(2,1)}), bf16[64,24,128]{2,1,0:T(8,128)(2,1)S(1)}, u32[]{:S(2)}, u32[]{:S(2)}) async-start(bf16[64,24,128]{2,1,0:T(8,128)(2,1)} %bitcast.31), calls=%async_computation.1 | async-start | bytes 786432 | tf_op jit(solution)/shard_map/all_to_all | solution.py:446
  32.8 2.8 %collective-permute-start.5 = (bf16[1024,128]{1,0:T(8,128)(2,1)S(1)}, bf16[1024,128]{1,0:T(8,128)(2,1)S(1)}, u32[]{:S(2)}, u32[]{:S(2)}) collective-permute-start(bf16[1024,128]{1,0:T(8,128)(2,1)S(1)} %copy-done.8), channel_id=1, source_target_pairs={{0,2},{1,3},{2,0},{3,1},{4,6},{5,7},{6,4},{7,5},{8,10},{9,11},{10,... | collective-permute-start | bytes 786440 | tf_op jit(solution)/shard_map/ppermute | solution.py:386
  35.9 2.4 %collective-permute-start.3 = (bf16[1024,128]{1,0:T(8,128)(2,1)S(1)}, bf16[1024,128]{1,0:T(8,128)(2,1)S(1)}, u32[]{:S(2)}, u32[]{:S(2)}) collective-permute-start(bf16[1024,128]{1,0:T(8,128)(2,1)S(1)} %copy-done.8), channel_id=1, source_target_pairs={{0,3},{1,0},{2,1},{3,2},{4,7},{5,4},{6,5},{7,6},{8,11},{9,8},{10,9... | collective-permute-start | bytes 786440 | tf_op jit(solution)/shard_map/ppermute | solution.py:386
  38.3 9.4 %all-to-all-done.1 = bf16[64,24,128]{2,1,0:T(8,128)(2,1)S(1)} async-done(((bf16[64,24,128]{2,1,0:T(8,128)(2,1)}), bf16[64,24,128]{2,1,0:T(8,128)(2,1)S(1)}, u32[]{:S(2)}, u32[]{:S(2)}) %all-to-all-start.1) | async-done | bytes 393248 | tf_op jit(solution)/shard_map/all_to_all | solution.py:446
  48.4 2.4 %place.1.x0 = bf16[1024,128]{1,0:T(8,128)(2,1)} custom-call(s32[8,128]{1,0:T(8,128)} %get-tuple-element.28.slot_ref, bf16[1536,128]{1,0:T(8,128)(2,1)} %bitcast.29), custom_call_target="tpu_custom_call" | custom-call | tf_op jit(solution)/shard_map/place/pallas_call | solution.py:134
  50.7 2.7 %collective-permute-start.2 = (bf16[1024,128]{1,0:T(8,128)(2,1)}, bf16[1024,128]{1,0:T(8,128)(2,1)S(1)}, u32[]{:S(2)}, u32[]{:S(2)}) collective-permute-start(bf16[1024,128]{1,0:T(8,128)(2,1)} %place.1.x0), channel_id=1, source_target_pairs={{0,2},{1,3},{2,0},{3,1},{4,6},{5,7},{6,4},{7,5},{8,10},{9,11},{10,... | collective-permute-start | bytes 786440 | tf_op jit(solution)/shard_map/ppermute | solution.py:386
  53.8 2.4 %collective-permute-start = (bf16[1024,128]{1,0:T(8,128)(2,1)}, bf16[1024,128]{1,0:T(8,128)(2,1)S(1)}, u32[]{:S(2)}, u32[]{:S(2)}) collective-permute-start(bf16[1024,128]{1,0:T(8,128)(2,1)} %place.1.x0), channel_id=1, source_target_pairs={{0,3},{1,0},{2,1},{3,2},{4,7},{5,4},{6,5},{7,6},{8,11},{9,8},{10,9... | collective-permute-start | bytes 786440 | tf_op jit(solution)/shard_map/ppermute | solution.py:386
  56.2 3.1 %collective-permute-done.2.x3 = bf16[1024,128]{1,0:T(8,128)(2,1)S(1)} collective-permute-done((bf16[1024,128]{1,0:T(8,128)(2,1)}, bf16[1024,128]{1,0:T(8,128)(2,1)S(1)}, u32[]{:S(2)}, u32[]{:S(2)}) %collective-permute-start.2) | collective-permute-done | bytes 262176 | tf_op jit(solution)/shard_map/ppermute | solution.py:386
  59.3 7.0 %collective-permute-done.1.x2 = bf16[1024,128]{1,0:T(8,128)(2,1)S(1)} collective-permute-done((bf16[1024,128]{1,0:T(8,128)(2,1)}, bf16[1024,128]{1,0:T(8,128)(2,1)S(1)}, u32[]{:S(2)}, u32[]{:S(2)}) %collective-permute-start.1) | collective-permute-done | bytes 262176 | tf_op jit(solution)/shard_map/ppermute | solution.py:386
  67.1 11.7 %layer.1 = (f32[1280,128]{1,0:T(8,128)}, bf16[1280,128]{1,0:T(8,128)(2,1)}, bf16[2048,128]{1,0:T(8,128)(2,1)}, bf16[2048,128]{1,0:T(8,128)(2,1)}, bf16[2048,128]{1,0:T(8,128)(2,1)}, /*index=5*/bf16[2048,128]{1,0:T(8,128)(2,1)}) custom-call(s32[1]{0:T(128)} %bitcast.7.pos_ref, s32[1]{0:T(128)} %bitcast.8.core_ref, s32[1,1024]{1,0:T(1,128)} %seg_ref.1, ...), custom_call_target="tpu_custom_call" | custom-call | tf_op jit(solution)/shard_map/layer/pallas_call | solution.py:277
  79.4 1.9 %collective-permute-start.10 = (bf16[2048,128]{1,0:T(8,128)(2,1)}, bf16[2048,128]{1,0:T(8,128)(2,1)S(1)}, u32[]{:S(2)}, u32[]{:S(2)}) collective-permute-start(bf16[2048,128]{1,0:T(8,128)(2,1)} %get-tuple-element.35), channel_id=1, source_target_pairs={{0,2},{1,3},{2,0},{3,1},{4,6},{5,7},{6,4},{7,5},{8,10},{9,11},{10,... | collective-permute-start | bytes 1572872 | tf_op jit(solution)/shard_map/ppermute | solution.py:386
  83.3 4.6 %collective-permute-done.9 = bf16[640,128]{1,0:T(8,128)(2,1)S(1)} collective-permute-done((bf16[640,128]{1,0:T(8,128)(2,1)S(1)}, bf16[640,128]{1,0:T(8,128)(2,1)S(1)}, u32[]{:S(2)}, u32[]{:S(2)}) %collective-permute-start.9) | collective-permute-done | bytes 163872 | tf_op jit(solution)/shard_map/ppermute | solution.py:386
  87.9 6.6 %collective-permute-done.10.d3 = bf16[2048,128]{1,0:T(8,128)(2,1)S(1)} collective-permute-done((bf16[2048,128]{1,0:T(8,128)(2,1)}, bf16[2048,128]{1,0:T(8,128)(2,1)S(1)}, u32[]{:S(2)}, u32[]{:S(2)}) %collective-permute-start.10) | collective-permute-done | bytes 524320 | tf_op jit(solution)/shard_map/ppermute | solution.py:386
  94.6 1.3 collective-permute-start.11
  95.9 1.3 collective-permute-start.6
  97.2 1.4 collective-permute-start.7
  99.2 2.0 %collective-permute-start.14 = (bf16[320,128]{1,0:T(8,128)(2,1)S(1)}, bf16[320,128]{1,0:T(8,128)(2,1)S(1)}, u32[]{:S(2)}, u32[]{:S(2)}) collective-permute-start(bf16[320,128]{1,0:T(8,128)(2,1)S(1)} %fusion.1), channel_id=1, source_target_pairs={{0,12},{4,8},{8,4},{12,0},{16,28},{20,24},{24,20},{28,16},{1,13},{... | collective-permute-start | bytes 245768 | tf_op jit(solution)/shard_map/ppermute | solution.py:386
  101.5 1.3 collective-permute-start.12
  102.8 1.6 %collective-permute-done.14 = bf16[320,128]{1,0:T(8,128)(2,1)S(1)} collective-permute-done((bf16[320,128]{1,0:T(8,128)(2,1)S(1)}, bf16[320,128]{1,0:T(8,128)(2,1)S(1)}, u32[]{:S(2)}, u32[]{:S(2)}) %collective-permute-start.14) | collective-permute-done | bytes 81952 | tf_op jit(solution)/shard_map/ppermute | solution.py:386
  104.4 4.6 %collective-permute-done.13 = bf16[320,128]{1,0:T(8,128)(2,1)S(1)} collective-permute-done((bf16[320,128]{1,0:T(8,128)(2,1)S(1)}, bf16[320,128]{1,0:T(8,128)(2,1)S(1)}, u32[]{:S(2)}, u32[]{:S(2)}) %collective-permute-start.13) | collective-permute-done | bytes 81952 | tf_op jit(solution)/shard_map/ppermute | solution.py:386
  110.8 2.8 %to_slots.1 = bf16[1536,128]{1,0:T(8,128)(2,1)} custom-call(s32[8,128]{1,0:T(8,128)} %get-tuple-element.28.slot_ref, bf16[1024,128]{1,0:T(8,128)(2,1)} %grad_ref.1, bf16[2048,128]{1,0:T(8,128)(2,1)} %get-tuple-element.38.d0, bf16[2048,128]{1,0:T(8,128)(2,1)} %copy-done.6, bf16[2048,128]{1,0:T(8,128)(2,1)} %copy-done.7, bf16[2048,128]{1,0:T(8,128)(2,1)} %copy-done.4), custom_call_target="tpu_custom_call" | custom-call | tf_op jit(solution)/shard_map/to_slots/pallas_call | solution.py:333
  114.2 8.4 %all-to-all-start.2 = ((bf16[64,24,128]{2,1,0:T(8,128)(2,1)}), bf16[64,24,128]{2,1,0:T(8,128)(2,1)S(1)}, u32[]{:S(2)}, u32[]{:S(2)}) async-start(bf16[64,24,128]{2,1,0:T(8,128)(2,1)} %bitcast.32), calls=%async_computation.2 | async-start | bytes 786432 | tf_op jit(solution)/shard_map/all_to_all | solution.py:458
  122.6 2.0 %all_gather.3.p0 = bf16[640,128]{1,0:T(8,128)(2,1)S(1)} all-gather(bf16[320,128]{1,0:T(8,128)(2,1)S(1)} %add_convert_fusion.1), channel_id=1, replica_groups={{0,32},{64,96},{128,160},{192,224},{1,33},{65,97},{129,161},{193,225},{..., dimensions={0}, use_global_device_ids=true | all-gather | bytes 245760 | tf_op jit(solution)/shard_map/all_gather | solution.py:432
  124.6 2.9 %collective-permute-start.18 = (bf16[640,128]{1,0:T(8,128)(2,1)S(1)}, bf16[640,128]{1,0:T(8,128)(2,1)S(1)}, u32[]{:S(2)}, u32[]{:S(2)}) collective-permute-start(bf16[640,128]{1,0:T(8,128)(2,1)S(1)} %all_gather.3.p0), channel_id=1, source_target_pairs={{0,128},{32,160},{64,192},{96,224},{128,0},{160,32},{192,64},{224,... | collective-permute-start | bytes 491528 | tf_op jit(solution)/shard_map/ppermute | solution.py:386
  128.0 2.3 %collective-permute-start.16 = (bf16[640,128]{1,0:T(8,128)(2,1)S(1)}, bf16[640,128]{1,0:T(8,128)(2,1)S(1)}, u32[]{:S(2)}, u32[]{:S(2)}) collective-permute-start(bf16[640,128]{1,0:T(8,128)(2,1)S(1)} %all_gather.3.p0), channel_id=1, source_target_pairs={{0,192},{32,224},{64,0},{96,32},{128,64},{160,96},{192,128},{224,1... | collective-permute-start | bytes 491528 | tf_op jit(solution)/shard_map/ppermute | solution.py:386
  130.3 1.9 %add_convert_fusion = bf16[1024,128]{1,0:T(8,128)(2,1)} fusion(bf16[1024,128]{1,0:T(8,128)(2,1)S(1)} %copy-done, bf16[2048,128]{1,0:T(8,128)(2,1)S(1)} %copy-done.5, bf16[2048,128]{1,0:T(8,128)(2,1)} %copy-done.7, bf16[2048,128]{1,0:T(8,128)(2,1)} %copy-done.6, bf16[2048,128]{1,0:T(8,128)(2,1)S(1)} %copy-done.3), kind=kLoop, calls=%fused_computation.1 | loop fusion | flops 1310720 | bytes 1572864 | tf_op jit(solution)/shard_map/convert_element_type | solution.py:470
  132.2 5.3 %all-to-all-done.2 = bf16[64,24,128]{2,1,0:T(8,128)(2,1)S(1)} async-done(((bf16[64,24,128]{2,1,0:T(8,128)(2,1)}), bf16[64,24,128]{2,1,0:T(8,128)(2,1)S(1)}, u32[]{:S(2)}, u32[]{:S(2)}) %all-to-all-start.2) | async-done | bytes 393248 | tf_op jit(solution)/shard_map/all_to_all | solution.py:458
  138.2 3.1 %add_rows.1 = f32[2048,128]{1,0:T(8,128)} custom-call(s32[12,128]{1,0:T(8,128)} %reshape.59.req_ref, bf16[1536,128]{1,0:T(8,128)(2,1)} %bitcast.30), custom_call_target="tpu_custom_call" | custom-call | tf_op jit(solution)/shard_map/add_rows/pallas_call | solution.py:352
  142.1 2.4 %unpack.1 = (f32[2048,128]{1,0:T(8,128)}, f32[128,512]{1,0:T(8,128)}) custom-call(s32[1]{0:T(128)} %bitcast.17.y_ref, bf16[640,128]{1,0:T(8,128)(2,1)} %copy-done.9, bf16[640,128]{1,0:T(8,128)(2,1)} %copy-done.19, bf16[640,128]{1,0:T(8,128)(2,1)} %copy-done.18, bf16[640,128]{1,0:T(8,128)(2,1)} %copy-done.17), custom_call_target="tpu_custom_call" | custom-call | tf_op jit(solution)/shard_map/unpack/pallas_call | solution.py:374
  (70 shorter events, 10.0 us)
Async XLA Ops:
  27.8 5.0 %copy-start.8 = (bf16[1024,128]{1,0:T(8,128)(2,1)S(1)}, bf16[1024,128]{1,0:T(8,128)(2,1)}, u32[]{:S(2)}) copy-start(bf16[1024,128]{1,0:T(8,128)(2,1)} %grad_ref.1) | copy-start | bytes 786436
  27.8 19.9 %all-to-all-start.1 = ((bf16[64,24,128]{2,1,0:T(8,128)(2,1)}), bf16[64,24,128]{2,1,0:T(8,128)(2,1)S(1)}, u32[]{:S(2)}, u32[]{:S(2)}) async-start(bf16[64,24,128]{2,1,0:T(8,128)(2,1)} %bitcast.31), calls=%async_computation.1 | async-start | bytes 786432 | tf_op jit(solution)/shard_map/all_to_all | solution.py:446
  32.8 21.0 %collective-permute-start.5 = (bf16[1024,128]{1,0:T(8,128)(2,1)S(1)}, bf16[1024,128]{1,0:T(8,128)(2,1)S(1)}, u32[]{:S(2)}, u32[]{:S(2)}) collective-permute-start(bf16[1024,128]{1,0:T(8,128)(2,1)S(1)} %copy-done.8), channel_id=1, source_target_pairs={{0,2},{1,3},{2,0},{3,1},{4,6},{5,7},{6,4},{7,5},{8,10},{9,11},{10,... | collective-permute-start | bytes 786440 | tf_op jit(solution)/shard_map/ppermute | solution.py:386
  35.6 20.6 %collective-permute-start.4 = (bf16[1024,128]{1,0:T(8,128)(2,1)S(1)}, bf16[1024,128]{1,0:T(8,128)(2,1)S(1)}, u32[]{:S(2)}, u32[]{:S(2)}) collective-permute-start(bf16[1024,128]{1,0:T(8,128)(2,1)S(1)} %copy-done.8), channel_id=1, source_target_pairs={{0,1},{1,2},{2,3},{3,0},{4,5},{5,6},{6,7},{7,4},{8,9},{9,10},{10,1... | collective-permute-start | bytes 786440 | tf_op jit(solution)/shard_map/ppermute | solution.py:386
  35.9 20.3 %collective-permute-start.3 = (bf16[1024,128]{1,0:T(8,128)(2,1)S(1)}, bf16[1024,128]{1,0:T(8,128)(2,1)S(1)}, u32[]{:S(2)}, u32[]{:S(2)}) collective-permute-start(bf16[1024,128]{1,0:T(8,128)(2,1)S(1)} %copy-done.8), channel_id=1, source_target_pairs={{0,3},{1,0},{2,1},{3,2},{4,7},{5,4},{6,5},{7,6},{8,11},{9,8},{10,9... | collective-permute-start | bytes 786440 | tf_op jit(solution)/shard_map/ppermute | solution.py:386
  50.7 8.5 %collective-permute-start.2 = (bf16[1024,128]{1,0:T(8,128)(2,1)}, bf16[1024,128]{1,0:T(8,128)(2,1)S(1)}, u32[]{:S(2)}, u32[]{:S(2)}) collective-permute-start(bf16[1024,128]{1,0:T(8,128)(2,1)} %place.1.x0), channel_id=1, source_target_pairs={{0,2},{1,3},{2,0},{3,1},{4,6},{5,7},{6,4},{7,5},{8,10},{9,11},{10,... | collective-permute-start | bytes 786440 | tf_op jit(solution)/shard_map/ppermute | solution.py:386
  53.5 12.8 %collective-permute-start.1 = (bf16[1024,128]{1,0:T(8,128)(2,1)}, bf16[1024,128]{1,0:T(8,128)(2,1)S(1)}, u32[]{:S(2)}, u32[]{:S(2)}) collective-permute-start(bf16[1024,128]{1,0:T(8,128)(2,1)} %place.1.x0), channel_id=1, source_target_pairs={{0,1},{1,2},{2,3},{3,0},{4,5},{5,6},{6,7},{7,4},{8,9},{9,10},{10,1... | collective-permute-start | bytes 786440 | tf_op jit(solution)/shard_map/ppermute | solution.py:386
  53.8 12.5 %copy-start.11 = (bf16[1024,128]{1,0:T(8,128)(2,1)}, bf16[1024,128]{1,0:T(8,128)(2,1)S(1)}, u32[]{:S(2)}) copy-start(bf16[1024,128]{1,0:T(8,128)(2,1)S(1)} %collective-permute-done.5.g3) | copy-start | bytes 786436
  53.8 12.5 %collective-permute-start = (bf16[1024,128]{1,0:T(8,128)(2,1)}, bf16[1024,128]{1,0:T(8,128)(2,1)S(1)}, u32[]{:S(2)}, u32[]{:S(2)}) collective-permute-start(bf16[1024,128]{1,0:T(8,128)(2,1)} %place.1.x0), channel_id=1, source_target_pairs={{0,3},{1,0},{2,1},{3,2},{4,7},{5,4},{6,5},{7,6},{8,11},{9,8},{10,9... | collective-permute-start | bytes 786440 | tf_op jit(solution)/shard_map/ppermute | solution.py:386
  56.2 10.1 %copy-start.12 = (bf16[1024,128]{1,0:T(8,128)(2,1)}, bf16[1024,128]{1,0:T(8,128)(2,1)S(1)}, u32[]{:S(2)}) copy-start(bf16[1024,128]{1,0:T(8,128)(2,1)S(1)} %collective-permute-done.4.g2) | copy-start | bytes 786436
  56.2 10.1 %copy-start.13 = (bf16[1024,128]{1,0:T(8,128)(2,1)}, bf16[1024,128]{1,0:T(8,128)(2,1)S(1)}, u32[]{:S(2)}) copy-start(bf16[1024,128]{1,0:T(8,128)(2,1)S(1)} %collective-permute-done.3.g1) | copy-start | bytes 786436
  59.3 7.1 %copy-start.14 = (bf16[1024,128]{1,0:T(8,128)(2,1)}, bf16[1024,128]{1,0:T(8,128)(2,1)S(1)}, u32[]{:S(2)}) copy-start(bf16[1024,128]{1,0:T(8,128)(2,1)S(1)} %collective-permute-done.2.x3) | copy-start | bytes 786436
  78.8 2.5 %collective-permute-start.8 = (bf16[1280,128]{1,0:T(8,128)(2,1)}, bf16[1280,128]{1,0:T(8,128)(2,1)S(1)}, u32[]{:S(2)}, u32[]{:S(2)}) collective-permute-start(bf16[1280,128]{1,0:T(8,128)(2,1)} %get-tuple-element.34), channel_id=1, source_target_pairs={{0,32},{32,0},{64,96},{96,64},{128,160},{160,128},{192,224},{224,1... | collective-permute-start | bytes 983048 | tf_op jit(solution)/shard_map/ppermute | solution.py:386
  79.4 15.1 %collective-permute-start.10 = (bf16[2048,128]{1,0:T(8,128)(2,1)}, bf16[2048,128]{1,0:T(8,128)(2,1)S(1)}, u32[]{:S(2)}, u32[]{:S(2)}) collective-permute-start(bf16[2048,128]{1,0:T(8,128)(2,1)} %get-tuple-element.35), channel_id=1, source_target_pairs={{0,2},{1,3},{2,0},{3,1},{4,6},{5,7},{6,4},{7,5},{8,10},{9,11},{10,... | collective-permute-start | bytes 1572872 | tf_op jit(solution)/shard_map/ppermute | solution.py:386
  82.5 14.7 %copy-start.20 = (bf16[2048,128]{1,0:T(8,128)(2,1)S(1)}, bf16[2048,128]{1,0:T(8,128)(2,1)}, u32[]{:S(2)}) copy-start(bf16[2048,128]{1,0:T(8,128)(2,1)} %get-tuple-element.32) | copy-start | bytes 1572868
  82.5 5.4 %collective-permute-start.9 = (bf16[640,128]{1,0:T(8,128)(2,1)S(1)}, bf16[640,128]{1,0:T(8,128)(2,1)S(1)}, u32[]{:S(2)}, u32[]{:S(2)}) collective-permute-start(bf16[640,128]{1,0:T(8,128)(2,1)S(1)} %fusion), channel_id=1, source_target_pairs={{0,64},{32,96},{64,0},{96,32},{128,192},{160,224},{192,128},{224,1... | collective-permute-start | bytes 491528 | tf_op jit(solution)/shard_map/ppermute | solution.py:386
  94.6 4.6 %collective-permute-start.11 = (bf16[320,128]{1,0:T(8,128)(2,1)S(1)}, bf16[320,128]{1,0:T(8,128)(2,1)S(1)}, u32[]{:S(2)}, u32[]{:S(2)}) collective-permute-start(bf16[320,128]{1,0:T(8,128)(2,1)S(1)} %fusion.2), channel_id=1, source_target_pairs={{0,192},{32,224},{64,128},{96,160},{128,64},{160,96},{192,0},{224,... | collective-permute-start | bytes 245768 | tf_op jit(solution)/shard_map/ppermute | solution.py:386
  95.9 14.0 %collective-permute-start.6 = (bf16[2048,128]{1,0:T(8,128)(2,1)}, bf16[2048,128]{1,0:T(8,128)(2,1)S(1)}, u32[]{:S(2)}, u32[]{:S(2)}) collective-permute-start(bf16[2048,128]{1,0:T(8,128)(2,1)} %get-tuple-element.31), channel_id=1, source_target_pairs={{0,1},{1,2},{2,3},{3,0},{4,5},{5,6},{6,7},{7,4},{8,9},{9,10},{10,1... | collective-permute-start | bytes 1572872 | tf_op jit(solution)/shard_map/ppermute | solution.py:386
  97.2 12.7 %collective-permute-start.7 = (bf16[2048,128]{1,0:T(8,128)(2,1)S(1)}, bf16[2048,128]{1,0:T(8,128)(2,1)S(1)}, u32[]{:S(2)}, u32[]{:S(2)}) collective-permute-start(bf16[2048,128]{1,0:T(8,128)(2,1)S(1)} %copy-done.20), channel_id=1, source_target_pairs={{0,3},{1,0},{2,1},{3,2},{4,7},{5,4},{6,5},{7,6},{8,11},{9,8},{10,9... | collective-permute-start | bytes 1572872 | tf_op jit(solution)/shard_map/ppermute | solution.py:386
  99.2 10.0 %copy-start.10 = (s32[64,1,128]{2,1,0:T(1,128)S(1)}, s32[64,1,128]{2,1,0:T(1,128)}, u32[]{:S(2)}) copy-start(s32[64,1,128]{2,1,0:T(1,128)} %all_to_all.21) | copy-start | bytes 98308
  99.2 5.2 %collective-permute-start.14 = (bf16[320,128]{1,0:T(8,128)(2,1)S(1)}, bf16[320,128]{1,0:T(8,128)(2,1)S(1)}, u32[]{:S(2)}, u32[]{:S(2)}) collective-permute-start(bf16[320,128]{1,0:T(8,128)(2,1)S(1)} %fusion.1), channel_id=1, source_target_pairs={{0,12},{4,8},{8,4},{12,0},{16,28},{20,24},{24,20},{28,16},{1,13},{... | collective-permute-start | bytes 245768 | tf_op jit(solution)/shard_map/ppermute | solution.py:386
  101.2 7.8 %collective-permute-start.13 = (bf16[320,128]{1,0:T(8,128)(2,1)S(1)}, bf16[320,128]{1,0:T(8,128)(2,1)S(1)}, u32[]{:S(2)}, u32[]{:S(2)}) collective-permute-start(bf16[320,128]{1,0:T(8,128)(2,1)S(1)} %fusion.1), channel_id=1, source_target_pairs={{0,8},{4,12},{8,0},{12,4},{16,24},{20,28},{24,16},{28,20},{1,9},{5... | collective-permute-start | bytes 245768 | tf_op jit(solution)/shard_map/ppermute | solution.py:386
  101.5 7.5 %collective-permute-start.12 = (bf16[320,128]{1,0:T(8,128)(2,1)S(1)}, bf16[320,128]{1,0:T(8,128)(2,1)S(1)}, u32[]{:S(2)}, u32[]{:S(2)}) collective-permute-start(bf16[320,128]{1,0:T(8,128)(2,1)S(1)} %fusion.1), channel_id=1, source_target_pairs={{0,4},{4,0},{8,12},{12,8},{16,20},{20,16},{24,28},{28,24},{1,5},{5... | collective-permute-start | bytes 245768 | tf_op jit(solution)/shard_map/ppermute | solution.py:386
  109.1 5.1 %collective-permute-start.15 = (bf16[320,128]{1,0:T(8,128)(2,1)S(1)}, bf16[320,128]{1,0:T(8,128)(2,1)S(1)}, u32[]{:S(2)}, u32[]{:S(2)}) collective-permute-start(bf16[320,128]{1,0:T(8,128)(2,1)S(1)} %add_convert_fusion.2), channel_id=1, source_target_pairs={{0,28},{4,24},{8,20},{12,16},{16,12},{20,8},{24,4},{28,0},{1,29},{... | collective-permute-start | bytes 245768 | tf_op jit(solution)/shard_map/ppermute | solution.py:386
  110.8 19.4 %copy-start.5 = (bf16[2048,128]{1,0:T(8,128)(2,1)S(1)}, bf16[2048,128]{1,0:T(8,128)(2,1)}, u32[]{:S(2)}) copy-start(bf16[2048,128]{1,0:T(8,128)(2,1)} %copy-done.4) | copy-start | bytes 1572868
  114.2 16.1 %copy-start.3 = (bf16[2048,128]{1,0:T(8,128)(2,1)S(1)}, bf16[2048,128]{1,0:T(8,128)(2,1)}, u32[]{:S(2)}) copy-start(bf16[2048,128]{1,0:T(8,128)(2,1)} %get-tuple-element.38.d0) | copy-start | bytes 1572868
  114.2 16.1 %copy-start = (bf16[1024,128]{1,0:T(8,128)(2,1)S(1)}, bf16[1024,128]{1,0:T(8,128)(2,1)}, u32[]{:S(2)}) copy-start(bf16[1024,128]{1,0:T(8,128)(2,1)} %place.1.x0) | copy-start | bytes 786436
  114.2 23.2 %all-to-all-start.2 = ((bf16[64,24,128]{2,1,0:T(8,128)(2,1)}), bf16[64,24,128]{2,1,0:T(8,128)(2,1)S(1)}, u32[]{:S(2)}, u32[]{:S(2)}) async-start(bf16[64,24,128]{2,1,0:T(8,128)(2,1)} %bitcast.32), calls=%async_computation.2 | async-start | bytes 786432 | tf_op jit(solution)/shard_map/all_to_all | solution.py:458
  124.6 7.5 %copy-start.9 = (bf16[640,128]{1,0:T(8,128)(2,1)}, bf16[640,128]{1,0:T(8,128)(2,1)S(1)}, u32[]{:S(2)}) copy-start(bf16[640,128]{1,0:T(8,128)(2,1)S(1)} %all_gather.3.p0) | copy-start | bytes 491524
  124.6 16.6 %collective-permute-start.18 = (bf16[640,128]{1,0:T(8,128)(2,1)S(1)}, bf16[640,128]{1,0:T(8,128)(2,1)S(1)}, u32[]{:S(2)}, u32[]{:S(2)}) collective-permute-start(bf16[640,128]{1,0:T(8,128)(2,1)S(1)} %all_gather.3.p0), channel_id=1, source_target_pairs={{0,128},{32,160},{64,192},{96,224},{128,0},{160,32},{192,64},{224,... | collective-permute-start | bytes 491528 | tf_op jit(solution)/shard_map/ppermute | solution.py:386
  127.6 13.7 %collective-permute-start.17 = (bf16[640,128]{1,0:T(8,128)(2,1)S(1)}, bf16[640,128]{1,0:T(8,128)(2,1)S(1)}, u32[]{:S(2)}, u32[]{:S(2)}) collective-permute-start(bf16[640,128]{1,0:T(8,128)(2,1)S(1)} %all_gather.3.p0), channel_id=1, source_target_pairs={{0,64},{32,96},{64,128},{96,160},{128,192},{160,224},{192,0},{224,... | collective-permute-start | bytes 491528 | tf_op jit(solution)/shard_map/ppermute | solution.py:386
  128.0 13.3 %collective-permute-start.16 = (bf16[640,128]{1,0:T(8,128)(2,1)S(1)}, bf16[640,128]{1,0:T(8,128)(2,1)S(1)}, u32[]{:S(2)}, u32[]{:S(2)}) collective-permute-start(bf16[640,128]{1,0:T(8,128)(2,1)S(1)} %all_gather.3.p0), channel_id=1, source_target_pairs={{0,192},{32,224},{64,0},{96,32},{128,64},{160,96},{192,128},{224,1... | collective-permute-start | bytes 491528 | tf_op jit(solution)/shard_map/ppermute | solution.py:386
  (10 other events, 11.6 us)

commit v13 on v11

--- a/solution.py
+++ b/solution.py
@@ -442,16 +442,17 @@
     gs = gather_pieces(grad_out)
     received = lax.all_to_all(requests, BOTH, split_axis=0, concat_axis=0, tiled=True)
     rows = fetch(received, table)
+    flat = received[:, :CAP].reshape(SLOTS // 128, 128)
     back = lax.all_to_all(rows.reshape(NOWN, CAP, 128), BOTH, split_axis=0, concat_axis=0, tiled=True)
+    back, flat = lax.optimization_barrier((back, flat))
     x = place(slot, back.reshape(SLOTS, 128))
     xs = gather_pieces(x)
     mine, other, c0, c1, c2, c3 = layer(pos, core, segment_ids, xs, gs, proj_in, proj_out)
     cparts = scatter_pieces([c0, c1, c2, c3])
     own, got = reduce_over_chips(mine, other)
-    flat = received[:, :CAP].reshape(SLOTS // 128, 128)
     got, cparts[3] = lax.optimization_barrier((got, cparts[3]))
     total = add_group((own + got.astype(F32)).astype(BF))
-    cparts, _, flat = lax.optimization_barrier((cparts, total, flat))
+    cparts, _ = lax.optimization_barrier((cparts, total))
     grads = to_slots(slot, grad_out, cparts)
     total = add_step(total, 7)
     grads, total = lax.optimization_barrier((grads, total))

time: 144 us -> 146 us (1.014)
  waiting for transfers between devices: 41.5 us -> 46.4 us
  starting transfers between devices: 41.6 us -> 38.6 us
    ppermute x19, waiting for transfers between devices: 27 us -> 30.1 us  [shift(): return lax.ppermute(x, axis, [(i, fn(i)) for i in range(n)])]
    ppermute x19, starting transfers between devices: 28.5 us -> 25.9 us  [shift(): return lax.ppermute(x, axis, [(i, fn(i)) for i in range(n)])]
  transfers between devices with their start and end apart: 21 -> 21, of which waited for: 10 -> 11; matrix products, arithmetic and copies ran while one was open for 2% -> 2% of each run, Pallas kernels for 6% -> 6%
where the time goes in v13:
time: 146 us; the launch traced here: 145 us
  waiting for transfers between devices  46.4 us (32%)
  starting transfers between devices  38.6 us (26%)
  Pallas kernels  27 us (18%)
  blocking collectives  24.4 us (17%)
  local copies, waits for them, and re-layouts  4.66 us (3%)
  other arithmetic  3.25 us (2%)
    ppermute x19, waiting for transfers between devices, shift(): return lax.ppermute(x, axis, [(i, fn(i)) for i in range(n)])  30.1 us
    ppermute x19, starting transfers between devices, shift(): return lax.ppermute(x, axis, [(i, fn(i)) for i in range(n)])  25.9 us
    all_to_all x1, blocking collectives, body(): lax.all_to_all(requests, BOTH, split_axis=0, concat_axis=0, tiled=True)  22.4 us
    pallas_call x1, Pallas kernels, layer(): pl.pallas_call(layer_kernel, out_shape=(jax.ShapeDtypeStruct((1280, 128),...  11.7 us
    all_to_all x1, waiting for transfers between devices, body(): lax.all_to_all(rows.reshape(NOWN, CAP, 128), BOTH, split_axis=0, concat_a...  9.9 us
    all_to_all x1, starting transfers between devices, body(): lax.all_to_all(grads.reshape(NOWN, CAP, 128), BOTH, split_axis=0, concat_...  7.76 us
    all_to_all x1, waiting for transfers between devices, body(): lax.all_to_all(grads.reshape(NOWN, CAP, 128), BOTH, split_axis=0, concat_...  6.41 us
    all_to_all x1, starting transfers between devices, body(): lax.all_to_all(rows.reshape(NOWN, CAP, 128), BOTH, split_axis=0, concat_a...  4.98 us
  transfers between devices with their start and end apart: 21, of which 11 were waited for; matrix products, arithmetic and copies ran while one was open for 2% of the time, Pallas kernels for 6%

profile of v13, /device:TPU:1, one launch (start us, length us, event | category | flops | bytes accessed | tf_op | source)
XLA Modules:
  0.0 145.2 jit_solution(13408735356346109710)
XLA Ops:
  0.6 1.8 %route.1 = (s32[64,128]{1,0:T(8,128)}, s32[8,128]{1,0:T(8,128)}) custom-call(s32[8,128]{1,0:T(8,128)} %bitcast.38, s32[8,128]{1,0:T(8,128)} %bitcast.39), custom_call_target="tpu_custom_call" | custom-call | tf_op jit(solution)/shard_map/route/pallas_call | solution.py:63
  2.5 22.4 %all_to_all.21 = s32[64,1,128]{2,1,0:T(1,128)} all-to-all(s32[64,1,128]{2,1,0:T(1,128)} %bitcast.37), channel_id=1, replica_groups=mesh['table'=8,'seq'=8,'tensor'=4] {'table','seq'}, dimensions={0} | all-to-all | bytes 65536 | tf_op jit(solution)/shard_map/all_to_all | solution.py:443
  24.9 2.9 %fetch.1 = bf16[1536,128]{1,0:T(8,128)(2,1)} custom-call(s32[64,128]{1,0:T(8,128)} %bitcast.35, bf16[2048,128]{1,0:T(8,128)(2,1)} %table_ref.1), custom_call_target="tpu_custom_call" | custom-call | tf_op jit(solution)/shard_map/fetch/pallas_call | solution.py:99
  27.8 5.0 %all-to-all-start.1 = ((bf16[64,24,128]{2,1,0:T(8,128)(2,1)}), bf16[64,24,128]{2,1,0:T(8,128)(2,1)S(1)}, u32[]{:S(2)}, u32[]{:S(2)}) async-start(bf16[64,24,128]{2,1,0:T(8,128)(2,1)} %bitcast.31), calls=%async_computation.1 | async-start | bytes 786432 | tf_op jit(solution)/shard_map/all_to_all | solution.py:446
  32.8 2.6 %collective-permute-start.3 = (bf16[1024,128]{1,0:T(8,128)(2,1)S(1)}, bf16[1024,128]{1,0:T(8,128)(2,1)S(1)}, u32[]{:S(2)}, u32[]{:S(2)}) collective-permute-start(bf16[1024,128]{1,0:T(8,128)(2,1)S(1)} %copy-done.7), channel_id=1, source_target_pairs={{0,3},{1,0},{2,1},{3,2},{4,7},{5,4},{6,5},{7,6},{8,11},{9,8},{10,9... | collective-permute-start | bytes 786440 | tf_op jit(solution)/shard_map/ppermute | solution.py:386
  35.3 1.7 %collective-permute-start.5 = (bf16[1024,128]{1,0:T(8,128)(2,1)S(1)}, bf16[1024,128]{1,0:T(8,128)(2,1)S(1)}, u32[]{:S(2)}, u32[]{:S(2)}) collective-permute-start(bf16[1024,128]{1,0:T(8,128)(2,1)S(1)} %copy-done.7), channel_id=1, source_target_pairs={{0,2},{1,3},{2,0},{3,1},{4,6},{5,7},{6,4},{7,5},{8,10},{9,11},{10,... | collective-permute-start | bytes 786440 | tf_op jit(solution)/shard_map/ppermute | solution.py:386
  37.7 9.9 %all-to-all-done.1 = bf16[64,24,128]{2,1,0:T(8,128)(2,1)S(1)} async-done(((bf16[64,24,128]{2,1,0:T(8,128)(2,1)}), bf16[64,24,128]{2,1,0:T(8,128)(2,1)S(1)}, u32[]{:S(2)}, u32[]{:S(2)}) %all-to-all-start.1) | async-done | bytes 393248 | tf_op jit(solution)/shard_map/all_to_all | solution.py:446
  48.4 2.4 %place.1.x0 = bf16[1024,128]{1,0:T(8,128)(2,1)} custom-call(s32[8,128]{1,0:T(8,128)} %get-tuple-element.29.slot_ref, bf16[1536,128]{1,0:T(8,128)(2,1)} %bitcast.29), custom_call_target="tpu_custom_call" | custom-call | tf_op jit(solution)/shard_map/place/pallas_call | solution.py:134
  50.7 2.5 %collective-permute-start = (bf16[1024,128]{1,0:T(8,128)(2,1)}, bf16[1024,128]{1,0:T(8,128)(2,1)S(1)}, u32[]{:S(2)}, u32[]{:S(2)}) collective-permute-start(bf16[1024,128]{1,0:T(8,128)(2,1)} %place.1.x0), channel_id=1, source_target_pairs={{0,3},{1,0},{2,1},{3,2},{4,7},{5,4},{6,5},{7,6},{8,11},{9,8},{10,9... | collective-permute-start | bytes 786440 | tf_op jit(solution)/shard_map/ppermute | solution.py:386
  53.2 1.7 %collective-permute-start.2 = (bf16[1024,128]{1,0:T(8,128)(2,1)}, bf16[1024,128]{1,0:T(8,128)(2,1)S(1)}, u32[]{:S(2)}, u32[]{:S(2)}) collective-permute-start(bf16[1024,128]{1,0:T(8,128)(2,1)} %place.1.x0), channel_id=1, source_target_pairs={{0,2},{1,3},{2,0},{3,1},{4,6},{5,7},{6,4},{7,5},{8,10},{9,11},{10,... | collective-permute-start | bytes 786440 | tf_op jit(solution)/shard_map/ppermute | solution.py:386
  55.0 3.7 %collective-permute-done.x1 = bf16[1024,128]{1,0:T(8,128)(2,1)S(1)} collective-permute-done((bf16[1024,128]{1,0:T(8,128)(2,1)}, bf16[1024,128]{1,0:T(8,128)(2,1)S(1)}, u32[]{:S(2)}, u32[]{:S(2)}) %collective-permute-start) | collective-permute-done | bytes 262176 | tf_op jit(solution)/shard_map/ppermute | solution.py:386
  58.7 3.4 %collective-permute-done.1.x2 = bf16[1024,128]{1,0:T(8,128)(2,1)S(1)} collective-permute-done((bf16[1024,128]{1,0:T(8,128)(2,1)}, bf16[1024,128]{1,0:T(8,128)(2,1)S(1)}, u32[]{:S(2)}, u32[]{:S(2)}) %collective-permute-start.1) | collective-permute-done | bytes 262176 | tf_op jit(solution)/shard_map/ppermute | solution.py:386
  62.1 3.8 %collective-permute-done.2.x3 = bf16[1024,128]{1,0:T(8,128)(2,1)S(1)} collective-permute-done((bf16[1024,128]{1,0:T(8,128)(2,1)}, bf16[1024,128]{1,0:T(8,128)(2,1)S(1)}, u32[]{:S(2)}, u32[]{:S(2)}) %collective-permute-start.2) | collective-permute-done | bytes 262176 | tf_op jit(solution)/shard_map/ppermute | solution.py:386
  66.6 11.7 %layer.1 = (f32[1280,128]{1,0:T(8,128)}, bf16[1280,128]{1,0:T(8,128)(2,1)}, bf16[2048,128]{1,0:T(8,128)(2,1)}, bf16[2048,128]{1,0:T(8,128)(2,1)}, bf16[2048,128]{1,0:T(8,128)(2,1)}, /*index=5*/bf16[2048,128]{1,0:T(8,128)(2,1)}) custom-call(s32[1]{0:T(128)} %bitcast.7.pos_ref, s32[1]{0:T(128)} %bitcast.8.core_ref, s32[1,1024]{1,0:T(1,128)} %seg_ref.1, ...), custom_call_target="tpu_custom_call" | custom-call | tf_op jit(solution)/shard_map/layer/pallas_call | solution.py:277
  78.3 3.3 %collective-permute-start.8 = (bf16[1280,128]{1,0:T(8,128)(2,1)}, bf16[1280,128]{1,0:T(8,128)(2,1)S(1)}, u32[]{:S(2)}, u32[]{:S(2)}) collective-permute-start(bf16[1280,128]{1,0:T(8,128)(2,1)} %get-tuple-element.36), channel_id=1, source_target_pairs={{0,32},{32,0},{64,96},{96,64},{128,160},{160,128},{192,224},{224,1... | collective-permute-start | bytes 983048 | tf_op jit(solution)/shard_map/ppermute | solution.py:386
  81.6 1.5 %collective-permute-done.8 = bf16[1280,128]{1,0:T(8,128)(2,1)S(1)} collective-permute-done((bf16[1280,128]{1,0:T(8,128)(2,1)}, bf16[1280,128]{1,0:T(8,128)(2,1)S(1)}, u32[]{:S(2)}, u32[]{:S(2)}) %collective-permute-start.8) | collective-permute-done | bytes 327712 | tf_op jit(solution)/shard_map/ppermute | solution.py:386
  85.3 4.4 %collective-permute-done.9 = bf16[640,128]{1,0:T(8,128)(2,1)S(1)} collective-permute-done((bf16[640,128]{1,0:T(8,128)(2,1)S(1)}, bf16[640,128]{1,0:T(8,128)(2,1)S(1)}, u32[]{:S(2)}, u32[]{:S(2)}) %collective-permute-start.9) | collective-permute-done | bytes 163872 | tf_op jit(solution)/shard_map/ppermute | solution.py:386
  91.1 2.7 %collective-permute-start.7 = (bf16[2048,128]{1,0:T(8,128)(2,1)S(1)}, bf16[2048,128]{1,0:T(8,128)(2,1)S(1)}, u32[]{:S(2)}, u32[]{:S(2)}) collective-permute-start(bf16[2048,128]{1,0:T(8,128)(2,1)S(1)} %copy-done.19), channel_id=1, source_target_pairs={{0,3},{1,0},{2,1},{3,2},{4,7},{5,4},{6,5},{7,6},{8,11},{9,8},{10,9... | collective-permute-start | bytes 1572872 | tf_op jit(solution)/shard_map/ppermute | solution.py:386
  93.8 5.9 %collective-permute-done.11.d3 = bf16[2048,128]{1,0:T(8,128)(2,1)S(1)} collective-permute-done((bf16[2048,128]{1,0:T(8,128)(2,1)}, bf16[2048,128]{1,0:T(8,128)(2,1)S(1)}, u32[]{:S(2)}, u32[]{:S(2)}) %collective-permute-start.11) | collective-permute-done | bytes 524320 | tf_op jit(solution)/shard_map/ppermute | solution.py:386
  99.7 1.6 %collective-permute-start.14 = (bf16[320,128]{1,0:T(8,128)(2,1)S(1)}, bf16[320,128]{1,0:T(8,128)(2,1)S(1)}, u32[]{:S(2)}, u32[]{:S(2)}) collective-permute-start(bf16[320,128]{1,0:T(8,128)(2,1)S(1)} %fusion.1), channel_id=1, source_target_pairs={{0,12},{4,8},{8,4},{12,0},{16,28},{20,24},{24,20},{28,16},{1,13},{... | collective-permute-start | bytes 245768 | tf_op jit(solution)/shard_map/ppermute | solution.py:386
  103.3 1.7 %collective-permute-done.14 = bf16[320,128]{1,0:T(8,128)(2,1)S(1)} collective-permute-done((bf16[320,128]{1,0:T(8,128)(2,1)S(1)}, bf16[320,128]{1,0:T(8,128)(2,1)S(1)}, u32[]{:S(2)}, u32[]{:S(2)}) %collective-permute-start.14) | collective-permute-done | bytes 81952 | tf_op jit(solution)/shard_map/ppermute | solution.py:386
  105.0 2.4 %collective-permute-done.13 = bf16[320,128]{1,0:T(8,128)(2,1)S(1)} collective-permute-done((bf16[320,128]{1,0:T(8,128)(2,1)S(1)}, bf16[320,128]{1,0:T(8,128)(2,1)S(1)}, u32[]{:S(2)}, u32[]{:S(2)}) %collective-permute-start.13) | collective-permute-done | bytes 81952 | tf_op jit(solution)/shard_map/ppermute | solution.py:386
  108.5 3.4 %collective-permute-done.6.d1 = bf16[2048,128]{1,0:T(8,128)(2,1)S(1)} collective-permute-done((bf16[2048,128]{1,0:T(8,128)(2,1)}, bf16[2048,128]{1,0:T(8,128)(2,1)S(1)}, u32[]{:S(2)}, u32[]{:S(2)}) %collective-permute-start.6) | collective-permute-done | bytes 524320 | tf_op jit(solution)/shard_map/ppermute | solution.py:386
  112.8 2.8 %to_slots.1 = bf16[1536,128]{1,0:T(8,128)(2,1)} custom-call(s32[8,128]{1,0:T(8,128)} %get-tuple-element.29.slot_ref, bf16[1024,128]{1,0:T(8,128)(2,1)} %grad_ref.1, bf16[2048,128]{1,0:T(8,128)(2,1)} %get-tuple-element.40.d0, bf16[2048,128]{1,0:T(8,128)(2,1)} %copy-done.5, bf16[2048,128]{1,0:T(8,128)(2,1)} %copy-done.6, bf16[2048,128]{1,0:T(8,128)(2,1)} %copy-done.4), custom_call_target="tpu_custom_call" | custom-call | tf_op jit(solution)/shard_map/to_slots/pallas_call | solution.py:333
  115.7 7.8 %all-to-all-start.2 = ((bf16[64,24,128]{2,1,0:T(8,128)(2,1)}), bf16[64,24,128]{2,1,0:T(8,128)(2,1)S(1)}, u32[]{:S(2)}, u32[]{:S(2)}) async-start(bf16[64,24,128]{2,1,0:T(8,128)(2,1)} %bitcast.32), calls=%async_computation.2 | async-start | bytes 786432 | tf_op jit(solution)/shard_map/all_to_all | solution.py:459
  123.4 2.0 %all_gather.3.p0 = bf16[640,128]{1,0:T(8,128)(2,1)S(1)} all-gather(bf16[320,128]{1,0:T(8,128)(2,1)S(1)} %add_convert_fusion.1), channel_id=1, replica_groups={{0,32},{64,96},{128,160},{192,224},{1,33},{65,97},{129,161},{193,225},{..., dimensions={0}, use_global_device_ids=true | all-gather | bytes 245760 | tf_op jit(solution)/shard_map/all_gather | solution.py:431
  125.5 2.7 %collective-permute-start.16 = (bf16[640,128]{1,0:T(8,128)(2,1)S(1)}, bf16[640,128]{1,0:T(8,128)(2,1)S(1)}, u32[]{:S(2)}, u32[]{:S(2)}) collective-permute-start(bf16[640,128]{1,0:T(8,128)(2,1)S(1)} %all_gather.3.p0), channel_id=1, source_target_pairs={{0,192},{32,224},{64,0},{96,32},{128,64},{160,96},{192,128},{224,1... | collective-permute-start | bytes 491528 | tf_op jit(solution)/shard_map/ppermute | solution.py:386
  128.2 1.6 %collective-permute-start.18 = (bf16[640,128]{1,0:T(8,128)(2,1)S(1)}, bf16[640,128]{1,0:T(8,128)(2,1)S(1)}, u32[]{:S(2)}, u32[]{:S(2)}) collective-permute-start(bf16[640,128]{1,0:T(8,128)(2,1)S(1)} %all_gather.3.p0), channel_id=1, source_target_pairs={{0,128},{32,160},{64,192},{96,224},{128,0},{160,32},{192,64},{224,... | collective-permute-start | bytes 491528 | tf_op jit(solution)/shard_map/ppermute | solution.py:386
  129.9 2.0 %add_convert_fusion = bf16[1024,128]{1,0:T(8,128)(2,1)} fusion(bf16[1024,128]{1,0:T(8,128)(2,1)S(1)} %copy-done, bf16[2048,128]{1,0:T(8,128)(2,1)} %copy-done.4, bf16[2048,128]{1,0:T(8,128)(2,1)} %copy-done.6, bf16[2048,128]{1,0:T(8,128)(2,1)} %copy-done.5, bf16[2048,128]{1,0:T(8,128)(2,1)S(1)} %copy-done.3), kind=kLoop, calls=%fused_computation.1 | loop fusion | flops 1310720 | bytes 1572864 | tf_op jit(solution)/shard_map/convert_element_type | solution.py:471
  131.8 6.4 %all-to-all-done.2 = bf16[64,24,128]{2,1,0:T(8,128)(2,1)S(1)} async-done(((bf16[64,24,128]{2,1,0:T(8,128)(2,1)}), bf16[64,24,128]{2,1,0:T(8,128)(2,1)S(1)}, u32[]{:S(2)}, u32[]{:S(2)}) %all-to-all-start.2) | async-done | bytes 393248 | tf_op jit(solution)/shard_map/all_to_all | solution.py:459
  139.0 3.1 %add_rows.1 = f32[2048,128]{1,0:T(8,128)} custom-call(s32[12,128]{1,0:T(8,128)} %reshape.54.req_ref, bf16[1536,128]{1,0:T(8,128)(2,1)} %bitcast.30), custom_call_target="tpu_custom_call" | custom-call | tf_op jit(solution)/shard_map/add_rows/pallas_call | solution.py:352
  142.9 2.4 %unpack.1 = (f32[2048,128]{1,0:T(8,128)}, f32[128,512]{1,0:T(8,128)}) custom-call(s32[1]{0:T(128)} %bitcast.17.y_ref, bf16[640,128]{1,0:T(8,128)(2,1)} %copy-done.8, bf16[640,128]{1,0:T(8,128)(2,1)} %copy-done.16, bf16[640,128]{1,0:T(8,128)(2,1)} %copy-done.17, bf16[640,128]{1,0:T(8,128)(2,1)} %copy-done.18), custom_call_target="tpu_custom_call" | custom-call | tf_op jit(solution)/shard_map/unpack/pallas_call | solution.py:374
  (68 shorter events, 11.4 us)
Async XLA Ops:
  27.8 5.0 %copy-start.7 = (bf16[1024,128]{1,0:T(8,128)(2,1)S(1)}, bf16[1024,128]{1,0:T(8,128)(2,1)}, u32[]{:S(2)}) copy-start(bf16[1024,128]{1,0:T(8,128)(2,1)} %grad_ref.1) | copy-start | bytes 786436
  27.8 9.3 %copy-start.9 = (s32[64,1,128]{2,1,0:T(1,128)S(1)}, s32[64,1,128]{2,1,0:T(1,128)}, u32[]{:S(2)}) copy-start(s32[64,1,128]{2,1,0:T(1,128)} %all_to_all.21) | copy-start | bytes 98308
  27.8 19.9 %all-to-all-start.1 = ((bf16[64,24,128]{2,1,0:T(8,128)(2,1)}), bf16[64,24,128]{2,1,0:T(8,128)(2,1)S(1)}, u32[]{:S(2)}, u32[]{:S(2)}) async-start(bf16[64,24,128]{2,1,0:T(8,128)(2,1)} %bitcast.31), calls=%async_computation.1 | async-start | bytes 786432 | tf_op jit(solution)/shard_map/all_to_all | solution.py:446
  32.8 20.5 %collective-permute-start.3 = (bf16[1024,128]{1,0:T(8,128)(2,1)S(1)}, bf16[1024,128]{1,0:T(8,128)(2,1)S(1)}, u32[]{:S(2)}, u32[]{:S(2)}) collective-permute-start(bf16[1024,128]{1,0:T(8,128)(2,1)S(1)} %copy-done.7), channel_id=1, source_target_pairs={{0,3},{1,0},{2,1},{3,2},{4,7},{5,4},{6,5},{7,6},{8,11},{9,8},{10,9... | collective-permute-start | bytes 786440 | tf_op jit(solution)/shard_map/ppermute | solution.py:386
  35.3 19.6 %collective-permute-start.4 = (bf16[1024,128]{1,0:T(8,128)(2,1)S(1)}, bf16[1024,128]{1,0:T(8,128)(2,1)S(1)}, u32[]{:S(2)}, u32[]{:S(2)}) collective-permute-start(bf16[1024,128]{1,0:T(8,128)(2,1)S(1)} %copy-done.7), channel_id=1, source_target_pairs={{0,1},{1,2},{2,3},{3,0},{4,5},{5,6},{6,7},{7,4},{8,9},{9,10},{10,1... | collective-permute-start | bytes 786440 | tf_op jit(solution)/shard_map/ppermute | solution.py:386
  35.3 19.6 %collective-permute-start.5 = (bf16[1024,128]{1,0:T(8,128)(2,1)S(1)}, bf16[1024,128]{1,0:T(8,128)(2,1)S(1)}, u32[]{:S(2)}, u32[]{:S(2)}) collective-permute-start(bf16[1024,128]{1,0:T(8,128)(2,1)S(1)} %copy-done.7), channel_id=1, source_target_pairs={{0,2},{1,3},{2,0},{3,1},{4,6},{5,7},{6,4},{7,5},{8,10},{9,11},{10,... | collective-permute-start | bytes 786440 | tf_op jit(solution)/shard_map/ppermute | solution.py:386
  50.7 7.9 %collective-permute-start = (bf16[1024,128]{1,0:T(8,128)(2,1)}, bf16[1024,128]{1,0:T(8,128)(2,1)S(1)}, u32[]{:S(2)}, u32[]{:S(2)}) collective-permute-start(bf16[1024,128]{1,0:T(8,128)(2,1)} %place.1.x0), channel_id=1, source_target_pairs={{0,3},{1,0},{2,1},{3,2},{4,7},{5,4},{6,5},{7,6},{8,11},{9,8},{10,9... | collective-permute-start | bytes 786440 | tf_op jit(solution)/shard_map/ppermute | solution.py:386
  53.2 8.9 %collective-permute-start.1 = (bf16[1024,128]{1,0:T(8,128)(2,1)}, bf16[1024,128]{1,0:T(8,128)(2,1)S(1)}, u32[]{:S(2)}, u32[]{:S(2)}) collective-permute-start(bf16[1024,128]{1,0:T(8,128)(2,1)} %place.1.x0), channel_id=1, source_target_pairs={{0,1},{1,2},{2,3},{3,0},{4,5},{5,6},{6,7},{7,4},{8,9},{9,10},{10,1... | collective-permute-start | bytes 786440 | tf_op jit(solution)/shard_map/ppermute | solution.py:386
  53.2 12.6 %copy-start.10 = (bf16[1024,128]{1,0:T(8,128)(2,1)}, bf16[1024,128]{1,0:T(8,128)(2,1)S(1)}, u32[]{:S(2)}) copy-start(bf16[1024,128]{1,0:T(8,128)(2,1)S(1)} %collective-permute-done.3.g1) | copy-start | bytes 786436
  53.2 12.6 %collective-permute-start.2 = (bf16[1024,128]{1,0:T(8,128)(2,1)}, bf16[1024,128]{1,0:T(8,128)(2,1)S(1)}, u32[]{:S(2)}, u32[]{:S(2)}) collective-permute-start(bf16[1024,128]{1,0:T(8,128)(2,1)} %place.1.x0), channel_id=1, source_target_pairs={{0,2},{1,3},{2,0},{3,1},{4,6},{5,7},{6,4},{7,5},{8,10},{9,11},{10,... | collective-permute-start | bytes 786440 | tf_op jit(solution)/shard_map/ppermute | solution.py:386
  55.0 10.9 %copy-start.11 = (bf16[1024,128]{1,0:T(8,128)(2,1)}, bf16[1024,128]{1,0:T(8,128)(2,1)S(1)}, u32[]{:S(2)}) copy-start(bf16[1024,128]{1,0:T(8,128)(2,1)S(1)} %collective-permute-done.4.g2) | copy-start | bytes 786436
  55.0 10.9 %copy-start.12 = (bf16[1024,128]{1,0:T(8,128)(2,1)}, bf16[1024,128]{1,0:T(8,128)(2,1)S(1)}, u32[]{:S(2)}) copy-start(bf16[1024,128]{1,0:T(8,128)(2,1)S(1)} %collective-permute-done.5.g3) | copy-start | bytes 786436
  58.7 7.2 %copy-start.13 = (bf16[1024,128]{1,0:T(8,128)(2,1)}, bf16[1024,128]{1,0:T(8,128)(2,1)S(1)}, u32[]{:S(2)}) copy-start(bf16[1024,128]{1,0:T(8,128)(2,1)S(1)} %collective-permute-done.x1) | copy-start | bytes 786436
  78.3 4.7 %collective-permute-start.8 = (bf16[1280,128]{1,0:T(8,128)(2,1)}, bf16[1280,128]{1,0:T(8,128)(2,1)S(1)}, u32[]{:S(2)}, u32[]{:S(2)}) collective-permute-start(bf16[1280,128]{1,0:T(8,128)(2,1)} %get-tuple-element.36), channel_id=1, source_target_pairs={{0,32},{32,0},{64,96},{96,64},{128,160},{160,128},{192,224},{224,1... | collective-permute-start | bytes 983048 | tf_op jit(solution)/shard_map/ppermute | solution.py:386
  84.2 6.9 %copy-start.19 = (bf16[2048,128]{1,0:T(8,128)(2,1)S(1)}, bf16[2048,128]{1,0:T(8,128)(2,1)}, u32[]{:S(2)}) copy-start(bf16[2048,128]{1,0:T(8,128)(2,1)} %get-tuple-element.34) | copy-start | bytes 1572868
  84.3 5.5 %collective-permute-start.9 = (bf16[640,128]{1,0:T(8,128)(2,1)S(1)}, bf16[640,128]{1,0:T(8,128)(2,1)S(1)}, u32[]{:S(2)}, u32[]{:S(2)}) collective-permute-start(bf16[640,128]{1,0:T(8,128)(2,1)S(1)} %fusion), channel_id=1, source_target_pairs={{0,64},{32,96},{64,0},{96,32},{128,192},{160,224},{192,128},{224,1... | collective-permute-start | bytes 491528 | tf_op jit(solution)/shard_map/ppermute | solution.py:386
  85.1 14.6 %collective-permute-start.11 = (bf16[2048,128]{1,0:T(8,128)(2,1)}, bf16[2048,128]{1,0:T(8,128)(2,1)S(1)}, u32[]{:S(2)}, u32[]{:S(2)}) collective-permute-start(bf16[2048,128]{1,0:T(8,128)(2,1)} %get-tuple-element.37), channel_id=1, source_target_pairs={{0,2},{1,3},{2,0},{3,1},{4,6},{5,7},{6,4},{7,5},{8,10},{9,11},{10,... | collective-permute-start | bytes 1572872 | tf_op jit(solution)/shard_map/ppermute | solution.py:386
  89.8 9.8 %collective-permute-start.10 = (bf16[320,128]{1,0:T(8,128)(2,1)S(1)}, bf16[320,128]{1,0:T(8,128)(2,1)S(1)}, u32[]{:S(2)}, u32[]{:S(2)}) collective-permute-start(bf16[320,128]{1,0:T(8,128)(2,1)S(1)} %fusion.2), channel_id=1, source_target_pairs={{0,192},{32,224},{64,128},{96,160},{128,64},{160,96},{192,0},{224,... | collective-permute-start | bytes 245768 | tf_op jit(solution)/shard_map/ppermute | solution.py:386
  91.1 20.8 %collective-permute-start.6 = (bf16[2048,128]{1,0:T(8,128)(2,1)}, bf16[2048,128]{1,0:T(8,128)(2,1)S(1)}, u32[]{:S(2)}, u32[]{:S(2)}) collective-permute-start(bf16[2048,128]{1,0:T(8,128)(2,1)} %get-tuple-element.33), channel_id=1, source_target_pairs={{0,1},{1,2},{2,3},{3,0},{4,5},{5,6},{6,7},{7,4},{8,9},{9,10},{10,1... | collective-permute-start | bytes 1572872 | tf_op jit(solution)/shard_map/ppermute | solution.py:386
  91.1 20.8 %collective-permute-start.7 = (bf16[2048,128]{1,0:T(8,128)(2,1)S(1)}, bf16[2048,128]{1,0:T(8,128)(2,1)S(1)}, u32[]{:S(2)}, u32[]{:S(2)}) collective-permute-start(bf16[2048,128]{1,0:T(8,128)(2,1)S(1)} %copy-done.19), channel_id=1, source_target_pairs={{0,3},{1,0},{2,1},{3,2},{4,7},{5,4},{6,5},{7,6},{8,11},{9,8},{10,9... | collective-permute-start | bytes 1572872 | tf_op jit(solution)/shard_map/ppermute | solution.py:386
  99.7 12.2 %copy-start.4 = (bf16[2048,128]{1,0:T(8,128)(2,1)}, bf16[2048,128]{1,0:T(8,128)(2,1)S(1)}, u32[]{:S(2)}) copy-start(bf16[2048,128]{1,0:T(8,128)(2,1)S(1)} %collective-permute-done.11.d3) | copy-start | bytes 1572868
  99.7 5.3 %collective-permute-start.14 = (bf16[320,128]{1,0:T(8,128)(2,1)S(1)}, bf16[320,128]{1,0:T(8,128)(2,1)S(1)}, u32[]{:S(2)}, u32[]{:S(2)}) collective-permute-start(bf16[320,128]{1,0:T(8,128)(2,1)S(1)} %fusion.1), channel_id=1, source_target_pairs={{0,12},{4,8},{8,4},{12,0},{16,28},{20,24},{24,20},{28,16},{1,13},{... | collective-permute-start | bytes 245768 | tf_op jit(solution)/shard_map/ppermute | solution.py:386
  101.3 6.1 %collective-permute-start.13 = (bf16[320,128]{1,0:T(8,128)(2,1)S(1)}, bf16[320,128]{1,0:T(8,128)(2,1)S(1)}, u32[]{:S(2)}, u32[]{:S(2)}) collective-permute-start(bf16[320,128]{1,0:T(8,128)(2,1)S(1)} %fusion.1), channel_id=1, source_target_pairs={{0,8},{4,12},{8,0},{12,4},{16,24},{20,28},{24,16},{28,20},{1,9},{5... | collective-permute-start | bytes 245768 | tf_op jit(solution)/shard_map/ppermute | solution.py:386
  102.3 5.1 %collective-permute-start.12 = (bf16[320,128]{1,0:T(8,128)(2,1)S(1)}, bf16[320,128]{1,0:T(8,128)(2,1)S(1)}, u32[]{:S(2)}, u32[]{:S(2)}) collective-permute-start(bf16[320,128]{1,0:T(8,128)(2,1)S(1)} %fusion.1), channel_id=1, source_target_pairs={{0,4},{4,0},{8,12},{12,8},{16,20},{20,16},{24,28},{28,24},{1,5},{5... | collective-permute-start | bytes 245768 | tf_op jit(solution)/shard_map/ppermute | solution.py:386
  107.5 8.1 %collective-permute-start.15 = (bf16[320,128]{1,0:T(8,128)(2,1)S(1)}, bf16[320,128]{1,0:T(8,128)(2,1)S(1)}, u32[]{:S(2)}, u32[]{:S(2)}) collective-permute-start(bf16[320,128]{1,0:T(8,128)(2,1)S(1)} %add_convert_fusion.2), channel_id=1, source_target_pairs={{0,28},{4,24},{8,20},{12,16},{16,12},{20,8},{24,4},{28,0},{1,29},{... | collective-permute-start | bytes 245768 | tf_op jit(solution)/shard_map/ppermute | solution.py:386
  115.7 14.2 %copy-start.3 = (bf16[2048,128]{1,0:T(8,128)(2,1)S(1)}, bf16[2048,128]{1,0:T(8,128)(2,1)}, u32[]{:S(2)}) copy-start(bf16[2048,128]{1,0:T(8,128)(2,1)} %get-tuple-element.40.d0) | copy-start | bytes 1572868
  115.7 14.2 %copy-start = (bf16[1024,128]{1,0:T(8,128)(2,1)S(1)}, bf16[1024,128]{1,0:T(8,128)(2,1)}, u32[]{:S(2)}) copy-start(bf16[1024,128]{1,0:T(8,128)(2,1)} %place.1.x0) | copy-start | bytes 786436
  115.7 22.6 %all-to-all-start.2 = ((bf16[64,24,128]{2,1,0:T(8,128)(2,1)}), bf16[64,24,128]{2,1,0:T(8,128)(2,1)S(1)}, u32[]{:S(2)}, u32[]{:S(2)}) async-start(bf16[64,24,128]{2,1,0:T(8,128)(2,1)} %bitcast.32), calls=%async_computation.2 | async-start | bytes 786432 | tf_op jit(solution)/shard_map/all_to_all | solution.py:459
  125.5 6.4 %copy-start.8 = (bf16[640,128]{1,0:T(8,128)(2,1)}, bf16[640,128]{1,0:T(8,128)(2,1)S(1)}, u32[]{:S(2)}) copy-start(bf16[640,128]{1,0:T(8,128)(2,1)S(1)} %all_gather.3.p0) | copy-start | bytes 491524
  125.5 16.6 %collective-permute-start.16 = (bf16[640,128]{1,0:T(8,128)(2,1)S(1)}, bf16[640,128]{1,0:T(8,128)(2,1)S(1)}, u32[]{:S(2)}, u32[]{:S(2)}) collective-permute-start(bf16[640,128]{1,0:T(8,128)(2,1)S(1)} %all_gather.3.p0), channel_id=1, source_target_pairs={{0,192},{32,224},{64,0},{96,32},{128,64},{160,96},{192,128},{224,1... | collective-permute-start | bytes 491528 | tf_op jit(solution)/shard_map/ppermute | solution.py:386
  128.2 13.9 %collective-permute-start.17 = (bf16[640,128]{1,0:T(8,128)(2,1)S(1)}, bf16[640,128]{1,0:T(8,128)(2,1)S(1)}, u32[]{:S(2)}, u32[]{:S(2)}) collective-permute-start(bf16[640,128]{1,0:T(8,128)(2,1)S(1)} %all_gather.3.p0), channel_id=1, source_target_pairs={{0,64},{32,96},{64,128},{96,160},{128,192},{160,224},{192,0},{224,... | collective-permute-start | bytes 491528 | tf_op jit(solution)/shard_map/ppermute | solution.py:386
  128.2 13.9 %collective-permute-start.18 = (bf16[640,128]{1,0:T(8,128)(2,1)S(1)}, bf16[640,128]{1,0:T(8,128)(2,1)S(1)}, u32[]{:S(2)}, u32[]{:S(2)}) collective-permute-start(bf16[640,128]{1,0:T(8,128)(2,1)S(1)} %all_gather.3.p0), channel_id=1, source_target_pairs={{0,128},{32,160},{64,192},{96,224},{128,0},{160,32},{192,64},{224,... | collective-permute-start | bytes 491528 | tf_op jit(solution)/shard_map/ppermute | solution.py:386
  (9 other events, 9.9 us)
